TPU v7x, 32 devices: a whole 2x2x4 slice. The times are simulated.
32 devices in a mesh: seq: 8 (over z, y), head: 4 (over x, core).
Axes of the slice: x: 2, y: 2, z: 4, core: 2. Of those that a mesh axis runs over, the one named last changes fastest.
Arguments:
- inputs: bfloat16 [4, 4096, 1024], P(None, 'seq'), may hold values from -6 to 6
- cotangent: bfloat16 [4, 4096, 1024], P(None, 'seq'), may hold values from -6 to 6
- lengths: int32 [4], replicated, may hold values from 1024 to 4096, as said below
- norm_gain: float32 [1024], replicated, may hold values from 0.5 to 1.5
- norm_gain_mean: float32 [1024], replicated, may hold values from -40 to 40
- norm_gain_square: float32 [1024], replicated, may hold values from 216.2688 to 861.7984
- proj_zx: float32 [1024, 2, 2048], P(None, None, 'head'), may hold values from -2 to 2
- proj_zx_mean: float32 [1024, 2, 2048], P(None, None, 'head'), may hold values from -24 to 24
- proj_zx_square: float32 [1024, 2, 2048], P(None, None, 'head'), may hold values from 77.66016 to 311.296
- proj_bc: float32 [1024, 256], replicated, may hold values from -0.1875 to 0.1875
- proj_bc_mean: float32 [1024, 256], replicated, may hold values from -24 to 24
- proj_bc_square: float32 [1024, 256], replicated, may hold values from 77.66016 to 311.296
- proj_step: float32 [1024, 32], P(None, 'head'), may hold values from -0.1875 to 0.1875
- proj_step_mean: float32 [1024, 32], P(None, 'head'), may hold values from -24 to 24
- proj_step_square: float32 [1024, 32], P(None, 'head'), may hold values from 77.66016 to 311.296
- conv_inner: float32 [5, 2048], P(None, 'head'), may hold values from -3 to 3
- conv_inner_mean: float32 [5, 2048], P(None, 'head'), may hold values from -24 to 24
- conv_inner_square: float32 [5, 2048], P(None, 'head'), may hold values from 77.66016 to 311.296
- conv_bc: float32 [5, 256], replicated, may hold values from -3 to 3
- conv_bc_mean: float32 [5, 256], replicated, may hold values from -24 to 24
- conv_bc_square: float32 [5, 256], replicated, may hold values from 77.66016 to 311.296
- head_params: float32 [3, 32], P(None, 'head'), may hold values from -16 to 16
- head_params_mean: float32 [3, 32], P(None, 'head'), may hold values from -160 to 160
- head_params_square: float32 [3, 32], P(None, 'head'), may hold values from 3440.64 to 13762.56
- gate_gain: float32 [2048], P('head'), may hold values from 0.5 to 1.5
- gate_gain_mean: float32 [2048], P('head'), may hold values from -40 to 40
- gate_gain_square: float32 [2048], P('head'), may hold values from 216.2688 to 861.7984
- proj_out: float32 [1024, 2048], P(None, 'head'), may hold values from -0.125 to 0.125
- proj_out_mean: float32 [1024, 2048], P(None, 'head'), may hold values from -64 to 64
- proj_out_square: float32 [1024, 2048], P(None, 'head'), may hold values from 552.1408 to 2211.84
Outputs:
- block_out: bfloat16 [4, 4096, 1024], P(None, 'seq')
- input_grad: float32 [4, 4096, 1024], P(None, 'seq')
- norm_gain_mean_new: float32 [1024], replicated
- norm_gain_square_new: float32 [1024], replicated
- norm_gain_new: float32 [1024], replicated
- proj_zx_mean_new: float32 [1024, 2, 2048], P(None, None, 'head')
- proj_zx_square_new: float32 [1024, 2, 2048], P(None, None, 'head')
- proj_zx_new: float32 [1024, 2, 2048], P(None, None, 'head')
- proj_bc_mean_new: float32 [1024, 256], replicated
- proj_bc_square_new: float32 [1024, 256], replicated
- proj_bc_new: float32 [1024, 256], replicated
- proj_step_mean_new: float32 [1024, 32], P(None, 'head')
- proj_step_square_new: float32 [1024, 32], P(None, 'head')
- proj_step_new: float32 [1024, 32], P(None, 'head')
- conv_inner_mean_new: float32 [5, 2048], P(None, 'head')
- conv_inner_square_new: float32 [5, 2048], P(None, 'head')
- conv_inner_new: float32 [5, 2048], P(None, 'head')
- conv_bc_mean_new: float32 [5, 256], replicated
- conv_bc_square_new: float32 [5, 256], replicated
- conv_bc_new: float32 [5, 256], replicated
- head_params_mean_new: float32 [3, 32], P(None, 'head')
- head_params_square_new: float32 [3, 32], P(None, 'head')
- head_params_new: float32 [3, 32], P(None, 'head')
- gate_gain_mean_new: float32 [2048], P('head')
- gate_gain_square_new: float32 [2048], P('head')
- gate_gain_new: float32 [2048], P('head')
- proj_out_mean_new: float32 [1024, 2048], P(None, 'head')
- proj_out_square_new: float32 [1024, 2048], P(None, 'head')
- proj_out_new: float32 [1024, 2048], P(None, 'head')
Inputs may be any that keep to these rules, and one draw needn't show every extreme that they name: `lengths`: one sequence has length 4096 and another has length 1024.
All inputs are finite; a program needn't handle non-finite values.
Results may differ from a plain program's by a relative error of at most 0.012.
The roundings to bfloat16 on the way count: a program that leaves them out, or rounds other values in their place, can miss the bound.
Values may be sent and summed in bfloat16 or wider, within the bound.
No kernel may reach another device: no remote copies, remote signals or barrier semaphores. Data moves between devices by JAX's collectives and lax.ppermute only.
A program may use at most 192 MiB of HBM per device.

v0:
```python
import jax
import jax.numpy as jnp
from jax import lax
from jax.sharding import PartitionSpec as P

INNER = 2048
CONV = 4
BLOCK_LEN = 256
STEP = 7


EPS = 1e-05
BETA_ONE = 0.9
BETA_TWO = 0.95
ADAM_EPS = 1e-08
LEARNING_RATES = (0.6, 0.09, 0.09, 0.09, 0.9, 0.9, 0.9, 0.6, 0.06)
WEIGHT_DECAYS = (0.0, 0.1, 0.1, 0.1, 0.0, 0.0, 0.0, 0.0, 0.1)
HIGHEST_PREC = lax.Precision.HIGHEST


def passed_along(block, axis, distance):
    devices = range(lax.axis_size(axis))
    route = [(i - distance, i) for i in devices if i - distance in devices]
    return lax.ppermute(block, axis, route)


def entering_2(value, axis, combine, identity):
    size, position = (lax.axis_size(axis), lax.axis_index(axis))
    everything = jax.tree.map(lambda part: lax.all_gather(part, axis), value)
    start = jax.tree.map(
        lambda part, zero: jnp.broadcast_to(jnp.asarray(zero, part.dtype), part.shape),
        value,
        identity,
    )

    def entering_turn(k, before):
        reached = k < position
        new = combine(before, jax.tree.map(lambda part: part[k], everything))
        return jax.tree.map(lambda a, b: jnp.where(reached, a, b), new, before)

    return lax.fori_loop(0, size, entering_turn, start)


def carried_in(value, axis, combine, identity):
    size, position = (lax.axis_size(axis), lax.axis_index(axis))
    everything = jax.tree.map(
        lambda part, kind: lax.all_gather(part.astype(kind), axis),
        value,
        jax.tree.map(lambda a: jnp.bfloat16 if a.dtype == jnp.float32 else a.dtype, value),
    )
    start = jax.tree.map(
        lambda part, zero: jnp.broadcast_to(jnp.asarray(zero, part.dtype), part.shape),
        value,
        identity,
    )

    def carried_turn(k, before):
        at = size - 1 - k
        reached = at > position
        new = combine(
            before, jax.tree.map(lambda part, own: part[at].astype(own.dtype), everything, value)
        )
        return jax.tree.map(lambda a, b: jnp.where(reached, a, b), new, before)

    return lax.fori_loop(0, size, carried_turn, start)


def block_step(carried_state, block_inputs):
    x_block, b_block, c_block, decay_block, step_block = block_inputs
    cumulative = jnp.cumsum(decay_block, axis=-1)
    length = cumulative.shape[-1]
    causal = jnp.arange(length)[:, None] >= jnp.arange(length)[None, :]
    between = jnp.where(causal, cumulative[..., :, None] - cumulative[..., None, :], 0.0)
    scores = jnp.einsum("btn,bsn->bts", c_block, b_block, precision=HIGHEST_PREC)
    mixing = jnp.where(causal, jnp.exp(between), 0.0) * scores[:, None] * step_block[..., None, :]
    within = jnp.einsum("bhts,bhsp->bhtp", mixing, x_block, precision=HIGHEST_PREC)
    from_state = jnp.exp(cumulative)[..., None] * jnp.einsum(
        "btn,bhpn->bhtp", c_block, carried_state, precision=HIGHEST_PREC
    )
    total_decay = cumulative[..., -1]
    weighted = x_block * (jnp.exp(total_decay[..., None] - cumulative) * step_block)[..., None]
    next_state = jnp.exp(total_decay)[..., None, None] * carried_state + jnp.einsum(
        "bhsp,bsn->bhpn", weighted, b_block, precision=HIGHEST_PREC
    )
    return (next_state, within + from_state)


def scan_blocks(x_heads, b_values, c_values, log_decay, step_size, first_state):
    batch_size, head_count, token_count, head_width = x_heads.shape
    block_count = token_count // BLOCK_LEN
    x_parts = x_heads.reshape(batch_size, head_count, block_count, BLOCK_LEN, head_width).transpose(
        2, 0, 1, 3, 4
    )
    b_parts = b_values.reshape(batch_size, block_count, BLOCK_LEN, -1).transpose(1, 0, 2, 3)
    c_parts = c_values.reshape(batch_size, block_count, BLOCK_LEN, -1).transpose(1, 0, 2, 3)
    decay_parts = log_decay.reshape(batch_size, head_count, block_count, BLOCK_LEN).transpose(
        2, 0, 1, 3
    )
    step_parts = step_size.reshape(batch_size, head_count, block_count, BLOCK_LEN).transpose(
        2, 0, 1, 3
    )
    final_state, outputs = lax.scan(
        jax.checkpoint(block_step),
        first_state,
        (x_parts, b_parts, c_parts, decay_parts, step_parts),
    )
    outputs = outputs.transpose(1, 2, 0, 3, 4).reshape(
        batch_size, head_count, token_count, head_width
    )
    return (outputs, final_state)


def chain_combine(earlier, subsequent):
    return (earlier[0] * subsequent[0], subsequent[0][..., None, None] * earlier[1] + subsequent[1])


def silu_slope(values):
    sigmoid_part = jax.nn.sigmoid(values)
    return sigmoid_part * (1.0 + values * (1.0 - sigmoid_part))


def adam_update(weight, mean_old, square_old, gradient, step_rate, decay_weight):
    mean_new = BETA_ONE * mean_old + (1.0 - BETA_ONE) * gradient
    square_new = BETA_TWO * square_old + (1.0 - BETA_TWO) * gradient * gradient
    corrected_mean = mean_new / (1.0 - BETA_ONE**STEP)
    corrected_square = square_new / (1.0 - BETA_TWO**STEP)
    weight_new = weight - step_rate * (
        corrected_mean / (jnp.sqrt(corrected_square) + ADAM_EPS) + decay_weight * weight
    )
    return (mean_new, square_new, weight_new)


def shards(
    inputs,
    cotangent,
    lengths,
    norm_gain,
    norm_gain_mean,
    norm_gain_square,
    proj_zx,
    proj_zx_mean,
    proj_zx_square,
    proj_bc,
    proj_bc_mean,
    proj_bc_square,
    proj_step,
    proj_step_mean,
    proj_step_square,
    conv_inner,
    conv_inner_mean,
    conv_inner_square,
    conv_bc,
    conv_bc_mean,
    conv_bc_square,
    head_params,
    head_params_mean,
    head_params_square,
    gate_gain,
    gate_gain_mean,
    gate_gain_square,
    proj_out,
    proj_out_mean,
    proj_out_square,
):
    seq_count, local_len, model_width = inputs.shape
    local_inner = proj_zx.shape[2]
    state_width = proj_bc.shape[1] // 2
    local_heads = proj_step.shape[1]
    head_width = local_inner // local_heads
    positions = lax.axis_index("seq") * local_len + jnp.arange(local_len)
    is_valid = (positions[None, :] < lengths[:, None]).astype(jnp.float32)
    tokens = inputs.astype(jnp.float32)
    inverse_rms = lax.rsqrt(jnp.mean(tokens * tokens, axis=-1, keepdims=True) + EPS)
    unit_tokens = tokens * inverse_rms
    normed = (unit_tokens * norm_gain).astype(jnp.bfloat16)
    zx_weight = proj_zx.astype(jnp.bfloat16)
    bc_weight = proj_bc.astype(jnp.bfloat16)
    step_weight = proj_step.astype(jnp.bfloat16)
    out_weight = proj_out.astype(jnp.bfloat16)
    zx_values = jnp.einsum("btd,dki->btki", normed, zx_weight, preferred_element_type=jnp.float32)
    bc_raw = jnp.einsum("btd,dc->btc", normed, bc_weight, preferred_element_type=jnp.float32)
    raw_step = jnp.einsum("btd,dh->bth", normed, step_weight, preferred_element_type=jnp.float32)
    gate_input = zx_values[:, :, 0]
    mixed_in = jnp.concatenate([zx_values[:, :, 1], bc_raw], axis=-1).astype(jnp.bfloat16)
    edge_in = passed_along(mixed_in[:, local_len - CONV + 1 :], "seq", 1)
    padded = jnp.concatenate([edge_in, mixed_in], axis=1)
    conv_weight = jnp.concatenate([conv_inner, conv_bc], axis=-1)
    convolved = conv_weight[CONV] + jnp.zeros(mixed_in.shape, jnp.float32)
    for tap_index in range(CONV):
        convolved = (
            convolved + conv_weight[tap_index] * padded[:, tap_index : tap_index + local_len]
        )
    activated = jax.nn.silu(convolved).astype(jnp.bfloat16)
    x_heads = (
        activated[..., :local_inner]
        .astype(jnp.float32)
        .reshape(seq_count, local_len, local_heads, head_width)
        .transpose(0, 2, 1, 3)
    )
    b_float = activated[..., local_inner : local_inner + state_width].astype(jnp.float32)
    c_float = activated[..., local_inner + state_width :].astype(jnp.float32)
    decay_log = head_params[0]
    step_bias = head_params[1]
    skip_gain = head_params[2]
    step_size = jax.nn.softplus(raw_step + step_bias)
    log_decay = -step_size * jnp.exp(decay_log)
    decay_heads = log_decay.transpose(0, 2, 1)
    step_heads = step_size.transpose(0, 2, 1)
    running = jnp.cumsum(decay_heads, axis=-1)
    device_decay = running[..., -1]
    local_state = jnp.einsum(
        "bhsp,bsn->bhpn",
        x_heads * (jnp.exp(device_decay[..., None] - running) * step_heads)[..., None],
        b_float,
        precision=HIGHEST_PREC,
    )
    unit_decay = jnp.exp(device_decay)
    identity = (jnp.ones_like(unit_decay), jnp.zeros_like(local_state))
    carried_decay, entering = entering_2((unit_decay, local_state), "seq", chain_combine, identity)
    (outputs, final_state), pullback = jax.vjp(
        scan_blocks, x_heads, b_float, c_float, decay_heads, step_heads, entering
    )
    outputs = outputs + skip_gain[None, :, None, None] * x_heads
    scanned = outputs.transpose(0, 2, 1, 3).reshape(seq_count, local_len, local_inner)
    gate_act = jax.nn.silu(gate_input)
    gated_values = scanned * gate_act
    square_sum = jnp.sum(gated_values * gated_values, axis=-1)
    scaled = (gated_values * gate_gain).astype(jnp.bfloat16)
    partial_out = jnp.einsum("bti,di->btd", scaled, out_weight, preferred_element_type=jnp.float32)
    projected, square_total = lax.psum((partial_out, square_sum), "head")
    out_scale = lax.rsqrt(square_total / INNER + EPS)
    block_out = (tokens + out_scale[..., None] * projected).astype(jnp.bfloat16)
    out_cotangent = cotangent.astype(jnp.float32) * is_valid[..., None]
    proj_grad = (out_scale[..., None] * out_cotangent).astype(jnp.bfloat16)
    scale_grad = jnp.sum(out_cotangent * projected, axis=-1)
    square_grad = -0.5 * scale_grad * out_scale * out_scale * out_scale / INNER
    out_weight_grad = jnp.einsum(
        "btd,bti->di", proj_grad, scaled, preferred_element_type=jnp.float32
    )
    scaled_grad = jnp.einsum(
        "btd,di->bti", proj_grad, out_weight, preferred_element_type=jnp.float32
    )
    gate_gain_grad = jnp.sum(scaled_grad * gated_values, axis=(0, 1))
    gated_grad = scaled_grad * gate_gain + 2.0 * gated_values * square_grad[..., None]
    scanned_grad = gated_grad * gate_act
    gate_grad = gated_grad * scanned * silu_slope(gate_input)
    output_heads = scanned_grad.reshape(seq_count, local_len, local_heads, head_width).transpose(
        0, 2, 1, 3
    )
    skip_grad = jnp.sum(output_heads * x_heads, axis=(0, 2, 3))
    local_back = jnp.einsum(
        "bhtp,btn->bhpn",
        output_heads * jnp.exp(running)[..., None],
        c_float,
        precision=HIGHEST_PREC,
    )
    reverse_decay, leaving_grad = carried_in(
        (unit_decay, local_back), "seq", chain_combine, identity
    )
    x_grad, b_grad, c_grad, decay_grad, step_grad, entering_grad = pullback(
        (output_heads, leaving_grad)
    )
    x_grad = x_grad + skip_gain[None, :, None, None] * output_heads
    bc_total = lax.psum(jnp.concatenate([b_grad, c_grad], axis=-1), "head")
    x_flat_grad = x_grad.transpose(0, 2, 1, 3).reshape(seq_count, local_len, local_inner)
    activated_grad = jnp.concatenate([x_flat_grad, bc_total], axis=-1)
    convolved_grad = activated_grad * silu_slope(convolved)
    channels = convolved_grad.shape[-1]
    tap_grads = []
    padded_grad = jnp.zeros((seq_count, local_len + CONV - 1, channels), jnp.float32)
    for tap_index in range(CONV):
        tap_grads.append(
            jnp.sum(convolved_grad * padded[:, tap_index : tap_index + local_len], axis=(0, 1))
        )
        padded_grad = padded_grad + jnp.pad(
            conv_weight[tap_index] * convolved_grad,
            ((0, 0), (tap_index, CONV - 1 - tap_index), (0, 0)),
        )
    tap_grads.append(jnp.sum(convolved_grad, axis=(0, 1)))
    conv_weight_grad = jnp.stack(tap_grads)
    edge_grad = passed_along(padded_grad[:, : CONV - 1], "seq", -1)
    mixed_grad = padded_grad[:, CONV - 1 :] + jnp.pad(
        edge_grad, ((0, 0), (local_len - CONV + 1, 0), (0, 0))
    )
    zx_in_grad = jnp.stack([gate_grad, mixed_grad[..., :local_inner]], axis=2).astype(jnp.bfloat16)
    bc_in_grad = mixed_grad[..., local_inner:].astype(jnp.bfloat16)
    decay_token_grad = decay_grad.transpose(0, 2, 1)
    step_total = step_grad.transpose(0, 2, 1) - jnp.exp(decay_log) * decay_token_grad
    pre_grad = step_total * jax.nn.sigmoid(raw_step + step_bias)
    head_grad = jnp.stack(
        [
            jnp.sum(decay_token_grad * log_decay, axis=(0, 1)),
            jnp.sum(pre_grad, axis=(0, 1)),
            skip_grad,
        ]
    )
    step_in_grad = pre_grad.astype(jnp.bfloat16)
    zx_weight_grad = jnp.einsum(
        "btd,btki->dki", normed, zx_in_grad, preferred_element_type=jnp.float32
    )
    bc_weight_grad = jnp.einsum(
        "btd,btc->dc", normed, bc_in_grad, preferred_element_type=jnp.float32
    )
    step_weight_grad = jnp.einsum(
        "btd,bth->dh", normed, step_in_grad, preferred_element_type=jnp.float32
    )
    normed_partial = jnp.einsum(
        "btki,dki->btd", zx_in_grad, zx_weight, preferred_element_type=jnp.float32
    )
    normed_partial = normed_partial + jnp.einsum(
        "bth,dh->btd", step_in_grad, step_weight, preferred_element_type=jnp.float32
    )
    normed_grad = lax.psum(normed_partial, "head")
    normed_grad = normed_grad + jnp.einsum(
        "btc,dc->btd", bc_in_grad, bc_weight, preferred_element_type=jnp.float32
    )
    norm_gain_grad = jnp.sum(normed_grad * unit_tokens, axis=(0, 1))
    unit_grad = normed_grad * norm_gain
    input_grad = out_cotangent + inverse_rms * (
        unit_grad - unit_tokens * jnp.mean(unit_grad * unit_tokens, axis=-1, keepdims=True)
    )
    conv_inner_grad = conv_weight_grad[:, :local_inner]
    conv_bc_grad = conv_weight_grad[:, local_inner:]
    summed_grads = lax.psum(
        (
            norm_gain_grad,
            zx_weight_grad,
            bc_weight_grad,
            step_weight_grad,
            conv_inner_grad,
            conv_bc_grad,
            head_grad,
            gate_gain_grad,
            out_weight_grad,
        ),
        "seq",
    )
    params = (
        norm_gain,
        proj_zx,
        proj_bc,
        proj_step,
        conv_inner,
        conv_bc,
        head_params,
        gate_gain,
        proj_out,
    )
    means = (
        norm_gain_mean,
        proj_zx_mean,
        proj_bc_mean,
        proj_step_mean,
        conv_inner_mean,
        conv_bc_mean,
        head_params_mean,
        gate_gain_mean,
        proj_out_mean,
    )
    squares = (
        norm_gain_square,
        proj_zx_square,
        proj_bc_square,
        proj_step_square,
        conv_inner_square,
        conv_bc_square,
        head_params_square,
        gate_gain_square,
        proj_out_square,
    )
    results = [block_out, input_grad]
    for weight, mean_old, square_old, gradient, step_rate, decay_weight in zip(
        params, means, squares, summed_grads, LEARNING_RATES, WEIGHT_DECAYS
    ):
        results.extend(adam_update(weight, mean_old, square_old, gradient, step_rate, decay_weight))
    return tuple(results)


def solution(mesh):
    in_specs = (
        P(None, "seq", None),
        P(None, "seq", None),
        P(),
        P(),
        P(),
        P(),
        P(None, None, "head"),
        P(None, None, "head"),
        P(None, None, "head"),
        P(),
        P(),
        P(),
        P(None, "head"),
        P(None, "head"),
        P(None, "head"),
        P(None, "head"),
        P(None, "head"),
        P(None, "head"),
        P(),
        P(),
        P(),
        P(None, "head"),
        P(None, "head"),
        P(None, "head"),
        P("head"),
        P("head"),
        P("head"),
        P(None, "head"),
        P(None, "head"),
        P(None, "head"),
    )
    out_specs = (
        P(None, "seq", None),
        P(None, "seq", None),
        P(),
        P(),
        P(),
        P(None, None, "head"),
        P(None, None, "head"),
        P(None, None, "head"),
        P(),
        P(),
        P(),
        P(None, "head"),
        P(None, "head"),
        P(None, "head"),
        P(None, "head"),
        P(None, "head"),
        P(None, "head"),
        P(),
        P(),
        P(),
        P(None, "head"),
        P(None, "head"),
        P(None, "head"),
        P("head"),
        P("head"),
        P("head"),
        P(None, "head"),
        P(None, "head"),
        P(None, "head"),
    )
    return jax.shard_map(shards, mesh=mesh, in_specs=in_specs, out_specs=out_specs, check_vma=False)
```

profile of v0, /device:TPU:0, one launch (start us, length us, event | category | flops | bytes accessed | tf_op | source)
XLA Modules:
  0.0 1332.9 jit_solution(9247115032727136338)
XLA Ops:
  12.1 4.6 copy.337
  16.7 7.5 fusion.117
  24.5 4.9 copy-done.10
  33.6 5.0 collective-permute-start
  38.7 3.5 fusion.180
  43.5 3.8 negate_multiply_fusion
  48.8 4.5 reduce-window.68
  65.4 7.2 multiply_convert_fusion.1
  83.2 27.1 %all-gather = f32[32,8,1]{1,2,0:T(1,128)S(1)} all-gather(f32[4,8,1]{1,2,0:T(1,128)S(1)} %bitcast.543), channel_id=2, replica_groups=mesh['seq'=8,'head'=4] {'seq'}, dimensions={0}, use_global_device_ids=true | all-gather | bytes 1152 | tf_op jit(solution)/shard_map/all_gather | solution.py:29
  110.4 5.9 reshape.570
  116.3 4.9 copy.348
  134.4 71.2 %all-gather.7.cloned.1.call-done = f32[32,8,64,128]{3,2,1,0:T(8,128)} async-done(((f32[4,8,64,128]{3,2,1,0:T(8,128)}), f32[32,8,64,128]{3,2,1,0:T(8,128)}) %all-gather.7.cloned.1.call-update) | async-done | bytes 8388624 | tf_op jit(solution)/shard_map/all_gather | solution.py:29
  205.6 12.0 while.74
  220.1 51.7 %while.73 = (s32[]{:T(128)}, f32[4,8,64,128]{3,2,1,0:T(8,128)S(1)}, f32[2,4,8,256,64]{3,4,2,1,0:T(8,128)}, f32[2,4,8,64,128]{4,3,2,1,0:T(8,128)S(1)}, f32[2,4,8,...) while((s32[]{:T(128)}, f32[4,8,64,128]{3,2,1,0:T(8,128)S(1)}, ...), condition=%wide.region_8.9_spmd.clone.clone, body=%wide.region_5.8_spmd.clone.clone.sunk | while | flops 3637526528 | bytes 70853848 | solution.py:102
  225.2 12.2 fusion.328
  251.1 12.2 fusion.328
  277.6 3.4 fusion.127
  281.0 6.2 psum.91
  287.3 9.5 multiply_reduce_fusion.4
  298.9 5.8 fusion.155
  306.3 149.4 %all-reduce.13.cloned.1.call-done = f32[4,512,1024]{2,1,0:T(8,128)} async-done(((f32[4,512,1024]{2,1,0:T(8,128)}), f32[4,512,1024]{2,1,0:T(8,128)}) %all-reduce.13.cloned.1.call-update) | async-done | bytes 8388624 | tf_op jit(solution)/shard_map/psum | solution.py:230
  455.7 8.9 multiply_reduce_fusion.3
  466.7 5.4 fusion.120
  477.2 26.6 %all-gather.3 = bf16[32,8,1]{1,2,0:T(2,128)(2,1)S(1)} all-gather(bf16[4,8,1]{1,2,0:T(2,128)(2,1)S(1)} %copy.352), channel_id=5, replica_groups=mesh['seq'=8,'head'=4] {'seq'}, dimensions={0}, use_global_device_ids=true | all-gather | bytes 576 | tf_op jit(solution)/shard_map/all_gather | solution.py:47
  503.8 4.9 convert_bitcast_fusion.2
  508.8 6.1 reshape.577
  514.8 36.2 %all-gather.9.cloned.1.call-done = bf16[32,8,64,128]{3,2,1,0:T(8,128)(2,1)} async-done(((bf16[4,8,64,128]{3,2,1,0:T(8,128)(2,1)}), bf16[32,8,64,128]{3,2,1,0:T(8,128)(2,1)}) %all-gather.9.cloned.1.call-update) | async-done | bytes 4194320 | tf_op jit(solution)/shard_map/all_gather | solution.py:47
  551.0 10.8 while.75
  567.7 202.1 %while.72 = (s32[]{:T(128)}, f32[4,8,64,128]{3,2,1,0:T(8,128)S(1)}, f32[2,4,8,256,64]{3,4,2,1,0:T(8,128)}, f32[2,4,256,128]{3,2,1,0:T(8,128)}, f32[2,4,256,128]{...) while((s32[]{:T(128)}, f32[4,8,64,128]{3,2,1,0:T(8,128)S(1)}, ...), condition=%wide.region_28.29_spmd, body=%wide.region_15.28_spmd.sunk | while | flops 8505679872 | bytes 122826248 | solution.py:102
  568.1 4.5 constant_dynamic-slice_fusion.4
  585.7 15.8 %fusion.304 = (f32[4,8,256]{2,1,0:T(8,128)S(1)}, f32[4,8,256]{2,1,0:T(8,128)S(1)}, f32[4,8,256]{2,1,0:T(8,128)}, f32[4,256,256]{2,1,0:T(8,128)}) fusion(f32[4,8,256]{2,1,0:T(8,128)S(1)} %copy.455, f32[4,256,256]{2,1,0:T(8,128)} %fusion.302, f32[4,8,256]{2,1,0:T(8,128)S(1)} %add_bitcast_fusion.4, pred[256,256]{1,0:T(8,128)(4,1)S(1)} %iota_compare_fusion.3, ...), kind=kOutput, calls=%fused_computation.10.clone.1 | convolution fusion | flops 1641783296 | bytes 6520832 | tf_op jit(solution)/shard_map/transpose(jvp())/while/body/eval_jaxpr/checkpoint/bhts,bhsp->bhtp/dot_general | solution.py:76
  624.4 9.9 reduce-window.86
  635.8 4.8 fusion.312
  644.8 5.2 fusion.310
  650.0 3.8 fusion.311
  653.8 9.1 bitcast_dynamic-update-slice_fusion.8
  665.8 4.5 constant_dynamic-slice_fusion.4
  683.4 15.8 %fusion.304 = (f32[4,8,256]{2,1,0:T(8,128)S(1)}, f32[4,8,256]{2,1,0:T(8,128)S(1)}, f32[4,8,256]{2,1,0:T(8,128)}, f32[4,256,256]{2,1,0:T(8,128)}) fusion(f32[4,8,256]{2,1,0:T(8,128)S(1)} %copy.455, f32[4,256,256]{2,1,0:T(8,128)} %fusion.302, f32[4,8,256]{2,1,0:T(8,128)S(1)} %add_bitcast_fusion.4, pred[256,256]{1,0:T(8,128)(4,1)S(1)} %iota_compare_fusion.3, ...), kind=kOutput, calls=%fused_computation.10.clone.1 | convolution fusion | flops 1641783296 | bytes 6520832 | tf_op jit(solution)/shard_map/transpose(jvp())/while/body/eval_jaxpr/checkpoint/bhts,bhsp->bhtp/dot_general | solution.py:76
  722.1 9.9 reduce-window.86
  733.5 4.8 fusion.312
  742.5 5.2 fusion.310
  747.7 3.7 fusion.311
  751.5 9.1 bitcast_dynamic-update-slice_fusion.8
  781.7 4.8 copy.420
  786.8 5.6 fusion.178
  796.5 30.9 %all-reduce.15.cloned.1.call-done = f32[4,512,256]{1,2,0:T(8,128)} async-done(((f32[4,512,256]{1,2,0:T(8,128)}), f32[4,512,256]{1,2,0:T(8,128)}) %all-reduce.15.cloned.1.call-update) | async-done | bytes 2097168 | tf_op jit(solution)/shard_map/psum | solution.py:264
  827.4 14.1 %fusion.198 = (f32[768]{0:T(1024)S(1)}, f32[768]{0:T(1024)S(1)}, f32[768]{0:T(1024)S(1)}, f32[768]{0:T(1024)S(1)}, f32[768]{0:T(1024)S(1)}, /*index=5*/f32[4,512,768]{1,2,0:T(8,128)}) fusion(bf16[4,512,256]{1,2,0:T(8,128)(2,1)S(1)} %copy-done.31, bf16[4,512,512]{1,2,0:T(8,128)(2,1)S(1)} %copy-done.18, bf16[4,515,768]{1,2,0:T(8,128)(2,1)} %copy-done.5, ...), kind=kLoop, calls=%fused_computation.334 | loop fusion | flops 39317760 | bytes 31472640 | tf_op jit(solution)/shard_map/reduce_sum | solution.py:279
  841.5 5.5 broadcast_multiply_fusion.3
  857.6 13.3 pad_add_fusion
  872.5 5.3 fusion.115
  880.8 9.3 bitcast_add_fusion.3
  890.8 8.0 fusion.146
  901.8 7.1 fusion.137
  909.0 3.6 multiply_reduce_fusion.5
  914.5 129.9 %all-reduce.17.cloned.1.call-done = f32[4,512,1024]{2,1,0:T(8,128)} async-done(((f32[4,512,1024]{2,1,0:T(8,128)}), f32[4,512,1024]{2,1,0:T(8,128)}) %all-reduce.17.cloned.1.call-update) | async-done | bytes 8388624 | tf_op jit(solution)/shard_map/psum | solution.py:313
  1044.4 9.0 fusion.104
  1053.4 40.4 %all-reduce.6 = (f32[1024]{0:T(1024)S(1)}, f32[1024,8]{0,1:T(8,128)S(1)}, f32[5,512]{1,0:T(8,128)S(1)}, f32[5,256]{1,0:T(8,128)S(1)}, f32[3,8]{1,0:T(4,128)S(1)}, /*index=5*/f32[512]{0:T(512)S(1)}) all-reduce(f32[1024]{0:T(1024)S(1)} %get-tuple-element.1069, ...), channel_id=1, replica_groups=mesh['seq'=8,'head'=4] {'seq'}, use_global_device_ids=true, to_apply=%region_33.34 | all-reduce | flops 13592 | bytes 108736 | tf_op jit(solution)/shard_map/psum | solution.py:324
  1097.6 10.3 fusion.103
  1107.9 187.3 %all-reduce.19.cloned.1.call-done = (f32[1024,2,512]{2,0,1:T(8,128)}, f32[1024,256]{1,0:T(8,128)}, f32[1024,512]{1,0:T(8,128)}) async-done(((f32[1024,2,512]{2,0,1:T(8,128)}, f32[1024,256]{1,0:T(8,128)}, f32[1024,512]{1,0:T(8,128)}), (f32[1024,2,512]{2,0,1:T(8,128)}, f32[1024,256]{1,0:T(8,128)}, f32[1024,512]{1,0:T(8,128)})) %all-reduce.19.cloned.1.call-update) | async-done | bytes 7340048 | tf_op jit(solution)/shard_map/psum | solution.py:324
  1295.1 8.8 multiply_subtract_fusion
  1303.9 5.2 copy.380
  1309.2 5.2 copy.381
  1314.4 5.2 copy.382
  1319.8 3.9 multiply_subtract_fusion.1
  (478 shorter events, 254.0 us)
Async XLA Ops:
  7.2 198.4 %all-gather.7.cloned.1.call-start = ((), (), s32[]{:S(2)}) async-start(), calls=%async_computation.3 | async-start | bytes 9437184 | tf_op jit(solution)/shard_map/all_gather | solution.py:29
  10.7 27.9 %copy-start.60 = (f32[4,512]{1,0:T(4,128)}, f32[4,512]{1,0:T(4,128)S(1)}, u32[]{:S(2)}) copy-start(f32[4,512]{1,0:T(4,128)S(1)} %add_rsqrt_fusion.1) | copy-start | bytes 24580
  16.7 7.8 copy-start.38
  29.4 35.9 %copy-start.17 = (bf16[4,512,512]{1,2,0:T(8,128)(2,1)}, bf16[4,512,512]{1,2,0:T(8,128)(2,1)S(1)}, u32[]{:S(2)}) copy-start(bf16[4,512,512]{1,2,0:T(8,128)(2,1)S(1)} %fusion.141) | copy-start | bytes 6291460
  30.9 34.4 %copy-start.30 = (bf16[4,512,256]{1,2,0:T(8,128)(2,1)}, bf16[4,512,256]{1,2,0:T(8,128)(2,1)S(1)}, u32[]{:S(2)}) copy-start(bf16[4,512,256]{1,2,0:T(8,128)(2,1)S(1)} %convolution_convert_fusion) | copy-start | bytes 3145732
  30.9 7.7 copy-start.58
  33.6 27.1 %collective-permute-start = (bf16[4,3,768]{2,0,1:T(4,128)(2,1)S(1)}, bf16[4,3,768]{2,0,1:T(4,128)(2,1)S(1)}, u32[]{:S(2)}, u32[]{:S(2)}) collective-permute-start(bf16[4,3,768]{2,0,1:T(4,128)(2,1)S(1)} %copy.340), channel_id=1, source_target_pairs={{0,4},{4,8},{8,12},{12,16},{16,20},{20,24},{24,28},{1,5},{5,9},{9,... | collective-permute-start | bytes 55304 | tf_op jit(solution)/shard_map/ppermute | solution.py:24
  42.1 13.5 %copy-start.80 = (f32[5,256]{1,0:T(8,128)S(1)}, f32[5,256]{1,0:T(8,128)}, u32[]{:S(2)}) copy-start(f32[5,256]{1,0:T(8,128)} %param.56) | copy-start | bytes 15364
  43.5 232.6 %copy-start.90 = (f32[8]{0:T(128)}, f32[8]{0:T(128)S(1)}, u32[]{:S(2)}) copy-start(f32[8]{0:T(128)S(1)} %get-tuple-element.1232) | copy-start | bytes 100
  80.1 375.6 %all-reduce.13.cloned.1.call-start = ((), (), s32[]{:S(2)}) async-start(), calls=%async_computation | async-start | bytes 16777216 | tf_op jit(solution)/shard_map/psum | solution.py:230
  80.2 30.2 %copy-start.103 = (s32[4]{0:T(128)S(1)}, s32[4]{0:T(128)}, u32[]{:S(2)}) copy-start(s32[4]{0:T(128)} %param.40) | copy-start | bytes 52
  110.4 345.3 %copy-start.62 = (f32[4,512]{1,0:T(4,128)}, f32[4,512]{1,0:T(4,128)S(1)}, u32[]{:S(2)}) copy-start(f32[4,512]{1,0:T(4,128)S(1)} %compare_convert_fusion) | copy-start | bytes 24580
  225.2 12.2 copy-start.23
  251.0 12.2 copy-start.23
  287.3 168.4 %copy-start.76 = (f32[4,512]{1,0:T(4,128)}, f32[4,512]{1,0:T(4,128)S(1)}, u32[]{:S(2)}) copy-start(f32[4,512]{1,0:T(4,128)S(1)} %add_rsqrt_fusion) | copy-start | bytes 24580
  287.3 11.6 copy-start.35
  287.3 11.6 copy-start.82
  304.7 246.3 %all-gather.9.cloned.1.call-start = ((), (), s32[]{:S(2)}) async-start(), calls=%async_computation.4 | async-start | bytes 4718592 | tf_op jit(solution)/shard_map/all_gather | solution.py:47
  455.7 9.0 copy-start.28
  455.7 9.8 copy-start.29
  455.7 11.0 copy-start.41
  477.1 350.2 %all-reduce.15.cloned.1.call-start = ((), (), s32[]{:S(2)}) async-start(), calls=%async_computation.1 | async-start | bytes 4194304 | tf_op jit(solution)/shard_map/psum | solution.py:264
  585.7 15.8 %copy-start = (f32[4,8,256,64]{2,3,1,0:T(8,128)S(1)}, f32[4,8,256,64]{2,3,1,0:T(8,128)}, u32[]{:S(2)}) copy-start(f32[4,8,256,64]{2,3,1,0:T(8,128)} %get-tuple-element.1464) | copy-start | bytes 6291460 | tf_op jit(solution)/shard_map/transpose(jvp())/while
  585.7 15.8 %copy-start.2 = (f32[4,256,128]{2,1,0:T(8,128)S(1)}, f32[4,256,128]{2,1,0:T(8,128)}, u32[]{:S(2)}) copy-start(f32[4,256,128]{2,1,0:T(8,128)} %get-tuple-element.1462) | copy-start | bytes 1572868 | tf_op jit(solution)/shard_map/transpose(jvp())/while
  620.0 14.4 %copy-start.54 = (f32[2,4,8,256]{3,2,1,0:T(8,128)S(1)}, f32[2,4,8,256]{3,2,1,0:T(8,128)}, u32[]{:S(2)}) copy-start(f32[2,4,8,256]{3,2,1,0:T(8,128)} %get-tuple-element.1607) | copy-start | bytes 196612 | tf_op jit(solution)/shard_map/transpose(jvp())/while
  634.6 15.4 %copy-start.55 = (f32[2,4,8,256]{3,2,1,0:T(8,128)}, f32[2,4,8,256]{3,2,1,0:T(8,128)S(1)}, u32[]{:S(2)}) copy-start(f32[2,4,8,256]{3,2,1,0:T(8,128)S(1)} %bitcast_dynamic-update-slice_fusion.9) | copy-start | bytes 196612 | tf_op jit(solution)/shard_map/transpose(jvp())/while
  644.8 9.0 copy-start.16
  644.8 9.0 copy-start.20
  653.8 9.7 copy-start.1
  683.4 15.8 %copy-start = (f32[4,8,256,64]{2,3,1,0:T(8,128)S(1)}, f32[4,8,256,64]{2,3,1,0:T(8,128)}, u32[]{:S(2)}) copy-start(f32[4,8,256,64]{2,3,1,0:T(8,128)} %get-tuple-element.1464) | copy-start | bytes 6291460 | tf_op jit(solution)/shard_map/transpose(jvp())/while
  683.4 15.8 %copy-start.2 = (f32[4,256,128]{2,1,0:T(8,128)S(1)}, f32[4,256,128]{2,1,0:T(8,128)}, u32[]{:S(2)}) copy-start(f32[4,256,128]{2,1,0:T(8,128)} %get-tuple-element.1462) | copy-start | bytes 1572868 | tf_op jit(solution)/shard_map/transpose(jvp())/while
  717.8 14.4 %copy-start.54 = (f32[2,4,8,256]{3,2,1,0:T(8,128)S(1)}, f32[2,4,8,256]{3,2,1,0:T(8,128)}, u32[]{:S(2)}) copy-start(f32[2,4,8,256]{3,2,1,0:T(8,128)} %get-tuple-element.1607) | copy-start | bytes 196612 | tf_op jit(solution)/shard_map/transpose(jvp())/while
  732.3 15.4 %copy-start.55 = (f32[2,4,8,256]{3,2,1,0:T(8,128)}, f32[2,4,8,256]{3,2,1,0:T(8,128)S(1)}, u32[]{:S(2)}) copy-start(f32[2,4,8,256]{3,2,1,0:T(8,128)S(1)} %bitcast_dynamic-update-slice_fusion.9) | copy-start | bytes 196612 | tf_op jit(solution)/shard_map/transpose(jvp())/while
  742.5 9.0 copy-start.16
  742.5 9.0 copy-start.20
  751.5 9.7 copy-start.1
  777.6 266.8 %all-reduce.17.cloned.1.call-start = ((), (), s32[]{:S(2)}) async-start(), calls=%async_computation.2 | async-start | bytes 16777216 | tf_op jit(solution)/shard_map/psum | solution.py:313
  793.3 34.0 %copy-start.18 = (bf16[4,512,512]{1,2,0:T(8,128)(2,1)S(1)}, bf16[4,512,512]{1,2,0:T(8,128)(2,1)}, u32[]{:S(2)}) copy-start(bf16[4,512,512]{1,2,0:T(8,128)(2,1)} %copy-done.17) | copy-start | bytes 6291460
  793.3 34.0 %copy-start.31 = (bf16[4,512,256]{1,2,0:T(8,128)(2,1)S(1)}, bf16[4,512,256]{1,2,0:T(8,128)(2,1)}, u32[]{:S(2)}) copy-start(bf16[4,512,256]{1,2,0:T(8,128)(2,1)} %copy-done.30) | copy-start | bytes 3145732
  827.4 14.1 %copy-start.69 = (f32[768]{0:T(1024)S(1)}, f32[768]{0:T(1024)}, u32[]{:S(2)}) copy-start(f32[768]{0:T(1024)} %copy-done.68) | copy-start | bytes 9220
  827.4 14.1 %copy-start.71 = (f32[768]{0:T(1024)S(1)}, f32[768]{0:T(1024)}, u32[]{:S(2)}) copy-start(f32[768]{0:T(1024)} %copy-done.70) | copy-start | bytes 9220
  827.4 14.1 %copy-start.73 = (f32[768]{0:T(1024)S(1)}, f32[768]{0:T(1024)}, u32[]{:S(2)}) copy-start(f32[768]{0:T(1024)} %copy-done.72) | copy-start | bytes 9220
  827.4 14.1 %copy-start.75 = (f32[768]{0:T(1024)S(1)}, f32[768]{0:T(1024)}, u32[]{:S(2)}) copy-start(f32[768]{0:T(1024)} %copy-done.74) | copy-start | bytes 9220
  856.3 14.6 %collective-permute-start.1 = (f32[4,3,768]{2,0,1:T(4,128)S(1)}, f32[4,3,768]{2,0,1:T(4,128)S(1)}, u32[]{:S(2)}, u32[]{:S(2)}) collective-permute-start(f32[4,3,768]{2,0,1:T(4,128)S(1)} %copy.361), channel_id=1, source_target_pairs={{4,0},{8,4},{12,8},{16,12},{20,16},{24,20},{28,24},{5,1},{9,5},{13... | collective-permute-start | bytes 110600 | tf_op jit(solution)/shard_map/ppermute | solution.py:24
  890.1 8.7 copy-start.61
  890.1 8.7 copy-start.67
  890.1 405.0 %all-reduce.19.cloned.1.call-start = ((), (), s32[]{:S(2)}) async-start(), calls=%async_computation.5 | async-start | bytes 14680064 | tf_op jit(solution)/shard_map/psum | solution.py:324
  890.8 8.0 copy-start.11
  914.3 139.1 %copy-start.102 = (f32[512]{0:T(512)S(1)}, f32[512]{0:T(512)}, u32[]{:S(2)}) copy-start(f32[512]{0:T(512)} %get-tuple-element.1194) | copy-start | bytes 6148
  914.3 179.5 %copy-start.98 = (f32[512]{0:T(512)S(1)}, f32[512]{0:T(512)}, u32[]{:S(2)}) copy-start(f32[512]{0:T(512)} %param.64) | copy-start | bytes 6148
  914.4 179.5 %copy-start.99 = (f32[512]{0:T(512)S(1)}, f32[512]{0:T(512)}, u32[]{:S(2)}) copy-start(f32[512]{0:T(512)} %param.63) | copy-start | bytes 6148
  914.4 180.1 %copy-start.89 = (f32[3,8]{1,0:T(4,128)S(1)}, f32[3,8]{1,0:T(4,128)}, u32[]{:S(2)}) copy-start(f32[3,8]{1,0:T(4,128)} %param.59) | copy-start | bytes 292
  914.4 180.1 %copy-start.100 = (f32[3,8]{1,0:T(4,128)S(1)}, f32[3,8]{1,0:T(4,128)}, u32[]{:S(2)}) copy-start(f32[3,8]{1,0:T(4,128)} %param.61) | copy-start | bytes 292
  914.4 180.0 %copy-start.101 = (f32[3,8]{1,0:T(4,128)S(1)}, f32[3,8]{1,0:T(4,128)}, u32[]{:S(2)}) copy-start(f32[3,8]{1,0:T(4,128)} %param.60) | copy-start | bytes 292
  914.4 180.6 %copy-start.96 = (f32[1024]{0:T(1024)S(1)}, f32[1024]{0:T(1024)}, u32[]{:S(2)}) copy-start(f32[1024]{0:T(1024)} %param.43) | copy-start | bytes 12292
  914.4 180.6 %copy-start.97 = (f32[1024]{0:T(1024)S(1)}, f32[1024]{0:T(1024)}, u32[]{:S(2)}) copy-start(f32[1024]{0:T(1024)} %param.42) | copy-start | bytes 12292
  914.4 181.3 %copy-start.81 = (f32[5,256]{1,0:T(8,128)S(1)}, f32[5,256]{1,0:T(8,128)}, u32[]{:S(2)}) copy-start(f32[5,256]{1,0:T(8,128)} %param.56) | copy-start | bytes 15364
  914.4 181.2 %copy-start.86 = (f32[5,256]{1,0:T(8,128)S(1)}, f32[5,256]{1,0:T(8,128)}, u32[]{:S(2)}) copy-start(f32[5,256]{1,0:T(8,128)} %param.58) | copy-start | bytes 15364
  914.5 181.2 %copy-start.87 = (f32[5,256]{1,0:T(8,128)S(1)}, f32[5,256]{1,0:T(8,128)}, u32[]{:S(2)}) copy-start(f32[5,256]{1,0:T(8,128)} %param.57) | copy-start | bytes 15364
  914.5 181.9 %copy-start.65 = (f32[5,512]{1,0:T(8,128)S(1)}, f32[5,512]{1,0:T(8,128)}, u32[]{:S(2)}) copy-start(f32[5,512]{1,0:T(8,128)} %param.53) | copy-start | bytes 30724
  914.5 181.8 %copy-start.84 = (f32[5,512]{1,0:T(8,128)S(1)}, f32[5,512]{1,0:T(8,128)}, u32[]{:S(2)}) copy-start(f32[5,512]{1,0:T(8,128)} %param.55) | copy-start | bytes 30724
  914.5 181.8 %copy-start.85 = (f32[5,512]{1,0:T(8,128)S(1)}, f32[5,512]{1,0:T(8,128)}, u32[]{:S(2)}) copy-start(f32[5,512]{1,0:T(8,128)} %param.54) | copy-start | bytes 30724
  914.5 182.5 %copy-start.78 = (f32[1024,8]{0,1:T(8,128)S(1)}, f32[1024,8]{0,1:T(8,128)}, u32[]{:S(2)}) copy-start(f32[1024,8]{0,1:T(8,128)} %param.52) | copy-start | bytes 98308
  914.5 182.5 %copy-start.79 = (f32[1024,8]{0,1:T(8,128)S(1)}, f32[1024,8]{0,1:T(8,128)}, u32[]{:S(2)}) copy-start(f32[1024,8]{0,1:T(8,128)} %param.51) | copy-start | bytes 98308
  (63 other events, 262.5 us)
Sparse Core Ops, SparseCore 0:
  80.2 125.3 all-gather.6
  304.8 150.8 all-reduce.12
  477.3 73.7 all-gather.8
  777.7 49.6 all-reduce.14
  890.2 154.1 all-reduce.16
  1051.0 244.1 all-reduce.18
where the time goes:
time: 1340 us; the launch traced here: 1330 us
  waiting for transfers between devices  605 us (45%)
  matrix products  225 us (17%)
  other arithmetic  211 us (16%)
  local copies, waits for them, and re-layouts  162 us (12%)
  blocking collectives  100 us (7%)
  between operations  15.4 us (1%)
    psum x1, waiting for transfers between devices, shards(): lax.psum((norm_gain_grad, zx_weight_grad, bc_weight_grad, step_weight_gra...  187 us
    psum x1, waiting for transfers between devices, shards(): projected, square_total = lax.psum((partial_out, square_sum), 'head')  149 us
    psum x1, waiting for transfers between devices, shards(): normed_grad = lax.psum(normed_partial, 'head')  130 us
    dot_general x6, matrix products, block_step(): jnp.einsum('bhts,bhsp->bhtp', mixing, x_block, precision=HIGHEST_PREC)  74.1 us
    all_gather x1, waiting for transfers between devices, entering_2(): everything = jax.tree.map(lambda part: lax.all_gather(part, axis), value)  71.2 us
    unnamed x186, local copies, waits for them, and re-layouts  46.1 us
    another operation x19, other arithmetic  44.4 us
    psum x1, blocking collectives, shards(): lax.psum((norm_gain_grad, zx_weight_grad, bc_weight_grad, step_weight_gra...  40.4 us
  transfers between devices with their start and end apart: 8, of which 6 were waited for; matrix products, arithmetic and copies ran while one was open for 10% of the time, Pallas kernels for 0%

commit v1 on v0

v1 whole, which is shorter than its diff:
```python
import functools

import jax
import jax.numpy as jnp
from jax import lax
from jax.experimental import pallas as pl
from jax.experimental.pallas import tpu as pltpu
from jax.sharding import PartitionSpec as P

INNER = 2048
CONV = 4
CHUNK = 128
STEP = 7


EPS = 1e-05
BETA_ONE = 0.9
BETA_TWO = 0.95
ADAM_EPS = 1e-08
LEARNING_RATES = (0.6, 0.09, 0.09, 0.09, 0.9, 0.9, 0.9, 0.6, 0.06)
WEIGHT_DECAYS = (0.0, 0.1, 0.1, 0.1, 0.0, 0.0, 0.0, 0.0, 0.1)
HIGHEST_PREC = lax.Precision.HIGHEST
F32 = jnp.float32
BF16 = jnp.bfloat16


def passed_along(block, axis, distance):
    devices = range(lax.axis_size(axis))
    route = [(i - distance, i) for i in devices if i - distance in devices]
    return lax.ppermute(block, axis, route)


def swapped(block, axis, mask):
    return lax.ppermute(block, axis, [(i, i ^ mask) for i in range(lax.axis_size(axis))])


def halving_sum(part, axis):
    index = lax.axis_index(axis)
    masks = [1 << k for k in range(lax.axis_size(axis).bit_length() - 1)]
    rest = part.shape[1:]
    for mask in masks[:-1]:
        bit = (index // mask) % 2
        halves = part.reshape((2, part.shape[0] // 2) + rest)
        sent = lax.dynamic_index_in_dim(halves, 1 - bit, 0, keepdims=False)
        kept = lax.dynamic_index_in_dim(halves, bit, 0, keepdims=False)
        got = swapped(sent, axis, mask)
        part = (kept.astype(F32) + got.astype(F32)).astype(BF16)
    got = swapped(part, axis, masks[-1])
    part = (part.astype(F32) + got.astype(F32)).astype(BF16)
    for mask in reversed(masks[:-1]):
        bit = (index // mask) % 2
        got = swapped(part, axis, mask)
        first = jnp.where(bit == 0, part, got)
        second = jnp.where(bit == 0, got, part)
        part = jnp.concatenate([first, second], axis=0)
    return part


def dot(a, b, dims=((1,), (0,)), precision=None):
    return lax.dot_general(a, b, (dims, ((), ())), precision=precision, preferred_element_type=F32)


def expander(heads, width):
    row = lax.broadcasted_iota(jnp.int32, (heads, heads * width), 0)
    column = lax.broadcasted_iota(jnp.int32, (heads, heads * width), 1)
    inside = (column >= row * width) & (column < (row + 1) * width)
    return jnp.where(inside, 1.0, 0.0).astype(BF16)


def split_dot(a, b, dims):
    high = a.astype(BF16)
    low = (a - high.astype(F32)).astype(BF16)
    return dot(high, b, dims) + dot(low, b, dims)


def spread(a, expand):
    return split_dot(a, expand, ((1,), (0,)))


def head_sums(a, expand):
    return split_dot(a, expand, ((1,), (1,)))


def pair_rows(a):
    lane = lax.broadcasted_iota(jnp.int32, a.shape, 1)
    first = lane < a.shape[1] // 2
    zero = jnp.zeros_like(a)
    return jnp.concatenate([jnp.where(first, a, zero), jnp.where(first, zero, a)], axis=0)


def chunk_decays(decay, decay_t):
    q = decay.shape[0]
    row = lax.broadcasted_iota(jnp.int32, (q, q), 0)
    column = lax.broadcasted_iota(jnp.int32, (q, q), 1)
    lower = jnp.where(row >= column, 1.0, 0.0).astype(F32)
    cum = dot(lower, decay, precision=HIGHEST_PREC)
    cum_t = dot(decay_t, lower, ((1,), (1,)), precision=HIGHEST_PREC)
    return cum, cum_t, row, column


def scan_kernel(x_ref, b_ref, c_ref, step_ref, decay_ref, decay_t_ref, enter_ref, y_ref, in_ref, state):
    heads = step_ref.shape[2]
    width = x_ref.shape[2] // heads

    @pl.when(pl.program_id(1) == 0)
    def _():
        state[...] = enter_ref[0]

    expand = expander(heads, width)
    cum, cum_t, row, column = chunk_decays(decay_ref[0], decay_t_ref[0])
    causal = row >= column
    q = cum.shape[0]
    total = cum[q - 1 : q, :]
    b, c = b_ref[0], c_ref[0]
    x = x_ref[0].astype(F32)
    step = step_ref[0]
    xs = (x * spread(step, expand)).astype(BF16)
    grown = spread(jnp.exp(cum), expand)
    xw = (x * spread(step * jnp.exp(total - cum), expand)).astype(BF16)
    scores = dot(c, b, ((1,), (1,)))
    before = state[...]
    in_ref[0, 0] = before
    from_state = grown * dot(c, before.astype(BF16))
    for pair in range(heads // 2):
        lanes = slice(pair * 2 * width, (pair + 1) * 2 * width)
        mixing = []
        for h in (2 * pair, 2 * pair + 1):
            between = cum[:, h : h + 1] - cum_t[h : h + 1, :]
            mixing.append((jnp.exp(jnp.where(causal, between, -1e30)) * scores).astype(BF16))
        within = dot(jnp.concatenate(mixing, axis=1), pair_rows(xs[:, lanes]))
        y_ref[0, :, lanes] = within + from_state[:, lanes]
    state[...] = grown[q - 1 : q, :] * before + dot(b, xw, ((0,), (0,)))


def back_kernel(
    x_ref, b_ref, c_ref, step_ref, decay_ref, decay_t_ref, skip_ref, dy_ref, y_ref, in_ref, leave_ref,
    dx_ref, dbc_ref, ldg_ref, dstep_ref, dskip_ref, grad
):
    heads = step_ref.shape[2]
    width = x_ref.shape[2] // heads

    @pl.when(pl.program_id(1) == 0)
    def _():
        grad[...] = leave_ref[0]

    expand = expander(heads, width)
    cum, cum_t, row, column = chunk_decays(decay_ref[0], decay_t_ref[0])
    later = column >= row
    q = cum.shape[0]
    total = cum[q - 1 : q, :]
    b, c = b_ref[0], c_ref[0]
    x = x_ref[0].astype(F32)
    step = step_ref[0]
    step_wide = spread(step, expand)
    xs = (x * step_wide).astype(BF16)
    grown = spread(jnp.exp(cum), expand)
    waned = spread(jnp.exp(total - cum), expand)
    xw = (x * step_wide * waned).astype(BF16)
    dy = dy_ref[0]
    dy_low = dy.astype(BF16)
    edy = (dy * grown).astype(BF16)
    before = in_ref[0, 0]
    after_grad = grad[...]
    after_low = after_grad.astype(BF16)
    scores_t = dot(b, c, ((1,), (1,)))
    v_state = waned * dot(b, after_low)
    dscores_t = jnp.zeros((q, q), F32)
    v_parts = []
    for pair in range(heads // 2):
        lanes = slice(pair * 2 * width, (pair + 1) * 2 * width)
        dy_pair = pair_rows(dy_low[:, lanes])
        xs_pair = pair_rows(xs[:, lanes])
        dmix = dot(xs_pair, dy_low[:, lanes], ((1,), (1,)))
        mixing = []
        for k, h in enumerate((2 * pair, 2 * pair + 1)):
            between = cum_t[h : h + 1, :] - cum[:, h : h + 1]
            fade = jnp.exp(jnp.where(later, between, -1e30))
            mixing.append((fade * scores_t).astype(BF16))
            dscores_t = dscores_t + fade * dmix[k * q : (k + 1) * q]
        v_parts.append(dot(jnp.concatenate(mixing, axis=1), dy_pair))
    v = jnp.concatenate(v_parts, axis=1) + v_state
    xs_wide = xs.astype(F32)
    etotal = grown[q - 1 : q, :]
    dx_ref[0] = step_wide * v + skip_ref[0] * dy
    end_row = jnp.sum(xs_wide * v_state, axis=0, keepdims=True) + jnp.sum(
        etotal * before * after_grad, axis=0, keepdims=True
    )
    crossing = dy_low.astype(F32) * y_ref[0] - xs_wide * v
    last = lax.broadcasted_iota(jnp.int32, crossing.shape, 0) == q - 1
    crossing = crossing + jnp.where(last, end_row, 0.0)
    upper = jnp.where(column >= row, 1.0, 0.0).astype(F32)
    ldg_ref[0] = dot(upper, head_sums(crossing, expand), precision=HIGHEST_PREC)
    dstep_ref[0] = head_sums(x * v, expand)
    dskip_ref[0] = head_sums(x * dy, expand)
    dscores_low = dscores_t.astype(BF16)
    state = b.shape[1]
    dbc_ref[0, :, :state] = (
        dot(dscores_low, c) + dot(xw, after_low, ((1,), (1,)))
    ).astype(BF16)
    dbc_ref[0, :, state:] = (
        dot(dscores_low, b, ((0,), (0,))) + dot(edy, before.astype(BF16), ((1,), (1,)))
    ).astype(BF16)
    grad[...] = etotal * after_grad + dot(c, edy, ((0,), (0,)))


def scan_forward(x, b, c, step, decay, decay_t, enter):
    seqs, length, inner = x.shape
    state, heads = b.shape[2], step.shape[2]
    chunks = length // CHUNK

    def block(lanes):
        return pl.BlockSpec((1, CHUNK, lanes), lambda s, k: (s, k, 0))

    return pl.pallas_call(
        scan_kernel,
        grid=(seqs, chunks),
        in_specs=[
            block(inner),
            block(state),
            block(state),
            block(heads),
            block(heads),
            pl.BlockSpec((1, heads, CHUNK), lambda s, k: (s, 0, k)),
            pl.BlockSpec((1, state, inner), lambda s, k: (s, 0, 0)),
        ],
        out_specs=[
            block(inner),
            pl.BlockSpec((1, 1, state, inner), lambda s, k: (s, k, 0, 0)),
        ],
        out_shape=[
            jax.ShapeDtypeStruct((seqs, length, inner), F32),
            jax.ShapeDtypeStruct((seqs, chunks, state, inner), F32),
        ],
        scratch_shapes=[pltpu.VMEM((state, inner), F32)],
        compiler_params=pltpu.CompilerParams(vmem_limit_bytes=40 << 20),
    )(x, b, c, step, decay, decay_t, enter)


def scan_backward(x, b, c, step, decay, decay_t, skip, dy, y, states, leave):
    seqs, length, inner = x.shape
    state, heads = b.shape[2], step.shape[2]
    chunks = length // CHUNK

    def block(lanes):
        return pl.BlockSpec((1, CHUNK, lanes), lambda s, k: (s, chunks - 1 - k, 0))

    return pl.pallas_call(
        back_kernel,
        grid=(seqs, chunks),
        in_specs=[
            block(inner),
            block(state),
            block(state),
            block(heads),
            block(heads),
            pl.BlockSpec((1, heads, CHUNK), lambda s, k: (s, 0, chunks - 1 - k)),
            pl.BlockSpec((1, 1, inner), lambda s, k: (0, 0, 0)),
            block(inner),
            block(inner),
            pl.BlockSpec((1, 1, state, inner), lambda s, k: (s, chunks - 1 - k, 0, 0)),
            pl.BlockSpec((1, state, inner), lambda s, k: (s, 0, 0)),
        ],
        out_specs=[block(inner), block(2 * state), block(heads), block(heads), block(heads)],
        out_shape=[
            jax.ShapeDtypeStruct((seqs, length, inner), F32),
            jax.ShapeDtypeStruct((seqs, length, 2 * state), BF16),
            jax.ShapeDtypeStruct((seqs, length, heads), F32),
            jax.ShapeDtypeStruct((seqs, length, heads), F32),
            jax.ShapeDtypeStruct((seqs, length, heads), F32),
        ],
        scratch_shapes=[pltpu.VMEM((state, inner), F32)],
        compiler_params=pltpu.CompilerParams(vmem_limit_bytes=40 << 20),
    )(x, b, c, step, decay, decay_t, skip, dy, y, states, leave)


def silu_slope(values):
    sigmoid_part = jax.nn.sigmoid(values)
    return sigmoid_part * (1.0 + values * (1.0 - sigmoid_part))


def adam_update(weight, mean_old, square_old, gradient, step_rate, decay_weight):
    mean_new = BETA_ONE * mean_old + (1.0 - BETA_ONE) * gradient
    square_new = BETA_TWO * square_old + (1.0 - BETA_TWO) * gradient * gradient
    corrected_mean = mean_new / (1.0 - BETA_ONE**STEP)
    corrected_square = square_new / (1.0 - BETA_TWO**STEP)
    weight_new = weight - step_rate * (
        corrected_mean / (jnp.sqrt(corrected_square) + ADAM_EPS) + decay_weight * weight
    )
    return (mean_new, square_new, weight_new)


def shards(
    inputs,
    cotangent,
    lengths,
    norm_gain,
    norm_gain_mean,
    norm_gain_square,
    proj_zx,
    proj_zx_mean,
    proj_zx_square,
    proj_bc,
    proj_bc_mean,
    proj_bc_square,
    proj_step,
    proj_step_mean,
    proj_step_square,
    conv_inner,
    conv_inner_mean,
    conv_inner_square,
    conv_bc,
    conv_bc_mean,
    conv_bc_square,
    head_params,
    head_params_mean,
    head_params_square,
    gate_gain,
    gate_gain_mean,
    gate_gain_square,
    proj_out,
    proj_out_mean,
    proj_out_square,
):
    seq_count, local_len, model_width = inputs.shape
    local_inner = proj_zx.shape[2]
    state_width = proj_bc.shape[1] // 2
    local_heads = proj_step.shape[1]
    head_width = local_inner // local_heads
    rows = seq_count * local_len
    seq_size, seq_index = lax.axis_size("seq"), lax.axis_index("seq")

    def wide(a):
        selector = jnp.repeat(jnp.eye(local_heads, dtype=F32), head_width, axis=1)
        return jnp.einsum("...h,hc->...c", a, selector, precision=HIGHEST_PREC)

    positions = seq_index * local_len + jnp.arange(local_len)
    is_valid = (positions[None, :] < lengths[:, None]).astype(F32)
    tokens = inputs.astype(F32)
    inverse_rms = lax.rsqrt(jnp.mean(tokens * tokens, axis=-1, keepdims=True) + EPS)
    unit_tokens = tokens * inverse_rms
    normed = (unit_tokens * norm_gain).astype(BF16)
    z_weight = proj_zx[:, 0].astype(BF16)
    x_weight = proj_zx[:, 1].astype(BF16)
    bc_weight = proj_bc.astype(BF16)
    step_weight = proj_step.astype(BF16)
    out_weight = proj_out.astype(BF16)
    xbc_weight = jnp.concatenate([x_weight, bc_weight], axis=1)
    mixed_in = jnp.einsum("btd,dc->btc", normed, xbc_weight, preferred_element_type=F32).astype(BF16)
    edge_in = passed_along(mixed_in[:, local_len - CONV + 1 :], "seq", 1)
    raw_step = jnp.einsum("btd,dh->bth", normed, step_weight, preferred_element_type=F32)
    gate_input = jnp.einsum("btd,dc->btc", normed, z_weight, preferred_element_type=F32)
    padded = jnp.concatenate([edge_in, mixed_in], axis=1)
    conv_weight = jnp.concatenate([conv_inner, conv_bc], axis=-1)
    convolved = conv_weight[CONV] + jnp.zeros(mixed_in.shape, F32)
    for tap_index in range(CONV):
        convolved = (
            convolved + conv_weight[tap_index] * padded[:, tap_index : tap_index + local_len]
        )
    activated = jax.nn.silu(convolved).astype(BF16)
    x_values = activated[..., :local_inner]
    b_values = activated[..., local_inner : local_inner + state_width]
    c_values = activated[..., local_inner + state_width :]
    decay_log, step_bias, skip_gain = head_params[0], head_params[1], head_params[2]
    step_size = jax.nn.softplus(raw_step + step_bias)
    log_decay = -step_size * jnp.exp(decay_log)
    earlier = jnp.tril(jnp.ones((local_len, local_len), F32))
    running = jnp.einsum("ts,bsh->bth", earlier, log_decay, precision=HIGHEST_PREC)
    device_decay = running[:, -1]
    decay_t = log_decay.transpose(0, 2, 1)

    weighted = x_values.astype(F32) * wide(jnp.exp(device_decay[:, None] - running) * step_size)
    local_state = jnp.einsum(
        "btn,btc->bnc", b_values, weighted.astype(BF16), preferred_element_type=F32
    )
    unit_decay = wide(jnp.exp(device_decay))[:, None]
    decay_high = unit_decay.astype(BF16)
    decay_low = (unit_decay - decay_high.astype(F32)).astype(BF16)
    packed = jnp.concatenate(
        [
            local_state.astype(BF16),
            decay_high,
            decay_low,
            jnp.zeros((seq_count, 14, local_inner), BF16),
        ],
        axis=1,
    )
    gathered = lax.all_gather(packed, "seq")
    all_decays = gathered[:, :, state_width : state_width + 1].astype(F32) + gathered[
        :, :, state_width + 1 : state_width + 2
    ].astype(F32)
    entering = jnp.zeros_like(local_state)
    for k in range(seq_size - 1):
        state_k = gathered[k, :, :state_width].astype(F32)
        entering = jnp.where(k < seq_index, all_decays[k] * entering + state_k, entering)

    scanned_raw, states = scan_forward(
        x_values, b_values, c_values, step_size, log_decay, decay_t, entering
    )
    skip_wide = jnp.repeat(skip_gain, head_width)[None, None]
    scanned = scanned_raw + skip_wide * x_values.astype(F32)
    gate_act = jax.nn.silu(gate_input)
    gated_values = scanned * gate_act
    square_sum = jnp.sum(gated_values * gated_values, axis=-1)
    scaled = (gated_values * gate_gain).astype(BF16)
    partial_out = jnp.einsum("bti,di->btd", scaled, out_weight, preferred_element_type=F32)
    out_cotangent = cotangent.astype(F32) * is_valid[..., None]
    partial_scale_grad = jnp.sum(out_cotangent * partial_out, axis=-1)
    square_total, scale_grad = lax.psum(jnp.stack([square_sum, partial_scale_grad]), "head")
    projected = halving_sum(partial_out.astype(BF16).reshape(rows, model_width), "head")
    projected = projected.reshape(inputs.shape).astype(F32)
    out_scale = lax.rsqrt(square_total / INNER + EPS)
    block_out = (tokens + out_scale[..., None] * projected).astype(BF16)
    proj_grad = (out_scale[..., None] * out_cotangent).astype(BF16)
    square_grad = -0.5 * scale_grad * out_scale * out_scale * out_scale / INNER
    out_weight_grad = jnp.einsum("btd,bti->di", proj_grad, scaled, preferred_element_type=F32)
    scaled_grad = jnp.einsum("btd,di->bti", proj_grad, out_weight, preferred_element_type=F32)
    gate_gain_grad = jnp.sum(scaled_grad * gated_values, axis=(0, 1))
    gated_grad = scaled_grad * gate_gain + 2.0 * gated_values * square_grad[..., None]
    scanned_grad = gated_grad * gate_act
    gate_grad = (gated_grad * scanned * silu_slope(gate_input)).astype(BF16)
    local_back = jnp.einsum(
        "btn,btc->bnc",
        c_values,
        (scanned_grad * wide(jnp.exp(running))).astype(BF16),
        preferred_element_type=F32,
    )
    gathered_back = lax.all_gather(local_back.astype(BF16), "seq")
    z_weight_grad = jnp.einsum("btd,btc->dc", normed, gate_grad, preferred_element_type=F32)
    early_sums = lax.psum((out_weight_grad.astype(BF16), z_weight_grad.astype(BF16)), "seq")
    leaving = jnp.zeros_like(local_back)
    for k in range(seq_size - 1, 0, -1):
        back_k = gathered_back[k].astype(F32)
        leaving = jnp.where(k > seq_index, all_decays[k] * leaving + back_k, leaving)

    x_grad, bc_grad, decay_grad, step_grad, skip_terms = scan_backward(
        x_values,
        b_values,
        c_values,
        step_size,
        log_decay,
        decay_t,
        skip_wide,
        scanned_grad,
        scanned_raw,
        states,
        leaving,
    )
    bc_total = halving_sum(bc_grad.reshape(rows, 2 * state_width), "head")
    bc_total = bc_total.reshape(bc_grad.shape).astype(F32)

    def conv_back(activated_grad, first, last):
        convolved_grad = activated_grad * silu_slope(convolved[..., first:last])
        taps = conv_weight[:, first:last]
        tap_grads = []
        padded_grad = jnp.zeros((seq_count, local_len + CONV - 1, last - first), F32)
        for tap_index in range(CONV):
            tap_grads.append(
                jnp.sum(
                    convolved_grad * padded[:, tap_index : tap_index + local_len, first:last],
                    axis=(0, 1),
                )
            )
            padded_grad = padded_grad + jnp.pad(
                taps[tap_index] * convolved_grad,
                ((0, 0), (tap_index, CONV - 1 - tap_index), (0, 0)),
            )
        tap_grads.append(jnp.sum(convolved_grad, axis=(0, 1)))
        edge_grad = passed_along(padded_grad[:, : CONV - 1], "seq", -1)
        mixed_grad = padded_grad[:, CONV - 1 :] + jnp.pad(
            edge_grad, ((0, 0), (local_len - CONV + 1, 0), (0, 0))
        )
        return mixed_grad.astype(BF16), jnp.stack(tap_grads)

    x_in_grad, conv_inner_grad = conv_back(x_grad, 0, local_inner)
    step_total = step_grad - jnp.exp(decay_log) * decay_grad
    pre_grad = step_total * jax.nn.sigmoid(raw_step + step_bias)
    head_grad = jnp.stack(
        [
            jnp.sum(decay_grad * log_decay, axis=(0, 1)),
            jnp.sum(pre_grad, axis=(0, 1)),
            jnp.sum(skip_terms, axis=(0, 1)),
        ]
    )
    step_in_grad = pre_grad.astype(BF16)
    normed_partial = (
        jnp.einsum("btc,dc->btd", gate_grad, z_weight, preferred_element_type=F32)
        + jnp.einsum("btc,dc->btd", x_in_grad, x_weight, preferred_element_type=F32)
        + jnp.einsum("bth,dh->btd", step_in_grad, step_weight, preferred_element_type=F32)
    )
    normed_sum = halving_sum(normed_partial.astype(BF16).reshape(rows, model_width), "head")
    norm_gain_partial = lax.psum(jnp.sum(normed_partial * unit_tokens, axis=(0, 1)), "head")
    bc_in_grad, conv_bc_grad = conv_back(bc_total, local_inner, local_inner + 2 * state_width)
    bc_normed = jnp.einsum("btc,dc->btd", bc_in_grad, bc_weight, preferred_element_type=F32)
    norm_gain_grad = norm_gain_partial + jnp.sum(bc_normed * unit_tokens, axis=(0, 1))
    x_weight_grad = jnp.einsum("btd,btc->dc", normed, x_in_grad, preferred_element_type=F32)
    bc_weight_grad = jnp.einsum("btd,btc->dc", normed, bc_in_grad, preferred_element_type=F32)
    step_weight_grad = jnp.einsum("btd,bth->hd", normed, step_in_grad, preferred_element_type=F32)
    late_sums = lax.psum((x_weight_grad.astype(BF16), bc_weight_grad.astype(BF16)), "seq")
    small_grads = (
        norm_gain_grad,
        step_weight_grad,
        conv_inner_grad,
        conv_bc_grad,
        head_grad,
        gate_gain_grad,
    )
    flat = jnp.concatenate([part.reshape(-1) for part in small_grads])
    count = flat.shape[0]
    flat = jnp.pad(flat, (0, -count % 1024)).reshape(-1, 128)
    flat = lax.psum(flat, "seq").reshape(-1)
    small_sums, at = [], 0
    for part in small_grads:
        small_sums.append(flat[at : at + part.size].reshape(part.shape))
        at += part.size

    normed_grad = normed_sum.reshape(inputs.shape).astype(F32) + bc_normed
    unit_grad = normed_grad * norm_gain
    input_grad = out_cotangent + inverse_rms * (
        unit_grad - unit_tokens * jnp.mean(unit_grad * unit_tokens, axis=-1, keepdims=True)
    )
    zx_sum = jnp.stack([early_sums[1], late_sums[0]], axis=1).astype(F32)
    summed_grads = (
        small_sums[0],
        zx_sum,
        late_sums[1].astype(F32),
        small_sums[1].T,
        small_sums[2],
        small_sums[3],
        small_sums[4],
        small_sums[5],
        early_sums[0].astype(F32),
    )
    params = (
        norm_gain,
        proj_zx,
        proj_bc,
        proj_step,
        conv_inner,
        conv_bc,
        head_params,
        gate_gain,
        proj_out,
    )
    means = (
        norm_gain_mean,
        proj_zx_mean,
        proj_bc_mean,
        proj_step_mean,
        conv_inner_mean,
        conv_bc_mean,
        head_params_mean,
        gate_gain_mean,
        proj_out_mean,
    )
    squares = (
        norm_gain_square,
        proj_zx_square,
        proj_bc_square,
        proj_step_square,
        conv_inner_square,
        conv_bc_square,
        head_params_square,
        gate_gain_square,
        proj_out_square,
    )
    results = [block_out, input_grad]
    for weight, mean_old, square_old, gradient, step_rate, decay_weight in zip(
        params, means, squares, summed_grads, LEARNING_RATES, WEIGHT_DECAYS
    ):
        results.extend(adam_update(weight, mean_old, square_old, gradient, step_rate, decay_weight))
    return tuple(results)


def solution(mesh):
    in_specs = (
        P(None, "seq", None),
        P(None, "seq", None),
        P(),
        P(),
        P(),
        P(),
        P(None, None, "head"),
        P(None, None, "head"),
        P(None, None, "head"),
        P(),
        P(),
        P(),
        P(None, "head"),
        P(None, "head"),
        P(None, "head"),
        P(None, "head"),
        P(None, "head"),
        P(None, "head"),
        P(),
        P(),
        P(),
        P(None, "head"),
        P(None, "head"),
        P(None, "head"),
        P("head"),
        P("head"),
        P("head"),
        P(None, "head"),
        P(None, "head"),
        P(None, "head"),
    )
    out_specs = (
        P(None, "seq", None),
        P(None, "seq", None),
        P(),
        P(),
        P(),
        P(None, None, "head"),
        P(None, None, "head"),
        P(None, None, "head"),
        P(),
        P(),
        P(),
        P(None, "head"),
        P(None, "head"),
        P(None, "head"),
        P(None, "head"),
        P(None, "head"),
        P(None, "head"),
        P(),
        P(),
        P(),
        P(None, "head"),
        P(None, "head"),
        P(None, "head"),
        P("head"),
        P("head"),
        P("head"),
        P(None, "head"),
        P(None, "head"),
        P(None, "head"),
    )
    return jax.shard_map(shards, mesh=mesh, in_specs=in_specs, out_specs=out_specs, check_vma=False)
```

time: 1340 us -> 615 us (0.46)
  waiting for transfers between devices: 605 us -> 244 us
  matrix products: 225 us -> 82.1 us
  local copies, waits for them, and re-layouts: 162 us -> 41.6 us
  other arithmetic: 211 us -> 118 us
  blocking collectives: 100 us -> 53 us
  Pallas kernels: 0 us -> 40.1 us
    psum x4 -> x1, waiting for transfers between devices: 497 us -> 89.7 us  [shards(): lax.psum((x_weight_grad.astype(BF16), bc_weight_grad.astype(BF16)), 'seq')]
    dot_general x41 -> x19, matrix products: 220 us -> 80.8 us  [the longest x1 11 us: shards(): jnp.einsum('btd,di->bti', proj_grad, out_weight, preferred_element_type=F32)]
    ppermute x0 -> x9, waiting for transfers between devices: none -> 69.7 us  [swapped(): lax.ppermute(block, axis, [(i, i ^ mask) for i in range(lax.axis_size(axi...]
    all_gather x2 -> x0, blocking collectives: 53.7 us -> none  [the longest x1 27.1 us: entering_2(): everything = jax.tree.map(lambda part: lax.all_gather(part, axis), value)]
    another operation x20 -> x2, other arithmetic: 44.5 us -> 0.62 us  [the longest x1 0.61 us: shards(): jnp.stack([square_sum, partial_scale_grad])]
    pallas_call x0 -> x2, Pallas kernels: none -> 40.1 us  [the longest x1 27 us: scan_backward(): pl.pallas_call(back_kernel, grid=(seqs, chunks), in_specs=[block(inner),...]
    all_gather x2, waiting for transfers between devices: 107 us -> 79.8 us  [the longest x1 72.9 us: shards(): gathered = lax.all_gather(packed, 'seq')]
    reshape x8 -> x9, local copies, waits for them, and re-layouts: 25.4 us -> 0.28 us  [the longest x2 0.16 us: wide(): selector = jnp.repeat(jnp.eye(local_heads, dtype=F32), head_width, axis=1)]
  transfers between devices with their start and end apart: 8 -> 15, of which waited for: 6 -> 9; matrix products, arithmetic and copies ran while one was open for 10% -> 24% of each run, Pallas kernels for 0% -> 4%
where the time goes in v1:
time: 615 us; the launch traced here: 607 us
  waiting for transfers between devices  244 us (40%)
  other arithmetic  118 us (19%)
  matrix products  82.1 us (13%)
  blocking collectives  53 us (9%)
  local copies, waits for them, and re-layouts  41.6 us (7%)
  Pallas kernels  40.1 us (7%)
  between operations  15.4 us (3%)
  starting transfers between devices  13.5 us (2%)
    psum x1, waiting for transfers between devices, shards(): lax.psum((x_weight_grad.astype(BF16), bc_weight_grad.astype(BF16)), 'seq')  89.7 us
    all_gather x1, waiting for transfers between devices, shards(): gathered = lax.all_gather(packed, 'seq')  72.9 us
    ppermute x9, waiting for transfers between devices, swapped(): lax.ppermute(block, axis, [(i, i ^ mask) for i in range(lax.axis_size(axi...  69.7 us
    psum x1, blocking collectives, shards(): flat = lax.psum(flat, 'seq').reshape(-1)  35.4 us
    unnamed x227, local copies, waits for them, and re-layouts  27.9 us
    pallas_call x1, Pallas kernels, scan_backward(): pl.pallas_call(back_kernel, grid=(seqs, chunks), in_specs=[block(inner),...  27 us
    sub x9, other arithmetic, adam_update(): weight - step_rate * (corrected_mean / (jnp.sqrt(corrected_square) + ADAM...  18.7 us
    add x1, other arithmetic, shards(): out_cotangent + inverse_rms * (unit_grad - unit_tokens * jnp.mean(unit_gr...  14 us
  transfers between devices with their start and end apart: 15, of which 9 were waited for; matrix products, arithmetic and copies ran while one was open for 24% of the time, Pallas kernels for 4%

profile of v1, /device:TPU:0, one launch (start us, length us, event | category | flops | bytes accessed | tf_op | source)
XLA Modules:
  0.0 607.2 jit_solution(5187752149380637690)
XLA Ops:
  7.3 3.2 fusion.12
  11.9 2.3 copy-done.19
  14.2 3.8 convolution_convert_fusion
  18.0 4.9 collective-permute-start
  23.1 4.1 negate_multiply_fusion
  28.5 5.8 multiply_convert_fusion.1
  34.2 4.2 fusion.15
  43.4 1.7 slice.319.x_ref
  45.1 2.3 fusion.145
  47.4 72.9 %all-gather.5.cloned.1.call-done = bf16[32,144,512]{2,1,0:T(8,128)(2,1)} async-done(((bf16[4,144,512]{2,1,0:T(8,128)(2,1)}), bf16[32,144,512]{2,1,0:T(8,128)(2,1)}) %all-gather.5.cloned.1.call-update) | async-done | bytes 4718608 | tf_op jit(solution)/shard_map/all_gather | solution.py:387
  122.2 3.1 fusion.46.enter_ref
  125.4 13.1 %shard_map.509 = (f32[4,512,512]{2,1,0:T(8,128)S(1)}, f32[4,4,128,512]{3,2,1,0:T(8,128)}) custom-call(bf16[4,512,512]{2,1,0:T(8,128)(2,1)S(1)} %slice.319.x_ref, bf16[4,512,128]{2,1,0:T(8,128)(2,1)S(1)} %copy-done.4, bf16[4,512,128]{2,1,0:T(8,128)(2,1)S(1)} %copy-done.2, f32[4,512,8]{2,1,0:T(8,128)S(1)} %copy-done, f32[4,512,8]{2,1,0:T(8,128)S(1)} %copy.131.decay_ref, ...), custom_call_target="tpu_custom_call" | custom-call | tf_op jit(solution)/shard_map/pallas_call | solution.py:214
  138.6 5.9 multiply_reduce_fusion.6
  145.7 6.9 %multiply_reduce_fusion = (f32[4,512]{1,0:T(4,128)S(1)}, bf16[4,512,1024]{2,1,0:T(8,128)(2,1)}) fusion(bf16[4,512,1024]{2,1,0:T(8,128)(2,1)S(1)} %copy-done.35, f32[4,512]{1,0:T(4,128)S(1)} %copy-done.64, f32[1024,512]{1,0:T(8,128)S(1)} %copy-done.37, f32[4,512,512]{2,1,0:T(8,128)} %get-tuple-element.215, f32[512]{0:T(512)S(1)} %copy-done.88), kind=kOutput, calls=%fused_computation.30 | convolution fusion | flops 2160588800 | bytes 14698496 | tf_op jit(solution)/shard_map/bti,di->btd/dot_general | solution.py:405
  153.2 10.7 %psum.49 = f32[2,4,512]{2,1,0:T(4,128)S(1)} all-reduce(f32[2,4,512]{2,1,0:T(4,128)} %pad_maximum_fusion.5), channel_id=1, replica_groups=mesh['seq'=8,'head'=4] {'head'}, use_global_device_ids=true, to_apply=%region_3.4 | all-reduce | flops 4096 | bytes 32768 | tf_op jit(solution)/shard_map/psum | solution.py:408
  164.0 11.0 %multiply_convert_fusion.3 = (bf16[4,512,512]{2,1,0:T(8,128)(2,1)}, f32[4,512,512]{2,1,0:T(8,128)S(1)}, f32[512]{0:T(512)}) fusion(f32[4,512,512]{2,1,0:T(8,128)} %get-tuple-element.266, f32[4,512,512]{2,1,0:T(8,128)} %copy-done.6, f32[512]{0:T(512)} %mul.835, f32[4,512,512]{2,1,0:T(8,128)} %get-tuple-element.215, f32[4,512]{1,0:T(4,128)S(1)} %fusion.101, ...), kind=kOutput, calls=%fused_computation.62 | convolution fusion | flops 2177367552 | bytes 27293696 | tf_op jit(solution)/shard_map/btd,di->bti/dot_general | solution.py:416
  175.0 2.0 copy-done.27
  177.0 3.9 multiply_convert_fusion.2
  180.9 2.4 convolution_convert_fusion.1
  183.7 3.1 dynamic-slice_bitcast_fusion.1
  186.8 4.5 collective-permute-done.1
  191.3 4.5 fusion.21
  195.8 1.7 collective-permute-start.2
  198.2 7.8 %fusion.68 = f32[4,512,1024]{2,1,0:T(8,128)} fusion(bf16[4,512,512]{2,1,0:T(8,128)(2,1)} %get-tuple-element.218, bf16[1024,2,512]{2,0,1:T(8,128)(2,1)} %copy-done.29), kind=kOutput, calls=%fused_computation.179 | convolution fusion | flops 2147483648 | bytes 11534336 | tf_op jit(solution)/shard_map/btc,dc->btd/dot_general | solution.py:486
  206.1 3.6 fusion.37
  209.8 4.0 bitcast_convert_fusion
  213.8 30.0 %collective-permute-done.2 = bf16[1024,1024]{1,0:T(8,128)(2,1)} collective-permute-done((bf16[1024,1024]{1,0:T(8,128)(2,1)}, bf16[1024,1024]{1,0:T(8,128)(2,1)}, u32[]{:S(2)}, u32[]{:S(2)}) %collective-permute-start.2) | collective-permute-done | bytes 2097184 | tf_op jit(solution)/shard_map/ppermute | solution.py:34
  243.8 4.5 add_convert_fusion.1
  248.3 6.9 %all-gather.7.cloned.1.call-done = bf16[32,128,512]{2,1,0:T(8,128)(2,1)} async-done(((bf16[4,128,512]{2,1,0:T(8,128)(2,1)}), bf16[32,128,512]{2,1,0:T(8,128)(2,1)}) %all-gather.7.cloned.1.call-update) | async-done | bytes 4194320 | tf_op jit(solution)/shard_map/all_gather | solution.py:427
  255.2 3.1 fusion.59.leave_ref
  258.4 27.0 %shard_map.510 = (f32[4,512,512]{2,1,0:T(8,128)}, bf16[4,512,256]{2,1,0:T(8,128)(2,1)S(1)}, f32[4,512,8]{2,1,0:T(8,128)S(1)}, f32[4,512,8]{2,1,0:T(8,128)S(1)}, f32[4,512,8]{2,1,0:T(8,128)S(1)}) custom-call(bf16[4,512,512]{2,1,0:T(8,128)(2,1)S(1)} %slice.319.x_ref, bf16[4,512,128]{2,1,0:T(8,128)(2,1)S(1)} %copy-done.5, bf16[4,512,128]{2,1,0:T(8,128)(2,1)S(1)} %copy-done.3, ...), custom_call_target="tpu_custom_call" | custom-call | tf_op jit(solution)/shard_map/pallas_call | solution.py:247
  285.4 8.1 %multiply_reduce_fusion.3 = (f32[512]{0:T(512)S(1)}, f32[512]{0:T(512)S(1)}, f32[512]{0:T(512)S(1)}, f32[512]{0:T(512)S(1)}, f32[512]{0:T(512)}, /*index=5*/f32[4,512,512]{2,1,0:T(8,128)}) fusion(bf16[4,512,768]{2,1,0:T(8,128)(2,1)S(1)} %copy-done.16, bf16[4,3,768]{2,1,0:T(4,128)(2,1)S(1)} %collective-permute-done, f32[4,512,512]{2,1,0:T(8,128)} %get-tuple-element.38, ...), kind=kLoop, calls=%fused_computation.56 | loop fusion | flops 31454720 | bytes 17860608 | tf_op jit(solution)/shard_map/reduce_sum | solution.py:458
  293.5 6.6 %broadcast_multiply_fusion.3 = (f32[4,512,512]{2,1,0:T(8,128)S(1)}, f32[4,512,512]{2,1,0:T(8,128)S(1)}, f32[4,512,512]{2,1,0:T(8,128)S(1)}, f32[4,512,512]{2,1,0:T(8,128)}) fusion(f32[4,512,512]{2,1,0:T(8,128)} %get-tuple-element.213, f32[512]{0:T(512)S(1)} %bitcast.259, f32[512]{0:T(512)S(1)} %bitcast.262, f32[512]{0:T(512)S(1)} %bitcast.260, ...), kind=kLoop, calls=%fused_computation.106 | loop fusion | flops 4194304 | bytes 20979712 | tf_op jit(solution)/shard_map/mul | solution.py:464
  300.1 2.0 copy-done.18
  303.0 7.8 %pad_add_fusion = f32[4,515,512]{2,1,0:T(8,128)} fusion(f32[4,512,512]{2,1,0:T(8,128)S(1)} %get-tuple-element.228, f32[4,512,512]{2,1,0:T(8,128)} %copy-done.18, f32[4,512,512]{2,1,0:T(8,128)} %get-tuple-element.230, f32[4,512,512]{2,1,0:T(8,128)S(1)} %get-tuple-element.227), kind=kLoop, calls=%fused_computation.38 | loop fusion | flops 3164160 | bytes 20996096 | tf_op jit(solution)/shard_map/add | solution.py:463
  315.1 1.5 collective-permute-start.9
  317.4 7.4 %fusion.148 = (bf16[4,512,1024]{2,1,0:T(8,128)(2,1)S(1)}, f32[4,512,1024]{2,1,0:T(8,128)}) fusion(f32[4,512,1024]{2,1,0:T(8,128)S(1)} %fusion.96, f32[4,512,1024]{2,1,0:T(8,128)} %fusion.68, bf16[1024,2,512]{2,0,1:T(8,128)(2,1)} %copy-done.29, f32[4,515,512]{2,1,0:T(8,128)S(1)} %bitcast.240, f32[4,3,512]{2,1,0:T(4,128)S(1)} %collective-permute-done.4), kind=kOutput, calls=%fused_computation.312 | convolution fusion | flops 2155872256 | bytes 34635776 | tf_op jit(solution)/shard_map/btc,dc->btd/dot_general | solution.py:487
  324.8 1.5 dynamic-slice_bitcast_fusion
  326.3 3.2 collective-permute-done.9
  330.8 3.7 fusion.38
  334.7 3.2 multiply_reduce_fusion.8
  338.7 1.7 collective-permute-start.11
  341.1 3.6 collective-permute-done.11
  344.7 2.8 fusion.40
  347.5 4.5 fusion.20
  353.5 2.9 broadcast_select_fusion.3
  356.5 2.5 pad_maximum_fusion
  359.5 3.4 convolution_bitcast_fusion.2
  362.9 4.7 fusion.71
  367.6 31.9 %collective-permute-done.6 = bf16[1024,1024]{1,0:T(8,128)(2,1)} collective-permute-done((bf16[1024,1024]{1,0:T(8,128)(2,1)}, bf16[1024,1024]{1,0:T(8,128)(2,1)}, u32[]{:S(2)}, u32[]{:S(2)}) %collective-permute-start.6) | collective-permute-done | bytes 2097184 | tf_op jit(solution)/shard_map/ppermute | solution.py:34
  399.5 3.2 add_convert_fusion
  402.8 89.7 %all-reduce.14.cloned.1.call-done = (bf16[1024,1,512]{2,0,1:T(8,128)(2,1)}, bf16[1024,1,512]{2,0,1:T(8,128)(2,1)}, bf16[1024,256]{1,0:T(8,128)(2,1)}, bf16[1024,512]{1,0:T(8,128)(2,1)}) async-done(((bf16[1024,1,512]{2,0,1:T(8,128)(2,1)}, bf16[1024,1,512]{2,0,1:T(8,128)(2,1)}, bf16[1024,256]{1,0:T(8,128)(2,1)}, bf16[1024,512]{1,0:T(8,128)(2,1)}), (bf16[1024,1,512]{2,0,1:T(8,128)(2,1)}, ...) | async-done | bytes 3670032 | tf_op jit(solution)/shard_map/psum | solution.py:498
  492.5 8.5 %multiply_subtract_fusion = (f32[1024,2,512]{2,0,1:T(8,128)S(1)}, f32[1024,2,512]{2,0,1:T(8,128)S(1)}, f32[1024,2,512]{2,0,1:T(8,128)S(1)}) fusion(f32[1024,2,512]{2,1,0:T(2,128)} %param.36, bf16[1024,1,512]{2,0,1:T(8,128)(2,1)} %get-tuple-element.179, bf16[1024,1,512]{2,0,1:T(8,128)(2,1)} %get-tuple-element.180, f32[1024,2,512]{2,1,0:T(2,128)} %param.38, ...), kind=kLoop, calls=%fused_computation.53 | loop fusion | flops 17825792 | bytes 27262976 | tf_op jit(solution)/shard_map/sub | solution.py:286
  501.0 5.2 copy.148
  506.3 5.2 copy.147
  511.5 5.2 copy.146
  516.8 2.2 multiply_subtract_fusion.2
  520.8 4.2 multiply_subtract_fusion.1
  525.0 3.3 broadcast_select_fusion.1
  528.3 4.3 pad_maximum_fusion.1
  533.9 5.4 fusion.11
  539.4 6.9 %psum.50 = f32[1024]{0:T(1024)S(1)} all-reduce(f32[1024]{0:T(1024)S(1)} %get-tuple-element.169), channel_id=1, replica_groups=mesh['seq'=8,'head'=4] {'head'}, use_global_device_ids=true, to_apply=%region_6.7 | all-reduce | flops 1024 | bytes 8192 | tf_op jit(solution)/shard_map/psum | solution.py:491
  546.4 35.4 %psum.51 = f32[112,128]{1,0:T(8,128)S(1)} all-reduce(f32[112,128]{1,0:T(8,128)S(1)} %pad_bitcast_fusion), channel_id=1, replica_groups=mesh['seq'=8,'head'=4] {'seq'}, use_global_device_ids=true, to_apply=%region_22.23 | all-reduce | flops 14336 | bytes 114688 | tf_op jit(solution)/shard_map/psum | solution.py:510
  582.6 14.0 %fusion.9 = (f32[4,512,1024]{2,1,0:T(8,128)}, bf16[4,512,1024]{2,1,0:T(8,128)(2,1)}) fusion(bf16[4,512,1024]{2,1,0:T(8,128)(2,1)} %param.30, bf16[4,512,1024]{2,1,0:T(8,128)(2,1)} %param.31, f32[4,512,1024]{2,1,0:T(8,128)} %fusion.71, f32[4,512]{1,0:T(4,128)S(1)} %broadcast_multiply_fusion.8, f32[4,512]{1,0:T(4,128)S(1)} %copy-done.66, ...), kind=kLoop, calls=%fused_computation.20 | loop fusion | flops 39845888 | bytes 37785600 | tf_op jit(solution)/shard_map/add | solution.py:518
  (317 shorter events, 31.0 us)
Async XLA Ops:
  7.2 113.1 %all-gather.5.cloned.1.call-start = ((), (), s32[]{:S(2)}) async-start(), calls=%async_computation | async-start | bytes 5308416 | tf_op jit(solution)/shard_map/all_gather | solution.py:387
  10.5 12.6 %copy-start.53 = (f32[4,512]{1,0:T(4,128)}, f32[4,512]{1,0:T(4,128)S(1)}, u32[]{:S(2)}) copy-start(f32[4,512]{1,0:T(4,128)S(1)} %add_rsqrt_fusion) | copy-start | bytes 24580
  14.1 8.7 %copy-start.75 = (f32[3,8]{1,0:T(4,128)S(1)}, f32[3,8]{1,0:T(4,128)}, u32[]{:S(2)}) copy-start(f32[3,8]{1,0:T(4,128)} %param.51) | copy-start | bytes 292
  14.1 8.7 %copy-start.48 = (f32[5,512]{1,0:T(8,128)S(1)}, f32[5,512]{1,0:T(8,128)}, u32[]{:S(2)}) copy-start(f32[5,512]{1,0:T(8,128)} %param.45) | copy-start | bytes 30724
  14.1 8.8 %copy-start.57 = (f32[5,256]{1,0:T(8,128)S(1)}, f32[5,256]{1,0:T(8,128)}, u32[]{:S(2)}) copy-start(f32[5,256]{1,0:T(8,128)} %param.48) | copy-start | bytes 15364
  14.1 9.0 %copy-start.47 = (f32[1024,8]{0,1:T(8,128)S(1)}, f32[1024,8]{0,1:T(8,128)}, u32[]{:S(2)}) copy-start(f32[1024,8]{0,1:T(8,128)} %param.42) | copy-start | bytes 98308
  17.9 10.5 %copy-start.15 = (bf16[4,512,768]{2,1,0:T(8,128)(2,1)}, bf16[4,512,768]{2,1,0:T(8,128)(2,1)S(1)}, u32[]{:S(2)}) copy-start(bf16[4,512,768]{2,1,0:T(8,128)(2,1)S(1)} %convolution_convert_fusion) | copy-start | bytes 9437188
  18.0 10.5 %collective-permute-start = (bf16[4,3,768]{2,1,0:T(4,128)(2,1)S(1)}, bf16[4,3,768]{2,1,0:T(4,128)(2,1)S(1)}, u32[]{:S(2)}, u32[]{:S(2)}) collective-permute-start(bf16[4,3,768]{2,1,0:T(4,128)(2,1)S(1)} %slice.309), channel_id=1, source_target_pairs={{0,4},{4,8},{8,12},{12,16},{16,20},{20,24},{24,28},{1,5},{5,9},{9,... | collective-permute-start | bytes 55304 | tf_op jit(solution)/shard_map/ppermute | solution.py:30
  22.9 20.4 %copy-start.77 = (f32[8]{0:T(128)}, f32[8]{0:T(128)S(1)}, u32[]{:S(2)}) copy-start(f32[8]{0:T(128)S(1)} %get-tuple-element.263) | copy-start | bytes 100
  39.9 215.2 %all-gather.7.cloned.1.call-start = ((), (), s32[]{:S(2)}) async-start(), calls=%async_computation.1 | async-start | bytes 4718592 | tf_op jit(solution)/shard_map/all_gather | solution.py:427
  122.2 16.3 %copy-start.49 = (f32[4,512]{1,0:T(4,128)}, f32[4,512]{1,0:T(4,128)S(1)}, u32[]{:S(2)}) copy-start(f32[4,512]{1,0:T(4,128)S(1)} %get-tuple-element.274) | copy-start | bytes 24580
  122.2 16.3 %copy-start.51 = (f32[4,512]{1,0:T(4,128)}, f32[4,512]{1,0:T(4,128)S(1)}, u32[]{:S(2)}) copy-start(f32[4,512]{1,0:T(4,128)S(1)} %get-tuple-element.275) | copy-start | bytes 24580
  122.2 16.3 %copy-start.25 = (bf16[4,512,768]{2,1,0:T(8,128)(2,1)S(1)}, bf16[4,512,768]{2,1,0:T(8,128)(2,1)}, u32[]{:S(2)}) copy-start(bf16[4,512,768]{2,1,0:T(8,128)(2,1)} %copy-done.24) | copy-start | bytes 9437188
  125.3 13.2 %copy-start.20 = (bf16[4,512,1024]{2,1,0:T(8,128)(2,1)S(1)}, bf16[4,512,1024]{2,1,0:T(8,128)(2,1)}, u32[]{:S(2)}) copy-start(bf16[4,512,1024]{2,1,0:T(8,128)(2,1)} %param.30) | copy-start | bytes 12582916
  125.3 13.2 %copy-start.30 = (bf16[1024,2,512]{2,0,1:T(8,128)(2,1)S(1)}, bf16[1024,2,512]{2,0,1:T(8,128)(2,1)}, u32[]{:S(2)}) copy-start(bf16[1024,2,512]{2,0,1:T(8,128)(2,1)} %copy-done.29) | copy-start | bytes 6291460
  125.4 13.2 %copy-start.54 = (f32[4,512]{1,0:T(4,128)S(1)}, f32[4,512]{1,0:T(4,128)}, u32[]{:S(2)}) copy-start(f32[4,512]{1,0:T(4,128)} %copy-done.53) | copy-start | bytes 24580
  125.4 13.2 %copy-start.96 = (f32[512]{0:T(512)S(1)}, f32[512]{0:T(512)}, u32[]{:S(2)}) copy-start(f32[512]{0:T(512)} %mul.835) | copy-start | bytes 6148
  145.7 18.2 %copy-start.89 = (f32[512]{0:T(512)S(1)}, f32[512]{0:T(512)}, u32[]{:S(2)}) copy-start(f32[512]{0:T(512)} %param.54) | copy-start | bytes 6148
  163.9 11.0 %copy-start.67 = (f32[4,512]{1,0:T(4,128)}, f32[4,512]{1,0:T(4,128)S(1)}, u32[]{:S(2)}) copy-start(f32[4,512]{1,0:T(4,128)S(1)} %fusion.106) | copy-start | bytes 24580
  183.3 309.3 %all-reduce.14.cloned.1.call-start = ((), (), s32[]{:S(2)}) async-start(), calls=%async_computation.2 | async-start | bytes 7340032 | tf_op jit(solution)/shard_map/psum | solution.py:498
  186.8 10.7 %copy-start.58 = (f32[5,256]{1,0:T(8,128)S(1)}, f32[5,256]{1,0:T(8,128)}, u32[]{:S(2)}) copy-start(f32[5,256]{1,0:T(8,128)} %param.48) | copy-start | bytes 15364
  186.8 11.4 %copy-start.63 = (f32[1,4,1,512]{3,2,1,0:T(1,128)S(1)}, f32[1,4,1,512]{3,2,1,0:T(1,128)}, u32[]{:S(2)}) copy-start(f32[1,4,1,512]{3,2,1,0:T(1,128)} %get-tuple-element.242) | copy-start | bytes 24580
  186.8 4.5 collective-permute-start.1
  195.8 48.0 %collective-permute-start.2 = (bf16[1024,1024]{1,0:T(8,128)(2,1)}, bf16[1024,1024]{1,0:T(8,128)(2,1)}, u32[]{:S(2)}, u32[]{:S(2)}) collective-permute-start(bf16[1024,1024]{1,0:T(8,128)(2,1)} %fusion.21), channel_id=1, source_target_pairs={{0,2},{1,3},{2,0},{3,1},{4,6},{5,7},{6,4},{7,5},{8,10},{9,11},{10,... | collective-permute-start | bytes 6291464 | tf_op jit(solution)/shard_map/ppermute | solution.py:34
  213.8 41.4 %copy-start.50 = (f32[4,512]{1,0:T(4,128)S(1)}, f32[4,512]{1,0:T(4,128)}, u32[]{:S(2)}) copy-start(f32[4,512]{1,0:T(4,128)} %copy-done.49) | copy-start | bytes 24580
  213.8 41.4 %copy-start.52 = (f32[4,512]{1,0:T(4,128)S(1)}, f32[4,512]{1,0:T(4,128)}, u32[]{:S(2)}) copy-start(f32[4,512]{1,0:T(4,128)} %copy-done.51) | copy-start | bytes 24580
  248.3 105.2 %collective-permute-start.3 = (bf16[1024,1024]{1,0:T(8,128)(2,1)}, bf16[1024,1024]{1,0:T(8,128)(2,1)}, u32[]{:S(2)}, u32[]{:S(2)}) collective-permute-start(bf16[1024,1024]{1,0:T(8,128)(2,1)} %add_convert_fusion.1), channel_id=1, source_target_pairs={{0,1},{1,0},{2,3},{3,2},{4,5},{5,4},{6,7},{7,6},{8,9},{9,8},{10,11... | collective-permute-start | bytes 6291464 | tf_op jit(solution)/shard_map/ppermute | solution.py:34
  255.2 30.1 %slice-start.4 = ((s8[6291456]{0:T(1024)(128)(4,1)}), s8[4194304]{0:T(1024)(128)(4,1)S(1)}, s32[]{:S(2)}) async-start(s8[6291456]{0:T(1024)(128)(4,1)} %bitcast.237), calls=%async_computation.7 | async-start | bytes 8388608
  258.3 27.0 %copy-start.16 = (bf16[4,512,768]{2,1,0:T(8,128)(2,1)S(1)}, bf16[4,512,768]{2,1,0:T(8,128)(2,1)}, u32[]{:S(2)}) copy-start(bf16[4,512,768]{2,1,0:T(8,128)(2,1)} %copy-done.15) | copy-start | bytes 9437188
  258.3 27.0 %slice-start.5 = ((s8[6291456]{0:T(1024)(128)(4,1)}), s8[2097152]{0:T(1024)(128)(4,1)S(1)}, s32[]{:S(2)}) async-start(s8[6291456]{0:T(1024)(128)(4,1)} %bitcast.237), calls=%async_computation.8 | async-start | bytes 4194304
  285.3 8.2 %copy-start.7 = (f32[4,512,8]{2,1,0:T(8,128)}, f32[4,512,8]{2,1,0:T(8,128)S(1)}, u32[]{:S(2)}) copy-start(f32[4,512,8]{2,1,0:T(8,128)S(1)} %get-tuple-element.42) | copy-start | bytes 196612
  285.3 8.2 %copy-start.9 = (f32[4,512,8]{2,1,0:T(8,128)}, f32[4,512,8]{2,1,0:T(8,128)S(1)}, u32[]{:S(2)}) copy-start(f32[4,512,8]{2,1,0:T(8,128)S(1)} %get-tuple-element.40) | copy-start | bytes 196612
  285.3 8.2 %copy-start.11 = (f32[4,512,8]{2,1,0:T(8,128)}, f32[4,512,8]{2,1,0:T(8,128)S(1)}, u32[]{:S(2)}) copy-start(f32[4,512,8]{2,1,0:T(8,128)S(1)} %get-tuple-element.39) | copy-start | bytes 196612
  303.0 8.4 %copy-start.14 = (bf16[4,512,256]{2,1,0:T(8,128)(2,1)S(1)}, bf16[4,512,256]{2,1,0:T(8,128)(2,1)}, u32[]{:S(2)}) copy-start(bf16[4,512,256]{2,1,0:T(8,128)(2,1)} %copy-done.13) | copy-start | bytes 3145732
  303.0 9.9 %copy-start.78 = (f32[8]{0:T(128)S(1)}, f32[8]{0:T(128)}, u32[]{:S(2)}) copy-start(f32[8]{0:T(128)} %copy-done.77) | copy-start | bytes 100
  311.5 3.4 collective-permute-start.8
  311.6 5.8 collective-permute-start.4
  315.1 14.5 %collective-permute-start.9 = (bf16[1024,256]{1,0:T(8,128)(2,1)S(1)}, bf16[1024,256]{1,0:T(8,128)(2,1)}, u32[]{:S(2)}, u32[]{:S(2)}) collective-permute-start(bf16[1024,256]{1,0:T(8,128)(2,1)S(1)} %fusion.45), channel_id=1, source_target_pairs={{0,2},{1,3},{2,0},{3,1},{4,6},{5,7},{6,4},{7,5},{8,10},{9,11},{10,... | collective-permute-start | bytes 1572872 | tf_op jit(solution)/shard_map/ppermute | solution.py:34
  324.8 9.7 %copy-start.26 = (bf16[4,512,1024]{2,1,0:T(8,128)(2,1)}, bf16[4,512,1024]{2,1,0:T(8,128)(2,1)S(1)}, u32[]{:S(2)}) copy-start(bf16[4,512,1024]{2,1,0:T(8,128)(2,1)S(1)} %get-tuple-element.268) | copy-start | bytes 12582916
  326.3 21.2 %collective-permute-start.5 = (bf16[1024,1024]{1,0:T(8,128)(2,1)}, bf16[1024,1024]{1,0:T(8,128)(2,1)}, u32[]{:S(2)}, u32[]{:S(2)}) collective-permute-start(bf16[1024,1024]{1,0:T(8,128)(2,1)} %dynamic-slice_bitcast_fusion), channel_id=1, source_target_pairs={{0,1},{1,0},{2,3},{3,2},{4,5},{5,4},{6,7},{7,6},{8,9},{9,8},{10,11... | collective-permute-start | bytes 6291464 | tf_op jit(solution)/shard_map/ppermute | solution.py:34
  330.7 3.8 collective-permute-start.10
  338.7 6.0 collective-permute-start.11
  352.1 47.5 %collective-permute-start.6 = (bf16[1024,1024]{1,0:T(8,128)(2,1)}, bf16[1024,1024]{1,0:T(8,128)(2,1)}, u32[]{:S(2)}, u32[]{:S(2)}) collective-permute-start(bf16[1024,1024]{1,0:T(8,128)(2,1)} %fusion.20), channel_id=1, source_target_pairs={{0,2},{1,3},{2,0},{3,1},{4,6},{5,7},{6,4},{7,5},{8,10},{9,11},{10,... | collective-permute-start | bytes 6291464 | tf_op jit(solution)/shard_map/ppermute | solution.py:34
  402.7 98.3 %copy-start.31 = (bf16[1024,1024]{1,0:T(8,128)(2,1)}, bf16[1024,1024]{1,0:T(8,128)(2,1)S(1)}, u32[]{:S(2)}) copy-start(bf16[1024,1024]{1,0:T(8,128)(2,1)S(1)} %add_convert_fusion) | copy-start | bytes 6291460
  402.7 122.3 %collective-permute-start.7 = (bf16[1024,1024]{1,0:T(8,128)(2,1)S(1)}, bf16[1024,1024]{1,0:T(8,128)(2,1)}, u32[]{:S(2)}, u32[]{:S(2)}) collective-permute-start(bf16[1024,1024]{1,0:T(8,128)(2,1)S(1)} %add_convert_fusion), channel_id=1, source_target_pairs={{0,1},{1,0},{2,3},{3,2},{4,5},{5,4},{6,7},{7,6},{8,9},{9,8},{10,11... | collective-permute-start | bytes 6291464 | tf_op jit(solution)/shard_map/ppermute | solution.py:34
  516.8 15.9 %slice-start.2 = ((s8[8388608]{0:T(1024)(128)(4,1)}), s8[4194304]{0:T(1024)(128)(4,1)S(1)}, s32[]{:S(2)}) async-start(s8[8388608]{0:T(1024)(128)(4,1)} %bitcast.235), calls=%async_computation.5 | async-start | bytes 8388608
  520.8 11.9 %slice-start.3 = ((s8[8388608]{0:T(1024)(128)(4,1)}), s8[4194304]{0:T(1024)(128)(4,1)S(1)}, s32[]{:S(2)}) async-start(s8[8388608]{0:T(1024)(128)(4,1)} %bitcast.235), calls=%async_computation.6 | async-start | bytes 8388608
  533.9 12.3 %copy-start.85 = (f32[512]{0:T(512)S(1)}, f32[512]{0:T(512)}, u32[]{:S(2)}) copy-start(f32[512]{0:T(512)} %get-tuple-element.220) | copy-start | bytes 6148
  533.9 48.4 %copy-start.66 = (f32[4,512]{1,0:T(4,128)S(1)}, f32[4,512]{1,0:T(4,128)}, u32[]{:S(2)}) copy-start(f32[4,512]{1,0:T(4,128)} %compare_convert_fusion) | copy-start | bytes 24580
  533.9 48.4 %copy-start.69 = (f32[4,512]{1,0:T(4,128)S(1)}, f32[4,512]{1,0:T(4,128)}, u32[]{:S(2)}) copy-start(f32[4,512]{1,0:T(4,128)} %copy-done.67) | copy-start | bytes 24580
  582.4 14.2 %copy-start.83 = (f32[1024]{0:T(1024)S(1)}, f32[1024]{0:T(1024)}, u32[]{:S(2)}) copy-start(f32[1024]{0:T(1024)} %param.35) | copy-start | bytes 12292
  582.4 14.2 %copy-start.84 = (f32[1024]{0:T(1024)S(1)}, f32[1024]{0:T(1024)}, u32[]{:S(2)}) copy-start(f32[1024]{0:T(1024)} %param.34) | copy-start | bytes 12292
  582.4 14.8 %copy-start.91 = (f32[512]{0:T(512)S(1)}, f32[512]{0:T(512)}, u32[]{:S(2)}) copy-start(f32[512]{0:T(512)} %param.54) | copy-start | bytes 6148
  582.4 14.8 %copy-start.92 = (f32[512]{0:T(512)S(1)}, f32[512]{0:T(512)}, u32[]{:S(2)}) copy-start(f32[512]{0:T(512)} %param.56) | copy-start | bytes 6148
  582.4 14.8 %copy-start.93 = (f32[512]{0:T(512)S(1)}, f32[512]{0:T(512)}, u32[]{:S(2)}) copy-start(f32[512]{0:T(512)} %param.55) | copy-start | bytes 6148
  582.5 15.5 %copy-start.73 = (f32[5,256]{1,0:T(8,128)S(1)}, f32[5,256]{1,0:T(8,128)}, u32[]{:S(2)}) copy-start(f32[5,256]{1,0:T(8,128)} %param.50) | copy-start | bytes 15364
  582.5 15.5 %copy-start.74 = (f32[5,256]{1,0:T(8,128)S(1)}, f32[5,256]{1,0:T(8,128)}, u32[]{:S(2)}) copy-start(f32[5,256]{1,0:T(8,128)} %param.49) | copy-start | bytes 15364
  582.5 16.1 %copy-start.70 = (f32[5,512]{1,0:T(8,128)S(1)}, f32[5,512]{1,0:T(8,128)}, u32[]{:S(2)}) copy-start(f32[5,512]{1,0:T(8,128)} %param.47) | copy-start | bytes 30724
  582.5 16.1 %copy-start.71 = (f32[5,512]{1,0:T(8,128)S(1)}, f32[5,512]{1,0:T(8,128)}, u32[]{:S(2)}) copy-start(f32[5,512]{1,0:T(8,128)} %param.46) | copy-start | bytes 30724
  582.5 16.7 %copy-start.61 = (f32[1024,8]{0,1:T(8,128)S(1)}, f32[1024,8]{0,1:T(8,128)}, u32[]{:S(2)}) copy-start(f32[1024,8]{0,1:T(8,128)} %param.44) | copy-start | bytes 98308
  582.5 16.7 %copy-start.62 = (f32[1024,8]{0,1:T(8,128)S(1)}, f32[1024,8]{0,1:T(8,128)}, u32[]{:S(2)}) copy-start(f32[1024,8]{0,1:T(8,128)} %param.43) | copy-start | bytes 98308
  582.5 17.3 %copy-start.76 = (f32[3,8]{1,0:T(4,128)S(1)}, f32[3,8]{1,0:T(4,128)}, u32[]{:S(2)}) copy-start(f32[3,8]{1,0:T(4,128)} %param.51) | copy-start | bytes 292
  582.5 17.3 %copy-start.94 = (f32[3,8]{1,0:T(4,128)S(1)}, f32[3,8]{1,0:T(4,128)}, u32[]{:S(2)}) copy-start(f32[3,8]{1,0:T(4,128)} %param.53) | copy-start | bytes 292
  582.5 17.3 %copy-start.95 = (f32[3,8]{1,0:T(4,128)S(1)}, f32[3,8]{1,0:T(4,128)}, u32[]{:S(2)}) copy-start(f32[3,8]{1,0:T(4,128)} %param.52) | copy-start | bytes 292
  (59 other events, 277.0 us)
Sparse Core Ops, SparseCore 0:
  40.1 80.1 all-gather.4
  183.4 71.7 all-gather.6
  347.7 144.8 all-reduce.13

commit v2 on v1

--- a/solution.py
+++ b/solution.py
@@ -34,7 +34,13 @@
     return lax.ppermute(block, axis, [(i, i ^ mask) for i in range(lax.axis_size(axis))])
 
 
-def halving_sum(part, axis):
+def doubling_sum(part, axis):
+    for k in range(lax.axis_size(axis).bit_length() - 1):
+        part = part + swapped(part, axis, 1 << k)
+    return part
+
+
+def halving_sum(part, axis, after=None):
     index = lax.axis_index(axis)
     masks = [1 << k for k in range(lax.axis_size(axis).bit_length() - 1)]
     rest = part.shape[1:]
@@ -46,6 +52,8 @@
         got = swapped(sent, axis, mask)
         part = (kept.astype(F32) + got.astype(F32)).astype(BF16)
     got = swapped(part, axis, masks[-1])
+    if after is not None:
+        got, _ = lax.optimization_barrier((got, after))
     part = (part.astype(F32) + got.astype(F32)).astype(BF16)
     for mask in reversed(masks[:-1]):
         bit = (index // mask) % 2
@@ -54,6 +62,52 @@
         second = jnp.where(bit == 0, got, part)
         part = jnp.concatenate([first, second], axis=0)
     return part
+
+
+def exchanged(blocks, axis):
+    return lax.all_to_all(blocks, axis, 0, 0, tiled=True)
+
+
+def to_blocks(state, count):
+    return state.astype(BF16).reshape(count, -1, state.shape[-1])
+
+
+def states_before(state, decay, axis):
+    size = lax.axis_size(axis)
+    blocks = to_blocks(state, size)
+    height = blocks.shape[1]
+    high = decay.astype(BF16)
+    low = (decay - high.astype(F32)).astype(BF16)
+    empty = jnp.zeros((decay.shape[0], 14, decay.shape[2]), BF16)
+    extra = jnp.concatenate([high, low, empty], axis=1)
+    extra = jnp.repeat(extra, size // decay.shape[0], axis=0)
+    got = exchanged(jnp.concatenate([blocks, extra], axis=1), axis).astype(F32)
+    decays = got[:, height : height + 1] + got[:, height + 1 : height + 2]
+    entering = [jnp.zeros(got[0, :height].shape, F32)]
+    for k in range(size - 1):
+        entering.append(decays[k] * entering[-1] + got[k, :height])
+    back = exchanged(jnp.stack(entering).astype(BF16), axis)
+    return back.reshape(state.shape).astype(F32), decays
+
+
+def states_after(state, decays, axis):
+    size = lax.axis_size(axis)
+    got = exchanged(to_blocks(state, size), axis).astype(F32)
+    leaving = [jnp.zeros(got[0].shape, F32)]
+    for k in range(size - 1, 0, -1):
+        leaving.append(decays[k] * leaving[-1] + got[k])
+    back = exchanged(jnp.stack(leaving[::-1]).astype(BF16), axis)
+    return back.reshape(state.shape).astype(F32)
+
+
+def lane_tiles(a):
+    rows, two, columns = a.shape
+    return a.reshape(rows, two, columns // 128, 128).transpose(0, 2, 1, 3).reshape(-1, 128)
+
+
+def from_lane_tiles(a, shape):
+    rows, two, columns = shape
+    return a.reshape(rows, columns // 128, two, 128).transpose(0, 2, 1, 3).reshape(shape)
 
 
 def dot(a, b, dims=((1,), (0,)), precision=None):
@@ -373,25 +427,7 @@
         "btn,btc->bnc", b_values, weighted.astype(BF16), preferred_element_type=F32
     )
     unit_decay = wide(jnp.exp(device_decay))[:, None]
-    decay_high = unit_decay.astype(BF16)
-    decay_low = (unit_decay - decay_high.astype(F32)).astype(BF16)
-    packed = jnp.concatenate(
-        [
-            local_state.astype(BF16),
-            decay_high,
-            decay_low,
-            jnp.zeros((seq_count, 14, local_inner), BF16),
-        ],
-        axis=1,
-    )
-    gathered = lax.all_gather(packed, "seq")
-    all_decays = gathered[:, :, state_width : state_width + 1].astype(F32) + gathered[
-        :, :, state_width + 1 : state_width + 2
-    ].astype(F32)
-    entering = jnp.zeros_like(local_state)
-    for k in range(seq_size - 1):
-        state_k = gathered[k, :, :state_width].astype(F32)
-        entering = jnp.where(k < seq_index, all_decays[k] * entering + state_k, entering)
+    entering, block_decays = states_before(local_state, unit_decay, "seq")
 
     scanned_raw, states = scan_forward(
         x_values, b_values, c_values, step_size, log_decay, decay_t, entering
@@ -406,10 +442,7 @@
     out_cotangent = cotangent.astype(F32) * is_valid[..., None]
     partial_scale_grad = jnp.sum(out_cotangent * partial_out, axis=-1)
     square_total, scale_grad = lax.psum(jnp.stack([square_sum, partial_scale_grad]), "head")
-    projected = halving_sum(partial_out.astype(BF16).reshape(rows, model_width), "head")
-    projected = projected.reshape(inputs.shape).astype(F32)
     out_scale = lax.rsqrt(square_total / INNER + EPS)
-    block_out = (tokens + out_scale[..., None] * projected).astype(BF16)
     proj_grad = (out_scale[..., None] * out_cotangent).astype(BF16)
     square_grad = -0.5 * scale_grad * out_scale * out_scale * out_scale / INNER
     out_weight_grad = jnp.einsum("btd,bti->di", proj_grad, scaled, preferred_element_type=F32)
@@ -424,14 +457,11 @@
         (scanned_grad * wide(jnp.exp(running))).astype(BF16),
         preferred_element_type=F32,
     )
-    gathered_back = lax.all_gather(local_back.astype(BF16), "seq")
+    leaving = states_after(local_back, block_decays, "seq")
     z_weight_grad = jnp.einsum("btd,btc->dc", normed, gate_grad, preferred_element_type=F32)
-    early_sums = lax.psum((out_weight_grad.astype(BF16), z_weight_grad.astype(BF16)), "seq")
-    leaving = jnp.zeros_like(local_back)
-    for k in range(seq_size - 1, 0, -1):
-        back_k = gathered_back[k].astype(F32)
-        leaving = jnp.where(k > seq_index, all_decays[k] * leaving + back_k, leaving)
-
+    early_grads = (out_weight_grad.astype(BF16), z_weight_grad.astype(BF16))
+    early_grads, _ = lax.optimization_barrier((early_grads, leaving))
+    early_sums = lax.psum(early_grads, "seq")
     x_grad, bc_grad, decay_grad, step_grad, skip_terms = scan_backward(
         x_values,
         b_values,
@@ -445,6 +475,11 @@
         states,
         leaving,
     )
+    projected = halving_sum(
+        partial_out.astype(BF16).reshape(rows, model_width), "head", after=bc_grad
+    )
+    projected = projected.reshape(inputs.shape).astype(F32)
+    block_out = (tokens + out_scale[..., None] * projected).astype(BF16)
     bc_total = halving_sum(bc_grad.reshape(rows, 2 * state_width), "head")
     bc_total = bc_total.reshape(bc_grad.shape).astype(F32)
 
@@ -488,14 +523,16 @@
         + jnp.einsum("bth,dh->btd", step_in_grad, step_weight, preferred_element_type=F32)
     )
     normed_sum = halving_sum(normed_partial.astype(BF16).reshape(rows, model_width), "head")
-    norm_gain_partial = lax.psum(jnp.sum(normed_partial * unit_tokens, axis=(0, 1)), "head")
+    norm_gain_partial = doubling_sum(jnp.sum(normed_partial * unit_tokens, axis=(0, 1)), "head")
     bc_in_grad, conv_bc_grad = conv_back(bc_total, local_inner, local_inner + 2 * state_width)
     bc_normed = jnp.einsum("btc,dc->btd", bc_in_grad, bc_weight, preferred_element_type=F32)
     norm_gain_grad = norm_gain_partial + jnp.sum(bc_normed * unit_tokens, axis=(0, 1))
     x_weight_grad = jnp.einsum("btd,btc->dc", normed, x_in_grad, preferred_element_type=F32)
     bc_weight_grad = jnp.einsum("btd,btc->dc", normed, bc_in_grad, preferred_element_type=F32)
     step_weight_grad = jnp.einsum("btd,bth->hd", normed, step_in_grad, preferred_element_type=F32)
-    late_sums = lax.psum((x_weight_grad.astype(BF16), bc_weight_grad.astype(BF16)), "seq")
+    late_grads = (x_weight_grad.astype(BF16), bc_weight_grad.astype(BF16))
+    late_grads, early_sums = lax.optimization_barrier((late_grads, early_sums))
+    late_sums = lax.psum(late_grads, "seq")
     small_grads = (
         norm_gain_grad,
         step_weight_grad,
@@ -507,7 +544,7 @@
     flat = jnp.concatenate([part.reshape(-1) for part in small_grads])
     count = flat.shape[0]
     flat = jnp.pad(flat, (0, -count % 1024)).reshape(-1, 128)
-    flat = lax.psum(flat, "seq").reshape(-1)
+    flat = doubling_sum(flat, "seq").reshape(-1)
     small_sums, at = [], 0
     for part in small_grads:
         small_sums.append(flat[at : at + part.size].reshape(part.shape))
@@ -518,7 +555,7 @@
     input_grad = out_cotangent + inverse_rms * (
         unit_grad - unit_tokens * jnp.mean(unit_grad * unit_tokens, axis=-1, keepdims=True)
     )
-    zx_sum = jnp.stack([early_sums[1], late_sums[0]], axis=1).astype(F32)
+    zx_sum = lane_tiles(jnp.stack([early_sums[1], late_sums[0]], axis=1)).astype(F32)
     summed_grads = (
         small_sums[0],
         zx_sum,
@@ -567,7 +604,13 @@
     for weight, mean_old, square_old, gradient, step_rate, decay_weight in zip(
         params, means, squares, summed_grads, LEARNING_RATES, WEIGHT_DECAYS
     ):
-        results.extend(adam_update(weight, mean_old, square_old, gradient, step_rate, decay_weight))
+        shape = weight.shape
+        if len(shape) == 3:
+            weight, mean_old, square_old = map(lane_tiles, (weight, mean_old, square_old))
+        updated = adam_update(weight, mean_old, square_old, gradient, step_rate, decay_weight)
+        if len(shape) == 3:
+            updated = [from_lane_tiles(part, shape) for part in updated]
+        results.extend(updated)
     return tuple(results)
 
 

time: 615 us -> 567 us (0.922)
  waiting for transfers between devices: 244 us -> 183 us
  blocking collectives: 53 us -> 10.1 us
  starting transfers between devices: 13.5 us -> 36.7 us
  matrix products: 82.1 us -> 99 us
  local copies, waits for them, and re-layouts: 41.6 us -> 55.3 us
    all_gather x2 -> x0, waiting for transfers between devices: 79.8 us -> none  [the longest x1 72.9 us: shards(): gathered = lax.all_gather(packed, 'seq')]
    ppermute x9 -> x14, waiting for transfers between devices: 69.7 us -> 19.1 us  [swapped(): lax.ppermute(block, axis, [(i, i ^ mask) for i in range(lax.axis_size(axi...]
    psum x2 -> x0, blocking collectives: 42.3 us -> none  [the longest x1 35.4 us: shards(): flat = lax.psum(flat, 'seq').reshape(-1)]
    psum x1 -> x2, waiting for transfers between devices: 89.7 us -> 131 us  [the longest x1 68.7 us: shards(): late_sums = lax.psum(late_grads, 'seq')]
    all_to_all x0 -> x4, waiting for transfers between devices: none -> 29.6 us  [exchanged(): return lax.all_to_all(blocks, axis, 0, 0, tiled=True)]
    all_to_all x0 -> x4, starting transfers between devices: none -> 18.3 us  [exchanged(): return lax.all_to_all(blocks, axis, 0, 0, tiled=True)]
    unnamed x4 -> x13, other arithmetic: 0.01 us -> 7.87 us
    unnamed x227 -> x220, local copies, waits for them, and re-layouts: 27.9 us -> 34.1 us
  transfers between devices with their start and end apart: 15 -> 23, of which waited for: 9 -> 10; matrix products, arithmetic and copies ran while one was open for 24% -> 34% of each run, Pallas kernels for 4% -> 5%
where the time goes in v2:
time: 567 us; the launch traced here: 559 us
  waiting for transfers between devices  183 us (32%)
  other arithmetic  119 us (21%)
  matrix products  99 us (17%)
  local copies, waits for them, and re-layouts  55.3 us (10%)
  Pallas kernels  39.9 us (7%)
  starting transfers between devices  36.7 us (6%)
  between operations  15.9 us (3%)
  blocking collectives  10.1 us (2%)
    psum x1, waiting for transfers between devices, shards(): late_sums = lax.psum(late_grads, 'seq')  68.7 us
    psum x1, waiting for transfers between devices, shards(): early_sums = lax.psum(early_grads, 'seq')  61.9 us
    unnamed x220, local copies, waits for them, and re-layouts  34.1 us
    all_to_all x4, waiting for transfers between devices, exchanged(): return lax.all_to_all(blocks, axis, 0, 0, tiled=True)  29.6 us
    pallas_call x1, Pallas kernels, scan_backward(): pl.pallas_call(back_kernel, grid=(seqs, chunks), in_specs=[block(inner),...  26.8 us
    sub x9, other arithmetic, adam_update(): weight - step_rate * (corrected_mean / (jnp.sqrt(corrected_square) + ADAM...  20.4 us
    ppermute x14, waiting for transfers between devices, swapped(): lax.ppermute(block, axis, [(i, i ^ mask) for i in range(lax.axis_size(axi...  19.1 us
    all_to_all x4, starting transfers between devices, exchanged(): return lax.all_to_all(blocks, axis, 0, 0, tiled=True)  18.3 us
  transfers between devices with their start and end apart: 23, of which 10 were waited for; matrix products, arithmetic and copies ran while one was open for 34% of the time, Pallas kernels for 5%

profile of v2, /device:TPU:0, one launch (start us, length us, event | category | flops | bytes accessed | tf_op | source)
XLA Modules:
  0.0 559.1 jit_solution(16817817468058718528)
XLA Ops:
  7.2 3.2 fusion.12
  11.8 2.3 copy-done.15
  14.1 3.7 convolution_convert_fusion
  18.6 4.9 collective-permute-start
  24.8 4.1 negate_multiply_fusion
  32.3 5.9 %multiply_convert_fusion.1 = (bf16[4,512,768]{2,1,0:T(8,128)(2,1)S(1)}, f32[4,512,768]{2,1,0:T(8,128)}) fusion(bf16[4,512,768]{2,1,0:T(8,128)(2,1)S(1)} %convolution_convert_fusion, f32[768]{0:T(1024)S(1)} %get-tuple-element.131, f32[768]{0:T(1024)S(1)} %get-tuple-element.132, f32[768]{0:T(1024)S(1)} %get-tuple-element.133, ...), kind=kLoop, calls=%fused_computation.33 | loop fusion | flops 40894464 | bytes 12616704 | tf_op jit(solution)/shard_map/convert_element_type | solution.py:413
  38.2 4.2 fusion.15
  43.8 4.9 all-to-all-start
  51.9 13.9 %all-to-all-done = bf16[8,80,512]{2,1,0:T(8,128)(2,1)S(1)} async-done(((bf16[8,80,512]{2,1,0:T(8,128)(2,1)}), bf16[8,80,512]{2,1,0:T(8,128)(2,1)S(1)}, u32[]{:S(2)}, u32[]{:S(2)}) %all-to-all-start) | async-done | bytes 655392 | tf_op jit(solution)/shard_map/all_to_all | solution.py:68
  71.1 4.3 all-to-all-start.1
  76.2 1.7 slice.312.x_ref
  77.9 2.3 fusion.135
  80.2 9.5 %all-to-all-done.1 = bf16[8,64,512]{2,1,0:T(8,128)(2,1)} async-done(((bf16[8,64,512]{2,1,0:T(8,128)(2,1)}), bf16[8,64,512]{2,1,0:T(8,128)(2,1)}, u32[]{:S(2)}, u32[]{:S(2)}) %all-to-all-start.1) | async-done | bytes 524320 | tf_op jit(solution)/shard_map/all_to_all | solution.py:68
  94.2 13.1 %shard_map.509 = (f32[4,512,512]{2,1,0:T(8,128)S(1)}, f32[4,4,128,512]{3,2,1,0:T(8,128)}) custom-call(bf16[4,512,512]{2,1,0:T(8,128)(2,1)S(1)} %slice.312.x_ref, bf16[4,512,128]{2,1,0:T(8,128)(2,1)S(1)} %copy-done.4, bf16[4,512,128]{2,1,0:T(8,128)(2,1)S(1)} %copy-done.2, f32[4,512,8]{2,1,0:T(8,128)S(1)} %copy-done, f32[4,512,8]{2,1,0:T(8,128)S(1)} %copy.87.decay_ref, ...), custom_call_target="tpu_custom_call" | custom-call | tf_op jit(solution)/shard_map/pallas_call | solution.py:268
  107.3 8.0 %multiply_reduce_fusion.6 = (f32[4,512]{1,0:T(4,128)S(1)}, f32[4,512,512]{2,1,0:T(8,128)}, f32[4,512,512]{2,1,0:T(8,128)}) fusion(f32[4,512,512]{2,1,0:T(8,128)S(1)} %get-tuple-element.43.y_ref, bf16[4,512,768]{2,1,0:T(8,128)(2,1)} %copy-done.21, f32[512]{0:T(512)S(1)} %mul.911, bf16[1024,2,512]{2,0,1:T(8,128)(2,1)S(1)} %copy-done.31, ...), kind=kOutput, calls=%fused_computation.66 | convolution fusion | flops 2166355968 | bytes 19945472 | tf_op jit(solution)/shard_map/btd,dc->btc/dot_general | solution.py:405
  115.3 6.8 %multiply_reduce_fusion = (f32[4,512]{1,0:T(4,128)S(1)}, bf16[4,512,1024]{2,1,0:T(8,128)(2,1)}) fusion(bf16[4,512,1024]{2,1,0:T(8,128)(2,1)S(1)} %copy-done.37, f32[4,512]{1,0:T(4,128)S(1)} %compare_convert_fusion, f32[1024,512]{1,0:T(8,128)S(1)} %copy-done.39, f32[4,512,512]{2,1,0:T(8,128)} %get-tuple-element.175, f32[512]{0:T(512)S(1)} %copy-done.93), kind=kOutput, calls=%fused_computation.30 | convolution fusion | flops 2160588800 | bytes 14698496 | tf_op jit(solution)/shard_map/bti,di->btd/dot_general | solution.py:441
  122.2 10.1 %psum.35 = f32[2,4,512]{2,1,0:T(4,128)S(1)} all-reduce(f32[2,4,512]{2,1,0:T(4,128)S(1)} %pad_maximum_fusion.6), channel_id=1, replica_groups=mesh['seq'=8,'head'=4] {'head'}, use_global_device_ids=true, to_apply=%region_3.4 | all-reduce | flops 4096 | bytes 32768 | tf_op jit(solution)/shard_map/psum | solution.py:444
  132.4 11.0 %multiply_convert_fusion.2 = (bf16[4,512,512]{2,1,0:T(8,128)(2,1)}, f32[4,512,512]{2,1,0:T(8,128)S(1)}, f32[512]{0:T(512)}) fusion(f32[4,512,512]{2,1,0:T(8,128)} %get-tuple-element.232, f32[4,512,512]{2,1,0:T(8,128)} %copy-done.6, f32[512]{0:T(512)} %copy-done.100, f32[4,512,512]{2,1,0:T(8,128)} %get-tuple-element.175, f32[4,512]{1,0:T(4,128)S(1)} %fusion.90, ...), kind=kOutput, calls=%fused_computation.61 | convolution fusion | flops 2177367552 | bytes 27293696 | tf_op jit(solution)/shard_map/btd,di->bti/dot_general | solution.py:449
  143.3 3.9 multiply_convert_fusion.3
  147.3 2.4 convolution_convert_fusion.1
  149.6 5.0 all-to-all-start.2
  154.6 7.7 %fusion.50 = f32[4,512,1024]{2,1,0:T(8,128)} fusion(bf16[4,512,512]{2,1,0:T(8,128)(2,1)} %get-tuple-element.184, bf16[1024,2,512]{2,0,1:T(8,128)(2,1)} %copy-done.30), kind=kOutput, calls=%fused_computation.147 | convolution fusion | flops 2147483648 | bytes 11534336 | tf_op jit(solution)/shard_map/btc,dc->btd/dot_general | solution.py:521
  162.4 3.6 bitcast_convert_fusion
  166.0 2.4 all-to-all-done.2
  174.8 4.2 all-to-all-start.3
  179.0 3.2 dynamic-slice_bitcast_fusion.1
  182.3 6.2 %bitcast_convert_fusion.1 = bf16[1024,512]{1,0:T(8,128)(2,1)} fusion(bf16[4,512,1024]{2,1,0:T(8,128)(2,1)S(1)} %copy-done.38, f32[4,512]{1,0:T(4,128)S(1)} %fusion.95, f32[4,512]{1,0:T(4,128)S(1)} %compare_convert_fusion, f32[4,512,512]{2,1,0:T(8,128)} %get-tuple-element.175, f32[512]{0:T(512)S(1)} %copy-done.94), kind=kOutput, calls=%fused_computation.95 | convolution fusion | flops 2158493696 | bytes 9455616 | tf_op jit(solution)/shard_map/btd,bti->di/dot_general | solution.py:448
  188.5 3.9 all-to-all-done.3
  196.8 26.8 %shard_map.510 = (f32[4,512,512]{2,1,0:T(8,128)}, bf16[4,512,256]{2,1,0:T(8,128)(2,1)S(1)}, f32[4,512,8]{2,1,0:T(8,128)S(1)}, f32[4,512,8]{2,1,0:T(8,128)S(1)}, f32[4,512,8]{2,1,0:T(8,128)S(1)}) custom-call(bf16[4,512,512]{2,1,0:T(8,128)(2,1)S(1)} %slice.312.x_ref, bf16[4,512,128]{2,1,0:T(8,128)(2,1)S(1)} %copy-done.5, bf16[4,512,128]{2,1,0:T(8,128)(2,1)S(1)} %copy-done.3, ...), custom_call_target="tpu_custom_call" | custom-call | tf_op jit(solution)/shard_map/pallas_call | solution.py:301
  223.7 9.0 %multiply_reduce_fusion.3 = (f32[512]{0:T(512)S(1)}, f32[512]{0:T(512)S(1)}, f32[512]{0:T(512)S(1)}, f32[512]{0:T(512)S(1)}, f32[512]{0:T(512)S(1)}, /*index=5*/f32[4,512,512]{2,1,0:T(8,128)}) fusion(bf16[4,512,768]{2,1,0:T(8,128)(2,1)S(1)} %copy-done.13, bf16[4,3,768]{2,1,0:T(4,128)(2,1)S(1)} %collective-permute-done, f32[4,512,512]{2,1,0:T(8,128)} %get-tuple-element.47, ...), kind=kLoop, calls=%fused_computation.56 | loop fusion | flops 31454720 | bytes 17860608 | tf_op jit(solution)/shard_map/reduce_sum | solution.py:493
  238.8 4.7 fusion.85
  243.5 6.6 %broadcast_multiply_fusion.3 = (f32[4,512,512]{2,1,0:T(8,128)S(1)}, f32[4,512,512]{2,1,0:T(8,128)S(1)}, f32[4,512,512]{2,1,0:T(8,128)S(1)}, f32[4,512,512]{2,1,0:T(8,128)}) fusion(f32[4,512,512]{2,1,0:T(8,128)} %get-tuple-element.169, f32[512]{0:T(512)S(1)} %bitcast.231, f32[512]{0:T(512)S(1)} %bitcast.234, f32[512]{0:T(512)S(1)} %bitcast.232, ...), kind=kLoop, calls=%fused_computation.106 | loop fusion | flops 4194304 | bytes 20979712 | tf_op jit(solution)/shard_map/mul | solution.py:499
  251.0 1.7 collective-permute-start.4
  252.7 6.3 %pad_add_fusion = f32[4,515,512]{2,1,0:T(8,128)} fusion(f32[4,512,512]{2,1,0:T(8,128)S(1)} %get-tuple-element.194, f32[4,512,512]{2,1,0:T(8,128)S(1)} %get-tuple-element.195, f32[4,512,512]{2,1,0:T(8,128)} %get-tuple-element.196, f32[4,512,512]{2,1,0:T(8,128)S(1)} %get-tuple-element.193), kind=kLoop, calls=%fused_computation.38 | loop fusion | flops 3164160 | bytes 20996096 | tf_op jit(solution)/shard_map/add | solution.py:498
  259.0 13.4 %fusion.138 = (bf16[4,512,1024]{2,1,0:T(8,128)(2,1)S(1)}, f32[4,512,1024]{2,1,0:T(8,128)}) fusion(f32[4,512,1024]{2,1,0:T(8,128)} %fusion.85, f32[4,512,1024]{2,1,0:T(8,128)} %fusion.50, bf16[1024,2,512]{2,0,1:T(8,128)(2,1)} %copy-done.30, f32[4,515,512]{2,1,0:T(8,128)} %pad_add_fusion, f32[4,3,512]{2,1,0:T(4,128)S(1)} %collective-permute-done.4), kind=kOutput, calls=%fused_computation.302 | convolution fusion | flops 2155872256 | bytes 34627584 | tf_op jit(solution)/shard_map/btc,dc->btd/dot_general | solution.py:522
  275.0 1.7 copy-done.18
  278.2 8.7 %collective-permute-done.9 = bf16[1024,256]{1,0:T(8,128)(2,1)S(1)} collective-permute-done((bf16[1024,256]{1,0:T(8,128)(2,1)S(1)}, bf16[1024,256]{1,0:T(8,128)(2,1)S(1)}, u32[]{:S(2)}, u32[]{:S(2)}) %collective-permute-start.9) | collective-permute-done | bytes 524320 | tf_op jit(solution)/shard_map/ppermute | solution.py:34
  287.1 7.2 %bitcast_convert_fusion.2 = bf16[1024,512]{1,0:T(8,128)(2,1)} fusion(f32[4,515,512]{2,1,0:T(8,128)} %pad_add_fusion, f32[4,3,512]{2,1,0:T(4,128)S(1)} %collective-permute-done.4, bf16[4,512,1024]{2,1,0:T(8,128)(2,1)} %param.30, f32[1024]{0:T(1024)S(1)} %copy-done.60, f32[4,512]{1,0:T(4,128)S(1)} %copy-done.55), kind=kOutput, calls=%fused_computation.96 | convolution fusion | flops 2158493696 | bytes 9474048 | tf_op jit(solution)/shard_map/btd,btc->dc/dot_general | solution.py:530
  294.3 4.1 fusion.21
  299.2 2.3 fusion.20
  302.8 3.2 multiply_reduce_fusion.8
  309.1 3.8 collective-permute-done.11
  312.9 5.0 fusion.38
  317.9 61.9 %all-reduce.18.cloned.1.call-done = (bf16[1024,512]{1,0:T(8,128)(2,1)}, bf16[1024,512]{1,0:T(8,128)(2,1)}) async-done(((bf16[1024,512]{1,0:T(8,128)(2,1)}, bf16[1024,512]{1,0:T(8,128)(2,1)}), (bf16[1024,512]{1,0:T(8,128)(2,1)}, bf16[1024,512]{1,0:T(8,128)(2,1)})) %all-reduce.18.cloned.1.call-update) | async-done | bytes 2097168 | tf_op jit(solution)/shard_map/psum | solution.py:464
  379.8 4.7 fusion.53
  384.5 7.5 %collective-permute-done.6 = bf16[1024,1024]{1,0:T(8,128)(2,1)} collective-permute-done((bf16[1024,1024]{1,0:T(8,128)(2,1)}, bf16[1024,1024]{1,0:T(8,128)(2,1)}, u32[]{:S(2)}, u32[]{:S(2)}) %collective-permute-start.6) | collective-permute-done | bytes 2097184 | tf_op jit(solution)/shard_map/ppermute | solution.py:34
  392.0 3.2 add_convert_fusion
  395.3 3.8 multiply_subtract_fusion.1
  399.1 4.8 add_convert_fusion.1
  404.4 68.7 %all-reduce.16.cloned.1.call-done = (bf16[1024,1,512]{2,0,1:T(8,128)(2,1)}, bf16[1024,256]{1,0:T(8,128)(2,1)}) async-done(((bf16[1024,1,512]{2,0,1:T(8,128)(2,1)}, bf16[1024,256]{1,0:T(8,128)(2,1)}), (bf16[1024,1,512]{2,0,1:T(8,128)(2,1)}, bf16[1024,256]{1,0:T(8,128)(2,1)})) %all-reduce.16.cloned.1.call-update) | async-done | bytes 1572880 | tf_op jit(solution)/shard_map/psum | solution.py:535
  473.1 10.5 %multiply_subtract_fusion = (f32[1024,2,512]{2,0,1:T(8,128)}, f32[1024,2,512]{2,0,1:T(8,128)}, f32[1024,2,512]{2,0,1:T(8,128)S(1)}) fusion(f32[1024,2,512]{2,1,0:T(2,128)} %param.36, bf16[1024,1,512]{2,0,1:T(8,128)(2,1)} %get-tuple-element.135, bf16[1024,1,512]{2,0,1:T(8,128)(2,1)S(1)} %bitcast.207, f32[1024,2,512]{2,1,0:T(2,128)} %param.38, ...), kind=kLoop, calls=%fused_computation.53 | loop fusion | flops 17825792 | bytes 27262976 | tf_op jit(solution)/shard_map/sub | solution.py:340
  483.7 2.0 broadcast_select_fusion.1
  485.7 2.6 pad_maximum_fusion.1
  491.6 7.1 %fusion.11 = (f32[1024]{0:T(1024)S(1)}, f32[4,512]{1,0:T(4,128)S(1)}, f32[1024]{0:T(1024)S(1)}) fusion(f32[4,512,1024]{2,1,0:T(8,128)S(1)} %bitcast.197, bf16[4,512,1024]{2,1,0:T(8,128)(2,1)S(1)} %copy-done.19, f32[4,512]{1,0:T(4,128)S(1)} %copy-done.55, f32[1024]{0:T(1024)S(1)} %copy-done.60, bf16[4,512,1024]{2,1,0:T(8,128)(2,1)} %bitcast.200, ...), kind=kLoop, calls=%fused_computation.22 | loop fusion | flops 23064576 | bytes 25194496 | tf_op jit(solution)/shard_map/reduce_sum | solution.py:529
  498.8 2.2 multiply_subtract_fusion.2
  502.0 5.2 copy.104
  507.3 5.2 copy.103
  512.5 5.2 copy.102
  517.8 1.5 collective-permute-start.13
  519.3 4.5 broadcast_select_fusion.3
  525.5 3.2 pad_maximum_fusion
  530.0 2.9 collective-permute-done.15
  532.9 1.8 collective-permute-start.16
  535.0 12.2 %fusion.9 = (f32[4,512,1024]{2,1,0:T(8,128)}, bf16[4,512,1024]{2,1,0:T(8,128)(2,1)}) fusion(bf16[4,512,1024]{2,1,0:T(8,128)(2,1)S(1)} %copy-done.20, bf16[4,512,1024]{2,1,0:T(8,128)(2,1)} %param.31, f32[4,512,1024]{2,1,0:T(8,128)} %fusion.53, f32[4,512]{1,0:T(4,128)S(1)} %broadcast_multiply_fusion.8, f32[4,512]{1,0:T(4,128)S(1)} %copy-done.64, ...), kind=kLoop, calls=%fused_computation.20 | loop fusion | flops 39845888 | bytes 37785600 | tf_op jit(solution)/shard_map/add | solution.py:555
  (342 shorter events, 61.5 us)
Async XLA Ops:
  10.5 14.3 %copy-start.53 = (f32[4,512]{1,0:T(4,128)}, f32[4,512]{1,0:T(4,128)S(1)}, u32[]{:S(2)}) copy-start(f32[4,512]{1,0:T(4,128)S(1)} %add_rsqrt_fusion) | copy-start | bytes 24580
  14.1 9.4 %copy-start.81 = (f32[3,8]{1,0:T(4,128)S(1)}, f32[3,8]{1,0:T(4,128)}, u32[]{:S(2)}) copy-start(f32[3,8]{1,0:T(4,128)} %param.51) | copy-start | bytes 292
  14.1 9.9 %copy-start.51 = (f32[5,512]{1,0:T(8,128)S(1)}, f32[5,512]{1,0:T(8,128)}, u32[]{:S(2)}) copy-start(f32[5,512]{1,0:T(8,128)} %param.45) | copy-start | bytes 30724
  14.1 10.6 %copy-start.50 = (f32[1024,8]{0,1:T(8,128)S(1)}, f32[1024,8]{0,1:T(8,128)}, u32[]{:S(2)}) copy-start(f32[1024,8]{0,1:T(8,128)} %param.42) | copy-start | bytes 98308
  17.9 14.4 %copy-start.12 = (bf16[4,512,768]{2,1,0:T(8,128)(2,1)}, bf16[4,512,768]{2,1,0:T(8,128)(2,1)S(1)}, u32[]{:S(2)}) copy-start(bf16[4,512,768]{2,1,0:T(8,128)(2,1)S(1)} %convolution_convert_fusion) | copy-start | bytes 9437188
  18.6 13.7 %collective-permute-start = (bf16[4,3,768]{2,1,0:T(4,128)(2,1)}, bf16[4,3,768]{2,1,0:T(4,128)(2,1)S(1)}, u32[]{:S(2)}, u32[]{:S(2)}) collective-permute-start(bf16[4,3,768]{2,1,0:T(4,128)(2,1)} %slice.302), channel_id=1, source_target_pairs={{0,4},{4,8},{8,12},{12,16},{16,20},{20,24},{24,28},{1,5},{5,9},{9,... | collective-permute-start | bytes 55304 | tf_op jit(solution)/shard_map/ppermute | solution.py:30
  38.2 10.5 %copy-start.101 = (f32[8]{0:T(128)S(1)}, f32[8]{0:T(128)}, u32[]{:S(2)}) copy-start(f32[8]{0:T(128)} %get-tuple-element.228) | copy-start | bytes 100
  43.8 21.9 %all-to-all-start = ((bf16[8,80,512]{2,1,0:T(8,128)(2,1)}), bf16[8,80,512]{2,1,0:T(8,128)(2,1)S(1)}, u32[]{:S(2)}, u32[]{:S(2)}) async-start(bf16[8,80,512]{2,1,0:T(8,128)(2,1)} %pad_maximum_fusion.5), calls=%async_computation | async-start | bytes 1310720 | tf_op jit(solution)/shard_map/all_to_all | solution.py:68
  48.7 26.7 %copy-start.102 = (s32[4]{0:T(128)S(1)}, s32[4]{0:T(128)}, u32[]{:S(2)}) copy-start(s32[4]{0:T(128)} %param.32) | copy-start | bytes 52
  48.7 27.4 %copy-start.84 = (f32[8]{0:T(128)S(1)}, f32[8]{0:T(128)}, u32[]{:S(2)}) copy-start(f32[8]{0:T(128)} %copy-done.83) | copy-start | bytes 100
  48.9 58.4 %copy-start.100 = (f32[512]{0:T(512)}, f32[512]{0:T(512)S(1)}, u32[]{:S(2)}) copy-start(f32[512]{0:T(512)S(1)} %mul.911) | copy-start | bytes 6148
  71.1 18.6 %all-to-all-start.1 = ((bf16[8,64,512]{2,1,0:T(8,128)(2,1)}), bf16[8,64,512]{2,1,0:T(8,128)(2,1)}, u32[]{:S(2)}, u32[]{:S(2)}) async-start(bf16[8,64,512]{2,1,0:T(8,128)(2,1)} %fusion.69), calls=%async_computation.1 | async-start | bytes 1048576 | tf_op jit(solution)/shard_map/all_to_all | solution.py:68
  75.5 106.8 %copy-start.63 = (f32[4,512]{1,0:T(4,128)}, f32[4,512]{1,0:T(4,128)S(1)}, u32[]{:S(2)}) copy-start(f32[4,512]{1,0:T(4,128)S(1)} %compare_convert_fusion) | copy-start | bytes 24580
  80.2 27.1 %copy-start.54 = (f32[4,512]{1,0:T(4,128)S(1)}, f32[4,512]{1,0:T(4,128)}, u32[]{:S(2)}) copy-start(f32[4,512]{1,0:T(4,128)} %copy-done.53) | copy-start | bytes 24580
  94.2 13.1 %copy-start.16 = (bf16[4,512,1024]{2,1,0:T(8,128)(2,1)S(1)}, bf16[4,512,1024]{2,1,0:T(8,128)(2,1)}, u32[]{:S(2)}) copy-start(bf16[4,512,1024]{2,1,0:T(8,128)(2,1)} %param.30) | copy-start | bytes 12582916
  94.2 13.1 %copy-start.31 = (bf16[1024,2,512]{2,0,1:T(8,128)(2,1)S(1)}, bf16[1024,2,512]{2,0,1:T(8,128)(2,1)}, u32[]{:S(2)}) copy-start(bf16[1024,2,512]{2,0,1:T(8,128)(2,1)} %copy-done.30) | copy-start | bytes 6291460
  132.3 50.0 %copy-start.65 = (f32[4,512]{1,0:T(4,128)}, f32[4,512]{1,0:T(4,128)S(1)}, u32[]{:S(2)}) copy-start(f32[4,512]{1,0:T(4,128)S(1)} %fusion.95) | copy-start | bytes 24580
  149.6 18.8 %all-to-all-start.2 = ((bf16[8,64,512]{2,1,0:T(8,128)(2,1)}), bf16[8,64,512]{2,1,0:T(8,128)(2,1)}, u32[]{:S(2)}, u32[]{:S(2)}) async-start(bf16[8,64,512]{2,1,0:T(8,128)(2,1)} %bitcast.204), calls=%async_computation.2 | async-start | bytes 1048576 | tf_op jit(solution)/shard_map/all_to_all | solution.py:68
  169.5 12.7 %copy-start.94 = (f32[512]{0:T(512)S(1)}, f32[512]{0:T(512)}, u32[]{:S(2)}) copy-start(f32[512]{0:T(512)} %param.54) | copy-start | bytes 6148
  174.8 17.5 %all-to-all-start.3 = ((bf16[8,64,512]{2,1,0:T(8,128)(2,1)}), bf16[8,64,512]{2,1,0:T(8,128)(2,1)}, u32[]{:S(2)}, u32[]{:S(2)}) async-start(bf16[8,64,512]{2,1,0:T(8,128)(2,1)} %constant_dynamic-update-slice_fusion.3), calls=%async_computation.3 | async-start | bytes 1048576 | tf_op jit(solution)/shard_map/all_to_all | solution.py:68
  179.0 200.8 %all-reduce.18.cloned.1.call-start = ((), (), s32[]{:S(2)}) async-start(), calls=%async_computation.5 | async-start | bytes 4194304 | tf_op jit(solution)/shard_map/psum | solution.py:464
  182.3 112.0 %collective-permute-start.1 = (bf16[1024,1024]{1,0:T(8,128)(2,1)}, bf16[1024,1024]{1,0:T(8,128)(2,1)}, u32[]{:S(2)}, u32[]{:S(2)}) collective-permute-start(bf16[1024,1024]{1,0:T(8,128)(2,1)} %dynamic-slice_bitcast_fusion.1), channel_id=1, source_target_pairs={{0,1},{1,0},{2,3},{3,2},{4,5},{5,4},{6,7},{7,6},{8,9},{9,8},{10,11... | collective-permute-start | bytes 6291464 | tf_op jit(solution)/shard_map/ppermute | solution.py:34
  196.8 26.8 %copy-start.13 = (bf16[4,512,768]{2,1,0:T(8,128)(2,1)S(1)}, bf16[4,512,768]{2,1,0:T(8,128)(2,1)}, u32[]{:S(2)}) copy-start(bf16[4,512,768]{2,1,0:T(8,128)(2,1)} %copy-done.12) | copy-start | bytes 9437188
  223.6 13.7 %copy-start.85 = (f32[8]{0:T(128)S(1)}, f32[8]{0:T(128)}, u32[]{:S(2)}) copy-start(f32[8]{0:T(128)} %copy-done.83) | copy-start | bytes 100
  238.7 33.7 %collective-permute-start.8 = (bf16[1024,256]{1,0:T(8,128)(2,1)S(1)}, bf16[1024,256]{1,0:T(8,128)(2,1)S(1)}, u32[]{:S(2)}, u32[]{:S(2)}) collective-permute-start(bf16[1024,256]{1,0:T(8,128)(2,1)S(1)} %dynamic-slice_bitcast_fusion.2), channel_id=1, source_target_pairs={{0,1},{1,0},{2,3},{3,2},{4,5},{5,4},{6,7},{7,6},{8,9},{9,8},{10,11... | collective-permute-start | bytes 1572872 | tf_op jit(solution)/shard_map/ppermute | solution.py:34
  251.0 8.0 %collective-permute-start.4 = (f32[4,3,512]{2,1,0:T(4,128)S(1)}, f32[4,3,512]{2,1,0:T(4,128)S(1)}, u32[]{:S(2)}, u32[]{:S(2)}) collective-permute-start(f32[4,3,512]{2,1,0:T(4,128)S(1)} %pad_add_fusion.2), channel_id=1, source_target_pairs={{4,0},{8,4},{12,8},{16,12},{20,16},{24,20},{28,24},{5,1},{9,5},{13... | collective-permute-start | bytes 73736 | tf_op jit(solution)/shard_map/ppermute | solution.py:30
  259.0 13.4 %copy-start.11 = (bf16[4,512,256]{2,1,0:T(8,128)(2,1)S(1)}, bf16[4,512,256]{2,1,0:T(8,128)(2,1)}, u32[]{:S(2)}) copy-start(bf16[4,512,256]{2,1,0:T(8,128)(2,1)} %copy-done.10) | copy-start | bytes 3145732
  272.6 14.4 %collective-permute-start.9 = (bf16[1024,256]{1,0:T(8,128)(2,1)S(1)}, bf16[1024,256]{1,0:T(8,128)(2,1)S(1)}, u32[]{:S(2)}, u32[]{:S(2)}) collective-permute-start(bf16[1024,256]{1,0:T(8,128)(2,1)S(1)} %fusion.43), channel_id=1, source_target_pairs={{0,2},{1,3},{2,0},{3,1},{4,6},{5,7},{6,4},{7,5},{8,10},{9,11},{10,... | collective-permute-start | bytes 1572872 | tf_op jit(solution)/shard_map/ppermute | solution.py:34
  274.9 24.3 %collective-permute-start.5 = (bf16[1024,1024]{1,0:T(8,128)(2,1)}, bf16[1024,1024]{1,0:T(8,128)(2,1)S(1)}, u32[]{:S(2)}, u32[]{:S(2)}) collective-permute-start(bf16[1024,1024]{1,0:T(8,128)(2,1)} %dynamic-slice_bitcast_fusion), channel_id=1, source_target_pairs={{0,1},{1,0},{2,3},{3,2},{4,5},{5,4},{6,7},{7,6},{8,9},{9,8},{10,11... | collective-permute-start | bytes 6291464 | tf_op jit(solution)/shard_map/ppermute | solution.py:34
  278.0 195.1 %all-reduce.16.cloned.1.call-start = ((), (), s32[]{:S(2)}) async-start(), calls=%async_computation.4 | async-start | bytes 3145728 | tf_op jit(solution)/shard_map/psum | solution.py:535
  287.1 12.0 %collective-permute-start.10 = (bf16[1024,256]{1,0:T(8,128)(2,1)S(1)}, bf16[1024,256]{1,0:T(8,128)(2,1)S(1)}, u32[]{:S(2)}, u32[]{:S(2)}) collective-permute-start(bf16[1024,256]{1,0:T(8,128)(2,1)S(1)} %add_convert_fusion.2), channel_id=1, source_target_pairs={{0,1},{1,0},{2,3},{3,2},{4,5},{5,4},{6,7},{7,6},{8,9},{9,8},{10,11... | collective-permute-start | bytes 1572872 | tf_op jit(solution)/shard_map/ppermute | solution.py:34
  298.4 100.7 %collective-permute-start.2 = (bf16[1024,1024]{1,0:T(8,128)(2,1)}, bf16[1024,1024]{1,0:T(8,128)(2,1)}, u32[]{:S(2)}, u32[]{:S(2)}) collective-permute-start(bf16[1024,1024]{1,0:T(8,128)(2,1)} %fusion.21), channel_id=1, source_target_pairs={{0,2},{1,3},{2,0},{3,1},{4,6},{5,7},{6,4},{7,5},{8,10},{9,11},{10,... | collective-permute-start | bytes 6291464 | tf_op jit(solution)/shard_map/ppermute | solution.py:34
  301.5 90.5 %collective-permute-start.6 = (bf16[1024,1024]{1,0:T(8,128)(2,1)}, bf16[1024,1024]{1,0:T(8,128)(2,1)}, u32[]{:S(2)}, u32[]{:S(2)}) collective-permute-start(bf16[1024,1024]{1,0:T(8,128)(2,1)} %fusion.20), channel_id=1, source_target_pairs={{0,2},{1,3},{2,0},{3,1},{4,6},{5,7},{6,4},{7,5},{8,10},{9,11},{10,... | collective-permute-start | bytes 6291464 | tf_op jit(solution)/shard_map/ppermute | solution.py:34
  306.9 6.0 %collective-permute-start.11 = (f32[4,3,256]{2,1,0:T(4,128)S(1)}, f32[4,3,256]{2,1,0:T(4,128)S(1)}, u32[]{:S(2)}, u32[]{:S(2)}) collective-permute-start(f32[4,3,256]{2,1,0:T(4,128)S(1)} %pad_add_fusion.3), channel_id=1, source_target_pairs={{4,0},{8,4},{12,8},{16,12},{20,16},{24,20},{28,24},{5,1},{9,5},{13... | collective-permute-start | bytes 36872 | tf_op jit(solution)/shard_map/ppermute | solution.py:30
  309.1 70.7 %copy-start.44 = (bf16[1024,256]{1,0:T(8,128)(2,1)S(1)}, bf16[1024,256]{1,0:T(8,128)(2,1)}, u32[]{:S(2)}) copy-start(bf16[1024,256]{1,0:T(8,128)(2,1)} %copy-done.43) | copy-start | bytes 1572868
  379.8 15.5 %copy-start.47 = (bf16[1024,512]{1,0:T(8,128)(2,1)S(1)}, bf16[1024,512]{1,0:T(8,128)(2,1)}, u32[]{:S(2)}) copy-start(bf16[1024,512]{1,0:T(8,128)(2,1)} %get-tuple-element.56) | copy-start | bytes 3145732
  384.5 10.8 %copy-start.40 = (f32[1024,512]{1,0:T(8,128)S(1)}, f32[1024,512]{1,0:T(8,128)}, u32[]{:S(2)}) copy-start(f32[1024,512]{1,0:T(8,128)} %param.57) | copy-start | bytes 6291460
  384.5 10.8 %copy-start.41 = (f32[1024,512]{1,0:T(8,128)S(1)}, f32[1024,512]{1,0:T(8,128)}, u32[]{:S(2)}) copy-start(f32[1024,512]{1,0:T(8,128)} %param.59) | copy-start | bytes 6291460
  384.5 10.8 %copy-start.42 = (f32[1024,512]{1,0:T(8,128)S(1)}, f32[1024,512]{1,0:T(8,128)}, u32[]{:S(2)}) copy-start(f32[1024,512]{1,0:T(8,128)} %param.58) | copy-start | bytes 6291460
  395.2 88.5 %collective-permute-start.7 = (bf16[1024,1024]{1,0:T(8,128)(2,1)S(1)}, bf16[1024,1024]{1,0:T(8,128)(2,1)}, u32[]{:S(2)}, u32[]{:S(2)}) collective-permute-start(bf16[1024,1024]{1,0:T(8,128)(2,1)S(1)} %add_convert_fusion), channel_id=1, source_target_pairs={{0,1},{1,0},{2,3},{3,2},{4,5},{5,4},{6,7},{7,6},{8,9},{9,8},{10,11... | collective-permute-start | bytes 6291464 | tf_op jit(solution)/shard_map/ppermute | solution.py:34
  399.1 74.0 %copy-start.48 = (bf16[1024,512]{1,0:T(8,128)(2,1)S(1)}, bf16[1024,512]{1,0:T(8,128)(2,1)}, u32[]{:S(2)}) copy-start(bf16[1024,512]{1,0:T(8,128)(2,1)} %get-tuple-element.53) | copy-start | bytes 3145732
  403.9 115.4 %collective-permute-start.3 = (bf16[1024,1024]{1,0:T(8,128)(2,1)}, bf16[1024,1024]{1,0:T(8,128)(2,1)}, u32[]{:S(2)}, u32[]{:S(2)}) collective-permute-start(bf16[1024,1024]{1,0:T(8,128)(2,1)} %add_convert_fusion.1), channel_id=1, source_target_pairs={{0,1},{1,0},{2,3},{3,2},{4,5},{5,4},{6,7},{7,6},{8,9},{9,8},{10,11... | collective-permute-start | bytes 6291464 | tf_op jit(solution)/shard_map/ppermute | solution.py:34
  473.1 10.6 %copy-start.33 = (bf16[1024,1024]{1,0:T(8,128)(2,1)S(1)}, bf16[1024,1024]{1,0:T(8,128)(2,1)}, u32[]{:S(2)}) copy-start(bf16[1024,1024]{1,0:T(8,128)(2,1)} %copy-done.32) | copy-start | bytes 6291460
  498.7 19.1 %collective-permute-start.12 = (f32[1024]{0:T(1024)S(1)}, f32[1024]{0:T(1024)S(1)}, u32[]{:S(2)}, u32[]{:S(2)}) collective-permute-start(f32[1024]{0:T(1024)S(1)} %get-tuple-element.125), channel_id=1, source_target_pairs={{0,1},{1,0},{2,3},{3,2},{4,5},{5,4},{6,7},{7,6},{8,9},{9,8},{10,11... | collective-permute-start | bytes 12296 | tf_op jit(solution)/shard_map/ppermute | solution.py:34
  517.8 6.0 %collective-permute-start.13 = (f32[1024]{0:T(1024)S(1)}, f32[1024]{0:T(1024)S(1)}, u32[]{:S(2)}, u32[]{:S(2)}) collective-permute-start(f32[1024]{0:T(1024)S(1)} %add.558), channel_id=1, source_target_pairs={{0,2},{1,3},{2,0},{3,1},{4,6},{5,7},{6,4},{7,5},{8,10},{9,11},{10,... | collective-permute-start | bytes 12296 | tf_op jit(solution)/shard_map/ppermute | solution.py:34
  523.9 4.7 collective-permute-start.14
  528.6 4.2 collective-permute-start.15
  532.9 14.3 %collective-permute-start.16 = (f32[112,128]{1,0:T(8,128)S(1)}, f32[112,128]{1,0:T(8,128)S(1)}, u32[]{:S(2)}, u32[]{:S(2)}) collective-permute-start(f32[112,128]{1,0:T(8,128)S(1)} %fusion.150), channel_id=1, source_target_pairs={{0,16},{4,20},{8,24},{12,28},{16,0},{20,4},{24,8},{28,12},{1,17},{... | collective-permute-start | bytes 172040 | tf_op jit(solution)/shard_map/ppermute | solution.py:34
  534.8 13.0 %copy-start.90 = (f32[1024]{0:T(1024)S(1)}, f32[1024]{0:T(1024)}, u32[]{:S(2)}) copy-start(f32[1024]{0:T(1024)} %param.35) | copy-start | bytes 12292
  534.8 13.0 %copy-start.91 = (f32[1024]{0:T(1024)S(1)}, f32[1024]{0:T(1024)}, u32[]{:S(2)}) copy-start(f32[1024]{0:T(1024)} %param.34) | copy-start | bytes 12292
  534.8 13.6 %copy-start.95 = (f32[512]{0:T(512)S(1)}, f32[512]{0:T(512)}, u32[]{:S(2)}) copy-start(f32[512]{0:T(512)} %param.54) | copy-start | bytes 6148
  534.8 13.6 %copy-start.96 = (f32[512]{0:T(512)S(1)}, f32[512]{0:T(512)}, u32[]{:S(2)}) copy-start(f32[512]{0:T(512)} %param.56) | copy-start | bytes 6148
  534.8 13.6 %copy-start.97 = (f32[512]{0:T(512)S(1)}, f32[512]{0:T(512)}, u32[]{:S(2)}) copy-start(f32[512]{0:T(512)} %param.55) | copy-start | bytes 6148
  534.8 14.3 %copy-start.59 = (f32[5,256]{1,0:T(8,128)S(1)}, f32[5,256]{1,0:T(8,128)}, u32[]{:S(2)}) copy-start(f32[5,256]{1,0:T(8,128)} %param.48) | copy-start | bytes 15364
  534.8 14.3 %copy-start.79 = (f32[5,256]{1,0:T(8,128)S(1)}, f32[5,256]{1,0:T(8,128)}, u32[]{:S(2)}) copy-start(f32[5,256]{1,0:T(8,128)} %param.50) | copy-start | bytes 15364
  534.9 14.3 %copy-start.80 = (f32[5,256]{1,0:T(8,128)S(1)}, f32[5,256]{1,0:T(8,128)}, u32[]{:S(2)}) copy-start(f32[5,256]{1,0:T(8,128)} %param.49) | copy-start | bytes 15364
  534.9 14.9 %copy-start.52 = (f32[5,512]{1,0:T(8,128)S(1)}, f32[5,512]{1,0:T(8,128)}, u32[]{:S(2)}) copy-start(f32[5,512]{1,0:T(8,128)} %param.45) | copy-start | bytes 30724
  534.9 14.9 %copy-start.72 = (f32[5,512]{1,0:T(8,128)S(1)}, f32[5,512]{1,0:T(8,128)}, u32[]{:S(2)}) copy-start(f32[5,512]{1,0:T(8,128)} %param.47) | copy-start | bytes 30724
  534.9 14.9 %copy-start.73 = (f32[5,512]{1,0:T(8,128)S(1)}, f32[5,512]{1,0:T(8,128)}, u32[]{:S(2)}) copy-start(f32[5,512]{1,0:T(8,128)} %param.46) | copy-start | bytes 30724
  534.9 15.5 %copy-start.61 = (f32[1024,8]{0,1:T(8,128)S(1)}, f32[1024,8]{0,1:T(8,128)}, u32[]{:S(2)}) copy-start(f32[1024,8]{0,1:T(8,128)} %param.44) | copy-start | bytes 98308
  534.9 15.5 %copy-start.62 = (f32[1024,8]{0,1:T(8,128)S(1)}, f32[1024,8]{0,1:T(8,128)}, u32[]{:S(2)}) copy-start(f32[1024,8]{0,1:T(8,128)} %param.43) | copy-start | bytes 98308
  534.9 16.1 %copy-start.82 = (f32[3,8]{1,0:T(4,128)S(1)}, f32[3,8]{1,0:T(4,128)}, u32[]{:S(2)}) copy-start(f32[3,8]{1,0:T(4,128)} %param.51) | copy-start | bytes 292
  534.9 16.1 %copy-start.98 = (f32[3,8]{1,0:T(4,128)S(1)}, f32[3,8]{1,0:T(4,128)}, u32[]{:S(2)}) copy-start(f32[3,8]{1,0:T(4,128)} %param.53) | copy-start | bytes 292
  534.9 16.1 %copy-start.99 = (f32[3,8]{1,0:T(4,128)S(1)}, f32[3,8]{1,0:T(4,128)}, u32[]{:S(2)}) copy-start(f32[3,8]{1,0:T(4,128)} %param.52) | copy-start | bytes 292
  (65 other events, 355.2 us)
Sparse Core Ops, SparseCore 0:
  278.1 101.5 all-reduce.17
  383.9 89.1 all-reduce.15

commit v3 on v2

--- a/solution.py
+++ b/solution.py
@@ -40,28 +40,46 @@
     return part
 
 
-def halving_sum(part, axis, after=None):
-    index = lax.axis_index(axis)
-    masks = [1 << k for k in range(lax.axis_size(axis).bit_length() - 1)]
-    rest = part.shape[1:]
-    for mask in masks[:-1]:
-        bit = (index // mask) % 2
-        halves = part.reshape((2, part.shape[0] // 2) + rest)
+def axis_masks(axis):
+    return [1 << k for k in range(lax.axis_size(axis).bit_length() - 1)]
+
+
+def near_bit(axis, mask):
+    return (lax.axis_index(axis) // mask) % 2
+
+
+def added(a, b):
+    return (a.astype(F32) + b.astype(F32)).astype(BF16)
+
+
+def halved(part, axis):
+    for mask in axis_masks(axis)[:-1]:
+        bit = near_bit(axis, mask)
+        halves = part.reshape((2, part.shape[0] // 2) + part.shape[1:])
         sent = lax.dynamic_index_in_dim(halves, 1 - bit, 0, keepdims=False)
         kept = lax.dynamic_index_in_dim(halves, bit, 0, keepdims=False)
-        got = swapped(sent, axis, mask)
-        part = (kept.astype(F32) + got.astype(F32)).astype(BF16)
-    got = swapped(part, axis, masks[-1])
-    if after is not None:
-        got, _ = lax.optimization_barrier((got, after))
-    part = (part.astype(F32) + got.astype(F32)).astype(BF16)
-    for mask in reversed(masks[:-1]):
-        bit = (index // mask) % 2
-        got = swapped(part, axis, mask)
-        first = jnp.where(bit == 0, part, got)
-        second = jnp.where(bit == 0, got, part)
-        part = jnp.concatenate([first, second], axis=0)
+        part = added(kept, swapped(sent, axis, mask))
     return part
+
+
+def joined(part, got, bit):
+    first = jnp.where(bit == 0, part, got)
+    second = jnp.where(bit == 0, got, part)
+    return jnp.concatenate([first, second], axis=0)
+
+
+def regathered(part, axis):
+    masks = axis_masks(axis)[:-1]
+    for mask in reversed(masks[1:]):
+        part = joined(part, swapped(part, axis, mask), near_bit(axis, mask))
+    return part, swapped(part, axis, masks[0])
+
+
+def halving_sum(part, axis):
+    part = halved(part, axis)
+    part = added(part, swapped(part, axis, axis_masks(axis)[-1]))
+    part, other = regathered(part, axis)
+    return joined(part, other, near_bit(axis, 1))
 
 
 def exchanged(blocks, axis):
@@ -102,7 +120,7 @@
 
 def lane_tiles(a):
     rows, two, columns = a.shape
-    return a.reshape(rows, two, columns // 128, 128).transpose(0, 2, 1, 3).reshape(-1, 128)
+    return a.reshape(rows, two, columns // 128, 128).transpose(0, 2, 1, 3).reshape(rows, -1, 128)
 
 
 def from_lane_tiles(a, shape):
@@ -287,6 +305,7 @@
         ],
         scratch_shapes=[pltpu.VMEM((state, inner), F32)],
         compiler_params=pltpu.CompilerParams(vmem_limit_bytes=40 << 20),
+        cost_estimate=load(13),
     )(x, b, c, step, decay, decay_t, enter)
 
 
@@ -324,7 +343,111 @@
         ],
         scratch_shapes=[pltpu.VMEM((state, inner), F32)],
         compiler_params=pltpu.CompilerParams(vmem_limit_bytes=40 << 20),
+        cost_estimate=load(27),
     )(x, b, c, step, decay, decay_t, skip, dy, y, states, leave)
+
+
+def picked(scalars_ref, part_ref, got_ref):
+    bit = scalars_ref[scalars_ref.shape[0] - 1]
+    half = pl.num_programs(0) // 2
+    own = (pl.program_id(0) // half) == bit
+    return jnp.where(own, part_ref[...].astype(F32), got_ref[...].astype(F32))
+
+
+def out_kernel(scalars_ref, part_ref, got_ref, tokens_ref, scale_ref, out_ref):
+    projected = picked(scalars_ref, part_ref, got_ref)
+    out_ref[...] = (tokens_ref[...].astype(F32) + scale_ref[...] * projected).astype(BF16)
+
+
+def tail_kernel(
+    local_len, scalars_ref, part_ref, got_ref, bc_ref, weight_ref, tokens_ref, back_ref, gain_ref,
+    out_ref, gain_grad_ref
+):
+    step = pl.program_id(0)
+    height = tokens_ref.shape[0]
+    normed_grad = picked(scalars_ref, part_ref, got_ref) + dot(
+        bc_ref[...], weight_ref[...], ((1,), (1,))
+    )
+    tokens = tokens_ref[...].astype(F32)
+    inverse_rms = lax.rsqrt(jnp.mean(tokens * tokens, axis=-1, keepdims=True) + EPS)
+    unit = tokens * inverse_rms
+
+    @pl.when(step == 0)
+    def _():
+        gain_grad_ref[...] = jnp.zeros_like(gain_grad_ref)
+
+    gain_grad_ref[...] += jnp.sum(normed_grad * unit, axis=0, keepdims=True)
+    unit_grad = normed_grad * gain_ref[...]
+    along = jnp.mean(unit_grad * unit, axis=-1, keepdims=True)
+    row = step * height
+    length = scalars_ref[row // local_len]
+    start = scalars_ref[scalars_ref.shape[0] - 2] + row % local_len
+    position = start + lax.broadcasted_iota(jnp.int32, tokens.shape, 0)
+    back = jnp.where(position < length, back_ref[...].astype(F32), 0.0)
+    out_ref[...] = back + inverse_rms * (unit_grad - unit * along)
+
+
+ROWS = 256
+
+
+def load(microseconds):
+    return pl.CostEstimate(flops=0, transcendentals=0, bytes_accessed=int(microseconds * 3.69e6))
+
+
+def merge_call(kernel, scalars, part, got, others, other_specs, out_specs, out_shape):
+    rows, width = 2 * part.shape[0], part.shape[1]
+    blocks = rows // ROWS
+    half = pl.BlockSpec((ROWS, width), lambda i, s: (i % (blocks // 2), 0))
+    return pl.pallas_call(
+        kernel,
+        grid_spec=pltpu.PrefetchScalarGridSpec(
+            num_scalar_prefetch=1,
+            grid=(blocks,),
+            in_specs=[half, half] + other_specs,
+            out_specs=out_specs,
+        ),
+        out_shape=out_shape,
+        compiler_params=pltpu.CompilerParams(vmem_limit_bytes=40 << 20),
+        cost_estimate=load(8),
+    )(scalars, part, got, *others)
+
+
+def row_block(lanes):
+    return pl.BlockSpec((ROWS, lanes), lambda i, s: (i, 0))
+
+
+def whole_block(shape):
+    return pl.BlockSpec(shape, lambda i, s: (0, 0))
+
+
+def adam_kernel(
+    step_rate, decay_weight, first_ref, second_ref, weight_ref, mean_ref, square_ref,
+    mean_out, square_out, weight_out
+):
+    for r in range(weight_ref.shape[1]):
+        source = first_ref if r % 2 == 0 else second_ref
+        gradient = source[:, (r // 2) * 128 : (r // 2 + 1) * 128].astype(F32)
+        updated = adam_update(
+            weight_ref[:, r], mean_ref[:, r], square_ref[:, r], gradient, step_rate, decay_weight
+        )
+        mean_out[:, r], square_out[:, r], weight_out[:, r] = updated
+
+
+def adam_pair(weight, mean_old, square_old, first, second, step_rate, decay_weight):
+    rows, _, columns = weight.shape
+    height = 128
+    narrow = pl.BlockSpec((height, columns), lambda i: (i, 0))
+    tiles = pl.BlockSpec((height, columns // 64, 128), lambda i: (i, 0, 0))
+    updated = pl.pallas_call(
+        functools.partial(adam_kernel, step_rate, decay_weight),
+        grid=(rows // height,),
+        in_specs=[narrow, narrow, tiles, tiles, tiles],
+        out_specs=[tiles, tiles, tiles],
+        out_shape=[jax.ShapeDtypeStruct((rows, columns // 64, 128), F32)] * 3,
+        compiler_params=pltpu.CompilerParams(vmem_limit_bytes=40 << 20),
+        cost_estimate=load(9),
+    )(first, second, lane_tiles(weight), lane_tiles(mean_old), lane_tiles(square_old))
+    return [from_lane_tiles(part, weight.shape) for part in updated]
 
 
 def silu_slope(values):
@@ -459,9 +582,12 @@
     )
     leaving = states_after(local_back, block_decays, "seq")
     z_weight_grad = jnp.einsum("btd,btc->dc", normed, gate_grad, preferred_element_type=F32)
-    early_grads = (out_weight_grad.astype(BF16), z_weight_grad.astype(BF16))
+    early_grads = jnp.concatenate([out_weight_grad, z_weight_grad], axis=0).astype(BF16)
     early_grads, _ = lax.optimization_barrier((early_grads, leaving))
-    early_sums = lax.psum(early_grads, "seq")
+    early_parts = exchanged(to_blocks(early_grads, seq_size), "seq")
+    projected = halved(partial_out.astype(BF16).reshape(rows, model_width), "head")
+    scanned_grad, projected = lax.optimization_barrier((scanned_grad, projected))
+    projected_far = swapped(projected, "head", axis_masks("head")[-1])
     x_grad, bc_grad, decay_grad, step_grad, skip_terms = scan_backward(
         x_values,
         b_values,
@@ -475,18 +601,20 @@
         states,
         leaving,
     )
-    projected = halving_sum(
-        partial_out.astype(BF16).reshape(rows, model_width), "head", after=bc_grad
-    )
-    projected = projected.reshape(inputs.shape).astype(F32)
-    block_out = (tokens + out_scale[..., None] * projected).astype(BF16)
+    x_grad_late, early_parts, projected_far = lax.optimization_barrier(
+        (x_grad, early_parts, projected_far)
+    )
+    projected_half, projected_other = regathered(added(projected, projected_far), "head")
+    early_own = jnp.sum(early_parts.astype(F32), axis=0).astype(BF16)
+    early_all = exchanged(jnp.broadcast_to(early_own[None], early_parts.shape), "seq")
     bc_total = halving_sum(bc_grad.reshape(rows, 2 * state_width), "head")
     bc_total = bc_total.reshape(bc_grad.shape).astype(F32)
 
-    def conv_back(activated_grad, first, last):
+    def conv_back(activated_grad, activated_grad_late, first, last):
         convolved_grad = activated_grad * silu_slope(convolved[..., first:last])
         taps = conv_weight[:, first:last]
         tap_grads = []
+        convolved_late = activated_grad_late * silu_slope(convolved[..., first:last])
         padded_grad = jnp.zeros((seq_count, local_len + CONV - 1, last - first), F32)
         for tap_index in range(CONV):
             tap_grads.append(
@@ -496,7 +624,7 @@
                 )
             )
             padded_grad = padded_grad + jnp.pad(
-                taps[tap_index] * convolved_grad,
+                taps[tap_index] * convolved_late,
                 ((0, 0), (tap_index, CONV - 1 - tap_index), (0, 0)),
             )
         tap_grads.append(jnp.sum(convolved_grad, axis=(0, 1)))
@@ -506,7 +634,7 @@
         )
         return mixed_grad.astype(BF16), jnp.stack(tap_grads)
 
-    x_in_grad, conv_inner_grad = conv_back(x_grad, 0, local_inner)
+    x_in_grad, conv_inner_grad = conv_back(x_grad, x_grad_late, 0, local_inner)
     step_total = step_grad - jnp.exp(decay_log) * decay_grad
     pre_grad = step_total * jax.nn.sigmoid(raw_step + step_bias)
     head_grad = jnp.stack(
@@ -522,19 +650,62 @@
         + jnp.einsum("btc,dc->btd", x_in_grad, x_weight, preferred_element_type=F32)
         + jnp.einsum("bth,dh->btd", step_in_grad, step_weight, preferred_element_type=F32)
     )
-    normed_sum = halving_sum(normed_partial.astype(BF16).reshape(rows, model_width), "head")
-    norm_gain_partial = doubling_sum(jnp.sum(normed_partial * unit_tokens, axis=(0, 1)), "head")
-    bc_in_grad, conv_bc_grad = conv_back(bc_total, local_inner, local_inner + 2 * state_width)
-    bc_normed = jnp.einsum("btc,dc->btd", bc_in_grad, bc_weight, preferred_element_type=F32)
-    norm_gain_grad = norm_gain_partial + jnp.sum(bc_normed * unit_tokens, axis=(0, 1))
-    x_weight_grad = jnp.einsum("btd,btc->dc", normed, x_in_grad, preferred_element_type=F32)
+    normed_sum = halved(normed_partial.astype(BF16).reshape(rows, model_width), "head")
+    normed_far = swapped(normed_sum, "head", axis_masks("head")[-1])
+    normed_half, normed_other = regathered(added(normed_sum, normed_far), "head")
+    bc_in_grad, conv_bc_grad = conv_back(
+        bc_total, bc_total, local_inner, local_inner + 2 * state_width
+    )
+    x_in_late, early_all = lax.optimization_barrier((x_in_grad, early_all))
+    early_sums = early_all.reshape(2, model_width, local_inner)
+    x_weight_grad = jnp.einsum("btd,btc->dc", normed, x_in_late, preferred_element_type=F32)
     bc_weight_grad = jnp.einsum("btd,btc->dc", normed, bc_in_grad, preferred_element_type=F32)
     step_weight_grad = jnp.einsum("btd,bth->hd", normed, step_in_grad, preferred_element_type=F32)
     late_grads = (x_weight_grad.astype(BF16), bc_weight_grad.astype(BF16))
-    late_grads, early_sums = lax.optimization_barrier((late_grads, early_sums))
     late_sums = lax.psum(late_grads, "seq")
+    scalars = jnp.concatenate(
+        [lengths, jnp.stack([seq_index * local_len, near_bit("head", 1)]).astype(jnp.int32)]
+    )
+    flat_tokens = inputs.reshape(rows, model_width)
+    input_grad, norm_gain_grad = merge_call(
+        functools.partial(tail_kernel, local_len),
+        scalars,
+        normed_half,
+        normed_other,
+        (
+            bc_in_grad.reshape(rows, 2 * state_width),
+            bc_weight,
+            flat_tokens,
+            cotangent.reshape(rows, model_width),
+            norm_gain[None],
+        ),
+        [
+            row_block(2 * state_width),
+            whole_block(bc_weight.shape),
+            row_block(model_width),
+            row_block(model_width),
+            whole_block((1, model_width)),
+        ],
+        [row_block(model_width), whole_block((1, model_width))],
+        [
+            jax.ShapeDtypeStruct((rows, model_width), F32),
+            jax.ShapeDtypeStruct((1, model_width), F32),
+        ],
+    )
+    input_grad = input_grad.reshape(inputs.shape)
+    block_out = merge_call(
+        out_kernel,
+        scalars,
+        projected_half,
+        projected_other,
+        (flat_tokens, out_scale.reshape(rows, 1)),
+        [row_block(model_width), row_block(1)],
+        row_block(model_width),
+        jax.ShapeDtypeStruct((rows, model_width), BF16),
+    ).reshape(inputs.shape)
+    late_sums, _, _ = lax.optimization_barrier((late_sums, input_grad, block_out))
     small_grads = (
-        norm_gain_grad,
+        norm_gain_grad[0],
         step_weight_grad,
         conv_inner_grad,
         conv_bc_grad,
@@ -550,15 +721,9 @@
         small_sums.append(flat[at : at + part.size].reshape(part.shape))
         at += part.size
 
-    normed_grad = normed_sum.reshape(inputs.shape).astype(F32) + bc_normed
-    unit_grad = normed_grad * norm_gain
-    input_grad = out_cotangent + inverse_rms * (
-        unit_grad - unit_tokens * jnp.mean(unit_grad * unit_tokens, axis=-1, keepdims=True)
-    )
-    zx_sum = lane_tiles(jnp.stack([early_sums[1], late_sums[0]], axis=1)).astype(F32)
     summed_grads = (
         small_sums[0],
-        zx_sum,
+        (early_sums[1], late_sums[0].reshape(model_width, local_inner)),
         late_sums[1].astype(F32),
         small_sums[1].T,
         small_sums[2],
@@ -604,12 +769,10 @@
     for weight, mean_old, square_old, gradient, step_rate, decay_weight in zip(
         params, means, squares, summed_grads, LEARNING_RATES, WEIGHT_DECAYS
     ):
-        shape = weight.shape
-        if len(shape) == 3:
-            weight, mean_old, square_old = map(lane_tiles, (weight, mean_old, square_old))
-        updated = adam_update(weight, mean_old, square_old, gradient, step_rate, decay_weight)
-        if len(shape) == 3:
-            updated = [from_lane_tiles(part, shape) for part in updated]
+        if weight.ndim == 3:
+            updated = adam_pair(weight, mean_old, square_old, *gradient, step_rate, decay_weight)
+        else:
+            updated = adam_update(weight, mean_old, square_old, gradient, step_rate, decay_weight)
         results.extend(updated)
     return tuple(results)
 

time: 567 us -> 523 us (0.922)
  waiting for transfers between devices: 183 us -> 131 us
  Pallas kernels: 39.9 us -> 86.1 us
  other arithmetic: 119 us -> 96.9 us
  local copies, waits for them, and re-layouts: 55.3 us -> 41.7 us
  matrix products: 99 us -> 85.7 us
  starting transfers between devices: 36.7 us -> 47.5 us
    psum x1 -> x0, waiting for transfers between devices: 61.9 us -> none  [shards(): early_sums = lax.psum(early_grads, 'seq')]
    pallas_call x0 -> x3, Pallas kernels: none -> 45.6 us  [the longest x1 24.4 us: adam_pair(): pl.pallas_call(functools.partial(adam_kernel, step_rate, decay_weight), g...]
    ppermute x14 -> x12, waiting for transfers between devices: 19.1 us -> 45.8 us  [swapped(): lax.ppermute(block, axis, [(i, i ^ mask) for i in range(lax.axis_size(axi...]
    psum x1, waiting for transfers between devices: 68.7 us -> 45.5 us  [shards(): late_sums = lax.psum(late_grads, 'seq')]
    unnamed x220 -> x197, local copies, waits for them, and re-layouts: 34.1 us -> 19.8 us
    add x4 -> x2, other arithmetic: 19.2 us -> 7.01 us  [conv_back(): padded_grad + jnp.pad(taps[tap_index] * convolved_late, ((0, 0), (tap_ind...]
    all_to_all x4 -> x6, starting transfers between devices: 18.3 us -> 30.2 us  [exchanged(): return lax.all_to_all(blocks, axis, 0, 0, tiled=True)]
    convert_element_type x6 -> x8, other arithmetic: 14.6 us -> 21 us  [the longest x6 17.8 us: added(): return (a.astype(F32) + b.astype(F32)).astype(BF16)]
  transfers between devices with their start and end apart: 23 -> 22, of which waited for: 10 -> 9; matrix products, arithmetic and copies ran while one was open for 34% -> 28% of each run, Pallas kernels for 5% -> 14%
where the time goes in v3:
time: 523 us; the launch traced here: 514 us
  waiting for transfers between devices  131 us (25%)
  other arithmetic  96.9 us (19%)
  Pallas kernels  86.1 us (16%)
  matrix products  85.7 us (16%)
  starting transfers between devices  47.5 us (9%)
  local copies, waits for them, and re-layouts  41.7 us (8%)
  between operations  15.7 us (3%)
  blocking collectives  10.1 us (2%)
    ppermute x12, waiting for transfers between devices, swapped(): lax.ppermute(block, axis, [(i, i ^ mask) for i in range(lax.axis_size(axi...  45.8 us
    psum x1, waiting for transfers between devices, shards(): late_sums = lax.psum(late_grads, 'seq')  45.5 us
    all_to_all x6, waiting for transfers between devices, exchanged(): return lax.all_to_all(blocks, axis, 0, 0, tiled=True)  35.6 us
    all_to_all x6, starting transfers between devices, exchanged(): return lax.all_to_all(blocks, axis, 0, 0, tiled=True)  30.2 us
    pallas_call x1, Pallas kernels, scan_backward(): pl.pallas_call(back_kernel, grid=(seqs, chunks), in_specs=[block(inner),...  27.4 us
    pallas_call x1, Pallas kernels, adam_pair(): pl.pallas_call(functools.partial(adam_kernel, step_rate, decay_weight), g...  24.4 us
    pallas_call x2, Pallas kernels, merge_call(): pl.pallas_call(kernel, grid_spec=pltpu.PrefetchScalarGridSpec(num_scalar_...  21.2 us
    unnamed x197, local copies, waits for them, and re-layouts  19.8 us
  transfers between devices with their start and end apart: 22, of which 9 were waited for; matrix products, arithmetic and copies ran while one was open for 28% of the time, Pallas kernels for 14%

profile of v3, /device:TPU:0, one launch (start us, length us, event | category | flops | bytes accessed | tf_op | source)
XLA Modules:
  0.0 514.2 jit_solution(3191616604424324638)
XLA Ops:
  7.2 3.2 fusion
  14.0 3.8 convolution_convert_fusion
  18.4 4.9 collective-permute-start
  23.9 2.0 negate_multiply_fusion
  28.5 6.5 %multiply_convert_fusion.1 = (bf16[4,512,768]{2,1,0:T(8,128)(2,1)S(1)}, f32[4,512,768]{2,1,0:T(8,128)}) fusion(bf16[4,512,768]{2,1,0:T(8,128)(2,1)S(1)} %convolution_convert_fusion, f32[768]{0:T(1024)S(1)} %get-tuple-element.86, f32[768]{0:T(1024)S(1)} %get-tuple-element.87, f32[768]{0:T(1024)} %get-tuple-element.88, ...), kind=kLoop, calls=%fused_computation.17 | loop fusion | flops 40894464 | bytes 12616704 | tf_op jit(solution)/shard_map/convert_element_type | solution.py:536
  35.1 4.2 fusion.3
  40.6 5.0 all-to-all-start
  46.3 16.3 %all-to-all-done = bf16[8,80,512]{2,1,0:T(8,128)(2,1)S(1)} async-done(((bf16[8,80,512]{2,1,0:T(8,128)(2,1)}), bf16[8,80,512]{2,1,0:T(8,128)(2,1)S(1)}, u32[]{:S(2)}, u32[]{:S(2)}) %all-to-all-start) | async-done | bytes 655392 | tf_op jit(solution)/shard_map/all_to_all | solution.py:86
  68.1 4.4 all-to-all-start.1
  74.4 1.7 slice.324.x_ref
  76.2 2.3 fusion.114
  78.4 8.3 %all-to-all-done.1 = bf16[8,64,512]{2,1,0:T(8,128)(2,1)} async-done(((bf16[8,64,512]{2,1,0:T(8,128)(2,1)}), bf16[8,64,512]{2,1,0:T(8,128)(2,1)}, u32[]{:S(2)}, u32[]{:S(2)}) %all-to-all-start.1) | async-done | bytes 524320 | tf_op jit(solution)/shard_map/all_to_all | solution.py:86
  91.5 13.1 %shard_map.509 = (f32[4,512,512]{2,1,0:T(8,128)S(1)}, f32[4,4,128,512]{3,2,1,0:T(8,128)}) custom-call(bf16[4,512,512]{2,1,0:T(8,128)(2,1)S(1)} %slice.324.x_ref, bf16[4,512,128]{2,1,0:T(8,128)(2,1)S(1)} %copy-done.11, bf16[4,512,128]{2,1,0:T(8,128)(2,1)S(1)} %copy-done.9, f32[4,512,8]{2,1,0:T(8,128)S(1)} %copy-done.7, f32[4,512,8]{2,1,0:T(8,128)S(1)} %copy.86.decay_ref, ...), custom_call_target="tpu_custom_call" | custom-call | bytes 47970000 | tf_op jit(solution)/shard_map/pallas_call | solution.py:286
  104.6 7.5 %multiply_reduce_fusion.6 = (f32[4,512]{1,0:T(4,128)S(1)}, f32[4,512,512]{2,1,0:T(8,128)S(1)}, f32[4,512,512]{2,1,0:T(8,128)}) fusion(f32[4,512,512]{2,1,0:T(8,128)S(1)} %get-tuple-element.51.y_ref, bf16[4,512,768]{2,1,0:T(8,128)(2,1)S(1)} %copy-done.34, f32[512]{0:T(512)S(1)} %mul.817, bf16[1024,2,512]{2,0,1:T(8,128)(2,1)} %copy-done.37, ...), kind=kOutput, calls=%fused_computation.43 | convolution fusion | flops 2166355968 | bytes 19945472 | tf_op jit(solution)/shard_map/btd,dc->btc/dot_general | solution.py:528
  112.2 4.6 fusion.113
  116.7 10.1 %psum.21 = f32[2,4,512]{2,1,0:T(4,128)S(1)} all-reduce(f32[2,4,512]{2,1,0:T(4,128)S(1)} %pad_maximum_fusion.4), channel_id=1, replica_groups=mesh['seq'=8,'head'=4] {'head'}, use_global_device_ids=true, to_apply=%region_3.4 | all-reduce | flops 4096 | bytes 32768 | tf_op jit(solution)/shard_map/psum | solution.py:567
  127.5 11.0 %multiply_convert_fusion.2 = (bf16[4,512,512]{2,1,0:T(8,128)(2,1)}, f32[4,512,512]{2,1,0:T(8,128)S(1)}, f32[512]{0:T(512)}) fusion(f32[4,512,512]{2,1,0:T(8,128)} %get-tuple-element.181, f32[4,512,512]{2,1,0:T(8,128)} %copy-done.17, f32[512]{0:T(512)} %copy-done.90, f32[4,512,512]{2,1,0:T(8,128)} %copy-done.94, f32[4,512]{1,0:T(4,128)S(1)} %fusion.70, ...), kind=kOutput, calls=%fused_computation.39 | convolution fusion | flops 2177367552 | bytes 27293696 | tf_op jit(solution)/shard_map/btd,di->bti/dot_general | solution.py:572
  138.5 3.8 multiply_convert_fusion.3
  142.2 2.3 convolution_convert_fusion.1
  144.6 5.0 all-to-all-start.2
  149.6 3.2 dynamic-slice_bitcast_fusion.1
  153.0 5.9 %bitcast_convert_fusion.2 = bf16[1024,512]{1,0:T(8,128)(2,1)} fusion(bf16[4,512,1024]{2,1,0:T(8,128)(2,1)S(1)} %copy-done.14, f32[4,512]{1,0:T(4,128)S(1)} %get-tuple-element.162, f32[4,512]{1,0:T(4,128)S(1)} %compare_convert_fusion, f32[4,512,512]{2,1,0:T(8,128)} %copy-done.94, f32[512]{0:T(512)S(1)} %copy-done.86), kind=kOutput, calls=%fused_computation.73 | convolution fusion | flops 2158493696 | bytes 9455616 | tf_op jit(solution)/shard_map/btd,bti->di/dot_general | solution.py:571
  158.8 4.5 all-to-all-done.2
  169.8 4.1 all-to-all-start.3
  174.0 5.5 %bitcast_convert_fusion.1 = bf16[1024,512]{1,0:T(8,128)(2,1)S(1)} fusion(bf16[4,512,512]{2,1,0:T(8,128)(2,1)} %get-tuple-element.135, bf16[4,512,1024]{2,1,0:T(8,128)(2,1)} %param.30, f32[1024]{0:T(1024)S(1)} %copy-done.29, f32[4,512]{1,0:T(4,128)S(1)} %copy-done.74), kind=kOutput, calls=%fused_computation.72 | convolution fusion | flops 2156396544 | bytes 7352320 | tf_op jit(solution)/shard_map/btd,btc->dc/dot_general | solution.py:584
  180.9 6.5 %all-to-all-done.3 = bf16[8,64,512]{2,1,0:T(8,128)(2,1)} async-done(((bf16[8,64,512]{2,1,0:T(8,128)(2,1)}), bf16[8,64,512]{2,1,0:T(8,128)(2,1)}, u32[]{:S(2)}, u32[]{:S(2)}) %all-to-all-start.3) | async-done | bytes 524320 | tf_op jit(solution)/shard_map/all_to_all | solution.py:86
  187.4 2.1 bitcast_convert_fusion.4.leave_ref
  189.5 4.8 all-to-all-start.4
  194.4 4.5 fusion.7
  200.3 7.7 %fusion.36 = f32[4,512,1024]{2,1,0:T(8,128)} fusion(bf16[4,512,512]{2,1,0:T(8,128)(2,1)} %get-tuple-element.135, bf16[1024,2,512]{2,0,1:T(8,128)(2,1)} %copy-done.37), kind=kOutput, calls=%fused_computation.120 | convolution fusion | flops 2147483648 | bytes 11534336 | tf_op jit(solution)/shard_map/btc,dc->btd/dot_general | solution.py:649
  208.1 27.4 %shard_map.510 = (f32[4,512,512]{2,1,0:T(8,128)}, bf16[4,512,256]{2,1,0:T(8,128)(2,1)S(1)}, f32[4,512,8]{2,1,0:T(8,128)S(1)}, f32[4,512,8]{2,1,0:T(8,128)S(1)}, f32[4,512,8]{2,1,0:T(8,128)S(1)}) custom-call(bf16[4,512,512]{2,1,0:T(8,128)(2,1)S(1)} %slice.324.x_ref, bf16[4,512,128]{2,1,0:T(8,128)(2,1)S(1)} %copy-done.12, bf16[4,512,128]{2,1,0:T(8,128)(2,1)S(1)} %copy-done.10, ...), custom_call_target="tpu_custom_call" | custom-call | bytes 99630000 | tf_op jit(solution)/shard_map/pallas_call | solution.py:320
  241.0 1.5 copy.94
  243.4 4.7 fusion.65
  248.2 6.4 %broadcast_multiply_fusion.3 = (f32[4,512,512]{2,1,0:T(8,128)S(1)}, f32[4,512,512]{2,1,0:T(8,128)}, f32[4,512,512]{2,1,0:T(8,128)}) fusion(f32[512]{0:T(512)S(1)} %bitcast.291, f32[4,512,512]{2,1,0:T(8,128)} %get-tuple-element.58, f32[4,512,768]{2,1,0:T(8,128)} %get-tuple-element.134), kind=kLoop, calls=%fused_computation.83 | loop fusion | flops 10485760 | bytes 20973568 | tf_op jit(solution)/shard_map/mul | solution.py:627
  254.6 5.5 %broadcast_multiply_fusion.2 = (f32[4,512,512]{2,1,0:T(8,128)S(1)}, f32[4,512,512]{2,1,0:T(8,128)S(1)}, f32[4,512,512]{2,1,0:T(8,128)S(1)}) fusion(f32[4,512,512]{2,1,0:T(8,128)} %get-tuple-element.120, f32[512]{0:T(512)S(1)} %bitcast.281, f32[512]{0:T(512)S(1)} %bitcast.282, f32[512]{0:T(512)S(1)} %bitcast.283), kind=kLoop, calls=%fused_computation.82 | loop fusion | flops 3145728 | bytes 16783360 | tf_op jit(solution)/shard_map/mul | solution.py:627
  261.7 6.4 %pad_add_fusion = f32[4,515,512]{2,1,0:T(8,128)} fusion(f32[4,512,512]{2,1,0:T(8,128)S(1)} %get-tuple-element.143, f32[4,512,512]{2,1,0:T(8,128)S(1)} %get-tuple-element.142, f32[4,512,512]{2,1,0:T(8,128)S(1)} %get-tuple-element.141, f32[4,512,512]{2,1,0:T(8,128)} %copy-done.32), kind=kLoop, calls=%fused_computation.21 | loop fusion | flops 3164160 | bytes 20996096 | tf_op jit(solution)/shard_map/add | solution.py:626
  268.0 3.0 fusion.5
  271.0 9.1 %add_convert_fusion = bf16[4,512,1024]{2,1,0:T(8,128)(2,1)S(1)} fusion(f32[4,512,1024]{2,1,0:T(8,128)} %fusion.65, f32[4,512,1024]{2,1,0:T(8,128)} %fusion.36, bf16[4,512,512]{2,1,0:T(8,128)(2,1)S(1)} %fusion.5, bf16[1024,2,512]{2,0,1:T(8,128)(2,1)S(1)} %copy-done.38), kind=kOutput, calls=%fused_computation.13 | convolution fusion | flops 2153775104 | bytes 24117248 | tf_op jit(solution)/shard_map/btc,dc->btd/dot_general | solution.py:650
  286.1 11.3 %collective-permute-done.9 = bf16[1024,256]{1,0:T(8,128)(2,1)S(1)} collective-permute-done((bf16[1024,256]{1,0:T(8,128)(2,1)S(1)}, bf16[1024,256]{1,0:T(8,128)(2,1)S(1)}, u32[]{:S(2)}, u32[]{:S(2)}) %collective-permute-start.9) | collective-permute-done | bytes 524320 | tf_op jit(solution)/shard_map/ppermute | solution.py:34
  298.4 3.3 convolution_bitcast_fusion.2
  301.8 2.0 reduce_sum.182
  305.2 6.9 %all-to-all-start.5 = ((bf16[8,256,512]{2,1,0:T(8,128)(2,1)}), bf16[8,256,512]{2,1,0:T(8,128)(2,1)}, u32[]{:S(2)}, u32[]{:S(2)}) async-start(bf16[8,256,512]{2,1,0:T(8,128)(2,1)} %broadcast_in_dim.53), calls=%async_computation.5 | async-start | bytes 4194304 | tf_op jit(solution)/shard_map/all_to_all | solution.py:86
  313.6 4.5 fusion.6
  319.4 3.1 multiply_reduce_fusion.8
  325.5 3.6 collective-permute-done.11
  329.4 4.5 add_convert_fusion.2.part_ref
  333.9 32.3 %collective-permute-done.6 = bf16[1024,1024]{1,0:T(8,128)(2,1)} collective-permute-done((bf16[1024,1024]{1,0:T(8,128)(2,1)}, bf16[1024,1024]{1,0:T(8,128)(2,1)}, u32[]{:S(2)}, u32[]{:S(2)}) %collective-permute-start.6) | collective-permute-done | bytes 2097184 | tf_op jit(solution)/shard_map/ppermute | solution.py:34
  366.2 3.2 add_convert_fusion.1.part_ref
  369.5 2.8 fusion.24
  372.2 6.4 %bitcast_convert_fusion = bf16[1024,512]{1,0:T(8,128)(2,1)} fusion(bf16[4,512,512]{2,1,0:T(8,128)(2,1)} %copy-done.39, bf16[4,512,1024]{2,1,0:T(8,128)(2,1)} %param.30, f32[1024]{0:T(1024)S(1)} %copy-done.29, f32[4,512]{1,0:T(4,128)S(1)} %copy-done.75), kind=kOutput, calls=%fused_computation.71 | convolution fusion | flops 2156396544 | bytes 7352320 | tf_op jit(solution)/shard_map/btd,btc->dc/dot_general | solution.py:661
  378.6 7.0 %multiply_reduce_fusion.3 = (f32[512]{0:T(512)S(1)}, f32[512]{0:T(512)S(1)}, f32[512]{0:T(512)S(1)}, f32[512]{0:T(512)S(1)}, f32[512]{0:T(512)S(1)}) fusion(f32[4,512,512]{2,1,0:T(8,128)} %get-tuple-element.140, bf16[4,512,768]{2,1,0:T(8,128)(2,1)} %copy-done.30, bf16[4,3,768]{2,1,0:T(4,128)(2,1)S(1)} %collective-permute-done), kind=kLoop, calls=%fused_computation.33 | loop fusion | flops 23066112 | bytes 9465856 | tf_op jit(solution)/shard_map/reduce_sum | solution.py:621
  385.6 2.2 copy-done.3
  389.1 10.0 %shard_map.511 = bf16[2048,1024]{1,0:T(8,128)(2,1)} custom-call(s32[6]{0:T(128)S(1)} %pad_add_fusion.4.scalars_ref, bf16[1024,1024]{1,0:T(8,128)(2,1)} %add_convert_fusion.2.part_ref, bf16[1024,1024]{1,0:T(8,128)(2,1)} %collective-permute-done.3.got_ref, bf16[2048,1024]{1,0:T(8,128)(2,1)S(1)} %bitcast.236, f32[2048,1]{1,0:T(8,128)S(1)} %bitcast.243), custom_call_target="tpu_custom_call" | custom-call | bytes 29520000 | tf_op jit(solution)/shard_map/pallas_call | solution.py:401
  399.1 11.2 %shard_map.512 = (f32[2048,1024]{1,0:T(8,128)}, f32[1,1024]{1,0:T(1,128)S(1)}) custom-call(s32[6]{0:T(128)S(1)} %pad_add_fusion.4.scalars_ref, bf16[1024,1024]{1,0:T(8,128)(2,1)S(1)} %add_convert_fusion.1.part_ref, bf16[1024,1024]{1,0:T(8,128)(2,1)} %collective-permute-done.7.got_ref, bf16[2048,256]{1,0:T(8,128)(2,1)S(1)} %bitcast.242, ...), custom_call_target="tpu_custom_call" | custom-call | bytes 29520000 | tf_op jit(solution)/shard_map/pallas_call | solution.py:401
  410.4 1.7 collective-permute-start.12
  412.1 1.7 fusion.115
  413.8 2.2 collective-permute-done.12
  416.0 1.8 collective-permute-start.13
  417.9 6.9 %multiply_subtract_fusion = (f32[1024,512]{1,0:T(8,128)}, f32[1024,512]{1,0:T(8,128)}, f32[1024,512]{1,0:T(8,128)}) fusion(f32[1024,512]{1,0:T(8,128)} %param.57, bf16[4,256,512]{2,1,0:T(8,128)(2,1)S(1)} %get-tuple-element.146, f32[1024,512]{1,0:T(8,128)} %param.59, f32[1024,512]{1,0:T(8,128)} %param.58), kind=kLoop, calls=%fused_computation.74 | loop fusion | flops 8388608 | bytes 13631488 | tf_op jit(solution)/shard_map/sub | solution.py:463
  424.8 45.5 %all-reduce.14.cloned.1.call-done = (bf16[1024,512]{1,0:T(8,128)(2,1)}, bf16[1024,256]{1,0:T(8,128)(2,1)}) async-done(((bf16[1024,512]{1,0:T(8,128)(2,1)}, bf16[1024,256]{1,0:T(8,128)(2,1)}), (bf16[1024,512]{1,0:T(8,128)(2,1)}, bf16[1024,256]{1,0:T(8,128)(2,1)})) %all-reduce.14.cloned.1.call-update) | async-done | bytes 1572880 | tf_op jit(solution)/shard_map/psum | solution.py:665
  470.3 1.8 collective-permute-start.14
  472.1 3.6 multiply_subtract_fusion.1
  475.8 2.2 copy-done.16
  478.1 24.4 %shard_map.513 = (f32[1024,8,128]{2,1,0:T(8,128)}, f32[1024,8,128]{2,1,0:T(8,128)}, f32[1024,8,128]{2,1,0:T(8,128)}) custom-call(bf16[1024,512]{1,0:T(8,128)(2,1)S(1)} %bitcast.239, bf16[1024,512]{1,0:T(8,128)(2,1)S(1)} %copy-done.22, f32[1024,8,128]{2,1,0:T(8,128)S(1)} %bitcast.238, f32[1024,8,128]{2,1,0:T(8,128)S(1)} %bitcast.241, f32[1024,8,128]{2,1,0:T(8,128)} %bitcast.251), custom_call_target="tpu_custom_call" | custom-call | bytes 33210000 | tf_op jit(solution)/shard_map/pallas_call | solution.py:441
  (315 shorter events, 59.6 us)
Async XLA Ops:
  10.7 13.2 %copy-start.73 = (f32[4,512]{1,0:T(4,128)}, f32[4,512]{1,0:T(4,128)S(1)}, u32[]{:S(2)}) copy-start(f32[4,512]{1,0:T(4,128)S(1)} %add_rsqrt_fusion) | copy-start | bytes 24580
  13.9 9.4 %copy-start.46 = (f32[5,512]{1,0:T(8,128)S(1)}, f32[5,512]{1,0:T(8,128)}, u32[]{:S(2)}) copy-start(f32[5,512]{1,0:T(8,128)} %param.45) | copy-start | bytes 30724
  13.9 9.4 %copy-start.77 = (f32[3,8]{1,0:T(4,128)S(1)}, f32[3,8]{1,0:T(4,128)}, u32[]{:S(2)}) copy-start(f32[3,8]{1,0:T(4,128)} %param.51) | copy-start | bytes 292
  13.9 9.9 %copy-start.45 = (f32[1024,8]{0,1:T(8,128)S(1)}, f32[1024,8]{0,1:T(8,128)}, u32[]{:S(2)}) copy-start(f32[1024,8]{0,1:T(8,128)} %param.42) | copy-start | bytes 98308
  17.7 10.8 %copy-start.30 = (bf16[4,512,768]{2,1,0:T(8,128)(2,1)}, bf16[4,512,768]{2,1,0:T(8,128)(2,1)S(1)}, u32[]{:S(2)}) copy-start(bf16[4,512,768]{2,1,0:T(8,128)(2,1)S(1)} %convolution_convert_fusion) | copy-start | bytes 9437188
  18.4 10.1 %collective-permute-start = (bf16[4,3,768]{2,1,0:T(4,128)(2,1)}, bf16[4,3,768]{2,1,0:T(4,128)(2,1)S(1)}, u32[]{:S(2)}, u32[]{:S(2)}) collective-permute-start(bf16[4,3,768]{2,1,0:T(4,128)(2,1)} %slice.314), channel_id=1, source_target_pairs={{0,4},{4,8},{8,12},{12,16},{16,20},{20,24},{24,28},{1,5},{5,9},{9,... | collective-permute-start | bytes 55304 | tf_op jit(solution)/shard_map/ppermute | solution.py:30
  40.6 32.1 %copy-start.48 = (f32[4,512,8]{1,2,0:T(8,128)S(1)}, f32[4,512,8]{1,2,0:T(8,128)}, u32[]{:S(2)}) copy-start(f32[4,512,8]{1,2,0:T(8,128)} %get-tuple-element.156) | copy-start | bytes 196612
  40.6 22.0 %all-to-all-start = ((bf16[8,80,512]{2,1,0:T(8,128)(2,1)}), bf16[8,80,512]{2,1,0:T(8,128)(2,1)S(1)}, u32[]{:S(2)}, u32[]{:S(2)}) async-start(bf16[8,80,512]{2,1,0:T(8,128)(2,1)} %pad_maximum_fusion.3), calls=%async_computation | async-start | bytes 1310720 | tf_op jit(solution)/shard_map/all_to_all | solution.py:86
  45.7 28.4 %copy-start.91 = (f32[8]{0:T(128)S(1)}, f32[8]{0:T(128)}, u32[]{:S(2)}) copy-start(f32[8]{0:T(128)} %get-tuple-element.177) | copy-start | bytes 100
  45.7 28.6 %copy-start.92 = (s32[4]{0:T(128)S(1)}, s32[4]{0:T(128)}, u32[]{:S(2)}) copy-start(s32[4]{0:T(128)} %param.32) | copy-start | bytes 52
  45.7 28.7 %copy-start.80 = (f32[8]{0:T(128)S(1)}, f32[8]{0:T(128)}, u32[]{:S(2)}) copy-start(f32[8]{0:T(128)} %copy-done.79) | copy-start | bytes 100
  68.1 18.6 %all-to-all-start.1 = ((bf16[8,64,512]{2,1,0:T(8,128)(2,1)}), bf16[8,64,512]{2,1,0:T(8,128)(2,1)}, u32[]{:S(2)}, u32[]{:S(2)}) async-start(bf16[8,64,512]{2,1,0:T(8,128)(2,1)} %fusion.49), calls=%async_computation.1 | async-start | bytes 1048576 | tf_op jit(solution)/shard_map/all_to_all | solution.py:86
  74.3 30.3 %copy-start.90 = (f32[512]{0:T(512)}, f32[512]{0:T(512)S(1)}, u32[]{:S(2)}) copy-start(f32[512]{0:T(512)S(1)} %mul.817) | copy-start | bytes 6148
  76.1 28.4 %copy-start.74 = (f32[4,512]{1,0:T(4,128)S(1)}, f32[4,512]{1,0:T(4,128)}, u32[]{:S(2)}) copy-start(f32[4,512]{1,0:T(4,128)} %copy-done.73) | copy-start | bytes 24580
  86.7 17.8 %copy-start.1 = (bf16[4,512,1024]{2,1,0:T(8,128)(2,1)S(1)}, bf16[4,512,1024]{2,1,0:T(8,128)(2,1)}, u32[]{:S(2)}) copy-start(bf16[4,512,1024]{2,1,0:T(8,128)(2,1)} %param.30) | copy-start | bytes 12582916
  91.4 13.1 %copy-start.34 = (bf16[4,512,768]{2,1,0:T(8,128)(2,1)S(1)}, bf16[4,512,768]{2,1,0:T(8,128)(2,1)}, u32[]{:S(2)}) copy-start(bf16[4,512,768]{2,1,0:T(8,128)(2,1)} %copy-done.33) | copy-start | bytes 9437188
  144.6 18.8 %all-to-all-start.2 = ((bf16[8,64,512]{2,1,0:T(8,128)(2,1)}), bf16[8,64,512]{2,1,0:T(8,128)(2,1)}, u32[]{:S(2)}, u32[]{:S(2)}) async-start(bf16[8,64,512]{2,1,0:T(8,128)(2,1)} %bitcast.255), calls=%async_computation.2 | async-start | bytes 1048576 | tf_op jit(solution)/shard_map/all_to_all | solution.py:86
  152.8 11.7 %copy-start.55 = (f32[1,1,512]{2,1,0:T(1,128)S(1)}, f32[1,1,512]{2,1,0:T(1,128)}, u32[]{:S(2)}) copy-start(f32[1,1,512]{2,1,0:T(1,128)} %copy-done.54) | copy-start | bytes 6148
  152.8 11.7 %copy-start.57 = (f32[1,1,512]{2,1,0:T(1,128)S(1)}, f32[1,1,512]{2,1,0:T(1,128)}, u32[]{:S(2)}) copy-start(f32[1,1,512]{2,1,0:T(1,128)} %copy-done.56) | copy-start | bytes 6148
  152.8 11.7 %copy-start.59 = (f32[1,1,512]{2,1,0:T(1,128)S(1)}, f32[1,1,512]{2,1,0:T(1,128)}, u32[]{:S(2)}) copy-start(f32[1,1,512]{2,1,0:T(1,128)} %copy-done.58) | copy-start | bytes 6148
  152.8 11.7 %copy-start.60 = (f32[1,1,512]{2,1,0:T(1,128)S(1)}, f32[1,1,512]{2,1,0:T(1,128)}, u32[]{:S(2)}) copy-start(f32[1,1,512]{2,1,0:T(1,128)} %get-tuple-element.163) | copy-start | bytes 6148
  152.8 11.7 %copy-start.62 = (f32[1,1,512]{2,1,0:T(1,128)S(1)}, f32[1,1,512]{2,1,0:T(1,128)}, u32[]{:S(2)}) copy-start(f32[1,1,512]{2,1,0:T(1,128)} %copy-done.61) | copy-start | bytes 6148
  152.9 11.7 %copy-start.64 = (f32[1,1,512]{2,1,0:T(1,128)S(1)}, f32[1,1,512]{2,1,0:T(1,128)}, u32[]{:S(2)}) copy-start(f32[1,1,512]{2,1,0:T(1,128)} %copy-done.63) | copy-start | bytes 6148
  152.9 41.5 %collective-permute-start.1 = (bf16[1024,1024]{1,0:T(8,128)(2,1)}, bf16[1024,1024]{1,0:T(8,128)(2,1)}, u32[]{:S(2)}, u32[]{:S(2)}) collective-permute-start(bf16[1024,1024]{1,0:T(8,128)(2,1)} %dynamic-slice_bitcast_fusion.1), channel_id=1, source_target_pairs={{0,1},{1,0},{2,3},{3,2},{4,5},{5,4},{6,7},{7,6},{8,9},{9,8},{10,11... | collective-permute-start | bytes 6291464 | tf_op jit(solution)/shard_map/ppermute | solution.py:34
  169.8 17.5 %all-to-all-start.3 = ((bf16[8,64,512]{2,1,0:T(8,128)(2,1)}), bf16[8,64,512]{2,1,0:T(8,128)(2,1)}, u32[]{:S(2)}, u32[]{:S(2)}) async-start(bf16[8,64,512]{2,1,0:T(8,128)(2,1)} %constant_dynamic-update-slice_fusion.3), calls=%async_computation.3 | async-start | bytes 1048576 | tf_op jit(solution)/shard_map/all_to_all | solution.py:86
  189.5 58.6 %all-to-all-start.4 = ((bf16[8,256,512]{2,1,0:T(8,128)(2,1)}), bf16[8,256,512]{2,1,0:T(8,128)(2,1)}, u32[]{:S(2)}, u32[]{:S(2)}) async-start(bf16[8,256,512]{2,1,0:T(8,128)(2,1)} %bitcast.250), calls=%async_computation.4 | async-start | bytes 4194304 | tf_op jit(solution)/shard_map/all_to_all | solution.py:86
  198.9 49.2 %collective-permute-start.2 = (bf16[1024,1024]{1,0:T(8,128)(2,1)}, bf16[1024,1024]{1,0:T(8,128)(2,1)}, u32[]{:S(2)}, u32[]{:S(2)}) collective-permute-start(bf16[1024,1024]{1,0:T(8,128)(2,1)} %fusion.7), channel_id=1, source_target_pairs={{0,2},{1,3},{2,0},{3,1},{4,6},{5,7},{6,4},{7,5},{8,10},{9,11},{10,... | collective-permute-start | bytes 6291464 | tf_op jit(solution)/shard_map/ppermute | solution.py:34
  239.4 42.9 %collective-permute-start.8 = (bf16[1024,256]{1,0:T(8,128)(2,1)S(1)}, bf16[1024,256]{1,0:T(8,128)(2,1)S(1)}, u32[]{:S(2)}, u32[]{:S(2)}) collective-permute-start(bf16[1024,256]{1,0:T(8,128)(2,1)S(1)} %dynamic-slice_bitcast_fusion.2), channel_id=1, source_target_pairs={{0,1},{1,0},{2,3},{3,2},{4,5},{5,4},{6,7},{7,6},{8,9},{9,8},{10,11... | collective-permute-start | bytes 1572872 | tf_op jit(solution)/shard_map/ppermute | solution.py:34
  260.2 7.9 %collective-permute-start.4 = (f32[4,3,512]{2,1,0:T(4,128)S(1)}, f32[4,3,512]{2,1,0:T(4,128)S(1)}, u32[]{:S(2)}, u32[]{:S(2)}) collective-permute-start(f32[4,3,512]{2,1,0:T(4,128)S(1)} %pad_add_fusion.2), channel_id=1, source_target_pairs={{4,0},{8,4},{12,8},{16,12},{20,16},{24,20},{28,24},{5,1},{9,5},{13... | collective-permute-start | bytes 73736 | tf_op jit(solution)/shard_map/ppermute | solution.py:30
  271.0 9.2 %copy-start.39 = (bf16[4,512,512]{2,1,0:T(8,128)(2,1)}, bf16[4,512,512]{2,1,0:T(8,128)(2,1)S(1)}, u32[]{:S(2)}) copy-start(bf16[4,512,512]{2,1,0:T(8,128)(2,1)S(1)} %fusion.5) | copy-start | bytes 6291460
  280.3 18.2 %copy-start.75 = (f32[4,512]{1,0:T(4,128)S(1)}, f32[4,512]{1,0:T(4,128)}, u32[]{:S(2)}) copy-start(f32[4,512]{1,0:T(4,128)} %copy-done.73) | copy-start | bytes 24580
  281.8 31.8 %collective-permute-start.5 = (bf16[1024,1024]{1,0:T(8,128)(2,1)}, bf16[1024,1024]{1,0:T(8,128)(2,1)}, u32[]{:S(2)}, u32[]{:S(2)}) collective-permute-start(bf16[1024,1024]{1,0:T(8,128)(2,1)} %dynamic-slice_bitcast_fusion), channel_id=1, source_target_pairs={{0,1},{1,0},{2,3},{3,2},{4,5},{5,4},{6,7},{7,6},{8,9},{9,8},{10,11... | collective-permute-start | bytes 6291464 | tf_op jit(solution)/shard_map/ppermute | solution.py:34
  283.1 14.3 %collective-permute-start.9 = (bf16[1024,256]{1,0:T(8,128)(2,1)S(1)}, bf16[1024,256]{1,0:T(8,128)(2,1)S(1)}, u32[]{:S(2)}, u32[]{:S(2)}) collective-permute-start(bf16[1024,256]{1,0:T(8,128)(2,1)S(1)} %fusion.29), channel_id=1, source_target_pairs={{0,2},{1,3},{2,0},{3,1},{4,6},{5,7},{6,4},{7,5},{8,10},{9,11},{10,... | collective-permute-start | bytes 1572872 | tf_op jit(solution)/shard_map/ppermute | solution.py:34
  298.3 13.8 %collective-permute-start.10 = (bf16[1024,256]{1,0:T(8,128)(2,1)}, bf16[1024,256]{1,0:T(8,128)(2,1)}, u32[]{:S(2)}, u32[]{:S(2)}) collective-permute-start(bf16[1024,256]{1,0:T(8,128)(2,1)} %add_convert_fusion.3), channel_id=1, source_target_pairs={{0,1},{1,0},{2,3},{3,2},{4,5},{5,4},{6,7},{7,6},{8,9},{9,8},{10,11... | collective-permute-start | bytes 1572872 | tf_op jit(solution)/shard_map/ppermute | solution.py:34
  305.2 67.0 %all-to-all-start.5 = ((bf16[8,256,512]{2,1,0:T(8,128)(2,1)}), bf16[8,256,512]{2,1,0:T(8,128)(2,1)}, u32[]{:S(2)}, u32[]{:S(2)}) async-start(bf16[8,256,512]{2,1,0:T(8,128)(2,1)} %broadcast_in_dim.53), calls=%async_computation.5 | async-start | bytes 4194304 | tf_op jit(solution)/shard_map/all_to_all | solution.py:86
  312.1 158.2 %all-reduce.14.cloned.1.call-start = ((), (), s32[]{:S(2)}) async-start(), calls=%async_computation.6 | async-start | bytes 3145728 | tf_op jit(solution)/shard_map/psum | solution.py:665
  318.1 48.1 %collective-permute-start.6 = (bf16[1024,1024]{1,0:T(8,128)(2,1)}, bf16[1024,1024]{1,0:T(8,128)(2,1)}, u32[]{:S(2)}, u32[]{:S(2)}) collective-permute-start(bf16[1024,1024]{1,0:T(8,128)(2,1)} %fusion.6), channel_id=1, source_target_pairs={{0,2},{1,3},{2,0},{3,1},{4,6},{5,7},{6,4},{7,5},{8,10},{9,11},{10,... | collective-permute-start | bytes 6291464 | tf_op jit(solution)/shard_map/ppermute | solution.py:34
  323.4 5.8 %collective-permute-start.11 = (f32[4,3,256]{2,1,0:T(4,128)S(1)}, f32[4,3,256]{2,1,0:T(4,128)S(1)}, u32[]{:S(2)}, u32[]{:S(2)}) collective-permute-start(f32[4,3,256]{2,1,0:T(4,128)S(1)} %pad_add_fusion.3), channel_id=1, source_target_pairs={{4,0},{8,4},{12,8},{16,12},{20,16},{24,20},{28,24},{5,1},{9,5},{13... | collective-permute-start | bytes 36872 | tf_op jit(solution)/shard_map/ppermute | solution.py:30
  333.9 35.6 %copy-start.2 = (bf16[4,512,1024]{2,1,0:T(8,128)(2,1)S(1)}, bf16[4,512,1024]{2,1,0:T(8,128)(2,1)}, u32[]{:S(2)}) copy-start(bf16[4,512,1024]{2,1,0:T(8,128)(2,1)} %param.30) | copy-start | bytes 12582916
  333.9 51.7 %collective-permute-start.3 = (bf16[1024,1024]{1,0:T(8,128)(2,1)}, bf16[1024,1024]{1,0:T(8,128)(2,1)}, u32[]{:S(2)}, u32[]{:S(2)}) collective-permute-start(bf16[1024,1024]{1,0:T(8,128)(2,1)} %add_convert_fusion.2.part_ref), channel_id=1, source_target_pairs={{0,1},{1,0},{2,3},{3,2},{4,5},{5,4},{6,7},{7,6},{8,9},{9,8},{10,11... | collective-permute-start | bytes 6291464 | tf_op jit(solution)/shard_map/ppermute | solution.py:34
  369.4 29.7 %collective-permute-start.7 = (bf16[1024,1024]{1,0:T(8,128)(2,1)S(1)}, bf16[1024,1024]{1,0:T(8,128)(2,1)}, u32[]{:S(2)}, u32[]{:S(2)}) collective-permute-start(bf16[1024,1024]{1,0:T(8,128)(2,1)S(1)} %add_convert_fusion.1.part_ref), channel_id=1, source_target_pairs={{0,1},{1,0},{2,3},{3,2},{4,5},{5,4},{6,7},{7,6},{8,9},{9,8},{10,11... | collective-permute-start | bytes 6291464 | tf_op jit(solution)/shard_map/ppermute | solution.py:34
  389.1 10.0 %copy-start.4 = (bf16[4,512,1024]{2,1,0:T(8,128)(2,1)S(1)}, bf16[4,512,1024]{2,1,0:T(8,128)(2,1)}, u32[]{:S(2)}) copy-start(bf16[4,512,1024]{2,1,0:T(8,128)(2,1)} %param.30) | copy-start | bytes 12582916
  389.1 10.0 %copy-start.15 = (bf16[4,512,1024]{2,1,0:T(8,128)(2,1)S(1)}, bf16[4,512,1024]{2,1,0:T(8,128)(2,1)}, u32[]{:S(2)}) copy-start(bf16[4,512,1024]{2,1,0:T(8,128)(2,1)} %param.31) | copy-start | bytes 12582916
  389.1 10.0 %copy-start.21 = (bf16[1024,256]{1,0:T(8,128)(2,1)S(1)}, bf16[1024,256]{1,0:T(8,128)(2,1)}, u32[]{:S(2)}) copy-start(bf16[1024,256]{1,0:T(8,128)(2,1)} %copy-done.20) | copy-start | bytes 1572868
  399.1 11.3 %copy-start.83 = (f32[512]{0:T(512)S(1)}, f32[512]{0:T(512)}, u32[]{:S(2)}) copy-start(f32[512]{0:T(512)} %get-tuple-element.137) | copy-start | bytes 6148
  410.4 5.6 %collective-permute-start.12 = (f32[112,128]{1,0:T(8,128)S(1)}, f32[112,128]{1,0:T(8,128)S(1)}, u32[]{:S(2)}, u32[]{:S(2)}) collective-permute-start(f32[112,128]{1,0:T(8,128)S(1)} %pad_bitcast_fusion), channel_id=1, source_target_pairs={{0,4},{4,0},{8,12},{12,8},{16,20},{20,16},{24,28},{28,24},{1,5},{5... | collective-permute-start | bytes 172040 | tf_op jit(solution)/shard_map/ppermute | solution.py:34
  416.0 54.2 %collective-permute-start.13 = (f32[112,128]{1,0:T(8,128)S(1)}, f32[112,128]{1,0:T(8,128)S(1)}, u32[]{:S(2)}, u32[]{:S(2)}) collective-permute-start(f32[112,128]{1,0:T(8,128)S(1)} %fusion.87), channel_id=1, source_target_pairs={{0,8},{4,12},{8,0},{12,4},{16,24},{20,28},{24,16},{28,20},{1,9},{5... | collective-permute-start | bytes 172040 | tf_op jit(solution)/shard_map/ppermute | solution.py:34
  417.9 54.3 %copy-start.41 = (f32[1024,256]{1,0:T(8,128)S(1)}, f32[1024,256]{1,0:T(8,128)}, u32[]{:S(2)}) copy-start(f32[1024,256]{1,0:T(8,128)} %param.39) | copy-start | bytes 3145732
  417.9 54.3 %copy-start.43 = (f32[1024,256]{1,0:T(8,128)S(1)}, f32[1024,256]{1,0:T(8,128)}, u32[]{:S(2)}) copy-start(f32[1024,256]{1,0:T(8,128)} %param.41) | copy-start | bytes 3145732
  470.3 32.2 %collective-permute-start.14 = (f32[112,128]{1,0:T(8,128)S(1)}, f32[112,128]{1,0:T(8,128)S(1)}, u32[]{:S(2)}, u32[]{:S(2)}) collective-permute-start(f32[112,128]{1,0:T(8,128)S(1)} %fusion.132), channel_id=1, source_target_pairs={{0,16},{4,20},{8,24},{12,28},{16,0},{20,4},{24,8},{28,12},{1,17},{... | collective-permute-start | bytes 172040 | tf_op jit(solution)/shard_map/ppermute | solution.py:34
  477.9 25.1 %copy-start.81 = (f32[1024]{0:T(1024)S(1)}, f32[1024]{0:T(1024)}, u32[]{:S(2)}) copy-start(f32[1024]{0:T(1024)} %param.35) | copy-start | bytes 12292
  477.9 25.1 %copy-start.82 = (f32[1024]{0:T(1024)S(1)}, f32[1024]{0:T(1024)}, u32[]{:S(2)}) copy-start(f32[1024]{0:T(1024)} %param.34) | copy-start | bytes 12292
  477.9 25.7 %copy-start.78 = (f32[3,8]{1,0:T(4,128)S(1)}, f32[3,8]{1,0:T(4,128)}, u32[]{:S(2)}) copy-start(f32[3,8]{1,0:T(4,128)} %param.51) | copy-start | bytes 292
  477.9 25.7 %copy-start.84 = (f32[3,8]{1,0:T(4,128)S(1)}, f32[3,8]{1,0:T(4,128)}, u32[]{:S(2)}) copy-start(f32[3,8]{1,0:T(4,128)} %param.53) | copy-start | bytes 292
  478.0 25.7 %copy-start.85 = (f32[3,8]{1,0:T(4,128)S(1)}, f32[3,8]{1,0:T(4,128)}, u32[]{:S(2)}) copy-start(f32[3,8]{1,0:T(4,128)} %param.52) | copy-start | bytes 292
  478.0 26.3 %copy-start.51 = (f32[1024,8]{0,1:T(8,128)S(1)}, f32[1024,8]{0,1:T(8,128)}, u32[]{:S(2)}) copy-start(f32[1024,8]{0,1:T(8,128)} %param.44) | copy-start | bytes 98308
  478.0 26.3 %copy-start.52 = (f32[1024,8]{0,1:T(8,128)S(1)}, f32[1024,8]{0,1:T(8,128)}, u32[]{:S(2)}) copy-start(f32[1024,8]{0,1:T(8,128)} %param.43) | copy-start | bytes 98308
  478.0 27.0 %copy-start.65 = (f32[5,512]{1,0:T(8,128)S(1)}, f32[5,512]{1,0:T(8,128)}, u32[]{:S(2)}) copy-start(f32[5,512]{1,0:T(8,128)} %param.47) | copy-start | bytes 30724
  478.0 27.0 %copy-start.66 = (f32[5,512]{1,0:T(8,128)S(1)}, f32[5,512]{1,0:T(8,128)}, u32[]{:S(2)}) copy-start(f32[5,512]{1,0:T(8,128)} %param.46) | copy-start | bytes 30724
  478.0 27.6 %copy-start.71 = (f32[5,256]{1,0:T(8,128)S(1)}, f32[5,256]{1,0:T(8,128)}, u32[]{:S(2)}) copy-start(f32[5,256]{1,0:T(8,128)} %param.50) | copy-start | bytes 15364
  478.0 27.6 %copy-start.72 = (f32[5,256]{1,0:T(8,128)S(1)}, f32[5,256]{1,0:T(8,128)}, u32[]{:S(2)}) copy-start(f32[5,256]{1,0:T(8,128)} %param.49) | copy-start | bytes 15364
  478.0 28.2 %copy-start.87 = (f32[512]{0:T(512)S(1)}, f32[512]{0:T(512)}, u32[]{:S(2)}) copy-start(f32[512]{0:T(512)} %param.54) | copy-start | bytes 6148
  478.0 28.2 %copy-start.88 = (f32[512]{0:T(512)S(1)}, f32[512]{0:T(512)}, u32[]{:S(2)}) copy-start(f32[512]{0:T(512)} %param.56) | copy-start | bytes 6148
  478.1 28.2 %copy-start.89 = (f32[512]{0:T(512)S(1)}, f32[512]{0:T(512)}, u32[]{:S(2)}) copy-start(f32[512]{0:T(512)} %param.55) | copy-start | bytes 6148
  (53 other events, 225.2 us)
Sparse Core Ops, SparseCore 0:
  378.7 91.4 all-reduce.13

commit v4 on v3

--- a/solution.py
+++ b/solution.py
@@ -204,10 +204,47 @@
     state[...] = grown[q - 1 : q, :] * before + dot(b, xw, ((0,), (0,)))
 
 
+def conv_back_step(act_grad, mixed, previous, taps, after_ref):
+    q = mixed.shape[0]
+    window = jnp.concatenate([previous, mixed], axis=0)
+    shifted = [window[8 - CONV + 1 + k : 8 - CONV + 1 + k + q] for k in range(CONV)]
+    convolved = taps[CONV : CONV + 1]
+    for k in range(CONV):
+        convolved = convolved + taps[k : k + 1] * shifted[k]
+    conv_grad = act_grad * silu_slope(convolved)
+    extended = jnp.concatenate([conv_grad, after_ref[...]], axis=0)
+    mixed_grad = taps[CONV - 1 : CONV] * conv_grad
+    for k in range(CONV - 1):
+        mixed_grad = mixed_grad + taps[k : k + 1] * extended[CONV - 1 - k : CONV - 1 - k + q]
+    sums = [jnp.sum(conv_grad * part, axis=0, keepdims=True) for part in shifted]
+    sums.append(jnp.sum(conv_grad, axis=0, keepdims=True))
+    sums.append(jnp.zeros((8 - CONV - 1, mixed.shape[1]), F32))
+    after_ref[...] = conv_grad[:8]
+    return conv_grad, mixed_grad, jnp.concatenate(sums, axis=0)
+
+
+def rows_before(edge_ref, previous_ref):
+    first = pl.program_id(1) == pl.num_programs(1) - 1
+    return jnp.where(first, edge_ref[0].astype(F32), previous_ref[0].astype(F32))[8:]
+
+
 def back_kernel(
     x_ref, b_ref, c_ref, step_ref, decay_ref, decay_t_ref, skip_ref, dy_ref, y_ref, in_ref, leave_ref,
-    dx_ref, dbc_ref, ldg_ref, dstep_ref, dskip_ref, grad
+    mixed_ref, previous_ref, edge_ref, taps_ref, slope_ref, rate_ref,
+    mixed_grad_ref, dbc_ref, pre_ref, first_ref, last_ref, tap_sums_ref, head_sums_ref,
+    grad, after
 ):
+    start = (pl.program_id(0) == 0) & (pl.program_id(1) == 0)
+
+    @pl.when(start)
+    def _():
+        tap_sums_ref[...] = jnp.zeros_like(tap_sums_ref)
+        head_sums_ref[...] = jnp.zeros_like(head_sums_ref)
+
+    @pl.when(pl.program_id(1) == 0)
+    def _():
+        after[...] = jnp.zeros_like(after)
+
     heads = step_ref.shape[2]
     width = x_ref.shape[2] // heads
 
@@ -253,7 +290,18 @@
     v = jnp.concatenate(v_parts, axis=1) + v_state
     xs_wide = xs.astype(F32)
     etotal = grown[q - 1 : q, :]
-    dx_ref[0] = step_wide * v + skip_ref[0] * dy
+    dx = step_wide * v + skip_ref[0] * dy
+    conv_grad, mixed_grad, tap_sums = conv_back_step(
+        dx, mixed_ref[0].astype(F32), rows_before(edge_ref, previous_ref), taps_ref[...], after
+    )
+    mixed_grad_ref[0] = mixed_grad.astype(BF16)
+    first_ref[0] = conv_grad[:8]
+
+    @pl.when(pl.program_id(1) == 0)
+    def _():
+        last_ref[0] = mixed_grad[q - 8 :]
+
+    tap_sums_ref[...] += tap_sums
     end_row = jnp.sum(xs_wide * v_state, axis=0, keepdims=True) + jnp.sum(
         etotal * before * after_grad, axis=0, keepdims=True
     )
@@ -261,9 +309,16 @@
     last = lax.broadcasted_iota(jnp.int32, crossing.shape, 0) == q - 1
     crossing = crossing + jnp.where(last, end_row, 0.0)
     upper = jnp.where(column >= row, 1.0, 0.0).astype(F32)
-    ldg_ref[0] = dot(upper, head_sums(crossing, expand), precision=HIGHEST_PREC)
-    dstep_ref[0] = head_sums(x * v, expand)
-    dskip_ref[0] = head_sums(x * dy, expand)
+    decay_grad = dot(upper, head_sums(crossing, expand), precision=HIGHEST_PREC)
+    pre_grad = (head_sums(x * v, expand) - rate_ref[...] * decay_grad) * slope_ref[0]
+    pre_ref[0] = pre_grad.astype(BF16)
+    sums = [
+        jnp.sum(decay_grad * decay_ref[0], axis=0, keepdims=True),
+        jnp.sum(pre_grad, axis=0, keepdims=True),
+        jnp.sum(head_sums(x * dy, expand), axis=0, keepdims=True),
+        jnp.zeros((5, heads), F32),
+    ]
+    head_sums_ref[...] += jnp.concatenate(sums, axis=0)
     dscores_low = dscores_t.astype(BF16)
     state = b.shape[1]
     dbc_ref[0, :, :state] = (
@@ -275,9 +330,16 @@
     grad[...] = etotal * after_grad + dot(c, edy, ((0,), (0,)))
 
 
-def scan_forward(x, b, c, step, decay, decay_t, enter):
-    seqs, length, inner = x.shape
-    state, heads = b.shape[2], step.shape[2]
+def act_blocks(inner, state, place):
+    def part(lanes, at):
+        return pl.BlockSpec((1, CHUNK, lanes), lambda s, k: (s, place(k), at))
+
+    return [part(inner, 0), part(state, inner // state), part(state, inner // state + 1)]
+
+
+def scan_forward(activated, step, decay, decay_t, enter):
+    seqs, length, heads = step.shape
+    state, inner = enter.shape[1:]
     chunks = length // CHUNK
 
     def block(lanes):
@@ -286,10 +348,8 @@
     return pl.pallas_call(
         scan_kernel,
         grid=(seqs, chunks),
-        in_specs=[
-            block(inner),
-            block(state),
-            block(state),
+        in_specs=act_blocks(inner, state, lambda k: k)
+        + [
             block(heads),
             block(heads),
             pl.BlockSpec((1, heads, CHUNK), lambda s, k: (s, 0, k)),
@@ -306,24 +366,53 @@
         scratch_shapes=[pltpu.VMEM((state, inner), F32)],
         compiler_params=pltpu.CompilerParams(vmem_limit_bytes=40 << 20),
         cost_estimate=load(13),
-    )(x, b, c, step, decay, decay_t, enter)
-
-
-def scan_backward(x, b, c, step, decay, decay_t, skip, dy, y, states, leave):
-    seqs, length, inner = x.shape
-    state, heads = b.shape[2], step.shape[2]
+    )(activated, activated, activated, step, decay, decay_t, enter)
+
+
+def conv_blocks(chunks, lanes, at):
+    tall = CHUNK // 16
+    return [
+        pl.BlockSpec((1, CHUNK, lanes), lambda s, k, *_: (s, chunks - 1 - k, at)),
+        pl.BlockSpec(
+            (1, 16, lanes), lambda s, k, *_: (s, jnp.maximum((chunks - 1 - k) * tall - 1, 0), at)
+        ),
+        pl.BlockSpec((1, 16, lanes), lambda s, k, *_: (s, 0, at)),
+        pl.BlockSpec((8, lanes), lambda s, k, *_: (0, at)),
+    ]
+
+
+def conv_outs(seqs, chunks, lanes):
+    specs = [
+        pl.BlockSpec((1, CHUNK, lanes), lambda s, k, *_: (s, chunks - 1 - k, 0)),
+        pl.BlockSpec((1, 8, lanes), lambda s, k, *_: (s, 0, 0)),
+        pl.BlockSpec((1, 8, lanes), lambda s, k, *_: (s, 0, 0)),
+        pl.BlockSpec((8, lanes), lambda s, k, *_: (0, 0)),
+    ]
+    shapes = [
+        jax.ShapeDtypeStruct((seqs, chunks * CHUNK, lanes), BF16),
+        jax.ShapeDtypeStruct((seqs, 8, lanes), F32),
+        jax.ShapeDtypeStruct((seqs, 8, lanes), F32),
+        jax.ShapeDtypeStruct((8, lanes), F32),
+    ]
+    return specs, shapes
+
+
+def scan_backward(
+    activated, step, decay, decay_t, skip, dy, y, states, leave, mixed, edge, taps, slope, rate
+):
+    seqs, length, heads = step.shape
+    state, inner = leave.shape[1:]
     chunks = length // CHUNK
 
     def block(lanes):
         return pl.BlockSpec((1, CHUNK, lanes), lambda s, k: (s, chunks - 1 - k, 0))
 
+    conv_specs, conv_shapes = conv_outs(seqs, chunks, inner)
     return pl.pallas_call(
         back_kernel,
         grid=(seqs, chunks),
-        in_specs=[
-            block(inner),
-            block(state),
-            block(state),
+        in_specs=act_blocks(inner, state, lambda k: chunks - 1 - k)
+        + [
             block(heads),
             block(heads),
             pl.BlockSpec((1, heads, CHUNK), lambda s, k: (s, 0, chunks - 1 - k)),
@@ -332,19 +421,119 @@
             block(inner),
             pl.BlockSpec((1, 1, state, inner), lambda s, k: (s, chunks - 1 - k, 0, 0)),
             pl.BlockSpec((1, state, inner), lambda s, k: (s, 0, 0)),
-        ],
-        out_specs=[block(inner), block(2 * state), block(heads), block(heads), block(heads)],
+        ]
+        + conv_blocks(chunks, inner, 0)
+        + [block(heads), pl.BlockSpec((1, heads), lambda s, k: (0, 0))],
+        out_specs=[conv_specs[0], block(2 * state), block(heads)]
+        + conv_specs[1:]
+        + [pl.BlockSpec((8, heads), lambda s, k: (0, 0))],
         out_shape=[
-            jax.ShapeDtypeStruct((seqs, length, inner), F32),
+            conv_shapes[0],
             jax.ShapeDtypeStruct((seqs, length, 2 * state), BF16),
-            jax.ShapeDtypeStruct((seqs, length, heads), F32),
-            jax.ShapeDtypeStruct((seqs, length, heads), F32),
-            jax.ShapeDtypeStruct((seqs, length, heads), F32),
-        ],
-        scratch_shapes=[pltpu.VMEM((state, inner), F32)],
+            jax.ShapeDtypeStruct((seqs, length, heads), BF16),
+        ]
+        + conv_shapes[1:]
+        + [jax.ShapeDtypeStruct((8, heads), F32)],
+        scratch_shapes=[pltpu.VMEM((state, inner), F32), pltpu.VMEM((8, inner), F32)],
         compiler_params=pltpu.CompilerParams(vmem_limit_bytes=40 << 20),
-        cost_estimate=load(27),
-    )(x, b, c, step, decay, decay_t, skip, dy, y, states, leave)
+        cost_estimate=load(30),
+    )(
+        activated, activated, activated, step, decay, decay_t, skip, dy, y, states, leave,
+        mixed, mixed, edge, taps, slope, rate
+    )
+
+
+def bc_kernel(
+    scalars_ref, part_ref, got_ref, mixed_ref, previous_ref, edge_ref, taps_ref,
+    mixed_grad_ref, first_ref, last_ref, tap_sums_ref, after
+):
+    start = (pl.program_id(0) == 0) & (pl.program_id(1) == 0)
+
+    @pl.when(start)
+    def _():
+        tap_sums_ref[...] = jnp.zeros_like(tap_sums_ref)
+
+    @pl.when(pl.program_id(1) == 0)
+    def _():
+        after[...] = jnp.zeros_like(after)
+
+    q = mixed_ref.shape[1]
+    act_grad = picked(scalars_ref, part_ref, got_ref)[0]
+    conv_grad, mixed_grad, tap_sums = conv_back_step(
+        act_grad, mixed_ref[0].astype(F32), rows_before(edge_ref, previous_ref), taps_ref[...], after
+    )
+    mixed_grad_ref[0] = mixed_grad.astype(BF16)
+    first_ref[0] = conv_grad[:8]
+
+    @pl.when(pl.program_id(1) == 0)
+    def _():
+        last_ref[0] = mixed_grad[q - 8 :]
+
+    tap_sums_ref[...] += tap_sums
+
+
+def bc_backward(scalars, part, got, mixed, edge, taps):
+    seqs, length, lanes = mixed.shape
+    chunks = length // CHUNK
+    half = pl.BlockSpec((1, CHUNK, lanes), lambda s, k, _: (s % (seqs // 2), chunks - 1 - k, 0))
+    conv_specs, conv_shapes = conv_outs(seqs, chunks, lanes)
+    return pl.pallas_call(
+        bc_kernel,
+        grid_spec=pltpu.PrefetchScalarGridSpec(
+            num_scalar_prefetch=1,
+            grid=(seqs, chunks),
+            in_specs=[half, half] + conv_blocks(chunks, lanes, 0),
+            out_specs=conv_specs,
+            scratch_shapes=[pltpu.VMEM((8, lanes), F32)],
+        ),
+        out_shape=conv_shapes,
+        compiler_params=pltpu.CompilerParams(vmem_limit_bytes=40 << 20),
+        cost_estimate=load(5),
+    )(
+        scalars,
+        part.reshape(seqs // 2, length, lanes),
+        got.reshape(seqs // 2, length, lanes),
+        mixed,
+        mixed,
+        edge,
+        taps,
+    )
+
+
+def joined_edges(mixed_grad, first, last, taps):
+    rows = []
+    for j in range(CONV - 1):
+        rows.append(sum(taps[k] * first[:, j - k] for k in range(j + 1)))
+    edge_grad = passed_along(jnp.stack(rows, axis=1), "seq", -1)
+    fixed = last + jnp.pad(edge_grad, ((0, 0), (8 - CONV + 1, 0), (0, 0)))
+    return lax.dynamic_update_slice(mixed_grad, fixed.astype(BF16), (0, mixed_grad.shape[1] - 8, 0))
+
+
+def normed_kernel(gate_ref, x_ref, step_ref, z_weight_ref, x_weight_ref, step_weight_ref, out_ref):
+    nt = ((1,), (1,))
+    total = dot(gate_ref[...], z_weight_ref[...], nt) + dot(x_ref[...], x_weight_ref[...], nt)
+    out_ref[...] = (total + dot(step_ref[...], step_weight_ref[...], nt)).astype(BF16)
+
+
+def normed_products(gate_grad, x_grad, step_grad, z_weight, x_weight, step_weight):
+    rows, width = gate_grad.shape[0], z_weight.shape[0]
+
+    def block(a):
+        return pl.BlockSpec((ROWS, a.shape[1]), lambda i: (i, 0))
+
+    def whole(a):
+        return pl.BlockSpec(a.shape, lambda i: (0, 0))
+
+    args = (gate_grad, x_grad, step_grad, z_weight, x_weight, step_weight)
+    return pl.pallas_call(
+        normed_kernel,
+        grid=(rows // ROWS,),
+        in_specs=[block(a) for a in args[:3]] + [whole(a) for a in args[3:]],
+        out_specs=pl.BlockSpec((ROWS, width), lambda i: (i, 0)),
+        out_shape=jax.ShapeDtypeStruct((rows, width), BF16),
+        compiler_params=pltpu.CompilerParams(vmem_limit_bytes=40 << 20),
+        cost_estimate=load(6),
+    )(*args)
 
 
 def picked(scalars_ref, part_ref, got_ref):
@@ -421,32 +610,31 @@
 
 
 def adam_kernel(
-    step_rate, decay_weight, first_ref, second_ref, weight_ref, mean_ref, square_ref,
+    step_rate, decay_weight, gradient_ref, weight_ref, mean_ref, square_ref,
     mean_out, square_out, weight_out
 ):
-    for r in range(weight_ref.shape[1]):
-        source = first_ref if r % 2 == 0 else second_ref
-        gradient = source[:, (r // 2) * 128 : (r // 2 + 1) * 128].astype(F32)
-        updated = adam_update(
-            weight_ref[:, r], mean_ref[:, r], square_ref[:, r], gradient, step_rate, decay_weight
-        )
-        mean_out[:, r], square_out[:, r], weight_out[:, r] = updated
-
-
-def adam_pair(weight, mean_old, square_old, first, second, step_rate, decay_weight):
+    mean_out[...], square_out[...], weight_out[...] = adam_update(
+        weight_ref[...],
+        mean_ref[...],
+        square_ref[...],
+        gradient_ref[...].astype(F32),
+        step_rate,
+        decay_weight,
+    )
+
+
+def adam_tiles(weight, mean_old, square_old, gradient, step_rate, decay_weight):
     rows, _, columns = weight.shape
-    height = 128
-    narrow = pl.BlockSpec((height, columns), lambda i: (i, 0))
-    tiles = pl.BlockSpec((height, columns // 64, 128), lambda i: (i, 0, 0))
+    tiles = pl.BlockSpec((128, columns // 64, 128), lambda i: (i, 0, 0))
     updated = pl.pallas_call(
         functools.partial(adam_kernel, step_rate, decay_weight),
-        grid=(rows // height,),
-        in_specs=[narrow, narrow, tiles, tiles, tiles],
-        out_specs=[tiles, tiles, tiles],
+        grid=(rows // 128,),
+        in_specs=[tiles] * 4,
+        out_specs=[tiles] * 3,
         out_shape=[jax.ShapeDtypeStruct((rows, columns // 64, 128), F32)] * 3,
         compiler_params=pltpu.CompilerParams(vmem_limit_bytes=40 << 20),
         cost_estimate=load(9),
-    )(first, second, lane_tiles(weight), lane_tiles(mean_old), lane_tiles(square_old))
+    )(*map(lane_tiles, (gradient, weight, mean_old, square_old)))
     return [from_lane_tiles(part, weight.shape) for part in updated]
 
 
@@ -552,9 +740,7 @@
     unit_decay = wide(jnp.exp(device_decay))[:, None]
     entering, block_decays = states_before(local_state, unit_decay, "seq")
 
-    scanned_raw, states = scan_forward(
-        x_values, b_values, c_values, step_size, log_decay, decay_t, entering
-    )
+    scanned_raw, states = scan_forward(activated, step_size, log_decay, decay_t, entering)
     skip_wide = jnp.repeat(skip_gain, head_width)[None, None]
     scanned = scanned_raw + skip_wide * x_values.astype(F32)
     gate_act = jax.nn.silu(gate_input)
@@ -588,10 +774,10 @@
     projected = halved(partial_out.astype(BF16).reshape(rows, model_width), "head")
     scanned_grad, projected = lax.optimization_barrier((scanned_grad, projected))
     projected_far = swapped(projected, "head", axis_masks("head")[-1])
-    x_grad, bc_grad, decay_grad, step_grad, skip_terms = scan_backward(
-        x_values,
-        b_values,
-        c_values,
+    taps = jnp.pad(conv_weight, ((0, 8 - CONV - 1), (0, 0)))
+    edge_rows = jnp.pad(edge_in, ((0, 0), (16 - CONV + 1, 0), (0, 0)))
+    x_raw, bc_grad, step_in_grad, x_first, x_last, x_tap_sums, head_totals = scan_backward(
+        activated,
         step_size,
         log_decay,
         decay_t,
@@ -600,73 +786,82 @@
         scanned_raw,
         states,
         leaving,
-    )
-    x_grad_late, early_parts, projected_far = lax.optimization_barrier(
-        (x_grad, early_parts, projected_far)
+        mixed_in,
+        edge_rows,
+        taps,
+        jax.nn.sigmoid(raw_step + step_bias),
+        jnp.exp(decay_log)[None],
+    )
+    x_raw, early_parts, projected_far = lax.optimization_barrier(
+        (x_raw, early_parts, projected_far)
     )
     projected_half, projected_other = regathered(added(projected, projected_far), "head")
     early_own = jnp.sum(early_parts.astype(F32), axis=0).astype(BF16)
     early_all = exchanged(jnp.broadcast_to(early_own[None], early_parts.shape), "seq")
-    bc_total = halving_sum(bc_grad.reshape(rows, 2 * state_width), "head")
-    bc_total = bc_total.reshape(bc_grad.shape).astype(F32)
-
-    def conv_back(activated_grad, activated_grad_late, first, last):
-        convolved_grad = activated_grad * silu_slope(convolved[..., first:last])
-        taps = conv_weight[:, first:last]
-        tap_grads = []
-        convolved_late = activated_grad_late * silu_slope(convolved[..., first:last])
-        padded_grad = jnp.zeros((seq_count, local_len + CONV - 1, last - first), F32)
-        for tap_index in range(CONV):
-            tap_grads.append(
-                jnp.sum(
-                    convolved_grad * padded[:, tap_index : tap_index + local_len, first:last],
-                    axis=(0, 1),
-                )
-            )
-            padded_grad = padded_grad + jnp.pad(
-                taps[tap_index] * convolved_late,
-                ((0, 0), (tap_index, CONV - 1 - tap_index), (0, 0)),
-            )
-        tap_grads.append(jnp.sum(convolved_grad, axis=(0, 1)))
-        edge_grad = passed_along(padded_grad[:, : CONV - 1], "seq", -1)
-        mixed_grad = padded_grad[:, CONV - 1 :] + jnp.pad(
-            edge_grad, ((0, 0), (local_len - CONV + 1, 0), (0, 0))
-        )
-        return mixed_grad.astype(BF16), jnp.stack(tap_grads)
-
-    x_in_grad, conv_inner_grad = conv_back(x_grad, x_grad_late, 0, local_inner)
-    step_total = step_grad - jnp.exp(decay_log) * decay_grad
-    pre_grad = step_total * jax.nn.sigmoid(raw_step + step_bias)
-    head_grad = jnp.stack(
-        [
-            jnp.sum(decay_grad * log_decay, axis=(0, 1)),
-            jnp.sum(pre_grad, axis=(0, 1)),
-            jnp.sum(skip_terms, axis=(0, 1)),
-        ]
-    )
-    step_in_grad = pre_grad.astype(BF16)
-    normed_partial = (
-        jnp.einsum("btc,dc->btd", gate_grad, z_weight, preferred_element_type=F32)
-        + jnp.einsum("btc,dc->btd", x_in_grad, x_weight, preferred_element_type=F32)
-        + jnp.einsum("bth,dh->btd", step_in_grad, step_weight, preferred_element_type=F32)
-    )
-    normed_sum = halved(normed_partial.astype(BF16).reshape(rows, model_width), "head")
+    bc_sum = halved(bc_grad.reshape(rows, 2 * state_width), "head")
+    bc_far = swapped(bc_sum, "head", axis_masks("head")[-1])
+
+    x_in_grad = joined_edges(x_raw, x_first, x_last, conv_weight[:, :local_inner])
+    x_in_grad, bc_far = lax.optimization_barrier((x_in_grad, bc_far))
+    bc_half, bc_other = regathered(added(bc_sum, bc_far), "head")
+    normed_partial = normed_products(
+        gate_grad.reshape(rows, local_inner),
+        x_in_grad.reshape(rows, local_inner),
+        step_in_grad.reshape(rows, local_heads),
+        z_weight,
+        x_weight,
+        step_weight,
+    )
+    x_weight_grad = jnp.einsum("btd,btc->dc", normed, x_in_grad, preferred_element_type=F32)
+    x_parts = exchanged(to_blocks(x_weight_grad, seq_size), "seq")
+    normed_sum = halved(normed_partial, "head")
     normed_far = swapped(normed_sum, "head", axis_masks("head")[-1])
-    normed_half, normed_other = regathered(added(normed_sum, normed_far), "head")
-    bc_in_grad, conv_bc_grad = conv_back(
-        bc_total, bc_total, local_inner, local_inner + 2 * state_width
-    )
-    x_in_late, early_all = lax.optimization_barrier((x_in_grad, early_all))
-    early_sums = early_all.reshape(2, model_width, local_inner)
-    x_weight_grad = jnp.einsum("btd,btc->dc", normed, x_in_late, preferred_element_type=F32)
-    bc_weight_grad = jnp.einsum("btd,btc->dc", normed, bc_in_grad, preferred_element_type=F32)
-    step_weight_grad = jnp.einsum("btd,bth->hd", normed, step_in_grad, preferred_element_type=F32)
-    late_grads = (x_weight_grad.astype(BF16), bc_weight_grad.astype(BF16))
-    late_sums = lax.psum(late_grads, "seq")
+
     scalars = jnp.concatenate(
         [lengths, jnp.stack([seq_index * local_len, near_bit("head", 1)]).astype(jnp.int32)]
     )
+    bc_half, early_all, _ = lax.optimization_barrier((bc_half, early_all, normed_sum))
+    early_sums = early_all.reshape(2, model_width, local_inner)
+    bc_raw_grad, bc_first, bc_last, bc_tap_sums = bc_backward(
+        scalars,
+        bc_half,
+        bc_other,
+        mixed_in[..., local_inner:],
+        edge_rows[..., local_inner:],
+        taps[:, local_inner:],
+    )
+    bc_in_grad = joined_edges(bc_raw_grad, bc_first, bc_last, conv_weight[:, local_inner:])
+    bc_in_grad, x_parts = lax.optimization_barrier((bc_in_grad, x_parts))
+    x_own = jnp.sum(x_parts.astype(F32), axis=0).astype(BF16)
+    x_all = exchanged(jnp.broadcast_to(x_own[None], x_parts.shape), "seq")
+    x_sum = x_all.reshape(model_width, local_inner)
+    bc_weight_grad = jnp.einsum("btd,btc->dc", normed, bc_in_grad, preferred_element_type=F32)
+    bc_blocks = to_blocks(bc_weight_grad, seq_size)
+    bc_parts = exchanged(bc_blocks, "seq")
     flat_tokens = inputs.reshape(rows, model_width)
+    block_out = merge_call(
+        out_kernel,
+        scalars,
+        projected_half,
+        projected_other,
+        (flat_tokens, out_scale.reshape(rows, 1)),
+        [row_block(model_width), row_block(1)],
+        row_block(model_width),
+        jax.ShapeDtypeStruct((rows, model_width), BF16),
+    )
+    out_updated = adam_update(
+        proj_out,
+        proj_out_mean,
+        proj_out_square,
+        early_sums[0].astype(F32),
+        LEARNING_RATES[-1],
+        WEIGHT_DECAYS[-1],
+    )
+    normed_far, block_out, out_updated, _ = lax.optimization_barrier(
+        (normed_far, block_out, out_updated, bc_blocks)
+    )
+    block_out = block_out.reshape(inputs.shape)
+    normed_half, normed_other = regathered(added(normed_sum, normed_far), "head")
     input_grad, norm_gain_grad = merge_call(
         functools.partial(tail_kernel, local_len),
         scalars,
@@ -693,17 +888,12 @@
         ],
     )
     input_grad = input_grad.reshape(inputs.shape)
-    block_out = merge_call(
-        out_kernel,
-        scalars,
-        projected_half,
-        projected_other,
-        (flat_tokens, out_scale.reshape(rows, 1)),
-        [row_block(model_width), row_block(1)],
-        row_block(model_width),
-        jax.ShapeDtypeStruct((rows, model_width), BF16),
-    ).reshape(inputs.shape)
-    late_sums, _, _ = lax.optimization_barrier((late_sums, input_grad, block_out))
+    bc_own = jnp.sum(bc_parts.astype(F32), axis=0).astype(BF16)
+    bc_all = exchanged(jnp.broadcast_to(bc_own[None], bc_parts.shape), "seq")
+    step_weight_grad = jnp.einsum("btd,bth->hd", normed, step_in_grad, preferred_element_type=F32)
+    conv_inner_grad = x_tap_sums[: CONV + 1]
+    conv_bc_grad = bc_tap_sums[: CONV + 1]
+    head_grad = head_totals[:3]
     small_grads = (
         norm_gain_grad[0],
         step_weight_grad,
@@ -723,14 +913,14 @@
 
     summed_grads = (
         small_sums[0],
-        (early_sums[1], late_sums[0].reshape(model_width, local_inner)),
-        late_sums[1].astype(F32),
+        jnp.stack([early_sums[1], x_sum], axis=1),
+        bc_all.reshape(bc_weight_grad.shape).astype(F32),
         small_sums[1].T,
         small_sums[2],
         small_sums[3],
         small_sums[4],
         small_sums[5],
-        early_sums[0].astype(F32),
+        None,
     )
     params = (
         norm_gain,
@@ -769,8 +959,10 @@
     for weight, mean_old, square_old, gradient, step_rate, decay_weight in zip(
         params, means, squares, summed_grads, LEARNING_RATES, WEIGHT_DECAYS
     ):
-        if weight.ndim == 3:
-            updated = adam_pair(weight, mean_old, square_old, *gradient, step_rate, decay_weight)
+        if gradient is None:
+            updated = out_updated
+        elif weight.ndim == 3:
+            updated = adam_tiles(weight, mean_old, square_old, gradient, step_rate, decay_weight)
         else:
             updated = adam_update(weight, mean_old, square_old, gradient, step_rate, decay_weight)
         results.extend(updated)

time: 523 us -> 489 us (0.935)
  waiting for transfers between devices: 131 us -> 85.6 us
  starting transfers between devices: 47.5 us -> 86.2 us
  other arithmetic: 96.9 us -> 72.5 us
  local copies, waits for them, and re-layouts: 41.7 us -> 61.1 us
  matrix products: 85.7 us -> 71 us
  between operations: 15.7 us -> 2.32 us
  Pallas kernels: 86.1 us -> 94.5 us
    psum x1 -> x0, waiting for transfers between devices: 45.5 us -> none  [shards(): late_sums = lax.psum(late_grads, 'seq')]
    all_to_all x6 -> x10, starting transfers between devices: 30.2 us -> 68.1 us  [exchanged(): return lax.all_to_all(blocks, axis, 0, 0, tiled=True)]
    ppermute x12, waiting for transfers between devices: 45.8 us -> 9.43 us  [swapped(): lax.ppermute(block, axis, [(i, i ^ mask) for i in range(lax.axis_size(axi...]
    all_to_all x6 -> x10, waiting for transfers between devices: 35.6 us -> 70.2 us  [exchanged(): return lax.all_to_all(blocks, axis, 0, 0, tiled=True)]
    dot_general x4 -> x1, matrix products: 27.9 us -> 3.45 us  [shards(): jnp.einsum('btd,btc->dc', normed, x_in_grad, preferred_element_type=F32)]
    mul x3 -> x0, other arithmetic: 12.8 us -> none  [conv_back(): taps[tap_index] * convolved_late]
    unnamed x197 -> x214, local copies, waits for them, and re-layouts: 19.8 us -> 32.5 us
    pallas_call x3 -> x5, Pallas kernels: 64.9 us -> 75.3 us  [the longest x1 36.4 us: scan_backward(): pl.pallas_call(back_kernel, grid=(seqs, chunks), in_specs=act_blocks(inne...]
  transfers between devices with their start and end apart: 22 -> 25, of which waited for: 9 -> 12; matrix products, arithmetic and copies ran while one was open for 28% -> 21% of each run, Pallas kernels for 14% -> 17%
where the time goes in v4:
time: 489 us; the launch traced here: 483 us
  Pallas kernels  94.5 us (19%)
  starting transfers between devices  86.2 us (18%)
  waiting for transfers between devices  85.6 us (18%)
  other arithmetic  72.5 us (15%)
  matrix products  71 us (15%)
  local copies, waits for them, and re-layouts  61.1 us (12%)
  blocking collectives  10.1 us (2%)
    all_to_all x10, waiting for transfers between devices, exchanged(): return lax.all_to_all(blocks, axis, 0, 0, tiled=True)  70.2 us
    all_to_all x10, starting transfers between devices, exchanged(): return lax.all_to_all(blocks, axis, 0, 0, tiled=True)  68.1 us
    pallas_call x1, Pallas kernels, scan_backward(): pl.pallas_call(back_kernel, grid=(seqs, chunks), in_specs=act_blocks(inne...  36.4 us
    unnamed x214, local copies, waits for them, and re-layouts  32.5 us
    pallas_call x2, Pallas kernels, merge_call(): pl.pallas_call(kernel, grid_spec=pltpu.PrefetchScalarGridSpec(num_scalar_...  19.2 us
    convert_element_type x6, other arithmetic, added(): return (a.astype(F32) + b.astype(F32)).astype(BF16)  16.2 us
    pallas_call x1, Pallas kernels, scan_forward(): pl.pallas_call(scan_kernel, grid=(seqs, chunks), in_specs=act_blocks(inne...  13.7 us
    sub x8, other arithmetic, adam_update(): weight - step_rate * (corrected_mean / (jnp.sqrt(corrected_square) + ADAM...  12.5 us
  transfers between devices with their start and end apart: 25, of which 12 were waited for; matrix products, arithmetic and copies ran while one was open for 21% of the time, Pallas kernels for 17%

profile of v4, /device:TPU:0, one launch (start us, length us, event | category | flops | bytes accessed | tf_op | source)
XLA Modules:
  0.0 483.4 jit_solution(4303482033721431638)
XLA Ops:
  2.0 3.0 copy.222
  7.3 3.7 convolution_convert_fusion.mixed_ref.previous_ref
  11.1 1.7 copy-done.5
  12.8 5.0 %collective-permute-start = (bf16[4,3,768]{2,1,0:T(4,128)(2,1)S(1)}, bf16[4,3,768]{2,1,0:T(4,128)(2,1)S(1)}, u32[]{:S(2)}, u32[]{:S(2)}) collective-permute-start(bf16[4,3,768]{2,1,0:T(4,128)(2,1)S(1)} %slice.326), channel_id=1, source_target_pairs={{0,4},{4,8},{8,12},{12,16},{16,20},{20,24},{24,28},{1,5},{5,9},{9,... | collective-permute-start | bytes 55304 | tf_op jit(solution)/shard_map/ppermute | solution.py:30
  18.6 5.8 %add_divide_fusion.1 = (f32[4,512,8]{2,1,0:T(8,128)}, f32[4,512,8]{2,1,0:T(8,128)S(1)}, f32[4,512,8]{2,1,0:T(8,128)}, f32[4,512,8]{2,1,0:T(8,128)}) fusion(f32[8]{0:T(128)S(1)} %get-tuple-element.179, f32[8]{0:T(128)S(1)} %get-tuple-element.180, bf16[1024,8]{1,0:T(8,128)(2,1)S(1)} %copy.171.step_weight_ref, bf16[4,512,1024]{2,1,0:T(8,128)(2,1)} %param.30, ...), kind=kOutput, calls=%fused_computation.87 | convolution fusion | flops 42139648 | bytes 4485184 | tf_op jit(solution)/shard_map/btd,dh->bth/dot_general | solution.py:715
  24.4 3.4 convolution_bitcast_fusion.1
  33.4 9.1 %multiply_convert_fusion.1.x_ref.b_ref.c_ref = bf16[4,512,768]{2,1,0:T(8,128)(2,1)S(1)} fusion(bf16[4,512,768]{2,1,0:T(8,128)(2,1)} %copy-done.5, bf16[4,3,768]{2,1,0:T(4,128)(2,1)} %copy-done.57, f32[768]{0:T(1024)S(1)} %get-tuple-element.102, f32[768]{0:T(1024)S(1)} %get-tuple-element.103, f32[768]{0:T(1024)S(1)} %get-tuple-element.104, ...), kind=kLoop, calls=%fused_computation.8 | loop fusion | flops 40894464 | bytes 6325248 | tf_op jit(solution)/shard_map/convert_element_type | solution.py:724
  42.6 5.5 %fusion.3 = bf16[4,512,512]{2,1,0:T(8,128)(2,1)S(1)} fusion(f32[8,512,1]{1,0,2:T(8,128)S(1)} %copy-done.60, bf16[4,512,768]{2,1,0:T(8,128)(2,1)S(1)} %multiply_convert_fusion.1.x_ref.b_ref.c_ref, f32[4,512,8]{2,1,0:T(8,128)S(1)} %copy-done.42, f32[4,512,8]{2,1,0:T(8,128)} %get-tuple-element.182), kind=kOutput, calls=%fused_computation.13 | convolution fusion | flops 103923712 | bytes 4341760 | tf_op jit(solution)/shard_map/...h,hc->...c/dot_general | solution.py:699
  49.5 4.9 %all-to-all-start = ((bf16[8,80,512]{2,1,0:T(8,128)(2,1)}), bf16[8,80,512]{2,1,0:T(8,128)(2,1)}, u32[]{:S(2)}, u32[]{:S(2)}) async-start(bf16[8,80,512]{2,1,0:T(8,128)(2,1)} %pad_maximum_fusion.2), calls=%async_computation | async-start | bytes 1310720 | tf_op jit(solution)/shard_map/all_to_all | solution.py:86
  55.0 16.5 %all-to-all-done = bf16[8,80,512]{2,1,0:T(8,128)(2,1)} async-done(((bf16[8,80,512]{2,1,0:T(8,128)(2,1)}), bf16[8,80,512]{2,1,0:T(8,128)(2,1)}, u32[]{:S(2)}, u32[]{:S(2)}) %all-to-all-start) | async-done | bytes 655392 | tf_op jit(solution)/shard_map/all_to_all | solution.py:86
  78.0 4.4 all-to-all-start.1
  82.4 2.8 fusion.22
  88.3 8.4 %all-to-all-done.1 = bf16[8,64,512]{2,1,0:T(8,128)(2,1)} async-done(((bf16[8,64,512]{2,1,0:T(8,128)(2,1)}), bf16[8,64,512]{2,1,0:T(8,128)(2,1)}, u32[]{:S(2)}, u32[]{:S(2)}) %all-to-all-start.1) | async-done | bytes 524320 | tf_op jit(solution)/shard_map/all_to_all | solution.py:86
  100.3 13.7 %shard_map.509 = (f32[4,512,512]{2,1,0:T(8,128)S(1)}, f32[4,4,128,512]{3,2,1,0:T(8,128)}) custom-call(bf16[4,512,768]{2,1,0:T(8,128)(2,1)S(1)} %multiply_convert_fusion.1.x_ref.b_ref.c_ref, bf16[4,512,768]{2,1,0:T(8,128)(2,1)S(1)} %multiply_convert_fusion.1.x_ref.b_ref.c_ref, bf16[4,512,768]{2,1,0:T(8,128)(2,1)S(1)} %multiply_convert_fusion.1.x_ref.b_ref.c_ref, ...), custom_call_target="tpu_custom_call" | custom-call | bytes 47970000 | tf_op jit(solution)/shard_map/pallas_call | solution.py:348
  114.0 5.9 %multiply_reduce_fusion.2 = (f32[4,512]{1,0:T(4,128)S(1)}, f32[4,512,512]{2,1,0:T(8,128)}, f32[4,512,512]{2,1,0:T(8,128)}) fusion(f32[4,512,512]{2,1,0:T(8,128)S(1)} %get-tuple-element.64.y_ref, bf16[4,512,768]{2,1,0:T(8,128)(2,1)S(1)} %multiply_convert_fusion.1.x_ref.b_ref.c_ref, f32[512]{0:T(512)S(1)} %mul.770, bf16[1024,2,512]{2,0,1:T(8,128)(2,1)S(1)} %copy-done.40, ...), kind=kOutput, calls=%fused_computation.27 | convolution fusion | flops 2166355968 | bytes 19945472 | tf_op jit(solution)/shard_map/btd,dc->btc/dot_general | solution.py:716
  121.1 6.9 %fusion.94 = (bf16[4,512,1024]{2,1,0:T(8,128)(2,1)}, f32[4,512]{1,0:T(4,128)S(1)}) fusion(f32[4,512]{1,0:T(4,128)S(1)} %compare_convert_fusion, bf16[4,512,1024]{2,1,0:T(8,128)(2,1)S(1)} %copy-done.12, f32[1024,512]{1,0:T(8,128)S(1)} %copy-done.45, f32[4,512,512]{2,1,0:T(8,128)} %get-tuple-element.135, f32[512]{0:T(512)S(1)} %copy-done.96), kind=kOutput, calls=%fused_computation.223 | convolution fusion | flops 2160588800 | bytes 14698496 | tf_op jit(solution)/shard_map/bti,di->btd/dot_general | solution.py:750
  128.0 10.1 %psum.7 = f32[2,4,512]{2,1,0:T(4,128)S(1)} all-reduce(f32[2,4,512]{2,1,0:T(4,128)S(1)} %pad_maximum_fusion.4), channel_id=1, replica_groups=mesh['seq'=8,'head'=4] {'head'}, use_global_device_ids=true, to_apply=%region_3.4 | all-reduce | flops 4096 | bytes 32768 | tf_op jit(solution)/shard_map/psum | solution.py:753
  138.8 10.5 %fusion.17 = (f32[4,512,512]{2,1,0:T(8,128)S(1)}, bf16[4,512,512]{2,1,0:T(8,128)(2,1)}, f32[512]{0:T(512)}) fusion(f32[4,512,512]{2,1,0:T(8,128)} %get-tuple-element.135, f32[4,512]{1,0:T(4,128)S(1)} %fusion.58, f32[512]{0:T(512)} %param.54, f32[4,512,512]{2,1,0:T(8,128)} %get-tuple-element.183, f32[4,512,512]{2,1,0:T(8,128)} %copy-done.22, ...), kind=kOutput, calls=%fused_computation.60 | convolution fusion | flops 2177367552 | bytes 27293696 | tf_op jit(solution)/shard_map/btd,di->bti/dot_general | solution.py:758
  149.3 3.9 multiply_convert_fusion.2
  154.6 5.1 %all-to-all-start.2 = ((bf16[8,64,512]{2,1,0:T(8,128)(2,1)}), bf16[8,64,512]{2,1,0:T(8,128)(2,1)}, u32[]{:S(2)}, u32[]{:S(2)}) async-start(bf16[8,64,512]{2,1,0:T(8,128)(2,1)} %bitcast.252), calls=%async_computation.2 | async-start | bytes 1048576 | tf_op jit(solution)/shard_map/all_to_all | solution.py:86
  159.8 3.2 dynamic-slice_bitcast_fusion.1
  163.0 6.1 %bitcast_convert_fusion.2 = bf16[1024,512]{1,0:T(8,128)(2,1)} fusion(bf16[4,512,1024]{2,1,0:T(8,128)(2,1)S(1)} %copy-done.13, f32[4,512]{1,0:T(4,128)S(1)} %copy-done.81, f32[4,512]{1,0:T(4,128)S(1)} %copy-done.86, f32[4,512,512]{2,1,0:T(8,128)} %get-tuple-element.135, f32[512]{0:T(512)S(1)} %copy-done.97), kind=kOutput, calls=%fused_computation.48 | convolution fusion | flops 2158493696 | bytes 9455616 | tf_op jit(solution)/shard_map/btd,bti->di/dot_general | solution.py:757
  169.1 4.4 all-to-all-done.2
  182.1 4.1 all-to-all-start.3
  186.2 5.4 %bitcast_convert_fusion.1 = bf16[1024,512]{1,0:T(8,128)(2,1)S(1)} fusion(bf16[4,512,512]{2,1,0:T(8,128)(2,1)} %get-tuple-element.143, bf16[4,512,1024]{2,1,0:T(8,128)(2,1)} %param.30, f32[1024]{0:T(1024)S(1)} %copy-done.34, f32[4,512]{1,0:T(4,128)} %copy-done.82), kind=kOutput, calls=%fused_computation.47 | convolution fusion | flops 2156396544 | bytes 7352320 | tf_op jit(solution)/shard_map/btd,btc->dc/dot_general | solution.py:770
  193.1 6.5 %all-to-all-done.3 = bf16[8,64,512]{2,1,0:T(8,128)(2,1)} async-done(((bf16[8,64,512]{2,1,0:T(8,128)(2,1)}), bf16[8,64,512]{2,1,0:T(8,128)(2,1)}, u32[]{:S(2)}, u32[]{:S(2)}) %all-to-all-start.3) | async-done | bytes 524320 | tf_op jit(solution)/shard_map/all_to_all | solution.py:86
  199.6 2.2 bitcast_convert_fusion.4.leave_ref
  201.8 4.4 all-to-all-start.4
  206.2 4.5 fusion.6
  211.6 1.9 copy-done.6
  218.4 36.4 %shard_map.510 = (bf16[4,512,512]{2,1,0:T(8,128)(2,1)S(1)}, bf16[4,512,256]{2,1,0:T(8,128)(2,1)S(1)}, bf16[4,512,8]{2,1,0:T(8,128)(2,1)S(1)}, f32[4,8,512]{2,1,0...) custom-call(bf16[4,512,768]{2,1,0:T(8,128)(2,1)S(1)} %multiply_convert_fusion.1.x_ref.b_ref.c_ref,, ...), custom_call_target="tpu_custom_call" | custom-call | bytes 110700000 | tf_op jit(solution)/shard_map/pallas_call | solution.py:411
  259.1 2.7 reduce_sum.75
  261.8 2.6 broadcast_in_dim.32
  264.4 5.9 %all-to-all-start.5 = ((bf16[8,256,512]{2,1,0:T(8,128)(2,1)}), bf16[8,256,512]{2,1,0:T(8,128)(2,1)}, u32[]{:S(2)}, u32[]{:S(2)}) async-start(bf16[8,256,512]{2,1,0:T(8,128)(2,1)} %broadcast_in_dim.32), calls=%async_computation.5 | async-start | bytes 4194304 | tf_op jit(solution)/shard_map/all_to_all | solution.py:86
  270.5 1.9 collective-permute-done.4
  276.4 6.0 %collective-permute-done.3 = f32[4,3,512]{2,1,0:T(4,128)S(1)} collective-permute-done((f32[4,3,512]{2,1,0:T(4,128)S(1)}, f32[4,3,512]{2,1,0:T(4,128)S(1)}, u32[]{:S(2)}, u32[]{:S(2)}) %collective-permute-start.3) | collective-permute-done | bytes 24608 | tf_op jit(solution)/shard_map/ppermute | solution.py:30
  283.0 3.5 collective-permute-done.5
  289.2 7.0 %shard_map.511 = bf16[2048,1024]{1,0:T(8,128)(2,1)S(1)} custom-call(bf16[2048,512]{1,0:T(8,128)(2,1)S(1)} %bitcast.237, bf16[2048,512]{1,0:T(8,128)(2,1)S(1)} %bitcast.238, bf16[2048,8]{1,0:T(8,128)(2,1)S(1)} %bitcast.241, bf16[1024,512]{1,0:T(8,128)(2,1)S(1)} %copy-done.19, bf16[1024,512]{1,0:T(8,128)(2,1)S(1)} %copy-done.21, ...), custom_call_target="tpu_custom_call" | custom-call | bytes 22140000 | tf_op jit(solution)/shard_map/pallas_call | solution.py:528
  297.9 3.7 add_convert_fusion.1.part_ref
  302.3 3.5 bitcast_convert_fusion
  305.8 11.3 %all-to-all-done.5 = bf16[8,256,512]{2,1,0:T(8,128)(2,1)} async-done(((bf16[8,256,512]{2,1,0:T(8,128)(2,1)}), bf16[8,256,512]{2,1,0:T(8,128)(2,1)}, u32[]{:S(2)}, u32[]{:S(2)}) %all-to-all-start.5) | async-done | bytes 2097184 | tf_op jit(solution)/shard_map/all_to_all | solution.py:86
  317.1 22.5 %all-to-all-start.6 = ((bf16[8,128,512]{2,1,0:T(8,128)(2,1)}), bf16[8,128,512]{2,1,0:T(8,128)(2,1)}, u32[]{:S(2)}, u32[]{:S(2)}) async-start(bf16[8,128,512]{2,1,0:T(8,128)(2,1)} %bitcast.254), calls=%async_computation.6 | async-start | bytes 2097152 | tf_op jit(solution)/shard_map/all_to_all | solution.py:86
  341.3 4.5 fusion.5
  347.1 8.4 %shard_map.513 = (bf16[4,512,256]{2,1,0:T(8,128)(2,1)}, f32[4,8,256]{2,1,0:T(8,128)S(1)}, f32[4,8,256]{2,1,0:T(8,128)S(1)}, f32[8,256]{1,0:T(8,128)S(1)}) custom-call(s32[6]{0:T(128)S(1)} %pad_add_fusion.scalars_ref, bf16[2,512,256]{2,1,0:T(8,128)(2,1)S(1)} %bitcast.236, bf16[2,512,256]{2,1,0:T(8,128)(2,1)S(1)} %bitcast.242, ...), custom_call_target="tpu_custom_call" | custom-call | bytes 18450000 | tf_op jit(solution)/shard_map/pallas_call | solution.py:480
  357.3 2.2 copy-done.3
  359.5 8.0 %shard_map.512 = bf16[2048,1024]{1,0:T(8,128)(2,1)} custom-call(s32[6]{0:T(128)S(1)} %pad_add_fusion.scalars_ref, bf16[1024,1024]{1,0:T(8,128)(2,1)S(1)} %add_convert_fusion.1.part_ref, bf16[1024,1024]{1,0:T(8,128)(2,1)} %collective-permute-done.8.got_ref, bf16[2048,1024]{1,0:T(8,128)(2,1)S(1)} %bitcast.227, f32[2048,1]{1,0:T(8,128)S(1)} %bitcast.235), custom_call_target="tpu_custom_call" | custom-call | bytes 29520000 | tf_op jit(solution)/shard_map/pallas_call | solution.py:590
  368.1 5.0 %fusion.18 = bf16[1024,256]{1,0:T(8,128)(2,1)} fusion(bf16[4,512,256]{2,1,0:T(8,128)(2,1)} %fusion.57, bf16[4,512,1024]{2,1,0:T(8,128)(2,1)} %param.30, f32[1024]{0:T(1024)S(1)} %copy-done.34, f32[4,512]{1,0:T(4,128)S(1)} %copy-done.84), kind=kOutput, calls=%fused_computation.63 | convolution fusion | flops 1082392576 | bytes 5779456 | tf_op jit(solution)/shard_map/btd,btc->dc/dot_general | solution.py:838
  373.1 7.3 %all-to-all-start.8 = ((bf16[8,128,256]{2,1,0:T(8,128)(2,1)}), bf16[8,128,256]{2,1,0:T(8,128)(2,1)S(1)}, u32[]{:S(2)}, u32[]{:S(2)}) async-start(bf16[8,128,256]{2,1,0:T(8,128)(2,1)} %bitcast.63), calls=%async_computation.8 | async-start | bytes 1048576 | tf_op jit(solution)/shard_map/all_to_all | solution.py:86
  380.4 2.8 fusion.95
  383.2 5.5 %multiply_subtract_fusion = (f32[1024,512]{1,0:T(8,128)}, f32[1024,512]{1,0:T(8,128)}, f32[1024,512]{1,0:T(8,128)}) fusion(f32[1024,512]{1,0:T(8,128)S(1)} %copy-done.46, bf16[4,256,512]{2,1,0:T(8,128)(2,1)S(1)} %get-tuple-element.148, f32[1024,512]{1,0:T(8,128)S(1)} %copy-done.47, f32[1024,512]{1,0:T(8,128)} %param.58), kind=kLoop, calls=%fused_computation.49 | loop fusion | flops 8388608 | bytes 13631488 | tf_op jit(solution)/shard_map/sub | solution.py:651
  390.2 4.0 collective-permute-done.7
  396.1 5.4 %all-to-all-start.7 = ((bf16[8,128,512]{1,2,0:T(8,128)(2,1)}), bf16[8,128,512]{1,2,0:T(8,128)(2,1)}, u32[]{:S(2)}, u32[]{:S(2)}) async-start(bf16[8,128,512]{1,2,0:T(8,128)(2,1)} %broadcast_in_dim.66), calls=%async_computation.7 | async-start | bytes 2097152 | tf_op jit(solution)/shard_map/all_to_all | solution.py:86
  401.5 3.2 add_convert_fusion.part_ref
  404.9 22.3 %all-to-all-done.7 = bf16[8,128,512]{1,2,0:T(8,128)(2,1)} async-done(((bf16[8,128,512]{1,2,0:T(8,128)(2,1)}), bf16[8,128,512]{1,2,0:T(8,128)(2,1)}, u32[]{:S(2)}, u32[]{:S(2)}) %all-to-all-start.7) | async-done | bytes 1048608 | tf_op jit(solution)/shard_map/all_to_all | solution.py:86
  428.1 4.1 all-to-all-start.9
  432.2 3.4 convolution_bitcast_fusion.2
  435.8 2.2 copy-done.4
  438.0 2.2 copy-done.14
  440.2 11.3 %shard_map.514 = (f32[2048,1024]{1,0:T(8,128)}, f32[1,1024]{1,0:T(1,128)S(1)}) custom-call(s32[6]{0:T(128)S(1)} %pad_add_fusion.scalars_ref, bf16[1024,1024]{1,0:T(8,128)(2,1)S(1)} %add_convert_fusion.part_ref, bf16[1024,1024]{1,0:T(8,128)(2,1)} %collective-permute-done.11.got_ref, bf16[2048,256]{1,0:T(8,128)(2,1)} %bitcast.65.bc_ref, ...), custom_call_target="tpu_custom_call" | custom-call | bytes 29520000 | tf_op jit(solution)/shard_map/pallas_call | solution.py:590
  451.5 1.9 collective-permute-start.12
  459.7 3.2 copy.198
  463.0 9.8 %shard_map.515 = (f32[1024,8,128]{2,1,0:T(8,128)}, f32[1024,8,128]{2,1,0:T(8,128)}, f32[1024,8,128]{2,1,0:T(8,128)}) custom-call(bf16[1024,8,128]{2,1,0:T(8,128)(2,1)S(1)} %bitcast.232, f32[1024,8,128]{2,1,0:T(8,128)S(1)} %bitcast.229, f32[1024,8,128]{2,1,0:T(8,128)S(1)} %bitcast.234, f32[1024,8,128]{2,1,0:T(8,128)} %bitcast.248), custom_call_target="tpu_custom_call" | custom-call | bytes 33210000 | tf_op jit(solution)/shard_map/pallas_call | solution.py:629
  473.0 2.5 collective-permute-start.14
  475.5 3.2 multiply_subtract_fusion.1
  (338 shorter events, 78.7 us)
Async XLA Ops:
  7.2 11.3 %copy-start.82 = (f32[4,512]{1,0:T(4,128)}, f32[4,512]{1,0:T(4,128)S(1)}, u32[]{:S(2)}) copy-start(f32[4,512]{1,0:T(4,128)S(1)} %add_rsqrt_fusion) | copy-start | bytes 24580
  7.3 10.6 %copy-start.64 = (f32[5,512]{1,0:T(8,128)S(1)}, f32[5,512]{1,0:T(8,128)}, u32[]{:S(2)}) copy-start(f32[5,512]{1,0:T(8,128)} %param.45) | copy-start | bytes 30724
  7.3 10.6 %copy-start.87 = (f32[3,8]{1,0:T(4,128)S(1)}, f32[3,8]{1,0:T(4,128)}, u32[]{:S(2)}) copy-start(f32[3,8]{1,0:T(4,128)} %param.51) | copy-start | bytes 292
  7.3 11.1 %copy-start.62 = (f32[1024,8]{0,1:T(8,128)S(1)}, f32[1024,8]{0,1:T(8,128)}, u32[]{:S(2)}) copy-start(f32[1024,8]{0,1:T(8,128)} %param.42) | copy-start | bytes 98308
  12.8 20.0 %collective-permute-start = (bf16[4,3,768]{2,1,0:T(4,128)(2,1)S(1)}, bf16[4,3,768]{2,1,0:T(4,128)(2,1)S(1)}, u32[]{:S(2)}, u32[]{:S(2)}) collective-permute-start(bf16[4,3,768]{2,1,0:T(4,128)(2,1)S(1)} %slice.326), channel_id=1, source_target_pairs={{0,4},{4,8},{8,12},{12,16},{16,20},{20,24},{24,28},{1,5},{5,9},{9,... | collective-permute-start | bytes 55304 | tf_op jit(solution)/shard_map/ppermute | solution.py:30
  18.6 10.8 %copy-start.66 = (f32[5,256]{1,0:T(8,128)S(1)}, f32[5,256]{1,0:T(8,128)}, u32[]{:S(2)}) copy-start(f32[5,256]{1,0:T(8,128)} %param.48) | copy-start | bytes 15364
  28.7 19.3 %copy-start.51 = (f32[4,512,8]{1,2,0:T(8,128)}, f32[4,512,8]{1,2,0:T(8,128)S(1)}, u32[]{:S(2)}) copy-start(f32[4,512,8]{1,2,0:T(8,128)S(1)} %convolution_bitcast_fusion.1) | copy-start | bytes 196612
  29.4 18.7 %copy-start.53 = (f32[5,768]{1,0:T(8,128)}, f32[5,768]{1,0:T(8,128)S(1)}, u32[]{:S(2)}) copy-start(f32[5,768]{1,0:T(8,128)S(1)} %constant_dynamic-update-slice_fusion) | copy-start | bytes 46084
  31.5 11.1 %copy-start.60 = (f32[8,512,1]{1,0,2:T(8,128)S(1)}, f32[8,512,1]{1,0,2:T(8,128)}, u32[]{:S(2)}) copy-start(f32[8,512,1]{1,0,2:T(8,128)} %reshape.791) | copy-start | bytes 49156
  32.8 9.8 %copy-start.42 = (f32[4,512,8]{2,1,0:T(8,128)S(1)}, f32[4,512,8]{2,1,0:T(8,128)}, u32[]{:S(2)}) copy-start(f32[4,512,8]{2,1,0:T(8,128)} %copy.175) | copy-start | bytes 196612
  48.6 33.8 %copy-start.93 = (f32[8]{0:T(128)S(1)}, f32[8]{0:T(128)}, u32[]{:S(2)}) copy-start(f32[8]{0:T(128)} %copy-done.92) | copy-start | bytes 100
  49.5 22.0 %all-to-all-start = ((bf16[8,80,512]{2,1,0:T(8,128)(2,1)}), bf16[8,80,512]{2,1,0:T(8,128)(2,1)}, u32[]{:S(2)}, u32[]{:S(2)}) async-start(bf16[8,80,512]{2,1,0:T(8,128)(2,1)} %pad_maximum_fusion.2), calls=%async_computation | async-start | bytes 1310720 | tf_op jit(solution)/shard_map/all_to_all | solution.py:86
  78.0 18.6 %all-to-all-start.1 = ((bf16[8,64,512]{2,1,0:T(8,128)(2,1)}), bf16[8,64,512]{2,1,0:T(8,128)(2,1)}, u32[]{:S(2)}, u32[]{:S(2)}) async-start(bf16[8,64,512]{2,1,0:T(8,128)(2,1)} %fusion.50), calls=%async_computation.1 | async-start | bytes 1048576 | tf_op jit(solution)/shard_map/all_to_all | solution.py:86
  87.5 26.4 %copy-start.101 = (f32[512]{0:T(512)}, f32[512]{0:T(512)S(1)}, u32[]{:S(2)}) copy-start(f32[512]{0:T(512)S(1)} %mul.770) | copy-start | bytes 6148
  88.3 31.8 %copy-start.85 = (f32[4,512]{1,0:T(4,128)}, f32[4,512]{1,0:T(4,128)S(1)}, u32[]{:S(2)}) copy-start(f32[4,512]{1,0:T(4,128)S(1)} %compare_convert_fusion) | copy-start | bytes 24580
  100.3 13.7 %copy-start.1 = (bf16[4,512,1024]{2,1,0:T(8,128)(2,1)S(1)}, bf16[4,512,1024]{2,1,0:T(8,128)(2,1)}, u32[]{:S(2)}) copy-start(bf16[4,512,1024]{2,1,0:T(8,128)(2,1)} %param.30) | copy-start | bytes 12582916
  100.3 13.7 %copy-start.40 = (bf16[1024,2,512]{2,0,1:T(8,128)(2,1)S(1)}, bf16[1024,2,512]{2,0,1:T(8,128)(2,1)}, u32[]{:S(2)}) copy-start(bf16[1024,2,512]{2,0,1:T(8,128)(2,1)} %copy-done.39) | copy-start | bytes 6291460
  100.3 13.7 %copy-start.83 = (f32[4,512]{1,0:T(4,128)S(1)}, f32[4,512]{1,0:T(4,128)}, u32[]{:S(2)}) copy-start(f32[4,512]{1,0:T(4,128)} %copy-done.82) | copy-start | bytes 24580
  138.8 10.5 %copy-start.80 = (f32[4,512]{1,0:T(4,128)}, f32[4,512]{1,0:T(4,128)S(1)}, u32[]{:S(2)}) copy-start(f32[4,512]{1,0:T(4,128)S(1)} %get-tuple-element.161) | copy-start | bytes 24580
  138.8 10.5 %copy-start.52 = (f32[4,512,8]{1,2,0:T(8,128)S(1)}, f32[4,512,8]{1,2,0:T(8,128)}, u32[]{:S(2)}) copy-start(f32[4,512,8]{1,2,0:T(8,128)} %copy-done.51) | copy-start | bytes 196612
  138.8 10.5 %copy-start.61 = (f32[8,512,1]{1,0,2:T(8,128)S(1)}, f32[8,512,1]{1,0,2:T(8,128)}, u32[]{:S(2)}) copy-start(f32[8,512,1]{1,0,2:T(8,128)} %reshape.791) | copy-start | bytes 49156
  153.2 9.8 %copy-start.81 = (f32[4,512]{1,0:T(4,128)S(1)}, f32[4,512]{1,0:T(4,128)}, u32[]{:S(2)}) copy-start(f32[4,512]{1,0:T(4,128)} %copy-done.80) | copy-start | bytes 24580
  153.2 9.8 %copy-start.86 = (f32[4,512]{1,0:T(4,128)S(1)}, f32[4,512]{1,0:T(4,128)}, u32[]{:S(2)}) copy-start(f32[4,512]{1,0:T(4,128)} %copy-done.85) | copy-start | bytes 24580
  153.2 9.8 %copy-start.97 = (f32[512]{0:T(512)S(1)}, f32[512]{0:T(512)}, u32[]{:S(2)}) copy-start(f32[512]{0:T(512)} %param.54) | copy-start | bytes 6148
  154.6 19.0 %all-to-all-start.2 = ((bf16[8,64,512]{2,1,0:T(8,128)(2,1)}), bf16[8,64,512]{2,1,0:T(8,128)(2,1)}, u32[]{:S(2)}, u32[]{:S(2)}) async-start(bf16[8,64,512]{2,1,0:T(8,128)(2,1)} %bitcast.252), calls=%async_computation.2 | async-start | bytes 1048576 | tf_op jit(solution)/shard_map/all_to_all | solution.py:86
  163.0 43.2 %collective-permute-start.1 = (bf16[1024,1024]{1,0:T(8,128)(2,1)}, bf16[1024,1024]{1,0:T(8,128)(2,1)}, u32[]{:S(2)}, u32[]{:S(2)}) collective-permute-start(bf16[1024,1024]{1,0:T(8,128)(2,1)} %dynamic-slice_bitcast_fusion.1), channel_id=1, source_target_pairs={{0,1},{1,0},{2,3},{3,2},{4,5},{5,4},{6,7},{7,6},{8,9},{9,8},{10,11... | collective-permute-start | bytes 6291464 | tf_op jit(solution)/shard_map/ppermute | solution.py:34
  182.1 17.5 %all-to-all-start.3 = ((bf16[8,64,512]{2,1,0:T(8,128)(2,1)}), bf16[8,64,512]{2,1,0:T(8,128)(2,1)}, u32[]{:S(2)}, u32[]{:S(2)}) async-start(bf16[8,64,512]{2,1,0:T(8,128)(2,1)} %constant_dynamic-update-slice_fusion.3), calls=%async_computation.3 | async-start | bytes 1048576 | tf_op jit(solution)/shard_map/all_to_all | solution.py:86
  201.8 57.3 %all-to-all-start.4 = ((bf16[8,256,512]{2,1,0:T(8,128)(2,1)}), bf16[8,256,512]{2,1,0:T(8,128)(2,1)}, u32[]{:S(2)}, u32[]{:S(2)}) async-start(bf16[8,256,512]{2,1,0:T(8,128)(2,1)} %bitcast.247), calls=%async_computation.4 | async-start | bytes 4194304 | tf_op jit(solution)/shard_map/all_to_all | solution.py:86
  210.8 48.3 %collective-permute-start.2 = (bf16[1024,1024]{1,0:T(8,128)(2,1)}, bf16[1024,1024]{1,0:T(8,128)(2,1)}, u32[]{:S(2)}, u32[]{:S(2)}) collective-permute-start(bf16[1024,1024]{1,0:T(8,128)(2,1)} %fusion.6), channel_id=1, source_target_pairs={{0,2},{1,3},{2,0},{3,1},{4,6},{5,7},{6,4},{7,5},{8,10},{9,11},{10,... | collective-permute-start | bytes 6291464 | tf_op jit(solution)/shard_map/ppermute | solution.py:34
  259.1 11.2 %copy-start.30 = (bf16[4,512,256]{2,1,0:T(8,128)(2,1)S(1)}, bf16[4,512,256]{2,1,0:T(8,128)(2,1)}, u32[]{:S(2)}) copy-start(bf16[4,512,256]{2,1,0:T(8,128)(2,1)} %copy-done.29) | copy-start | bytes 3145732
  261.8 24.7 %copy-start.19 = (bf16[1024,512]{1,0:T(8,128)(2,1)S(1)}, bf16[1024,512]{1,0:T(8,128)(2,1)}, u32[]{:S(2)}) copy-start(bf16[1024,512]{1,0:T(8,128)(2,1)} %get-tuple-element.149.z_weight_ref) | copy-start | bytes 3145732
  261.8 24.7 %copy-start.21 = (bf16[1024,512]{1,0:T(8,128)(2,1)S(1)}, bf16[1024,512]{1,0:T(8,128)(2,1)}, u32[]{:S(2)}) copy-start(bf16[1024,512]{1,0:T(8,128)(2,1)} %copy-done.20) | copy-start | bytes 3145732
  264.4 52.6 %all-to-all-start.5 = ((bf16[8,256,512]{2,1,0:T(8,128)(2,1)}), bf16[8,256,512]{2,1,0:T(8,128)(2,1)}, u32[]{:S(2)}, u32[]{:S(2)}) async-start(bf16[8,256,512]{2,1,0:T(8,128)(2,1)} %broadcast_in_dim.32), calls=%async_computation.5 | async-start | bytes 4194304 | tf_op jit(solution)/shard_map/all_to_all | solution.py:86
  270.3 16.2 %copy-start.25 = (bf16[4,512,512]{2,1,0:T(8,128)(2,1)S(1)}, bf16[4,512,512]{2,1,0:T(8,128)(2,1)}, u32[]{:S(2)}) copy-start(bf16[4,512,512]{2,1,0:T(8,128)(2,1)} %get-tuple-element.143) | copy-start | bytes 6291460
  270.4 2.0 collective-permute-start.4
  272.5 23.7 %copy-start.43 = (bf16[1024,256]{1,0:T(8,128)(2,1)}, bf16[1024,256]{1,0:T(8,128)(2,1)S(1)}, u32[]{:S(2)}) copy-start(bf16[1024,256]{1,0:T(8,128)(2,1)S(1)} %fusion.23) | copy-start | bytes 1572868
  272.5 14.0 %collective-permute-start.5 = (bf16[1024,256]{1,0:T(8,128)(2,1)S(1)}, bf16[1024,256]{1,0:T(8,128)(2,1)S(1)}, u32[]{:S(2)}, u32[]{:S(2)}) collective-permute-start(bf16[1024,256]{1,0:T(8,128)(2,1)S(1)} %fusion.23), channel_id=1, source_target_pairs={{0,2},{1,3},{2,0},{3,1},{4,6},{5,7},{6,4},{7,5},{8,10},{9,11},{10,... | collective-permute-start | bytes 1572872 | tf_op jit(solution)/shard_map/ppermute | solution.py:34
  274.9 7.5 %collective-permute-start.3 = (f32[4,3,512]{2,1,0:T(4,128)S(1)}, f32[4,3,512]{2,1,0:T(4,128)S(1)}, u32[]{:S(2)}, u32[]{:S(2)}) collective-permute-start(f32[4,3,512]{2,1,0:T(4,128)S(1)} %pad_maximum_fusion.3), channel_id=1, source_target_pairs={{4,0},{8,4},{12,8},{16,12},{20,16},{24,20},{28,24},{5,1},{9,5},{13... | collective-permute-start | bytes 73736 | tf_op jit(solution)/shard_map/ppermute | solution.py:30
  297.9 43.4 %collective-permute-start.6 = (bf16[1024,1024]{1,0:T(8,128)(2,1)}, bf16[1024,1024]{1,0:T(8,128)(2,1)}, u32[]{:S(2)}, u32[]{:S(2)}) collective-permute-start(bf16[1024,1024]{1,0:T(8,128)(2,1)} %dynamic-slice_bitcast_fusion), channel_id=1, source_target_pairs={{0,1},{1,0},{2,3},{3,2},{4,5},{5,4},{6,7},{7,6},{8,9},{9,8},{10,11... | collective-permute-start | bytes 6291464 | tf_op jit(solution)/shard_map/ppermute | solution.py:34
  301.6 55.7 %collective-permute-start.8 = (bf16[1024,1024]{1,0:T(8,128)(2,1)S(1)}, bf16[1024,1024]{1,0:T(8,128)(2,1)}, u32[]{:S(2)}, u32[]{:S(2)}) collective-permute-start(bf16[1024,1024]{1,0:T(8,128)(2,1)S(1)} %add_convert_fusion.1.part_ref), channel_id=1, source_target_pairs={{0,1},{1,0},{2,3},{3,2},{4,5},{5,4},{6,7},{7,6},{8,9},{9,8},{10,11... | collective-permute-start | bytes 6291464 | tf_op jit(solution)/shard_map/ppermute | solution.py:34
  305.7 35.1 %copy-start.55 = (f32[5,768]{1,0:T(8,128)S(1)}, f32[5,768]{1,0:T(8,128)}, u32[]{:S(2)}) copy-start(f32[5,768]{1,0:T(8,128)} %copy-done.53) | copy-start | bytes 46084
  305.7 35.2 %copy-start.67 = (f32[5,256]{1,0:T(8,128)S(1)}, f32[5,256]{1,0:T(8,128)}, u32[]{:S(2)}) copy-start(f32[5,256]{1,0:T(8,128)} %param.48) | copy-start | bytes 15364
  305.7 35.2 %copy-start.44 = (bf16[1024,256]{1,0:T(8,128)(2,1)S(1)}, bf16[1024,256]{1,0:T(8,128)(2,1)}, u32[]{:S(2)}) copy-start(bf16[1024,256]{1,0:T(8,128)(2,1)} %copy-done.43) | copy-start | bytes 1572868
  305.7 35.5 %copy-start.102 = (s32[4]{0:T(128)S(1)}, s32[4]{0:T(128)}, u32[]{:S(2)}) copy-start(s32[4]{0:T(128)} %param.32) | copy-start | bytes 52
  305.8 35.5 %copy-start.59 = (bf16[4,3,768]{2,1,0:T(4,128)(2,1)S(1)}, bf16[4,3,768]{2,1,0:T(4,128)(2,1)}, u32[]{:S(2)}) copy-start(bf16[4,3,768]{2,1,0:T(4,128)(2,1)} %copy-done.57) | copy-start | bytes 55300
  317.1 51.0 %all-to-all-start.6 = ((bf16[8,128,512]{2,1,0:T(8,128)(2,1)}), bf16[8,128,512]{2,1,0:T(8,128)(2,1)}, u32[]{:S(2)}, u32[]{:S(2)}) async-start(bf16[8,128,512]{2,1,0:T(8,128)(2,1)} %bitcast.254), calls=%async_computation.6 | async-start | bytes 2097152 | tf_op jit(solution)/shard_map/all_to_all | solution.py:86
  341.1 6.1 %collective-permute-start.9 = (bf16[1024,256]{1,0:T(8,128)(2,1)S(1)}, bf16[1024,256]{1,0:T(8,128)(2,1)S(1)}, u32[]{:S(2)}, u32[]{:S(2)}) collective-permute-start(bf16[1024,256]{1,0:T(8,128)(2,1)S(1)} %add_convert_fusion.2), channel_id=1, source_target_pairs={{0,1},{1,0},{2,3},{3,2},{4,5},{5,4},{6,7},{7,6},{8,9},{9,8},{10,11... | collective-permute-start | bytes 1572872 | tf_op jit(solution)/shard_map/ppermute | solution.py:34
  341.3 15.6 %copy-start.70 = (f32[1,1,4,512]{3,2,1,0:T(4,128)S(1)}, f32[1,1,4,512]{3,2,1,0:T(4,128)}, u32[]{:S(2)}) copy-start(f32[1,1,4,512]{3,2,1,0:T(4,128)} %get-tuple-element.160) | copy-start | bytes 24580
  345.8 48.3 %collective-permute-start.7 = (bf16[1024,1024]{1,0:T(8,128)(2,1)}, bf16[1024,1024]{1,0:T(8,128)(2,1)}, u32[]{:S(2)}, u32[]{:S(2)}) collective-permute-start(bf16[1024,1024]{1,0:T(8,128)(2,1)} %fusion.5), channel_id=1, source_target_pairs={{0,2},{1,3},{2,0},{3,1},{4,6},{5,7},{6,4},{7,5},{8,10},{9,11},{10,... | collective-permute-start | bytes 6291464 | tf_op jit(solution)/shard_map/ppermute | solution.py:34
  355.6 11.9 %collective-permute-start.10 = (f32[4,3,256]{2,1,0:T(4,128)S(1)}, f32[4,3,256]{2,1,0:T(4,128)S(1)}, u32[]{:S(2)}, u32[]{:S(2)}) collective-permute-start(f32[4,3,256]{2,1,0:T(4,128)S(1)} %pad_maximum_fusion.5), channel_id=1, source_target_pairs={{4,0},{8,4},{12,8},{16,12},{20,16},{24,20},{28,24},{5,1},{9,5},{13... | collective-permute-start | bytes 36872 | tf_op jit(solution)/shard_map/ppermute | solution.py:30
  373.1 10.1 %copy-start.46 = (f32[1024,512]{1,0:T(8,128)S(1)}, f32[1024,512]{1,0:T(8,128)}, u32[]{:S(2)}) copy-start(f32[1024,512]{1,0:T(8,128)} %param.57) | copy-start | bytes 6291460
  373.1 21.8 %all-to-all-start.8 = ((bf16[8,128,256]{2,1,0:T(8,128)(2,1)}), bf16[8,128,256]{2,1,0:T(8,128)(2,1)S(1)}, u32[]{:S(2)}, u32[]{:S(2)}) async-start(bf16[8,128,256]{2,1,0:T(8,128)(2,1)} %bitcast.63), calls=%async_computation.8 | async-start | bytes 1048576 | tf_op jit(solution)/shard_map/all_to_all | solution.py:86
  396.1 31.2 %all-to-all-start.7 = ((bf16[8,128,512]{1,2,0:T(8,128)(2,1)}), bf16[8,128,512]{1,2,0:T(8,128)(2,1)}, u32[]{:S(2)}, u32[]{:S(2)}) async-start(bf16[8,128,512]{1,2,0:T(8,128)(2,1)} %broadcast_in_dim.66), calls=%async_computation.7 | async-start | bytes 2097152 | tf_op jit(solution)/shard_map/all_to_all | solution.py:86
  401.5 30.7 %copy-start.33 = (bf16[4,512,8]{2,1,0:T(8,128)(2,1)S(1)}, bf16[4,512,8]{2,1,0:T(8,128)(2,1)}, u32[]{:S(2)}) copy-start(bf16[4,512,8]{2,1,0:T(8,128)(2,1)} %copy-done.31) | copy-start | bytes 98308
  404.8 31.0 %collective-permute-start.11 = (bf16[1024,1024]{1,0:T(8,128)(2,1)S(1)}, bf16[1024,1024]{1,0:T(8,128)(2,1)}, u32[]{:S(2)}, u32[]{:S(2)}) collective-permute-start(bf16[1024,1024]{1,0:T(8,128)(2,1)S(1)} %add_convert_fusion.part_ref), channel_id=1, source_target_pairs={{0,1},{1,0},{2,3},{3,2},{4,5},{5,4},{6,7},{7,6},{8,9},{9,8},{10,11... | collective-permute-start | bytes 6291464 | tf_op jit(solution)/shard_map/ppermute | solution.py:34
  428.1 47.4 %all-to-all-start.9 = ((bf16[8,128,256]{2,1,0:T(8,128)(2,1)}), bf16[8,128,256]{2,1,0:T(8,128)(2,1)}, u32[]{:S(2)}, u32[]{:S(2)}) async-start(bf16[8,128,256]{2,1,0:T(8,128)(2,1)} %broadcast_in_dim.67), calls=%async_computation.9 | async-start | bytes 1048576 | tf_op jit(solution)/shard_map/all_to_all | solution.py:86
  440.2 11.3 %copy-start.91 = (f32[512]{0:T(512)S(1)}, f32[512]{0:T(512)}, u32[]{:S(2)}) copy-start(f32[512]{0:T(512)} %get-tuple-element.144) | copy-start | bytes 6148
  451.5 5.0 %collective-permute-start.12 = (f32[112,128]{1,0:T(8,128)S(1)}, f32[112,128]{1,0:T(8,128)S(1)}, u32[]{:S(2)}, u32[]{:S(2)}) collective-permute-start(f32[112,128]{1,0:T(8,128)S(1)} %pad_bitcast_fusion), channel_id=1, source_target_pairs={{0,4},{4,0},{8,12},{12,8},{16,20},{20,16},{24,28},{28,24},{1,5},{5... | collective-permute-start | bytes 172040 | tf_op jit(solution)/shard_map/ppermute | solution.py:34
  456.6 16.2 %collective-permute-start.13 = (f32[112,128]{1,0:T(8,128)S(1)}, f32[112,128]{1,0:T(8,128)S(1)}, u32[]{:S(2)}, u32[]{:S(2)}) collective-permute-start(f32[112,128]{1,0:T(8,128)S(1)} %fusion.74), channel_id=1, source_target_pairs={{0,8},{4,12},{8,0},{12,4},{16,24},{20,28},{24,16},{28,20},{1,9},{5... | collective-permute-start | bytes 172040 | tf_op jit(solution)/shard_map/ppermute | solution.py:34
  462.9 12.5 %copy-start.41 = (f32[1024,256]{1,0:T(8,128)S(1)}, f32[1024,256]{1,0:T(8,128)}, u32[]{:S(2)}) copy-start(f32[1024,256]{1,0:T(8,128)} %param.39) | copy-start | bytes 3145732
  462.9 12.5 %copy-start.48 = (f32[1024,256]{1,0:T(8,128)S(1)}, f32[1024,256]{1,0:T(8,128)}, u32[]{:S(2)}) copy-start(f32[1024,256]{1,0:T(8,128)} %param.41) | copy-start | bytes 3145732
  463.0 12.5 %copy-start.49 = (f32[1024,256]{1,0:T(8,128)S(1)}, f32[1024,256]{1,0:T(8,128)}, u32[]{:S(2)}) copy-start(f32[1024,256]{1,0:T(8,128)} %param.40) | copy-start | bytes 3145732
  473.0 9.6 %copy-start.98 = (f32[512]{0:T(512)S(1)}, f32[512]{0:T(512)}, u32[]{:S(2)}) copy-start(f32[512]{0:T(512)} %param.54) | copy-start | bytes 6148
  473.0 5.7 %collective-permute-start.14 = (f32[112,128]{1,0:T(8,128)S(1)}, f32[112,128]{1,0:T(8,128)S(1)}, u32[]{:S(2)}, u32[]{:S(2)}) collective-permute-start(f32[112,128]{1,0:T(8,128)S(1)} %fusion.109), channel_id=1, source_target_pairs={{0,16},{4,20},{8,24},{12,28},{16,0},{20,4},{24,8},{28,12},{1,17},{... | collective-permute-start | bytes 172040 | tf_op jit(solution)/shard_map/ppermute | solution.py:34
  (64 other events, 283.9 us)

commit v5 on v4

--- a/solution.py
+++ b/solution.py
@@ -90,22 +90,14 @@
     return state.astype(BF16).reshape(count, -1, state.shape[-1])
 
 
-def states_before(state, decay, axis):
+def states_before(packed, height, axis):
     size = lax.axis_size(axis)
-    blocks = to_blocks(state, size)
-    height = blocks.shape[1]
-    high = decay.astype(BF16)
-    low = (decay - high.astype(F32)).astype(BF16)
-    empty = jnp.zeros((decay.shape[0], 14, decay.shape[2]), BF16)
-    extra = jnp.concatenate([high, low, empty], axis=1)
-    extra = jnp.repeat(extra, size // decay.shape[0], axis=0)
-    got = exchanged(jnp.concatenate([blocks, extra], axis=1), axis).astype(F32)
+    got = exchanged(packed, axis).astype(F32)
     decays = got[:, height : height + 1] + got[:, height + 1 : height + 2]
     entering = [jnp.zeros(got[0, :height].shape, F32)]
     for k in range(size - 1):
         entering.append(decays[k] * entering[-1] + got[k, :height])
-    back = exchanged(jnp.stack(entering).astype(BF16), axis)
-    return back.reshape(state.shape).astype(F32), decays
+    return exchanged(jnp.stack(entering).astype(BF16), axis), decays
 
 
 def states_after(state, decays, axis):
@@ -114,8 +106,7 @@
     leaving = [jnp.zeros(got[0].shape, F32)]
     for k in range(size - 1, 0, -1):
         leaving.append(decays[k] * leaving[-1] + got[k])
-    back = exchanged(jnp.stack(leaving[::-1]).astype(BF16), axis)
-    return back.reshape(state.shape).astype(F32)
+    return exchanged(jnp.stack(leaving[::-1]).astype(BF16), axis)
 
 
 def lane_tiles(a):
@@ -160,26 +151,26 @@
     return jnp.concatenate([jnp.where(first, a, zero), jnp.where(first, zero, a)], axis=0)
 
 
-def chunk_decays(decay, decay_t):
+def chunk_decays(decay):
     q = decay.shape[0]
     row = lax.broadcasted_iota(jnp.int32, (q, q), 0)
     column = lax.broadcasted_iota(jnp.int32, (q, q), 1)
     lower = jnp.where(row >= column, 1.0, 0.0).astype(F32)
     cum = dot(lower, decay, precision=HIGHEST_PREC)
-    cum_t = dot(decay_t, lower, ((1,), (1,)), precision=HIGHEST_PREC)
+    cum_t = dot(decay, lower, ((0,), (1,)), precision=HIGHEST_PREC)
     return cum, cum_t, row, column
 
 
-def scan_kernel(x_ref, b_ref, c_ref, step_ref, decay_ref, decay_t_ref, enter_ref, y_ref, in_ref, state):
+def scan_kernel(x_ref, b_ref, c_ref, step_ref, decay_ref, enter_ref, y_ref, in_ref, state):
     heads = step_ref.shape[2]
     width = x_ref.shape[2] // heads
 
     @pl.when(pl.program_id(1) == 0)
     def _():
-        state[...] = enter_ref[0]
+        state[...] = enter_ref[0].astype(F32)
 
     expand = expander(heads, width)
-    cum, cum_t, row, column = chunk_decays(decay_ref[0], decay_t_ref[0])
+    cum, cum_t, row, column = chunk_decays(decay_ref[0])
     causal = row >= column
     q = cum.shape[0]
     total = cum[q - 1 : q, :]
@@ -206,8 +197,7 @@
 
 def conv_back_step(act_grad, mixed, previous, taps, after_ref):
     q = mixed.shape[0]
-    window = jnp.concatenate([previous, mixed], axis=0)
-    shifted = [window[8 - CONV + 1 + k : 8 - CONV + 1 + k + q] for k in range(CONV)]
+    shifted = conv_windows(mixed, previous)
     convolved = taps[CONV : CONV + 1]
     for k in range(CONV):
         convolved = convolved + taps[k : k + 1] * shifted[k]
@@ -229,7 +219,7 @@
 
 
 def back_kernel(
-    x_ref, b_ref, c_ref, step_ref, decay_ref, decay_t_ref, skip_ref, dy_ref, y_ref, in_ref, leave_ref,
+    x_ref, b_ref, c_ref, step_ref, decay_ref, skip_ref, dy_ref, y_ref, in_ref, leave_ref,
     mixed_ref, previous_ref, edge_ref, taps_ref, slope_ref, rate_ref,
     mixed_grad_ref, dbc_ref, pre_ref, first_ref, last_ref, tap_sums_ref, head_sums_ref,
     grad, after
@@ -250,10 +240,10 @@
 
     @pl.when(pl.program_id(1) == 0)
     def _():
-        grad[...] = leave_ref[0]
+        grad[...] = leave_ref[0].astype(F32)
 
     expand = expander(heads, width)
-    cum, cum_t, row, column = chunk_decays(decay_ref[0], decay_t_ref[0])
+    cum, cum_t, row, column = chunk_decays(decay_ref[0])
     later = column >= row
     q = cum.shape[0]
     total = cum[q - 1 : q, :]
@@ -337,7 +327,88 @@
     return [part(inner, 0), part(state, inner // state), part(state, inner // state + 1)]
 
 
-def scan_forward(activated, step, decay, decay_t, enter):
+def conv_windows(mixed, previous):
+    q = mixed.shape[0]
+    window = jnp.concatenate([previous, mixed], axis=0)
+    return [window[8 - CONV + 1 + k : 8 - CONV + 1 + k + q] for k in range(CONV)]
+
+
+def first_kernel(
+    mixed_ref, previous_ref, edge_ref, taps_ref, step_ref, decay_ref, act_ref, packed_ref, state, total
+):
+    chunk = pl.program_id(1)
+
+    @pl.when(chunk == 0)
+    def _():
+        state[...] = jnp.zeros_like(state)
+        total[...] = jnp.zeros_like(total)
+
+    previous = jnp.where(
+        chunk == 0, edge_ref[0].astype(F32), previous_ref[0].astype(F32)
+    )[8:]
+    convolved = taps_ref[CONV : CONV + 1]
+    for k, part in enumerate(conv_windows(mixed_ref[0].astype(F32), previous)):
+        convolved = convolved + taps_ref[k : k + 1] * part
+    activated = jax.nn.silu(convolved).astype(BF16)
+    act_ref[0] = activated
+    heads, (state_width, inner) = step_ref.shape[2], state.shape
+    expand = expander(heads, inner // heads)
+    cum = chunk_decays(decay_ref[0])[0]
+    q = cum.shape[0]
+    last = cum[q - 1 : q, :]
+    weights = spread(step_ref[0] * jnp.exp(last - cum), expand)
+    xw = (activated[:, :inner].astype(F32) * weights).astype(BF16)
+    b = activated[:, inner : inner + state_width]
+    kept = spread(jnp.exp(cum), expand)[q - 1 : q]
+    state[...] = kept * state[...] + dot(b, xw, ((0,), (0,)))
+    total[...] = total[...] + last
+
+    @pl.when(chunk == pl.num_programs(1) - 1)
+    def _():
+        decay = spread(jnp.exp(jnp.broadcast_to(total[...], (8, heads))), expand)[:1]
+        high = decay.astype(BF16).astype(F32)
+        tail = jnp.concatenate([high, decay - high, jnp.zeros((14, inner), F32)], axis=0)
+        height = packed_ref.shape[2] - 16
+        for part in range(packed_ref.shape[1]):
+            rows = state[part * height : (part + 1) * height]
+            packed_ref[0, part] = jnp.concatenate([rows, tail], axis=0).astype(BF16)
+
+
+def conv_forward(mixed, edge, taps, step, decay, state, parts):
+    seqs, length, lanes = mixed.shape
+    heads, inner = step.shape[2], lanes - 2 * state
+    chunks, tall = length // CHUNK, CHUNK // 16
+    height = state // parts + 16
+
+    def block(width):
+        return pl.BlockSpec((1, CHUNK, width), lambda s, k: (s, k, 0))
+
+    return pl.pallas_call(
+        first_kernel,
+        grid=(seqs, chunks),
+        in_specs=[
+            block(lanes),
+            pl.BlockSpec((1, 16, lanes), lambda s, k: (s, jnp.maximum(k * tall - 1, 0), 0)),
+            pl.BlockSpec((1, 16, lanes), lambda s, k: (s, 0, 0)),
+            pl.BlockSpec((8, lanes), lambda s, k: (0, 0)),
+            block(heads),
+            block(heads),
+        ],
+        out_specs=[
+            block(lanes),
+            pl.BlockSpec((1, parts, height, inner), lambda s, k: (s, 0, 0, 0)),
+        ],
+        out_shape=[
+            jax.ShapeDtypeStruct(mixed.shape, BF16),
+            jax.ShapeDtypeStruct((seqs, parts, height, inner), BF16),
+        ],
+        scratch_shapes=[pltpu.VMEM((state, inner), F32), pltpu.VMEM((1, heads), F32)],
+        compiler_params=pltpu.CompilerParams(vmem_limit_bytes=40 << 20),
+        cost_estimate=load(9),
+    )(mixed, mixed, edge, taps, step, decay)
+
+
+def scan_forward(activated, step, decay, enter):
     seqs, length, heads = step.shape
     state, inner = enter.shape[1:]
     chunks = length // CHUNK
@@ -352,7 +423,6 @@
         + [
             block(heads),
             block(heads),
-            pl.BlockSpec((1, heads, CHUNK), lambda s, k: (s, 0, k)),
             pl.BlockSpec((1, state, inner), lambda s, k: (s, 0, 0)),
         ],
         out_specs=[
@@ -366,7 +436,7 @@
         scratch_shapes=[pltpu.VMEM((state, inner), F32)],
         compiler_params=pltpu.CompilerParams(vmem_limit_bytes=40 << 20),
         cost_estimate=load(13),
-    )(activated, activated, activated, step, decay, decay_t, enter)
+    )(activated, activated, activated, step, decay, enter)
 
 
 def conv_blocks(chunks, lanes, at):
@@ -398,7 +468,7 @@
 
 
 def scan_backward(
-    activated, step, decay, decay_t, skip, dy, y, states, leave, mixed, edge, taps, slope, rate
+    activated, step, decay, skip, dy, y, states, leave, mixed, edge, taps, slope, rate
 ):
     seqs, length, heads = step.shape
     state, inner = leave.shape[1:]
@@ -415,7 +485,6 @@
         + [
             block(heads),
             block(heads),
-            pl.BlockSpec((1, heads, CHUNK), lambda s, k: (s, 0, chunks - 1 - k)),
             pl.BlockSpec((1, 1, inner), lambda s, k: (0, 0, 0)),
             block(inner),
             block(inner),
@@ -438,7 +507,7 @@
         compiler_params=pltpu.CompilerParams(vmem_limit_bytes=40 << 20),
         cost_estimate=load(30),
     )(
-        activated, activated, activated, step, decay, decay_t, skip, dy, y, states, leave,
+        activated, activated, activated, step, decay, skip, dy, y, states, leave,
         mixed, mixed, edge, taps, slope, rate
     )
 
@@ -714,33 +783,26 @@
     edge_in = passed_along(mixed_in[:, local_len - CONV + 1 :], "seq", 1)
     raw_step = jnp.einsum("btd,dh->bth", normed, step_weight, preferred_element_type=F32)
     gate_input = jnp.einsum("btd,dc->btc", normed, z_weight, preferred_element_type=F32)
-    padded = jnp.concatenate([edge_in, mixed_in], axis=1)
     conv_weight = jnp.concatenate([conv_inner, conv_bc], axis=-1)
-    convolved = conv_weight[CONV] + jnp.zeros(mixed_in.shape, F32)
-    for tap_index in range(CONV):
-        convolved = (
-            convolved + conv_weight[tap_index] * padded[:, tap_index : tap_index + local_len]
-        )
-    activated = jax.nn.silu(convolved).astype(BF16)
-    x_values = activated[..., :local_inner]
-    b_values = activated[..., local_inner : local_inner + state_width]
-    c_values = activated[..., local_inner + state_width :]
+    taps = jnp.pad(conv_weight, ((0, 8 - CONV - 1), (0, 0)))
+    edge_rows = jnp.pad(edge_in, ((0, 0), (16 - CONV + 1, 0), (0, 0)))
     decay_log, step_bias, skip_gain = head_params[0], head_params[1], head_params[2]
     step_size = jax.nn.softplus(raw_step + step_bias)
     log_decay = -step_size * jnp.exp(decay_log)
+    parts = seq_size // seq_count
+    activated, packed = conv_forward(
+        mixed_in, edge_rows, taps, step_size, log_decay, state_width, parts
+    )
+    entering, block_decays = states_before(
+        packed.reshape((seq_size,) + packed.shape[2:]), state_width // parts, "seq"
+    )
+    entering = entering.reshape(seq_count, state_width, local_inner)
+    x_values = activated[..., :local_inner]
+    c_values = activated[..., local_inner + state_width :]
     earlier = jnp.tril(jnp.ones((local_len, local_len), F32))
     running = jnp.einsum("ts,bsh->bth", earlier, log_decay, precision=HIGHEST_PREC)
-    device_decay = running[:, -1]
-    decay_t = log_decay.transpose(0, 2, 1)
-
-    weighted = x_values.astype(F32) * wide(jnp.exp(device_decay[:, None] - running) * step_size)
-    local_state = jnp.einsum(
-        "btn,btc->bnc", b_values, weighted.astype(BF16), preferred_element_type=F32
-    )
-    unit_decay = wide(jnp.exp(device_decay))[:, None]
-    entering, block_decays = states_before(local_state, unit_decay, "seq")
-
-    scanned_raw, states = scan_forward(activated, step_size, log_decay, decay_t, entering)
+
+    scanned_raw, states = scan_forward(activated, step_size, log_decay, entering)
     skip_wide = jnp.repeat(skip_gain, head_width)[None, None]
     scanned = scanned_raw + skip_wide * x_values.astype(F32)
     gate_act = jax.nn.silu(gate_input)
@@ -767,20 +829,18 @@
         preferred_element_type=F32,
     )
     leaving = states_after(local_back, block_decays, "seq")
+    projected = halved(partial_out.astype(BF16).reshape(rows, model_width), "head")
+    leaving, projected = lax.optimization_barrier((leaving, projected))
+    leaving = leaving.reshape(local_back.shape)
     z_weight_grad = jnp.einsum("btd,btc->dc", normed, gate_grad, preferred_element_type=F32)
     early_grads = jnp.concatenate([out_weight_grad, z_weight_grad], axis=0).astype(BF16)
     early_grads, _ = lax.optimization_barrier((early_grads, leaving))
     early_parts = exchanged(to_blocks(early_grads, seq_size), "seq")
-    projected = halved(partial_out.astype(BF16).reshape(rows, model_width), "head")
-    scanned_grad, projected = lax.optimization_barrier((scanned_grad, projected))
     projected_far = swapped(projected, "head", axis_masks("head")[-1])
-    taps = jnp.pad(conv_weight, ((0, 8 - CONV - 1), (0, 0)))
-    edge_rows = jnp.pad(edge_in, ((0, 0), (16 - CONV + 1, 0), (0, 0)))
     x_raw, bc_grad, step_in_grad, x_first, x_last, x_tap_sums, head_totals = scan_backward(
         activated,
         step_size,
         log_decay,
-        decay_t,
         skip_wide,
         scanned_grad,
         scanned_raw,
@@ -797,13 +857,11 @@
     )
     projected_half, projected_other = regathered(added(projected, projected_far), "head")
     early_own = jnp.sum(early_parts.astype(F32), axis=0).astype(BF16)
-    early_all = exchanged(jnp.broadcast_to(early_own[None], early_parts.shape), "seq")
+    early_all = lax.all_gather(early_own, "seq")
     bc_sum = halved(bc_grad.reshape(rows, 2 * state_width), "head")
+    x_in_grad = joined_edges(x_raw, x_first, x_last, conv_weight[:, :local_inner])
+    x_in_grad, bc_sum = lax.optimization_barrier((x_in_grad, bc_sum))
     bc_far = swapped(bc_sum, "head", axis_masks("head")[-1])
-
-    x_in_grad = joined_edges(x_raw, x_first, x_last, conv_weight[:, :local_inner])
-    x_in_grad, bc_far = lax.optimization_barrier((x_in_grad, bc_far))
-    bc_half, bc_other = regathered(added(bc_sum, bc_far), "head")
     normed_partial = normed_products(
         gate_grad.reshape(rows, local_inner),
         x_in_grad.reshape(rows, local_inner),
@@ -813,8 +871,12 @@
         step_weight,
     )
     x_weight_grad = jnp.einsum("btd,btc->dc", normed, x_in_grad, preferred_element_type=F32)
-    x_parts = exchanged(to_blocks(x_weight_grad, seq_size), "seq")
     normed_sum = halved(normed_partial, "head")
+    bc_added = added(bc_sum, bc_far)
+    normed_sum, bc_added = lax.optimization_barrier((normed_sum, bc_added))
+    bc_half, bc_other = regathered(bc_added, "head")
+    x_blocks, _ = lax.optimization_barrier((to_blocks(x_weight_grad, seq_size), normed_sum))
+    x_parts = exchanged(x_blocks, "seq")
     normed_far = swapped(normed_sum, "head", axis_masks("head")[-1])
 
     scalars = jnp.concatenate(
@@ -833,7 +895,7 @@
     bc_in_grad = joined_edges(bc_raw_grad, bc_first, bc_last, conv_weight[:, local_inner:])
     bc_in_grad, x_parts = lax.optimization_barrier((bc_in_grad, x_parts))
     x_own = jnp.sum(x_parts.astype(F32), axis=0).astype(BF16)
-    x_all = exchanged(jnp.broadcast_to(x_own[None], x_parts.shape), "seq")
+    x_all = lax.all_gather(x_own, "seq")
     x_sum = x_all.reshape(model_width, local_inner)
     bc_weight_grad = jnp.einsum("btd,btc->dc", normed, bc_in_grad, preferred_element_type=F32)
     bc_blocks = to_blocks(bc_weight_grad, seq_size)
@@ -889,7 +951,7 @@
     )
     input_grad = input_grad.reshape(inputs.shape)
     bc_own = jnp.sum(bc_parts.astype(F32), axis=0).astype(BF16)
-    bc_all = exchanged(jnp.broadcast_to(bc_own[None], bc_parts.shape), "seq")
+    bc_all = lax.all_gather(bc_own, "seq")
     step_weight_grad = jnp.einsum("btd,bth->hd", normed, step_in_grad, preferred_element_type=F32)
     conv_inner_grad = x_tap_sums[: CONV + 1]
     conv_bc_grad = bc_tap_sums[: CONV + 1]

time: 489 us -> 463 us (0.947)
  starting transfers between devices: 86.2 us -> 50.6 us
  blocking collectives: 10.1 us -> 42.6 us
  waiting for transfers between devices: 85.6 us -> 53.5 us
  Pallas kernels: 94.5 us -> 113 us
  other arithmetic: 72.5 us -> 56.1 us
  between operations: 2.32 us -> 15.6 us
  matrix products: 71 us -> 63.9 us
    all_to_all x10 -> x7, waiting for transfers between devices: 70.2 us -> 32.9 us  [exchanged(): return lax.all_to_all(blocks, axis, 0, 0, tiled=True)]
    all_to_all x10 -> x7, starting transfers between devices: 68.1 us -> 35.8 us  [exchanged(): return lax.all_to_all(blocks, axis, 0, 0, tiled=True)]
    all_gather x0 -> x1, blocking collectives: none -> 31.9 us  [shards(): bc_all = lax.all_gather(bc_own, 'seq')]
    pallas_call x0 -> x1, Pallas kernels: none -> 15.4 us  [conv_forward(): pl.pallas_call(first_kernel, grid=(seqs, chunks), in_specs=[block(lanes),...]
    convert_element_type x4 -> x1, other arithmetic: 13.8 us -> 1.25 us  [states_before(): got = exchanged(packed, axis).astype(F32)]
    ppermute x12, waiting for transfers between devices: 9.43 us -> 20.1 us  [swapped(): lax.ppermute(block, axis, [(i, i ^ mask) for i in range(lax.axis_size(axi...]
    ppermute x3, waiting for transfers between devices: 6.04 us -> 0.4 us  [passed_along(): return lax.ppermute(block, axis, route)]
    dot_general x3 -> x1, matrix products: 9.51 us -> 3.9 us  [wide(): return jnp.einsum('...h,hc->...c', a, selector, precision=HIGHEST_PREC)]
  transfers between devices with their start and end apart: 25 -> 24, of which waited for: 12 -> 8; matrix products, arithmetic and copies ran while one was open for 21% -> 21% of each run, Pallas kernels for 17% -> 18%
where the time goes in v5:
time: 463 us; the launch traced here: 454 us
  Pallas kernels  113 us (24%)
  matrix products  63.9 us (14%)
  local copies, waits for them, and re-layouts  59 us (13%)
  other arithmetic  56.1 us (12%)
  waiting for transfers between devices  53.5 us (12%)
  starting transfers between devices  50.6 us (11%)
  blocking collectives  42.6 us (9%)
  between operations  15.6 us (3%)
    unnamed x215, local copies, waits for them, and re-layouts  37.8 us
    pallas_call x1, Pallas kernels, scan_backward(): pl.pallas_call(back_kernel, grid=(seqs, chunks), in_specs=act_blocks(inne...  36.1 us
    all_to_all x7, starting transfers between devices, exchanged(): return lax.all_to_all(blocks, axis, 0, 0, tiled=True)  35.8 us
    all_to_all x7, waiting for transfers between devices, exchanged(): return lax.all_to_all(blocks, axis, 0, 0, tiled=True)  32.9 us
    all_gather x1, blocking collectives, shards(): bc_all = lax.all_gather(bc_own, 'seq')  31.9 us
    ppermute x12, waiting for transfers between devices, swapped(): lax.ppermute(block, axis, [(i, i ^ mask) for i in range(lax.axis_size(axi...  20.1 us
    pallas_call x2, Pallas kernels, merge_call(): pl.pallas_call(kernel, grid_spec=pltpu.PrefetchScalarGridSpec(num_scalar_...  19.1 us
    pallas_call x1, Pallas kernels, conv_forward(): pl.pallas_call(first_kernel, grid=(seqs, chunks), in_specs=[block(lanes),...  15.4 us
  transfers between devices with their start and end apart: 24, of which 8 were waited for; matrix products, arithmetic and copies ran while one was open for 21% of the time, Pallas kernels for 18%

profile of v5, /device:TPU:0, one launch (start us, length us, event | category | flops | bytes accessed | tf_op | source)
XLA Modules:
  0.0 454.1 jit_solution(10097870532935056805)
XLA Ops:
  7.2 3.2 fusion
  13.8 2.0 copy-done.3
  15.7 3.7 convolution_convert_fusion.mixed_ref.previous_ref
  19.5 1.7 copy-done
  21.2 4.9 %collective-permute-start = (bf16[4,3,768]{2,1,0:T(4,128)(2,1)S(1)}, bf16[4,3,768]{2,1,0:T(4,128)(2,1)S(1)}, u32[]{:S(2)}, u32[]{:S(2)}) collective-permute-start(bf16[4,3,768]{2,1,0:T(4,128)(2,1)S(1)} %slice.284), channel_id=1, source_target_pairs={{0,4},{4,8},{8,12},{12,16},{16,20},{20,24},{24,28},{1,5},{5,9},{9,... | collective-permute-start | bytes 55304 | tf_op jit(solution)/shard_map/ppermute | solution.py:30
  26.8 5.6 %add_divide_fusion.1 = (f32[4,512,8]{2,1,0:T(8,128)}, f32[4,512,8]{2,1,0:T(8,128)S(1)}, f32[4,512,8]{2,1,0:T(8,128)S(1)}, f32[4,512,8]{2,1,0:T(8,128)}) fusion(f32[8]{0:T(128)S(1)} %get-tuple-element.180, f32[8]{0:T(128)S(1)} %get-tuple-element.181, bf16[1024,8]{1,0:T(8,128)(2,1)S(1)} %copy.113.step_weight_ref, bf16[4,512,1024]{2,1,0:T(8,128)(2,1)} %param.30, ...), kind=kOutput, calls=%fused_computation.71 | convolution fusion | flops 42139648 | bytes 4485184 | tf_op jit(solution)/shard_map/btd,dh->bth/dot_general | solution.py:784
  33.2 15.4 %shard_map.509 = (bf16[4,512,768]{2,1,0:T(8,128)(2,1)S(1)}, bf16[4,2,80,512]{3,2,1,0:T(8,128)(2,1)S(1)}) custom-call(bf16[4,512,768]{2,1,0:T(8,128)(2,1)S(1)} %copy-done.1, bf16[4,512,768]{2,1,0:T(8,128)(2,1)S(1)} %copy-done.1, bf16[4,16,768]{2,1,0:T(8,128)(2,1)S(1)} %pad.20.edge_ref, f32[8,768]{1,0:T(8,128)S(1)} %select_maximum_fusion.taps_ref, ...), custom_call_target="tpu_custom_call" | custom-call | bytes 33210000 | tf_op jit(solution)/shard_map/pallas_call | solution.py:386
  49.4 4.9 %all-to-all-start = ((bf16[8,80,512]{2,1,0:T(8,128)(2,1)}), bf16[8,80,512]{2,1,0:T(8,128)(2,1)}, u32[]{:S(2)}, u32[]{:S(2)}) async-start(bf16[8,80,512]{2,1,0:T(8,128)(2,1)} %bitcast.206), calls=%async_computation | async-start | bytes 1310720 | tf_op jit(solution)/shard_map/all_to_all | solution.py:86
  54.9 16.5 %all-to-all-done = bf16[8,80,512]{2,1,0:T(8,128)(2,1)} async-done(((bf16[8,80,512]{2,1,0:T(8,128)(2,1)}), bf16[8,80,512]{2,1,0:T(8,128)(2,1)}, u32[]{:S(2)}, u32[]{:S(2)}) %all-to-all-start) | async-done | bytes 655392 | tf_op jit(solution)/shard_map/all_to_all | solution.py:86
  77.9 4.4 all-to-all-start.1
  87.2 5.6 %fusion.20 = f32[4,512,8]{1,2,0:T(8,128)} fusion(f32[8]{0:T(128)} %copy-done.102, f32[4,512,8]{2,1,0:T(8,128)} %get-tuple-element.183), kind=kOutput, calls=%fused_computation.56 | convolution fusion | flops 101318656 | bytes 131104 | tf_op jit(solution)/shard_map/ts,bsh->bth/dot_general | solution.py:803
  92.8 3.8 all-to-all-done.1
  99.0 14.6 %shard_map.510 = (f32[4,512,512]{2,1,0:T(8,128)S(1)}, f32[4,4,128,512]{3,2,1,0:T(8,128)S(1)}) custom-call(bf16[4,512,768]{2,1,0:T(8,128)(2,1)S(1)} %get-tuple-element.69.x_ref.b_ref.c_ref, bf16[4,512,768]{2,1,0:T(8,128)(2,1)S(1)} %get-tuple-element.69.x_ref.b_ref.c_ref, bf16[4,512,768]{2,1,0:T(8,128)(2,1)S(1)} %get-tuple-element.69.x_ref.b_ref.c_ref, ...), custom_call_target="tpu_custom_call" | custom-call | bytes 47970000 | tf_op jit(solution)/shard_map/pallas_call | solution.py:419
  113.7 2.0 copy-done.21
  115.8 5.1 %multiply_reduce_fusion.2 = (f32[4,512]{1,0:T(4,128)S(1)}, f32[4,512,512]{2,1,0:T(8,128)S(1)}, f32[4,512,512]{2,1,0:T(8,128)}) fusion(f32[4,512,512]{2,1,0:T(8,128)S(1)} %get-tuple-element.71.y_ref, bf16[4,512,768]{2,1,0:T(8,128)(2,1)S(1)} %get-tuple-element.69.x_ref.b_ref.c_ref, f32[512]{0:T(512)S(1)} %copy-done.100, ...), kind=kOutput, calls=%fused_computation.20 | convolution fusion | flops 2166355968 | bytes 19945472 | tf_op jit(solution)/shard_map/btd,dc->btc/dot_general | solution.py:785
  121.5 4.4 fusion.90
  126.5 10.7 %psum.7 = f32[2,4,512]{2,1,0:T(4,128)S(1)} all-reduce(f32[2,4,512]{2,1,0:T(4,128)} %pad_maximum_fusion.2), channel_id=1, replica_groups=mesh['seq'=8,'head'=4] {'head'}, use_global_device_ids=true, to_apply=%region_3.4 | all-reduce | flops 4096 | bytes 32768 | tf_op jit(solution)/shard_map/psum | solution.py:815
  137.8 10.5 %fusion.15 = (f32[4,512,512]{2,1,0:T(8,128)S(1)}, bf16[4,512,512]{2,1,0:T(8,128)(2,1)}, f32[512]{0:T(512)}) fusion(f32[4,512,512]{2,1,0:T(8,128)} %copy-done.103, f32[4,512]{1,0:T(4,128)S(1)} %fusion.55, f32[512]{0:T(512)} %param.54, f32[4,512,512]{2,1,0:T(8,128)} %get-tuple-element.184, f32[4,512,512]{2,1,0:T(8,128)} %copy-done.20, ...), kind=kOutput, calls=%fused_computation.52 | convolution fusion | flops 2177367552 | bytes 27293696 | tf_op jit(solution)/shard_map/btd,di->bti/dot_general | solution.py:820
  148.3 3.9 multiply_convert_fusion.1
  153.6 5.1 %all-to-all-start.2 = ((bf16[8,64,512]{2,1,0:T(8,128)(2,1)}), bf16[8,64,512]{2,1,0:T(8,128)(2,1)}, u32[]{:S(2)}, u32[]{:S(2)}) async-start(bf16[8,64,512]{2,1,0:T(8,128)(2,1)} %bitcast.219), calls=%async_computation.2 | async-start | bytes 1048576 | tf_op jit(solution)/shard_map/all_to_all | solution.py:86
  158.7 3.2 dynamic-slice_bitcast_fusion.1
  162.0 6.2 %bitcast_convert_fusion.2 = bf16[1024,512]{1,0:T(8,128)(2,1)} fusion(bf16[4,512,1024]{2,1,0:T(8,128)(2,1)S(1)} %copy-done.17, f32[4,512]{1,0:T(4,128)} %copy-done.84, f32[4,512]{1,0:T(4,128)} %compare_convert_fusion, f32[4,512,512]{2,1,0:T(8,128)} %copy-done.103, f32[512]{0:T(512)} %param.54), kind=kOutput, calls=%fused_computation.38 | convolution fusion | flops 2158493696 | bytes 9455616 | tf_op jit(solution)/shard_map/btd,bti->di/dot_general | solution.py:819
  168.3 4.2 all-to-all-done.2
  179.6 4.1 all-to-all-start.3
  183.7 5.4 %bitcast_convert_fusion.1 = bf16[1024,512]{1,0:T(8,128)(2,1)S(1)} fusion(bf16[4,512,512]{2,1,0:T(8,128)(2,1)} %get-tuple-element.146, bf16[4,512,1024]{2,1,0:T(8,128)(2,1)} %param.30, f32[1024]{0:T(1024)S(1)} %copy-done.39, f32[4,512]{1,0:T(4,128)} %copy-done.85), kind=kOutput, calls=%fused_computation.37 | convolution fusion | flops 2156396544 | bytes 7352320 | tf_op jit(solution)/shard_map/btd,btc->dc/dot_general | solution.py:835
  190.7 1.5 copy-done.48
  192.1 3.9 fusion.4
  197.1 4.8 %all-to-all-start.4 = ((bf16[8,256,512]{2,1,0:T(8,128)(2,1)}), bf16[8,256,512]{2,1,0:T(8,128)(2,1)}, u32[]{:S(2)}, u32[]{:S(2)}) async-start(bf16[8,256,512]{2,1,0:T(8,128)(2,1)} %bitcast.212), calls=%async_computation.4 | async-start | bytes 4194304 | tf_op jit(solution)/shard_map/all_to_all | solution.py:86
  202.9 1.9 copy-done.2
  209.1 36.1 %shard_map.511 = (bf16[4,512,512]{2,1,0:T(8,128)(2,1)S(1)}, bf16[4,512,256]{2,1,0:T(8,128)(2,1)S(1)}, bf16[4,512,8]{2,1,0:T(8,128)(2,1)S(1)}, f32[4,8,512]{2,1,0...) custom-call(bf16[4,512,768]{2,1,0:T(8,128)(2,1)S(1)} %get-tuple-element.69.x_ref.b_ref.c_ref, ...), custom_call_target="tpu_custom_call" | custom-call | bytes 110700000 | tf_op jit(solution)/shard_map/pallas_call | solution.py:481
  247.8 1.8 collective-permute-start.3
  250.5 2.7 reduce_sum.75
  253.6 1.5 fusion.51
  255.0 1.6 copy-done.28
  256.6 1.6 copy-done.30
  259.3 7.0 %shard_map.512 = bf16[2048,1024]{1,0:T(8,128)(2,1)S(1)} custom-call(bf16[2048,512]{1,0:T(8,128)(2,1)S(1)} %bitcast.201, bf16[2048,512]{1,0:T(8,128)(2,1)S(1)} %bitcast.202, bf16[2048,8]{1,0:T(8,128)(2,1)S(1)} %bitcast.207, bf16[1024,512]{1,0:T(8,128)(2,1)S(1)} %copy-done.23, bf16[1024,512]{1,0:T(8,128)(2,1)S(1)} %copy-done.25, ...), custom_call_target="tpu_custom_call" | custom-call | bytes 22140000 | tf_op jit(solution)/shard_map/pallas_call | solution.py:597
  267.9 2.6 add_convert_fusion.1.part_ref
  272.1 9.0 %collective-permute-done.6 = bf16[1024,256]{1,0:T(8,128)(2,1)S(1)} collective-permute-done((bf16[1024,256]{1,0:T(8,128)(2,1)}, bf16[1024,256]{1,0:T(8,128)(2,1)S(1)}, u32[]{:S(2)}, u32[]{:S(2)}) %collective-permute-start.6) | collective-permute-done | bytes 524320 | tf_op jit(solution)/shard_map/ppermute | solution.py:34
  281.2 2.0 add_convert_fusion.2
  283.1 2.3 fusion.3
  285.4 3.5 bitcast_convert_fusion
  288.9 6.7 %all-to-all-start.5 = ((bf16[8,128,512]{2,1,0:T(8,128)(2,1)}), bf16[8,128,512]{2,1,0:T(8,128)(2,1)}, u32[]{:S(2)}, u32[]{:S(2)}) async-start(bf16[8,128,512]{2,1,0:T(8,128)(2,1)} %bitcast.220), calls=%async_computation.5 | async-start | bytes 2097152 | tf_op jit(solution)/shard_map/all_to_all | solution.py:86
  298.3 2.2 copy-done.6
  301.8 8.0 %shard_map.513 = bf16[2048,1024]{1,0:T(8,128)(2,1)} custom-call(s32[6]{0:T(128)S(1)} %pad_add_fusion.scalars_ref, bf16[1024,1024]{1,0:T(8,128)(2,1)S(1)} %add_convert_fusion.1.part_ref, bf16[1024,1024]{1,0:T(8,128)(2,1)} %collective-permute-done.8.got_ref, bf16[2048,1024]{1,0:T(8,128)(2,1)S(1)} %bitcast.192, f32[2048,1]{1,0:T(8,128)S(1)} %bitcast.200), custom_call_target="tpu_custom_call" | custom-call | bytes 29520000 | tf_op jit(solution)/shard_map/pallas_call | solution.py:659
  309.8 10.9 %shard_map.514 = (bf16[4,512,256]{2,1,0:T(8,128)(2,1)S(1)}, f32[4,8,256]{2,1,0:T(8,128)S(1)}, f32[4,8,256]{2,1,0:T(8,128)S(1)}, f32[8,256]{1,0:T(8,128)S(1)}) custom-call(s32[6]{0:T(128)S(1)} %pad_add_fusion.scalars_ref, bf16[2,512,256]{2,1,0:T(8,128)(2,1)} %bitcast.51.part_ref, bf16[2,512,256]{2,1,0:T(8,128)(2,1)} %bitcast.52.got_ref, ...), custom_call_target="tpu_custom_call" | custom-call | bytes 18450000 | tf_op jit(solution)/shard_map/pallas_call | solution.py:549
  323.3 5.5 %multiply_subtract_fusion = (f32[1024,512]{1,0:T(8,128)}, f32[1024,512]{1,0:T(8,128)}, f32[1024,512]{1,0:T(8,128)}) fusion(f32[1024,512]{1,0:T(8,128)S(1)} %copy-done.53, bf16[4,256,512]{2,1,0:T(8,128)(2,1)S(1)} %get-tuple-element.151, f32[1024,512]{1,0:T(8,128)S(1)} %copy-done.54, f32[1024,512]{1,0:T(8,128)} %param.58), kind=kLoop, calls=%fused_computation.39 | loop fusion | flops 8388608 | bytes 13631488 | tf_op jit(solution)/shard_map/sub | solution.py:720
  328.9 5.2 %fusion.16 = bf16[1024,256]{1,0:T(8,128)(2,1)} fusion(bf16[4,512,256]{2,1,0:T(8,128)(2,1)S(1)} %fusion.54, bf16[4,512,1024]{2,1,0:T(8,128)(2,1)} %param.30, f32[1024]{0:T(1024)S(1)} %copy-done.39, f32[4,512]{1,0:T(4,128)S(1)} %copy-done.87), kind=kOutput, calls=%fused_computation.54 | convolution fusion | flops 1082392576 | bytes 5779456 | tf_op jit(solution)/shard_map/btd,btc->dc/dot_general | solution.py:900
  334.0 11.1 %collective-permute-done.7 = bf16[1024,1024]{1,0:T(8,128)(2,1)} collective-permute-done((bf16[1024,1024]{1,0:T(8,128)(2,1)}, bf16[1024,1024]{1,0:T(8,128)(2,1)}, u32[]{:S(2)}, u32[]{:S(2)}) %collective-permute-start.7) | collective-permute-done | bytes 2097184 | tf_op jit(solution)/shard_map/ppermute | solution.py:34
  345.1 2.6 add_convert_fusion.part_ref
  347.8 5.7 %all-to-all-start.6 = ((bf16[8,128,256]{2,1,0:T(8,128)(2,1)}), bf16[8,128,256]{2,1,0:T(8,128)(2,1)}, u32[]{:S(2)}, u32[]{:S(2)}) async-start(bf16[8,128,256]{2,1,0:T(8,128)(2,1)} %bitcast.59), calls=%async_computation.6 | async-start | bytes 1048576 | tf_op jit(solution)/shard_map/all_to_all | solution.py:86
  353.6 2.1 reduce_sum.77
  355.7 3.4 convolution_bitcast_fusion.1
  359.2 2.1 stack.65
  361.4 7.4 %all-to-all-done.6 = bf16[8,128,256]{2,1,0:T(8,128)(2,1)} async-done(((bf16[8,128,256]{2,1,0:T(8,128)(2,1)}), bf16[8,128,256]{2,1,0:T(8,128)(2,1)}, u32[]{:S(2)}, u32[]{:S(2)}) %all-to-all-start.6) | async-done | bytes 524320 | tf_op jit(solution)/shard_map/all_to_all | solution.py:86
  369.9 2.2 copy-done.7
  372.1 2.2 copy-done.18
  375.5 11.2 %shard_map.515 = (f32[2048,1024]{1,0:T(8,128)}, f32[1,1024]{1,0:T(1,128)S(1)}) custom-call(s32[6]{0:T(128)S(1)} %pad_add_fusion.scalars_ref, bf16[1024,1024]{1,0:T(8,128)(2,1)S(1)} %add_convert_fusion.part_ref, bf16[1024,1024]{1,0:T(8,128)(2,1)} %collective-permute-done.11.got_ref, bf16[2048,256]{1,0:T(8,128)(2,1)S(1)} %bitcast.203, ...), custom_call_target="tpu_custom_call" | custom-call | bytes 29520000 | tf_op jit(solution)/shard_map/pallas_call | solution.py:659
  386.8 1.5 collective-permute-start.12
  388.3 31.9 %all-gather.2 = bf16[1024,256]{1,0:T(8,128)(2,1)S(1)} all-gather(bf16[128,256]{1,0:T(8,128)(2,1)S(1)} %reduce_sum.78), channel_id=4, replica_groups=mesh['seq'=8,'head'=4] {'seq'}, dimensions={0}, use_global_device_ids=true | all-gather | bytes 589824 | tf_op jit(solution)/shard_map/all_gather | solution.py:954
  420.3 4.1 multiply_subtract_fusion.1
  424.4 1.5 copy.130
  427.8 1.5 maximum_bitcast_fusion
  429.3 3.2 copy.132
  432.8 9.7 %shard_map.516 = (f32[1024,8,128]{2,1,0:T(8,128)}, f32[1024,8,128]{2,1,0:T(8,128)}, f32[1024,8,128]{2,1,0:T(8,128)}) custom-call(bf16[1024,8,128]{2,1,0:T(8,128)(2,1)S(1)} %bitcast.197, f32[1024,8,128]{2,1,0:T(8,128)S(1)} %bitcast.194, f32[1024,8,128]{2,1,0:T(8,128)S(1)} %bitcast.199, f32[1024,8,128]{2,1,0:T(8,128)} %bitcast.213), custom_call_target="tpu_custom_call" | custom-call | bytes 33210000 | tf_op jit(solution)/shard_map/pallas_call | solution.py:698
  (316 shorter events, 62.1 us)
Async XLA Ops:
  10.7 16.1 %copy-start.85 = (f32[4,512]{1,0:T(4,128)}, f32[4,512]{1,0:T(4,128)S(1)}, u32[]{:S(2)}) copy-start(f32[4,512]{1,0:T(4,128)S(1)} %add_rsqrt_fusion) | copy-start | bytes 24580
  15.7 10.9 %copy-start.56 = (f32[1024,8]{0,1:T(8,128)S(1)}, f32[1024,8]{0,1:T(8,128)}, u32[]{:S(2)}) copy-start(f32[1024,8]{0,1:T(8,128)} %param.42) | copy-start | bytes 98308
  21.2 11.3 %collective-permute-start = (bf16[4,3,768]{2,1,0:T(4,128)(2,1)S(1)}, bf16[4,3,768]{2,1,0:T(4,128)(2,1)S(1)}, u32[]{:S(2)}, u32[]{:S(2)}) collective-permute-start(bf16[4,3,768]{2,1,0:T(4,128)(2,1)S(1)} %slice.284), channel_id=1, source_target_pairs={{0,4},{4,8},{8,12},{12,16},{16,20},{20,24},{24,28},{1,5},{5,9},{9,... | collective-permute-start | bytes 55304 | tf_op jit(solution)/shard_map/ppermute | solution.py:30
  32.4 16.1 %copy-start.10 = (f32[4,512,8]{2,1,0:T(8,128)}, f32[4,512,8]{2,1,0:T(8,128)S(1)}, u32[]{:S(2)}) copy-start(f32[4,512,8]{2,1,0:T(8,128)S(1)} %get-tuple-element.155.decay_ref) | copy-start | bytes 196612
  32.4 16.1 %copy-start.13 = (f32[4,512,8]{2,1,0:T(8,128)}, f32[4,512,8]{2,1,0:T(8,128)S(1)}, u32[]{:S(2)}) copy-start(f32[4,512,8]{2,1,0:T(8,128)S(1)} %get-tuple-element.156.step_ref) | copy-start | bytes 196612
  49.4 22.0 %all-to-all-start = ((bf16[8,80,512]{2,1,0:T(8,128)(2,1)}), bf16[8,80,512]{2,1,0:T(8,128)(2,1)}, u32[]{:S(2)}, u32[]{:S(2)}) async-start(bf16[8,80,512]{2,1,0:T(8,128)(2,1)} %bitcast.206), calls=%async_computation | async-start | bytes 1310720 | tf_op jit(solution)/shard_map/all_to_all | solution.py:86
  73.3 40.4 %copy-start.73 = (f32[1,1,512]{2,1,0:T(1,128)}, f32[1,1,512]{2,1,0:T(1,128)S(1)}, u32[]{:S(2)}) copy-start(f32[1,1,512]{2,1,0:T(1,128)S(1)} %get-tuple-element.171) | copy-start | bytes 6148
  73.3 40.4 %copy-start.75 = (f32[1,1,512]{2,1,0:T(1,128)}, f32[1,1,512]{2,1,0:T(1,128)S(1)}, u32[]{:S(2)}) copy-start(f32[1,1,512]{2,1,0:T(1,128)S(1)} %get-tuple-element.173) | copy-start | bytes 6148
  77.9 18.7 %all-to-all-start.1 = ((bf16[8,64,512]{2,1,0:T(8,128)(2,1)}), bf16[8,64,512]{2,1,0:T(8,128)(2,1)}, u32[]{:S(2)}, u32[]{:S(2)}) async-start(bf16[8,64,512]{2,1,0:T(8,128)(2,1)} %fusion.48), calls=%async_computation.1 | async-start | bytes 1048576 | tf_op jit(solution)/shard_map/all_to_all | solution.py:86
  83.1 30.6 %copy-start.66 = (f32[8,64]{1,0:T(8,128)}, f32[8,64]{1,0:T(8,128)S(1)}, u32[]{:S(2)}) copy-start(f32[8,64]{1,0:T(8,128)S(1)} %broadcast_in_dim.12) | copy-start | bytes 6148
  99.0 16.7 %copy-start.4 = (bf16[4,512,1024]{2,1,0:T(8,128)(2,1)S(1)}, bf16[4,512,1024]{2,1,0:T(8,128)(2,1)}, u32[]{:S(2)}) copy-start(bf16[4,512,1024]{2,1,0:T(8,128)(2,1)} %param.30) | copy-start | bytes 12582916
  99.0 16.7 %copy-start.47 = (bf16[1024,2,512]{2,0,1:T(8,128)(2,1)S(1)}, bf16[1024,2,512]{2,0,1:T(8,128)(2,1)}, u32[]{:S(2)}) copy-start(bf16[1024,2,512]{2,0,1:T(8,128)(2,1)} %copy-done.46) | copy-start | bytes 6291460
  99.0 16.7 %copy-start.86 = (f32[4,512]{1,0:T(4,128)S(1)}, f32[4,512]{1,0:T(4,128)}, u32[]{:S(2)}) copy-start(f32[4,512]{1,0:T(4,128)} %copy-done.85) | copy-start | bytes 24580
  99.0 16.7 %copy-start.100 = (f32[512]{0:T(512)S(1)}, f32[512]{0:T(512)}, u32[]{:S(2)}) copy-start(f32[512]{0:T(512)} %mul.699) | copy-start | bytes 6148
  137.8 10.5 %copy-start.84 = (f32[4,512]{1,0:T(4,128)}, f32[4,512]{1,0:T(4,128)S(1)}, u32[]{:S(2)}) copy-start(f32[4,512]{1,0:T(4,128)S(1)} %get-tuple-element.164) | copy-start | bytes 24580
  153.6 18.9 %all-to-all-start.2 = ((bf16[8,64,512]{2,1,0:T(8,128)(2,1)}), bf16[8,64,512]{2,1,0:T(8,128)(2,1)}, u32[]{:S(2)}, u32[]{:S(2)}) async-start(bf16[8,64,512]{2,1,0:T(8,128)(2,1)} %bitcast.219), calls=%async_computation.2 | async-start | bytes 1048576 | tf_op jit(solution)/shard_map/all_to_all | solution.py:86
  161.9 11.7 %copy-start.72 = (f32[1,1,512]{2,1,0:T(1,128)S(1)}, f32[1,1,512]{2,1,0:T(1,128)}, u32[]{:S(2)}) copy-start(f32[1,1,512]{2,1,0:T(1,128)} %copy-done.71) | copy-start | bytes 6148
  161.9 11.7 %copy-start.74 = (f32[1,1,512]{2,1,0:T(1,128)S(1)}, f32[1,1,512]{2,1,0:T(1,128)}, u32[]{:S(2)}) copy-start(f32[1,1,512]{2,1,0:T(1,128)} %copy-done.73) | copy-start | bytes 6148
  161.9 11.7 %copy-start.76 = (f32[1,1,512]{2,1,0:T(1,128)S(1)}, f32[1,1,512]{2,1,0:T(1,128)}, u32[]{:S(2)}) copy-start(f32[1,1,512]{2,1,0:T(1,128)} %copy-done.75) | copy-start | bytes 6148
  162.0 11.7 %copy-start.77 = (f32[1,1,512]{2,1,0:T(1,128)S(1)}, f32[1,1,512]{2,1,0:T(1,128)}, u32[]{:S(2)}) copy-start(f32[1,1,512]{2,1,0:T(1,128)} %get-tuple-element.168) | copy-start | bytes 6148
  162.0 28.7 %collective-permute-start.1 = (bf16[1024,1024]{1,0:T(8,128)(2,1)}, bf16[1024,1024]{1,0:T(8,128)(2,1)}, u32[]{:S(2)}, u32[]{:S(2)}) collective-permute-start(bf16[1024,1024]{1,0:T(8,128)(2,1)} %dynamic-slice_bitcast_fusion.1), channel_id=1, source_target_pairs={{0,1},{1,0},{2,3},{3,2},{4,5},{5,4},{6,7},{7,6},{8,9},{9,8},{10,11... | collective-permute-start | bytes 6291464 | tf_op jit(solution)/shard_map/ppermute | solution.py:34
  179.6 17.5 %all-to-all-start.3 = ((bf16[8,64,512]{2,1,0:T(8,128)(2,1)}), bf16[8,64,512]{2,1,0:T(8,128)(2,1)}, u32[]{:S(2)}, u32[]{:S(2)}) async-start(bf16[8,64,512]{2,1,0:T(8,128)(2,1)} %constant_dynamic-update-slice_fusion.1), calls=%async_computation.3 | async-start | bytes 1048576 | tf_op jit(solution)/shard_map/all_to_all | solution.py:86
  190.7 12.1 %copy-start.67 = (f32[8,64]{1,0:T(8,128)S(1)}, f32[8,64]{1,0:T(8,128)}, u32[]{:S(2)}) copy-start(f32[8,64]{1,0:T(8,128)} %copy-done.66) | copy-start | bytes 6148
  197.1 53.4 %all-to-all-start.4 = ((bf16[8,256,512]{2,1,0:T(8,128)(2,1)}), bf16[8,256,512]{2,1,0:T(8,128)(2,1)}, u32[]{:S(2)}, u32[]{:S(2)}) async-start(bf16[8,256,512]{2,1,0:T(8,128)(2,1)} %bitcast.212), calls=%async_computation.4 | async-start | bytes 4194304 | tf_op jit(solution)/shard_map/all_to_all | solution.py:86
  201.9 107.8 %all-gather.6.cloned.1.call-start = ((), (), s32[]{:S(2)}) async-start(), calls=%async_computation.7 | async-start | bytes 2359296 | tf_op jit(solution)/shard_map/all_gather | solution.py:860
  202.0 48.5 %collective-permute-start.2 = (bf16[1024,1024]{1,0:T(8,128)(2,1)}, bf16[1024,1024]{1,0:T(8,128)(2,1)}, u32[]{:S(2)}, u32[]{:S(2)}) collective-permute-start(bf16[1024,1024]{1,0:T(8,128)(2,1)} %fusion.4), channel_id=1, source_target_pairs={{0,2},{1,3},{2,0},{3,1},{4,6},{5,7},{6,4},{7,5},{8,10},{9,11},{10,... | collective-permute-start | bytes 6291464 | tf_op jit(solution)/shard_map/ppermute | solution.py:34
  246.6 3.0 collective-permute-start.4
  247.8 5.8 %collective-permute-start.3 = (f32[4,3,512]{2,1,0:T(4,128)S(1)}, f32[4,3,512]{2,1,0:T(4,128)S(1)}, u32[]{:S(2)}, u32[]{:S(2)}) collective-permute-start(f32[4,3,512]{2,1,0:T(4,128)S(1)} %pad_maximum_fusion.1), channel_id=1, source_target_pairs={{4,0},{8,4},{12,8},{16,12},{20,16},{24,20},{28,24},{5,1},{9,5},{13... | collective-permute-start | bytes 73736 | tf_op jit(solution)/shard_map/ppermute | solution.py:30
  266.5 16.6 %collective-permute-start.5 = (bf16[1024,1024]{1,0:T(8,128)(2,1)S(1)}, bf16[1024,1024]{1,0:T(8,128)(2,1)S(1)}, u32[]{:S(2)}, u32[]{:S(2)}) collective-permute-start(bf16[1024,1024]{1,0:T(8,128)(2,1)S(1)} %dynamic-slice_bitcast_fusion), channel_id=1, source_target_pairs={{0,1},{1,0},{2,3},{3,2},{4,5},{5,4},{6,7},{7,6},{8,9},{9,8},{10,11... | collective-permute-start | bytes 6291464 | tf_op jit(solution)/shard_map/ppermute | solution.py:34
  266.6 14.6 %collective-permute-start.6 = (bf16[1024,256]{1,0:T(8,128)(2,1)}, bf16[1024,256]{1,0:T(8,128)(2,1)S(1)}, u32[]{:S(2)}, u32[]{:S(2)}) collective-permute-start(bf16[1024,256]{1,0:T(8,128)(2,1)} %fusion.25), channel_id=1, source_target_pairs={{0,2},{1,3},{2,0},{3,1},{4,6},{5,7},{6,4},{7,5},{8,10},{9,11},{10,... | collective-permute-start | bytes 1572872 | tf_op jit(solution)/shard_map/ppermute | solution.py:34
  270.5 27.9 %collective-permute-start.8 = (bf16[1024,1024]{1,0:T(8,128)(2,1)S(1)}, bf16[1024,1024]{1,0:T(8,128)(2,1)}, u32[]{:S(2)}, u32[]{:S(2)}) collective-permute-start(bf16[1024,1024]{1,0:T(8,128)(2,1)S(1)} %add_convert_fusion.1.part_ref), channel_id=1, source_target_pairs={{0,1},{1,0},{2,3},{3,2},{4,5},{5,4},{6,7},{7,6},{8,9},{9,8},{10,11... | collective-permute-start | bytes 6291464 | tf_op jit(solution)/shard_map/ppermute | solution.py:34
  272.0 13.4 %copy-start.5 = (bf16[4,512,1024]{2,1,0:T(8,128)(2,1)S(1)}, bf16[4,512,1024]{2,1,0:T(8,128)(2,1)}, u32[]{:S(2)}) copy-start(bf16[4,512,1024]{2,1,0:T(8,128)(2,1)} %param.30) | copy-start | bytes 12582916
  272.0 13.4 %copy-start.87 = (f32[4,512]{1,0:T(4,128)S(1)}, f32[4,512]{1,0:T(4,128)}, u32[]{:S(2)}) copy-start(f32[4,512]{1,0:T(4,128)} %copy-done.85) | copy-start | bytes 24580
  285.4 24.3 %collective-permute-start.9 = (bf16[1024,256]{1,0:T(8,128)(2,1)}, bf16[1024,256]{1,0:T(8,128)(2,1)}, u32[]{:S(2)}, u32[]{:S(2)}) collective-permute-start(bf16[1024,256]{1,0:T(8,128)(2,1)} %add_convert_fusion.2), channel_id=1, source_target_pairs={{0,1},{1,0},{2,3},{3,2},{4,5},{5,4},{6,7},{7,6},{8,9},{9,8},{10,11... | collective-permute-start | bytes 1572872 | tf_op jit(solution)/shard_map/ppermute | solution.py:34
  288.9 40.0 %all-to-all-start.5 = ((bf16[8,128,512]{2,1,0:T(8,128)(2,1)}), bf16[8,128,512]{2,1,0:T(8,128)(2,1)}, u32[]{:S(2)}, u32[]{:S(2)}) async-start(bf16[8,128,512]{2,1,0:T(8,128)(2,1)} %bitcast.220), calls=%async_computation.5 | async-start | bytes 2097152 | tf_op jit(solution)/shard_map/all_to_all | solution.py:86
  297.1 48.0 %collective-permute-start.7 = (bf16[1024,1024]{1,0:T(8,128)(2,1)}, bf16[1024,1024]{1,0:T(8,128)(2,1)}, u32[]{:S(2)}, u32[]{:S(2)}) collective-permute-start(bf16[1024,1024]{1,0:T(8,128)(2,1)} %fusion.3), channel_id=1, source_target_pairs={{0,2},{1,3},{2,0},{3,1},{4,6},{5,7},{6,4},{7,5},{8,10},{9,11},{10,... | collective-permute-start | bytes 6291464 | tf_op jit(solution)/shard_map/ppermute | solution.py:34
  309.7 12.4 %copy-start.51 = (bf16[2048,512]{1,0:T(8,128)(2,1)S(1)}, bf16[2048,512]{1,0:T(8,128)(2,1)}, u32[]{:S(2)}) copy-start(bf16[2048,512]{1,0:T(8,128)(2,1)} %all-gather.6.cloned.1.call-done) | copy-start | bytes 6291460
  309.7 13.6 %copy-start.53 = (f32[1024,512]{1,0:T(8,128)S(1)}, f32[1024,512]{1,0:T(8,128)}, u32[]{:S(2)}) copy-start(f32[1024,512]{1,0:T(8,128)} %param.57) | copy-start | bytes 6291460
  309.7 13.6 %copy-start.54 = (f32[1024,512]{1,0:T(8,128)S(1)}, f32[1024,512]{1,0:T(8,128)}, u32[]{:S(2)}) copy-start(f32[1024,512]{1,0:T(8,128)} %param.59) | copy-start | bytes 6291460
  320.7 8.1 %collective-permute-start.10 = (f32[4,3,256]{2,1,0:T(4,128)S(1)}, f32[4,3,256]{2,1,0:T(4,128)S(1)}, u32[]{:S(2)}, u32[]{:S(2)}) collective-permute-start(f32[4,3,256]{2,1,0:T(4,128)S(1)} %pad_maximum_fusion.3), channel_id=1, source_target_pairs={{4,0},{8,4},{12,8},{16,12},{20,16},{24,20},{28,24},{5,1},{9,5},{13... | collective-permute-start | bytes 36872 | tf_op jit(solution)/shard_map/ppermute | solution.py:30
  328.9 16.3 %copy-start.45 = (bf16[1024,1024]{1,0:T(8,128)(2,1)S(1)}, bf16[1024,1024]{1,0:T(8,128)(2,1)}, u32[]{:S(2)}) copy-start(bf16[1024,1024]{1,0:T(8,128)(2,1)} %fusion.3) | copy-start | bytes 6291460
  345.1 10.6 %copy-start.37 = (bf16[4,512,8]{2,1,0:T(8,128)(2,1)S(1)}, bf16[4,512,8]{2,1,0:T(8,128)(2,1)}, u32[]{:S(2)}) copy-start(bf16[4,512,8]{2,1,0:T(8,128)(2,1)} %copy-done.35) | copy-start | bytes 98308
  347.7 22.2 %collective-permute-start.11 = (bf16[1024,1024]{1,0:T(8,128)(2,1)S(1)}, bf16[1024,1024]{1,0:T(8,128)(2,1)}, u32[]{:S(2)}, u32[]{:S(2)}) collective-permute-start(bf16[1024,1024]{1,0:T(8,128)(2,1)S(1)} %add_convert_fusion.part_ref), channel_id=1, source_target_pairs={{0,1},{1,0},{2,3},{3,2},{4,5},{5,4},{6,7},{7,6},{8,9},{9,8},{10,11... | collective-permute-start | bytes 6291464 | tf_op jit(solution)/shard_map/ppermute | solution.py:34
  347.8 21.0 %all-to-all-start.6 = ((bf16[8,128,256]{2,1,0:T(8,128)(2,1)}), bf16[8,128,256]{2,1,0:T(8,128)(2,1)}, u32[]{:S(2)}, u32[]{:S(2)}) async-start(bf16[8,128,256]{2,1,0:T(8,128)(2,1)} %bitcast.59), calls=%async_computation.6 | async-start | bytes 1048576 | tf_op jit(solution)/shard_map/all_to_all | solution.py:86
  353.5 70.9 %all-gather.8.cloned.1.call-start = ((), (), s32[]{:S(2)}) async-start(), calls=%async_computation.8 | async-start | bytes 1179648 | tf_op jit(solution)/shard_map/all_gather | solution.py:898
  355.7 14.2 %copy-start.27 = (bf16[1024,256]{1,0:T(8,128)(2,1)S(1)}, bf16[1024,256]{1,0:T(8,128)(2,1)}, u32[]{:S(2)}) copy-start(bf16[1024,256]{1,0:T(8,128)(2,1)} %copy-done.26) | copy-start | bytes 1572868
  375.5 11.2 %copy-start.93 = (f32[512]{0:T(512)S(1)}, f32[512]{0:T(512)}, u32[]{:S(2)}) copy-start(f32[512]{0:T(512)} %get-tuple-element.147) | copy-start | bytes 6148
  386.8 33.4 %collective-permute-start.12 = (f32[112,128]{1,0:T(8,128)S(1)}, f32[112,128]{1,0:T(8,128)S(1)}, u32[]{:S(2)}, u32[]{:S(2)}) collective-permute-start(f32[112,128]{1,0:T(8,128)S(1)} %pad_bitcast_fusion), channel_id=1, source_target_pairs={{0,4},{4,0},{8,12},{12,8},{16,20},{20,16},{24,28},{28,24},{1,5},{5... | collective-permute-start | bytes 172040 | tf_op jit(solution)/shard_map/ppermute | solution.py:34
  420.3 6.4 %collective-permute-start.13 = (f32[112,128]{1,0:T(8,128)S(1)}, f32[112,128]{1,0:T(8,128)S(1)}, u32[]{:S(2)}, u32[]{:S(2)}) collective-permute-start(f32[112,128]{1,0:T(8,128)S(1)} %fusion.70), channel_id=1, source_target_pairs={{0,8},{4,12},{8,0},{12,4},{16,24},{20,28},{24,16},{28,20},{1,9},{5... | collective-permute-start | bytes 172040 | tf_op jit(solution)/shard_map/ppermute | solution.py:34
  426.7 15.8 %collective-permute-start.14 = (f32[112,128]{1,0:T(8,128)S(1)}, f32[112,128]{1,0:T(8,128)S(1)}, u32[]{:S(2)}, u32[]{:S(2)}) collective-permute-start(f32[112,128]{1,0:T(8,128)S(1)} %fusion.101), channel_id=1, source_target_pairs={{0,16},{4,20},{8,24},{12,28},{16,0},{20,4},{24,8},{28,12},{1,17},{... | collective-permute-start | bytes 172040 | tf_op jit(solution)/shard_map/ppermute | solution.py:34
  432.6 11.1 %copy-start.90 = (f32[3,8]{1,0:T(4,128)S(1)}, f32[3,8]{1,0:T(4,128)}, u32[]{:S(2)}) copy-start(f32[3,8]{1,0:T(4,128)} %param.51) | copy-start | bytes 292
  432.6 11.1 %copy-start.94 = (f32[3,8]{1,0:T(4,128)S(1)}, f32[3,8]{1,0:T(4,128)}, u32[]{:S(2)}) copy-start(f32[3,8]{1,0:T(4,128)} %param.53) | copy-start | bytes 292
  432.6 11.1 %copy-start.95 = (f32[3,8]{1,0:T(4,128)S(1)}, f32[3,8]{1,0:T(4,128)}, u32[]{:S(2)}) copy-start(f32[3,8]{1,0:T(4,128)} %param.52) | copy-start | bytes 292
  432.7 11.7 %copy-start.57 = (f32[1024,8]{0,1:T(8,128)S(1)}, f32[1024,8]{0,1:T(8,128)}, u32[]{:S(2)}) copy-start(f32[1024,8]{0,1:T(8,128)} %param.42) | copy-start | bytes 98308
  432.7 11.7 %copy-start.68 = (f32[1024,8]{0,1:T(8,128)S(1)}, f32[1024,8]{0,1:T(8,128)}, u32[]{:S(2)}) copy-start(f32[1024,8]{0,1:T(8,128)} %param.44) | copy-start | bytes 98308
  432.7 11.7 %copy-start.69 = (f32[1024,8]{0,1:T(8,128)S(1)}, f32[1024,8]{0,1:T(8,128)}, u32[]{:S(2)}) copy-start(f32[1024,8]{0,1:T(8,128)} %param.43) | copy-start | bytes 98308
  432.7 12.3 %copy-start.61 = (f32[5,512]{1,0:T(8,128)S(1)}, f32[5,512]{1,0:T(8,128)}, u32[]{:S(2)}) copy-start(f32[5,512]{1,0:T(8,128)} %param.45) | copy-start | bytes 30724
  432.7 12.3 %copy-start.80 = (f32[5,512]{1,0:T(8,128)S(1)}, f32[5,512]{1,0:T(8,128)}, u32[]{:S(2)}) copy-start(f32[5,512]{1,0:T(8,128)} %param.47) | copy-start | bytes 30724
  432.7 12.3 %copy-start.81 = (f32[5,512]{1,0:T(8,128)S(1)}, f32[5,512]{1,0:T(8,128)}, u32[]{:S(2)}) copy-start(f32[5,512]{1,0:T(8,128)} %param.46) | copy-start | bytes 30724
  432.7 13.0 %copy-start.82 = (f32[5,256]{1,0:T(8,128)S(1)}, f32[5,256]{1,0:T(8,128)}, u32[]{:S(2)}) copy-start(f32[5,256]{1,0:T(8,128)} %param.50) | copy-start | bytes 15364
  432.7 12.9 %copy-start.83 = (f32[5,256]{1,0:T(8,128)S(1)}, f32[5,256]{1,0:T(8,128)}, u32[]{:S(2)}) copy-start(f32[5,256]{1,0:T(8,128)} %param.49) | copy-start | bytes 15364
  432.8 13.6 %copy-start.97 = (f32[512]{0:T(512)S(1)}, f32[512]{0:T(512)}, u32[]{:S(2)}) copy-start(f32[512]{0:T(512)} %param.54) | copy-start | bytes 6148
  432.8 13.6 %copy-start.98 = (f32[512]{0:T(512)S(1)}, f32[512]{0:T(512)}, u32[]{:S(2)}) copy-start(f32[512]{0:T(512)} %param.56) | copy-start | bytes 6148
  432.8 13.5 %copy-start.99 = (f32[512]{0:T(512)S(1)}, f32[512]{0:T(512)}, u32[]{:S(2)}) copy-start(f32[512]{0:T(512)} %param.55) | copy-start | bytes 6148
  (64 other events, 289.5 us)
Sparse Core Ops, SparseCore 0:
  253.3 55.6 all-gather.5
  357.1 43.1 all-gather.7

commit v6 on v5

--- a/solution.py
+++ b/solution.py
@@ -10,6 +10,7 @@
 INNER = 2048
 CONV = 4
 CHUNK = 128
+GROUP = 2
 STEP = 7
 
 
@@ -123,6 +124,12 @@
     return lax.dot_general(a, b, (dims, ((), ())), precision=precision, preferred_element_type=F32)
 
 
+def alternately(bodies):
+    bodies = list(bodies)
+    while bodies:
+        bodies = [body for body in bodies if next(body, bodies) is not bodies]
+
+
 def expander(heads, width):
     row = lax.broadcasted_iota(jnp.int32, (heads, heads * width), 0)
     column = lax.broadcasted_iota(jnp.int32, (heads, heads * width), 1)
@@ -162,60 +169,67 @@
 
 
 def scan_kernel(x_ref, b_ref, c_ref, step_ref, decay_ref, enter_ref, y_ref, in_ref, state):
-    heads = step_ref.shape[2]
+    group, _, heads = step_ref.shape
     width = x_ref.shape[2] // heads
 
     @pl.when(pl.program_id(1) == 0)
     def _():
-        state[...] = enter_ref[0].astype(F32)
+        state[...] = enter_ref[...].astype(F32)
 
     expand = expander(heads, width)
-    cum, cum_t, row, column = chunk_decays(decay_ref[0])
-    causal = row >= column
-    q = cum.shape[0]
-    total = cum[q - 1 : q, :]
-    b, c = b_ref[0], c_ref[0]
-    x = x_ref[0].astype(F32)
-    step = step_ref[0]
-    xs = (x * spread(step, expand)).astype(BF16)
-    grown = spread(jnp.exp(cum), expand)
-    xw = (x * spread(step * jnp.exp(total - cum), expand)).astype(BF16)
-    scores = dot(c, b, ((1,), (1,)))
-    before = state[...]
-    in_ref[0, 0] = before
-    from_state = grown * dot(c, before.astype(BF16))
-    for pair in range(heads // 2):
-        lanes = slice(pair * 2 * width, (pair + 1) * 2 * width)
-        mixing = []
-        for h in (2 * pair, 2 * pair + 1):
-            between = cum[:, h : h + 1] - cum_t[h : h + 1, :]
-            mixing.append((jnp.exp(jnp.where(causal, between, -1e30)) * scores).astype(BF16))
-        within = dot(jnp.concatenate(mixing, axis=1), pair_rows(xs[:, lanes]))
-        y_ref[0, :, lanes] = within + from_state[:, lanes]
-    state[...] = grown[q - 1 : q, :] * before + dot(b, xw, ((0,), (0,)))
-
-
-def conv_back_step(act_grad, mixed, previous, taps, after_ref):
+
+    def body(i):
+        cum, cum_t, row, column = chunk_decays(decay_ref[i])
+        causal = row >= column
+        q = cum.shape[0]
+        total = cum[q - 1 : q, :]
+        b, c = b_ref[i], c_ref[i]
+        x = x_ref[i].astype(F32)
+        step = step_ref[i]
+        yield
+        xs = (x * spread(step, expand)).astype(BF16)
+        grown = spread(jnp.exp(cum), expand)
+        xw = (x * spread(step * jnp.exp(total - cum), expand)).astype(BF16)
+        yield
+        scores = dot(c, b, ((1,), (1,)))
+        before = state[i]
+        in_ref[i, 0] = before
+        from_state = grown * dot(c, before.astype(BF16))
+        yield
+        for pair in range(heads // 2):
+            lanes = slice(pair * 2 * width, (pair + 1) * 2 * width)
+            mixing = []
+            for h in (2 * pair, 2 * pair + 1):
+                between = cum[:, h : h + 1] - cum_t[h : h + 1, :]
+                mixing.append((jnp.exp(jnp.where(causal, between, -1e30)) * scores).astype(BF16))
+            within = dot(jnp.concatenate(mixing, axis=1), pair_rows(xs[:, lanes]))
+            y_ref[i, :, lanes] = within + from_state[:, lanes]
+            yield
+        state[i] = grown[q - 1 : q, :] * before + dot(b, xw, ((0,), (0,)))
+
+    alternately(body(i) for i in range(group))
+
+
+def conv_back_step(act_grad, mixed, previous, taps, after):
     q = mixed.shape[0]
     shifted = conv_windows(mixed, previous)
     convolved = taps[CONV : CONV + 1]
     for k in range(CONV):
         convolved = convolved + taps[k : k + 1] * shifted[k]
     conv_grad = act_grad * silu_slope(convolved)
-    extended = jnp.concatenate([conv_grad, after_ref[...]], axis=0)
+    extended = jnp.concatenate([conv_grad, after], axis=0)
     mixed_grad = taps[CONV - 1 : CONV] * conv_grad
     for k in range(CONV - 1):
         mixed_grad = mixed_grad + taps[k : k + 1] * extended[CONV - 1 - k : CONV - 1 - k + q]
     sums = [jnp.sum(conv_grad * part, axis=0, keepdims=True) for part in shifted]
     sums.append(jnp.sum(conv_grad, axis=0, keepdims=True))
     sums.append(jnp.zeros((8 - CONV - 1, mixed.shape[1]), F32))
-    after_ref[...] = conv_grad[:8]
     return conv_grad, mixed_grad, jnp.concatenate(sums, axis=0)
 
 
-def rows_before(edge_ref, previous_ref):
-    first = pl.program_id(1) == pl.num_programs(1) - 1
-    return jnp.where(first, edge_ref[0].astype(F32), previous_ref[0].astype(F32))[8:]
+def rows_before(edge_ref, previous_ref, i, chunk):
+    first = pl.program_id(1) == chunk
+    return jnp.where(first, edge_ref[i].astype(F32), previous_ref[i].astype(F32))[8:]
 
 
 def back_kernel(
@@ -224,6 +238,8 @@
     mixed_grad_ref, dbc_ref, pre_ref, first_ref, last_ref, tap_sums_ref, head_sums_ref,
     grad, after
 ):
+    group, _, heads = step_ref.shape
+    width = x_ref.shape[2] // heads
     start = (pl.program_id(0) == 0) & (pl.program_id(1) == 0)
 
     @pl.when(start)
@@ -234,95 +250,99 @@
     @pl.when(pl.program_id(1) == 0)
     def _():
         after[...] = jnp.zeros_like(after)
-
-    heads = step_ref.shape[2]
-    width = x_ref.shape[2] // heads
-
-    @pl.when(pl.program_id(1) == 0)
-    def _():
-        grad[...] = leave_ref[0].astype(F32)
+        grad[...] = leave_ref[...].astype(F32)
 
     expand = expander(heads, width)
-    cum, cum_t, row, column = chunk_decays(decay_ref[0])
-    later = column >= row
-    q = cum.shape[0]
-    total = cum[q - 1 : q, :]
-    b, c = b_ref[0], c_ref[0]
-    x = x_ref[0].astype(F32)
-    step = step_ref[0]
-    step_wide = spread(step, expand)
-    xs = (x * step_wide).astype(BF16)
-    grown = spread(jnp.exp(cum), expand)
-    waned = spread(jnp.exp(total - cum), expand)
-    xw = (x * step_wide * waned).astype(BF16)
-    dy = dy_ref[0]
-    dy_low = dy.astype(BF16)
-    edy = (dy * grown).astype(BF16)
-    before = in_ref[0, 0]
-    after_grad = grad[...]
-    after_low = after_grad.astype(BF16)
-    scores_t = dot(b, c, ((1,), (1,)))
-    v_state = waned * dot(b, after_low)
-    dscores_t = jnp.zeros((q, q), F32)
-    v_parts = []
-    for pair in range(heads // 2):
-        lanes = slice(pair * 2 * width, (pair + 1) * 2 * width)
-        dy_pair = pair_rows(dy_low[:, lanes])
-        xs_pair = pair_rows(xs[:, lanes])
-        dmix = dot(xs_pair, dy_low[:, lanes], ((1,), (1,)))
-        mixing = []
-        for k, h in enumerate((2 * pair, 2 * pair + 1)):
-            between = cum_t[h : h + 1, :] - cum[:, h : h + 1]
-            fade = jnp.exp(jnp.where(later, between, -1e30))
-            mixing.append((fade * scores_t).astype(BF16))
-            dscores_t = dscores_t + fade * dmix[k * q : (k + 1) * q]
-        v_parts.append(dot(jnp.concatenate(mixing, axis=1), dy_pair))
-    v = jnp.concatenate(v_parts, axis=1) + v_state
-    xs_wide = xs.astype(F32)
-    etotal = grown[q - 1 : q, :]
-    dx = step_wide * v + skip_ref[0] * dy
-    conv_grad, mixed_grad, tap_sums = conv_back_step(
-        dx, mixed_ref[0].astype(F32), rows_before(edge_ref, previous_ref), taps_ref[...], after
-    )
-    mixed_grad_ref[0] = mixed_grad.astype(BF16)
-    first_ref[0] = conv_grad[:8]
-
-    @pl.when(pl.program_id(1) == 0)
-    def _():
-        last_ref[0] = mixed_grad[q - 8 :]
-
-    tap_sums_ref[...] += tap_sums
-    end_row = jnp.sum(xs_wide * v_state, axis=0, keepdims=True) + jnp.sum(
-        etotal * before * after_grad, axis=0, keepdims=True
-    )
-    crossing = dy_low.astype(F32) * y_ref[0] - xs_wide * v
-    last = lax.broadcasted_iota(jnp.int32, crossing.shape, 0) == q - 1
-    crossing = crossing + jnp.where(last, end_row, 0.0)
-    upper = jnp.where(column >= row, 1.0, 0.0).astype(F32)
-    decay_grad = dot(upper, head_sums(crossing, expand), precision=HIGHEST_PREC)
-    pre_grad = (head_sums(x * v, expand) - rate_ref[...] * decay_grad) * slope_ref[0]
-    pre_ref[0] = pre_grad.astype(BF16)
-    sums = [
-        jnp.sum(decay_grad * decay_ref[0], axis=0, keepdims=True),
-        jnp.sum(pre_grad, axis=0, keepdims=True),
-        jnp.sum(head_sums(x * dy, expand), axis=0, keepdims=True),
-        jnp.zeros((5, heads), F32),
-    ]
-    head_sums_ref[...] += jnp.concatenate(sums, axis=0)
-    dscores_low = dscores_t.astype(BF16)
-    state = b.shape[1]
-    dbc_ref[0, :, :state] = (
-        dot(dscores_low, c) + dot(xw, after_low, ((1,), (1,)))
-    ).astype(BF16)
-    dbc_ref[0, :, state:] = (
-        dot(dscores_low, b, ((0,), (0,))) + dot(edy, before.astype(BF16), ((1,), (1,)))
-    ).astype(BF16)
-    grad[...] = etotal * after_grad + dot(c, edy, ((0,), (0,)))
+    last_chunk = pl.program_id(1) == 0
+
+    def body(i):
+        cum, cum_t, row, column = chunk_decays(decay_ref[i])
+        later = column >= row
+        q = cum.shape[0]
+        total = cum[q - 1 : q, :]
+        b, c = b_ref[i], c_ref[i]
+        x = x_ref[i].astype(F32)
+        step_wide = spread(step_ref[i], expand)
+        yield
+        xs = (x * step_wide).astype(BF16)
+        grown = spread(jnp.exp(cum), expand)
+        waned = spread(jnp.exp(total - cum), expand)
+        yield
+        xw = (x * step_wide * waned).astype(BF16)
+        dy = dy_ref[i]
+        dy_low = dy.astype(BF16)
+        edy = (dy * grown).astype(BF16)
+        before = in_ref[i, 0]
+        after_grad = grad[i]
+        after_low = after_grad.astype(BF16)
+        yield
+        scores_t = dot(b, c, ((1,), (1,)))
+        v_state = waned * dot(b, after_low)
+        dscores_t = jnp.zeros((q, q), F32)
+        v_parts = []
+        yield
+        for pair in range(heads // 2):
+            lanes = slice(pair * 2 * width, (pair + 1) * 2 * width)
+            dy_pair = pair_rows(dy_low[:, lanes])
+            xs_pair = pair_rows(xs[:, lanes])
+            dmix = dot(xs_pair, dy_low[:, lanes], ((1,), (1,)))
+            mixing = []
+            for k, h in enumerate((2 * pair, 2 * pair + 1)):
+                between = cum_t[h : h + 1, :] - cum[:, h : h + 1]
+                fade = jnp.exp(jnp.where(later, between, -1e30))
+                mixing.append((fade * scores_t).astype(BF16))
+                dscores_t = dscores_t + fade * dmix[k * q : (k + 1) * q]
+            v_parts.append(dot(jnp.concatenate(mixing, axis=1), dy_pair))
+            yield
+        v = jnp.concatenate(v_parts, axis=1) + v_state
+        xs_wide = xs.astype(F32)
+        etotal = grown[q - 1 : q, :]
+        end_row = jnp.sum(xs_wide * v_state, axis=0, keepdims=True) + jnp.sum(
+            etotal * before * after_grad, axis=0, keepdims=True
+        )
+        crossing = dy_low.astype(F32) * y_ref[i] - xs_wide * v
+        last = lax.broadcasted_iota(jnp.int32, crossing.shape, 0) == q - 1
+        crossing = crossing + jnp.where(last, end_row, 0.0)
+        upper = jnp.where(column >= row, 1.0, 0.0).astype(F32)
+        yield
+        decay_grad = dot(upper, head_sums(crossing, expand), precision=HIGHEST_PREC)
+        pre_grad = (head_sums(x * v, expand) - rate_ref[...] * decay_grad) * slope_ref[i]
+        pre_ref[i] = pre_grad.astype(BF16)
+        sums = [
+            jnp.sum(decay_grad * decay_ref[i], axis=0, keepdims=True),
+            jnp.sum(pre_grad, axis=0, keepdims=True),
+            jnp.sum(head_sums(x * dy, expand), axis=0, keepdims=True),
+            jnp.zeros((5, heads), F32),
+        ]
+        head_sums_ref[...] += jnp.concatenate(sums, axis=0)
+        yield
+        dscores_low = dscores_t.astype(BF16)
+        state = b.shape[1]
+        dbc_ref[i, :, :state] = (
+            dot(dscores_low, c) + dot(xw, after_low, ((1,), (1,)))
+        ).astype(BF16)
+        dbc_ref[i, :, state:] = (
+            dot(dscores_low, b, ((0,), (0,))) + dot(edy, before.astype(BF16), ((1,), (1,)))
+        ).astype(BF16)
+        grad[i] = etotal * after_grad + dot(c, edy, ((0,), (0,)))
+        yield
+        dx = step_wide * v + skip_ref[0] * dy
+        previous = rows_before(edge_ref, previous_ref, i, pl.num_programs(1) - 1)
+        conv_grad, mixed_grad, tap_sums = conv_back_step(
+            dx, mixed_ref[i].astype(F32), previous, taps_ref[...], after[i]
+        )
+        mixed_grad_ref[i] = mixed_grad.astype(BF16)
+        first_ref[i] = conv_grad[:8]
+        after[i] = conv_grad[:8]
+        last_ref[i] = jnp.where(last_chunk, mixed_grad[q - 8 :], last_ref[i])
+        tap_sums_ref[...] += tap_sums
+
+    alternately(body(i) for i in range(group))
 
 
 def act_blocks(inner, state, place):
     def part(lanes, at):
-        return pl.BlockSpec((1, CHUNK, lanes), lambda s, k: (s, place(k), at))
+        return pl.BlockSpec((GROUP, CHUNK, lanes), lambda s, k: (s, place(k), at))
 
     return [part(inner, 0), part(state, inner // state), part(state, inner // state + 1)]
 
@@ -337,41 +357,48 @@
     mixed_ref, previous_ref, edge_ref, taps_ref, step_ref, decay_ref, act_ref, packed_ref, state, total
 ):
     chunk = pl.program_id(1)
+    group, _, heads = step_ref.shape
+    state_width, inner = state.shape[1:]
 
     @pl.when(chunk == 0)
     def _():
         state[...] = jnp.zeros_like(state)
         total[...] = jnp.zeros_like(total)
 
-    previous = jnp.where(
-        chunk == 0, edge_ref[0].astype(F32), previous_ref[0].astype(F32)
-    )[8:]
-    convolved = taps_ref[CONV : CONV + 1]
-    for k, part in enumerate(conv_windows(mixed_ref[0].astype(F32), previous)):
-        convolved = convolved + taps_ref[k : k + 1] * part
-    activated = jax.nn.silu(convolved).astype(BF16)
-    act_ref[0] = activated
-    heads, (state_width, inner) = step_ref.shape[2], state.shape
     expand = expander(heads, inner // heads)
-    cum = chunk_decays(decay_ref[0])[0]
-    q = cum.shape[0]
-    last = cum[q - 1 : q, :]
-    weights = spread(step_ref[0] * jnp.exp(last - cum), expand)
-    xw = (activated[:, :inner].astype(F32) * weights).astype(BF16)
-    b = activated[:, inner : inner + state_width]
-    kept = spread(jnp.exp(cum), expand)[q - 1 : q]
-    state[...] = kept * state[...] + dot(b, xw, ((0,), (0,)))
-    total[...] = total[...] + last
+
+    def body(i):
+        previous = rows_before(edge_ref, previous_ref, i, 0)
+        cum = chunk_decays(decay_ref[i])[0]
+        q = cum.shape[0]
+        last = cum[q - 1 : q, :]
+        yield
+        weights = spread(step_ref[i] * jnp.exp(last - cum), expand)
+        kept = spread(jnp.exp(cum), expand)[q - 1 : q]
+        yield
+        convolved = taps_ref[CONV : CONV + 1]
+        for k, part in enumerate(conv_windows(mixed_ref[i].astype(F32), previous)):
+            convolved = convolved + taps_ref[k : k + 1] * part
+        activated = jax.nn.silu(convolved).astype(BF16)
+        act_ref[i] = activated
+        yield
+        xw = (activated[:, :inner].astype(F32) * weights).astype(BF16)
+        b = activated[:, inner : inner + state_width]
+        state[i] = kept * state[i] + dot(b, xw, ((0,), (0,)))
+        total[i] = total[i] + last
+
+    alternately(body(i) for i in range(group))
 
     @pl.when(chunk == pl.num_programs(1) - 1)
     def _():
-        decay = spread(jnp.exp(jnp.broadcast_to(total[...], (8, heads))), expand)[:1]
-        high = decay.astype(BF16).astype(F32)
-        tail = jnp.concatenate([high, decay - high, jnp.zeros((14, inner), F32)], axis=0)
         height = packed_ref.shape[2] - 16
-        for part in range(packed_ref.shape[1]):
-            rows = state[part * height : (part + 1) * height]
-            packed_ref[0, part] = jnp.concatenate([rows, tail], axis=0).astype(BF16)
+        for i in range(group):
+            decay = spread(jnp.exp(jnp.broadcast_to(total[i], (8, heads))), expand)[:1]
+            high = decay.astype(BF16).astype(F32)
+            tail = jnp.concatenate([high, decay - high, jnp.zeros((14, inner), F32)], axis=0)
+            for part in range(packed_ref.shape[1]):
+                rows = state[i, part * height : (part + 1) * height]
+                packed_ref[i, part] = jnp.concatenate([rows, tail], axis=0).astype(BF16)
 
 
 def conv_forward(mixed, edge, taps, step, decay, state, parts):
@@ -381,28 +408,28 @@
     height = state // parts + 16
 
     def block(width):
-        return pl.BlockSpec((1, CHUNK, width), lambda s, k: (s, k, 0))
+        return pl.BlockSpec((GROUP, CHUNK, width), lambda s, k: (s, k, 0))
 
     return pl.pallas_call(
         first_kernel,
-        grid=(seqs, chunks),
+        grid=(seqs // GROUP, chunks),
         in_specs=[
             block(lanes),
-            pl.BlockSpec((1, 16, lanes), lambda s, k: (s, jnp.maximum(k * tall - 1, 0), 0)),
-            pl.BlockSpec((1, 16, lanes), lambda s, k: (s, 0, 0)),
+            pl.BlockSpec((GROUP, 16, lanes), lambda s, k: (s, jnp.maximum(k * tall - 1, 0), 0)),
+            pl.BlockSpec((GROUP, 16, lanes), lambda s, k: (s, 0, 0)),
             pl.BlockSpec((8, lanes), lambda s, k: (0, 0)),
             block(heads),
             block(heads),
         ],
         out_specs=[
             block(lanes),
-            pl.BlockSpec((1, parts, height, inner), lambda s, k: (s, 0, 0, 0)),
+            pl.BlockSpec((GROUP, parts, height, inner), lambda s, k: (s, 0, 0, 0)),
         ],
         out_shape=[
             jax.ShapeDtypeStruct(mixed.shape, BF16),
             jax.ShapeDtypeStruct((seqs, parts, height, inner), BF16),
         ],
-        scratch_shapes=[pltpu.VMEM((state, inner), F32), pltpu.VMEM((1, heads), F32)],
+        scratch_shapes=[pltpu.VMEM((GROUP, state, inner), F32), pltpu.VMEM((GROUP, 1, heads), F32)],
         compiler_params=pltpu.CompilerParams(vmem_limit_bytes=40 << 20),
         cost_estimate=load(9),
     )(mixed, mixed, edge, taps, step, decay)
@@ -414,26 +441,26 @@
     chunks = length // CHUNK
 
     def block(lanes):
-        return pl.BlockSpec((1, CHUNK, lanes), lambda s, k: (s, k, 0))
+        return pl.BlockSpec((GROUP, CHUNK, lanes), lambda s, k: (s, k, 0))
 
     return pl.pallas_call(
         scan_kernel,
-        grid=(seqs, chunks),
+        grid=(seqs // GROUP, chunks),
         in_specs=act_blocks(inner, state, lambda k: k)
         + [
             block(heads),
             block(heads),
-            pl.BlockSpec((1, state, inner), lambda s, k: (s, 0, 0)),
+            pl.BlockSpec((GROUP, state, inner), lambda s, k: (s, 0, 0)),
         ],
         out_specs=[
             block(inner),
-            pl.BlockSpec((1, 1, state, inner), lambda s, k: (s, k, 0, 0)),
+            pl.BlockSpec((GROUP, 1, state, inner), lambda s, k: (s, k, 0, 0)),
         ],
         out_shape=[
             jax.ShapeDtypeStruct((seqs, length, inner), F32),
             jax.ShapeDtypeStruct((seqs, chunks, state, inner), F32),
         ],
-        scratch_shapes=[pltpu.VMEM((state, inner), F32)],
+        scratch_shapes=[pltpu.VMEM((GROUP, state, inner), F32)],
         compiler_params=pltpu.CompilerParams(vmem_limit_bytes=40 << 20),
         cost_estimate=load(13),
     )(activated, activated, activated, step, decay, enter)
@@ -442,20 +469,20 @@
 def conv_blocks(chunks, lanes, at):
     tall = CHUNK // 16
     return [
-        pl.BlockSpec((1, CHUNK, lanes), lambda s, k, *_: (s, chunks - 1 - k, at)),
+        pl.BlockSpec((GROUP, CHUNK, lanes), lambda s, k, *_: (s, chunks - 1 - k, at)),
         pl.BlockSpec(
-            (1, 16, lanes), lambda s, k, *_: (s, jnp.maximum((chunks - 1 - k) * tall - 1, 0), at)
+            (GROUP, 16, lanes), lambda s, k, *_: (s, jnp.maximum((chunks - 1 - k) * tall - 1, 0), at)
         ),
-        pl.BlockSpec((1, 16, lanes), lambda s, k, *_: (s, 0, at)),
+        pl.BlockSpec((GROUP, 16, lanes), lambda s, k, *_: (s, 0, at)),
         pl.BlockSpec((8, lanes), lambda s, k, *_: (0, at)),
     ]
 
 
 def conv_outs(seqs, chunks, lanes):
     specs = [
-        pl.BlockSpec((1, CHUNK, lanes), lambda s, k, *_: (s, chunks - 1 - k, 0)),
-        pl.BlockSpec((1, 8, lanes), lambda s, k, *_: (s, 0, 0)),
-        pl.BlockSpec((1, 8, lanes), lambda s, k, *_: (s, 0, 0)),
+        pl.BlockSpec((GROUP, CHUNK, lanes), lambda s, k, *_: (s, chunks - 1 - k, 0)),
+        pl.BlockSpec((GROUP, 8, lanes), lambda s, k, *_: (s, 0, 0)),
+        pl.BlockSpec((GROUP, 8, lanes), lambda s, k, *_: (s, 0, 0)),
         pl.BlockSpec((8, lanes), lambda s, k, *_: (0, 0)),
     ]
     shapes = [
@@ -475,12 +502,12 @@
     chunks = length // CHUNK
 
     def block(lanes):
-        return pl.BlockSpec((1, CHUNK, lanes), lambda s, k: (s, chunks - 1 - k, 0))
+        return pl.BlockSpec((GROUP, CHUNK, lanes), lambda s, k: (s, chunks - 1 - k, 0))
 
     conv_specs, conv_shapes = conv_outs(seqs, chunks, inner)
     return pl.pallas_call(
         back_kernel,
-        grid=(seqs, chunks),
+        grid=(seqs // GROUP, chunks),
         in_specs=act_blocks(inner, state, lambda k: chunks - 1 - k)
         + [
             block(heads),
@@ -488,8 +515,8 @@
             pl.BlockSpec((1, 1, inner), lambda s, k: (0, 0, 0)),
             block(inner),
             block(inner),
-            pl.BlockSpec((1, 1, state, inner), lambda s, k: (s, chunks - 1 - k, 0, 0)),
-            pl.BlockSpec((1, state, inner), lambda s, k: (s, 0, 0)),
+            pl.BlockSpec((GROUP, 1, state, inner), lambda s, k: (s, chunks - 1 - k, 0, 0)),
+            pl.BlockSpec((GROUP, state, inner), lambda s, k: (s, 0, 0)),
         ]
         + conv_blocks(chunks, inner, 0)
         + [block(heads), pl.BlockSpec((1, heads), lambda s, k: (0, 0))],
@@ -503,7 +530,7 @@
         ]
         + conv_shapes[1:]
         + [jax.ShapeDtypeStruct((8, heads), F32)],
-        scratch_shapes=[pltpu.VMEM((state, inner), F32), pltpu.VMEM((8, inner), F32)],
+        scratch_shapes=[pltpu.VMEM((GROUP, state, inner), F32), pltpu.VMEM((GROUP, 8, inner), F32)],
         compiler_params=pltpu.CompilerParams(vmem_limit_bytes=40 << 20),
         cost_estimate=load(30),
     )(
@@ -516,44 +543,50 @@
     scalars_ref, part_ref, got_ref, mixed_ref, previous_ref, edge_ref, taps_ref,
     mixed_grad_ref, first_ref, last_ref, tap_sums_ref, after
 ):
-    start = (pl.program_id(0) == 0) & (pl.program_id(1) == 0)
+    group, q, _ = mixed_ref.shape
+    last_chunk = pl.program_id(1) == 0
+    start = (pl.program_id(0) == 0) & last_chunk
 
     @pl.when(start)
     def _():
         tap_sums_ref[...] = jnp.zeros_like(tap_sums_ref)
 
-    @pl.when(pl.program_id(1) == 0)
+    @pl.when(last_chunk)
     def _():
         after[...] = jnp.zeros_like(after)
 
-    q = mixed_ref.shape[1]
-    act_grad = picked(scalars_ref, part_ref, got_ref)[0]
-    conv_grad, mixed_grad, tap_sums = conv_back_step(
-        act_grad, mixed_ref[0].astype(F32), rows_before(edge_ref, previous_ref), taps_ref[...], after
-    )
-    mixed_grad_ref[0] = mixed_grad.astype(BF16)
-    first_ref[0] = conv_grad[:8]
-
-    @pl.when(pl.program_id(1) == 0)
-    def _():
-        last_ref[0] = mixed_grad[q - 8 :]
-
-    tap_sums_ref[...] += tap_sums
+    act_grad = picked(scalars_ref, part_ref, got_ref)
+
+    def body(i):
+        previous = rows_before(edge_ref, previous_ref, i, pl.num_programs(1) - 1)
+        yield
+        conv_grad, mixed_grad, tap_sums = conv_back_step(
+            act_grad[i], mixed_ref[i].astype(F32), previous, taps_ref[...], after[i]
+        )
+        mixed_grad_ref[i] = mixed_grad.astype(BF16)
+        first_ref[i] = conv_grad[:8]
+        after[i] = conv_grad[:8]
+        last_ref[i] = jnp.where(last_chunk, mixed_grad[q - 8 :], last_ref[i])
+        tap_sums_ref[...] += tap_sums
+
+    alternately(body(i) for i in range(group))
 
 
 def bc_backward(scalars, part, got, mixed, edge, taps):
-    seqs, length, lanes = mixed.shape
-    chunks = length // CHUNK
-    half = pl.BlockSpec((1, CHUNK, lanes), lambda s, k, _: (s % (seqs // 2), chunks - 1 - k, 0))
+    seqs, length, _ = mixed.shape
+    lanes = part.shape[1]
+    chunks, at = length // CHUNK, mixed.shape[2] // lanes - 1
+    halves = seqs // 2 // GROUP
+    half = pl.BlockSpec((GROUP, CHUNK, lanes), lambda s, k, _: (s % halves, chunks - 1 - k, 0))
     conv_specs, conv_shapes = conv_outs(seqs, chunks, lanes)
     return pl.pallas_call(
         bc_kernel,
         grid_spec=pltpu.PrefetchScalarGridSpec(
             num_scalar_prefetch=1,
-            grid=(seqs, chunks),
-            in_specs=[half, half] + conv_blocks(chunks, lanes, 0),
+            grid=(seqs // GROUP, chunks),
+            in_specs=[half, half] + conv_blocks(chunks, lanes, at),
             out_specs=conv_specs,
-            scratch_shapes=[pltpu.VMEM((8, lanes), F32)],
+            scratch_shapes=[pltpu.VMEM((GROUP, 8, lanes), F32)],
         ),
         out_shape=conv_shapes,
         compiler_params=pltpu.CompilerParams(vmem_limit_bytes=40 << 20),
@@ -860,8 +893,9 @@
     early_all = lax.all_gather(early_own, "seq")
     bc_sum = halved(bc_grad.reshape(rows, 2 * state_width), "head")
     x_in_grad = joined_edges(x_raw, x_first, x_last, conv_weight[:, :local_inner])
-    x_in_grad, bc_sum = lax.optimization_barrier((x_in_grad, bc_sum))
     bc_far = swapped(bc_sum, "head", axis_masks("head")[-1])
+    x_in_grad, bc_added = lax.optimization_barrier((x_in_grad, added(bc_sum, bc_far)))
+    bc_half, bc_other = regathered(bc_added, "head")
     normed_partial = normed_products(
         gate_grad.reshape(rows, local_inner),
         x_in_grad.reshape(rows, local_inner),
@@ -872,25 +906,23 @@
     )
     x_weight_grad = jnp.einsum("btd,btc->dc", normed, x_in_grad, preferred_element_type=F32)
     normed_sum = halved(normed_partial, "head")
-    bc_added = added(bc_sum, bc_far)
-    normed_sum, bc_added = lax.optimization_barrier((normed_sum, bc_added))
-    bc_half, bc_other = regathered(bc_added, "head")
-    x_blocks, _ = lax.optimization_barrier((to_blocks(x_weight_grad, seq_size), normed_sum))
+    x_blocks, bc_other, _ = lax.optimization_barrier(
+        (to_blocks(x_weight_grad, seq_size), bc_other, normed_sum)
+    )
     x_parts = exchanged(x_blocks, "seq")
     normed_far = swapped(normed_sum, "head", axis_masks("head")[-1])
 
     scalars = jnp.concatenate(
         [lengths, jnp.stack([seq_index * local_len, near_bit("head", 1)]).astype(jnp.int32)]
     )
-    bc_half, early_all, _ = lax.optimization_barrier((bc_half, early_all, normed_sum))
     early_sums = early_all.reshape(2, model_width, local_inner)
     bc_raw_grad, bc_first, bc_last, bc_tap_sums = bc_backward(
         scalars,
         bc_half,
         bc_other,
-        mixed_in[..., local_inner:],
-        edge_rows[..., local_inner:],
-        taps[:, local_inner:],
+        mixed_in,
+        edge_rows,
+        taps,
     )
     bc_in_grad = joined_edges(bc_raw_grad, bc_first, bc_last, conv_weight[:, local_inner:])
     bc_in_grad, x_parts = lax.optimization_barrier((bc_in_grad, x_parts))
@@ -951,7 +983,7 @@
     )
     input_grad = input_grad.reshape(inputs.shape)
     bc_own = jnp.sum(bc_parts.astype(F32), axis=0).astype(BF16)
-    bc_all = lax.all_gather(bc_own, "seq")
+    bc_all = exchanged(jnp.broadcast_to(bc_own[None], bc_parts.shape), "seq")
     step_weight_grad = jnp.einsum("btd,bth->hd", normed, step_in_grad, preferred_element_type=F32)
     conv_inner_grad = x_tap_sums[: CONV + 1]
     conv_bc_grad = bc_tap_sums[: CONV + 1]

time: 463 us -> 444 us (0.959)
  blocking collectives: 42.6 us -> 10.7 us
  waiting for transfers between devices: 53.5 us -> 66.1 us
  Pallas kernels: 113 us -> 103 us
  starting transfers between devices: 50.6 us -> 57.7 us
    all_gather x1 -> x0, blocking collectives: 31.9 us -> none  [shards(): bc_all = lax.all_gather(bc_own, 'seq')]
    all_gather x1, waiting for transfers between devices: 0.01 us -> 15.4 us  [shards(): early_all = lax.all_gather(early_own, 'seq')]
    ppermute x12, waiting for transfers between devices: 20.1 us -> 12 us  [swapped(): lax.ppermute(block, axis, [(i, i ^ mask) for i in range(lax.axis_size(axi...]
    pallas_call x3, Pallas kernels: 66 us -> 58.8 us  [the longest x1 33.5 us: scan_backward(): pl.pallas_call(back_kernel, grid=(seqs // GROUP, chunks), in_specs=act_bl...]
    all_to_all x7 -> x8, waiting for transfers between devices: 32.9 us -> 38.6 us  [exchanged(): return lax.all_to_all(blocks, axis, 0, 0, tiled=True)]
    unnamed x215 -> x213, local copies, waits for them, and re-layouts: 37.8 us -> 42.6 us
    all_to_all x7 -> x8, starting transfers between devices: 35.8 us -> 39.2 us  [exchanged(): return lax.all_to_all(blocks, axis, 0, 0, tiled=True)]
  transfers between devices with their start and end apart: 24 -> 25, of which waited for: 8 -> 9; matrix products, arithmetic and copies ran while one was open for 21% -> 21% of each run, Pallas kernels for 18% -> 18%
where the time goes in v6:
time: 444 us; the launch traced here: 436 us
  Pallas kernels  103 us (23%)
  waiting for transfers between devices  66.1 us (15%)
  matrix products  63.6 us (14%)
  local copies, waits for them, and re-layouts  62.4 us (14%)
  starting transfers between devices  57.7 us (13%)
  other arithmetic  56.8 us (13%)
  between operations  15.7 us (4%)
  blocking collectives  10.7 us (2%)
    unnamed x213, local copies, waits for them, and re-layouts  42.6 us
    all_to_all x8, starting transfers between devices, exchanged(): return lax.all_to_all(blocks, axis, 0, 0, tiled=True)  39.2 us
    all_to_all x8, waiting for transfers between devices, exchanged(): return lax.all_to_all(blocks, axis, 0, 0, tiled=True)  38.6 us
    pallas_call x1, Pallas kernels, scan_backward(): pl.pallas_call(back_kernel, grid=(seqs // GROUP, chunks), in_specs=act_bl...  33.5 us
    pallas_call x2, Pallas kernels, merge_call(): pl.pallas_call(kernel, grid_spec=pltpu.PrefetchScalarGridSpec(num_scalar_...  20 us
    all_gather x1, waiting for transfers between devices, shards(): early_all = lax.all_gather(early_own, 'seq')  15.4 us
    sub x8, other arithmetic, adam_update(): weight - step_rate * (corrected_mean / (jnp.sqrt(corrected_square) + ADAM...  14.7 us
    convert_element_type x6, other arithmetic, added(): return (a.astype(F32) + b.astype(F32)).astype(BF16)  14 us
  transfers between devices with their start and end apart: 25, of which 9 were waited for; matrix products, arithmetic and copies ran while one was open for 21% of the time, Pallas kernels for 18%

profile of v6, /device:TPU:0, one launch (start us, length us, event | category | flops | bytes accessed | tf_op | source)
XLA Modules:
  0.0 435.7 jit_solution(16544824509453945148)
XLA Ops:
  7.2 3.2 fusion
  13.8 2.0 copy-done.4
  15.7 3.7 convolution_convert_fusion.mixed_ref.previous_ref
  19.5 1.7 copy-done
  21.2 4.9 %collective-permute-start = (bf16[4,3,768]{2,1,0:T(4,128)(2,1)S(1)}, bf16[4,3,768]{2,1,0:T(4,128)(2,1)S(1)}, u32[]{:S(2)}, u32[]{:S(2)}) collective-permute-start(bf16[4,3,768]{2,1,0:T(4,128)(2,1)S(1)} %slice.274), channel_id=1, source_target_pairs={{0,4},{4,8},{8,12},{12,16},{16,20},{20,24},{24,28},{1,5},{5,9},{9,... | collective-permute-start | bytes 55304 | tf_op jit(solution)/shard_map/ppermute | solution.py:31
  27.1 5.6 %add_divide_fusion.1 = (f32[4,512,8]{2,1,0:T(8,128)}, f32[4,512,8]{2,1,0:T(8,128)S(1)}, f32[4,512,8]{2,1,0:T(8,128)S(1)}, f32[4,512,8]{2,1,0:T(8,128)}) fusion(f32[8]{0:T(128)S(1)} %get-tuple-element.172, f32[8]{0:T(128)S(1)} %get-tuple-element.173, bf16[1024,8]{1,0:T(8,128)(2,1)S(1)} %copy.114.step_weight_ref, bf16[4,512,1024]{2,1,0:T(8,128)(2,1)} %param.30, ...), kind=kOutput, calls=%fused_computation.71 | convolution fusion | flops 42139648 | bytes 4485184 | tf_op jit(solution)/shard_map/btd,dh->bth/dot_general | solution.py:817
  32.8 12.4 %shard_map.509 = (bf16[4,512,768]{2,1,0:T(8,128)(2,1)S(1)}, bf16[4,2,80,512]{3,2,1,0:T(8,128)(2,1)S(1)}) custom-call(bf16[4,512,768]{2,1,0:T(8,128)(2,1)S(1)} %copy-done.1, bf16[4,512,768]{2,1,0:T(8,128)(2,1)S(1)} %copy-done.1, bf16[4,16,768]{2,1,0:T(8,128)(2,1)S(1)} %pad.20.edge_ref, f32[8,768]{1,0:T(8,128)S(1)} %select_maximum_fusion.taps_ref, ...), custom_call_target="tpu_custom_call" | custom-call | bytes 33210000 | tf_op jit(solution)/shard_map/pallas_call | solution.py:413
  46.1 4.9 %all-to-all-start = ((bf16[8,80,512]{2,1,0:T(8,128)(2,1)}), bf16[8,80,512]{2,1,0:T(8,128)(2,1)}, u32[]{:S(2)}, u32[]{:S(2)}) async-start(bf16[8,80,512]{2,1,0:T(8,128)(2,1)} %bitcast.206), calls=%async_computation | async-start | bytes 1310720 | tf_op jit(solution)/shard_map/all_to_all | solution.py:87
  51.6 16.5 %all-to-all-done = bf16[8,80,512]{2,1,0:T(8,128)(2,1)} async-done(((bf16[8,80,512]{2,1,0:T(8,128)(2,1)}), bf16[8,80,512]{2,1,0:T(8,128)(2,1)}, u32[]{:S(2)}, u32[]{:S(2)}) %all-to-all-start) | async-done | bytes 655392 | tf_op jit(solution)/shard_map/all_to_all | solution.py:87
  74.6 4.6 %all-to-all-start.1 = ((bf16[8,64,512]{2,1,0:T(8,128)(2,1)}), bf16[8,64,512]{2,1,0:T(8,128)(2,1)}, u32[]{:S(2)}, u32[]{:S(2)}) async-start(bf16[8,64,512]{2,1,0:T(8,128)(2,1)} %fusion.48), calls=%async_computation.1 | async-start | bytes 1048576 | tf_op jit(solution)/shard_map/all_to_all | solution.py:87
  84.1 5.6 %fusion.20 = f32[4,512,8]{1,2,0:T(8,128)} fusion(f32[8]{0:T(128)} %copy-done.101, f32[4,512,8]{2,1,0:T(8,128)} %get-tuple-element.175), kind=kOutput, calls=%fused_computation.56 | convolution fusion | flops 101318656 | bytes 131104 | tf_op jit(solution)/shard_map/ts,bsh->bth/dot_general | solution.py:836
  89.7 3.8 all-to-all-done.1
  96.0 12.8 %shard_map.510 = (f32[4,512,512]{2,1,0:T(8,128)S(1)}, f32[4,4,128,512]{3,2,1,0:T(8,128)S(1)}) custom-call(bf16[4,512,768]{2,1,0:T(8,128)(2,1)S(1)} %get-tuple-element.66.x_ref.b_ref.c_ref, bf16[4,512,768]{2,1,0:T(8,128)(2,1)S(1)} %get-tuple-element.66.x_ref.b_ref.c_ref, bf16[4,512,768]{2,1,0:T(8,128)(2,1)S(1)} %get-tuple-element.66.x_ref.b_ref.c_ref, ...), custom_call_target="tpu_custom_call" | custom-call | bytes 47970000 | tf_op jit(solution)/shard_map/pallas_call | solution.py:446
  108.9 2.0 copy-done.22
  110.9 5.1 %multiply_reduce_fusion.2 = (f32[4,512]{1,0:T(4,128)S(1)}, f32[4,512,512]{2,1,0:T(8,128)S(1)}, f32[4,512,512]{2,1,0:T(8,128)}) fusion(f32[4,512,512]{2,1,0:T(8,128)S(1)} %get-tuple-element.68.y_ref, bf16[4,512,768]{2,1,0:T(8,128)(2,1)S(1)} %get-tuple-element.66.x_ref.b_ref.c_ref, f32[512]{0:T(512)S(1)} %copy-done.99, ...), kind=kOutput, calls=%fused_computation.20 | convolution fusion | flops 2166355968 | bytes 19945472 | tf_op jit(solution)/shard_map/btd,dc->btc/dot_general | solution.py:818
  116.6 4.4 %fusion.90 = (bf16[4,512,1024]{2,1,0:T(8,128)(2,1)}, f32[4,512]{1,0:T(4,128)S(1)}) fusion(f32[4,512]{1,0:T(4,128)S(1)} %copy-done.87, bf16[4,512,1024]{2,1,0:T(8,128)(2,1)S(1)} %copy-done.17, f32[1024,512]{1,0:T(8,128)S(1)} %copy-done.55, f32[4,512,512]{2,1,0:T(8,128)S(1)} %get-tuple-element.132, f32[512]{0:T(512)S(1)} %copy-done.95), kind=kOutput, calls=%fused_computation.189 | convolution fusion | flops 2160588800 | bytes 14698496 | tf_op jit(solution)/shard_map/bti,di->btd/dot_general | solution.py:845
  121.7 10.7 %psum.7 = f32[2,4,512]{2,1,0:T(4,128)S(1)} all-reduce(f32[2,4,512]{2,1,0:T(4,128)} %pad_maximum_fusion.2), channel_id=1, replica_groups=mesh['seq'=8,'head'=4] {'head'}, use_global_device_ids=true, to_apply=%region_3.4 | all-reduce | flops 4096 | bytes 32768 | tf_op jit(solution)/shard_map/psum | solution.py:848
  133.0 10.5 %fusion.15 = (f32[4,512,512]{2,1,0:T(8,128)S(1)}, bf16[4,512,512]{2,1,0:T(8,128)(2,1)}, f32[512]{0:T(512)}) fusion(f32[4,512,512]{2,1,0:T(8,128)} %copy-done.102, f32[4,512]{1,0:T(4,128)S(1)} %fusion.55, f32[512]{0:T(512)} %param.54, f32[4,512,512]{2,1,0:T(8,128)} %get-tuple-element.176, f32[4,512,512]{2,1,0:T(8,128)} %copy-done.21, ...), kind=kOutput, calls=%fused_computation.52 | convolution fusion | flops 2177367552 | bytes 27293696 | tf_op jit(solution)/shard_map/btd,di->bti/dot_general | solution.py:853
  143.5 3.9 multiply_convert_fusion.1
  148.7 5.0 %all-to-all-start.2 = ((bf16[8,64,512]{2,1,0:T(8,128)(2,1)}), bf16[8,64,512]{2,1,0:T(8,128)(2,1)}, u32[]{:S(2)}, u32[]{:S(2)}) async-start(bf16[8,64,512]{2,1,0:T(8,128)(2,1)} %bitcast.220), calls=%async_computation.2 | async-start | bytes 1048576 | tf_op jit(solution)/shard_map/all_to_all | solution.py:87
  153.7 3.2 dynamic-slice_bitcast_fusion.1
  157.1 6.2 %bitcast_convert_fusion.2 = bf16[1024,512]{1,0:T(8,128)(2,1)} fusion(bf16[4,512,1024]{2,1,0:T(8,128)(2,1)S(1)} %copy-done.18, f32[4,512]{1,0:T(4,128)} %copy-done.83, f32[4,512]{1,0:T(4,128)} %compare_convert_fusion, f32[4,512,512]{2,1,0:T(8,128)} %copy-done.102, f32[512]{0:T(512)} %param.54), kind=kOutput, calls=%fused_computation.38 | convolution fusion | flops 2158493696 | bytes 9455616 | tf_op jit(solution)/shard_map/btd,bti->di/dot_general | solution.py:852
  163.3 4.2 all-to-all-done.2
  174.7 4.2 all-to-all-start.3
  178.8 5.5 %bitcast_convert_fusion.1 = bf16[1024,512]{1,0:T(8,128)(2,1)S(1)} fusion(bf16[4,512,512]{2,1,0:T(8,128)(2,1)} %get-tuple-element.140, bf16[4,512,1024]{2,1,0:T(8,128)(2,1)} %param.30, f32[1024]{0:T(1024)S(1)} %copy-done.43, f32[4,512]{1,0:T(4,128)} %copy-done.84), kind=kOutput, calls=%fused_computation.37 | convolution fusion | flops 2156396544 | bytes 7352320 | tf_op jit(solution)/shard_map/btd,btc->dc/dot_general | solution.py:868
  187.3 3.9 fusion.4
  192.2 4.8 %all-to-all-start.4 = ((bf16[8,256,512]{2,1,0:T(8,128)(2,1)}), bf16[8,256,512]{2,1,0:T(8,128)(2,1)}, u32[]{:S(2)}, u32[]{:S(2)}) async-start(bf16[8,256,512]{2,1,0:T(8,128)(2,1)} %bitcast.213), calls=%async_computation.4 | async-start | bytes 4194304 | tf_op jit(solution)/shard_map/all_to_all | solution.py:87
  197.9 1.9 copy-done.2
  204.2 33.5 %shard_map.511 = (bf16[4,512,512]{2,1,0:T(8,128)(2,1)S(1)}, bf16[4,512,256]{2,1,0:T(8,128)(2,1)S(1)}, bf16[4,512,8]{2,1,0:T(8,128)(2,1)S(1)}, f32[4,8,512]{2,1,0...) custom-call(bf16[4,512,768]{2,1,0:T(8,128)(2,1)S(1)} %get-tuple-element.66.x_ref.b_ref.c_ref, ...), custom_call_target="tpu_custom_call" | custom-call | bytes 110700000 | tf_op jit(solution)/shard_map/pallas_call | solution.py:508
  239.1 1.9 collective-permute-done.4
  245.6 9.6 %collective-permute-done.5 = bf16[1024,256]{1,0:T(8,128)(2,1)S(1)} collective-permute-done((bf16[1024,256]{1,0:T(8,128)(2,1)S(1)}, bf16[1024,256]{1,0:T(8,128)(2,1)S(1)}, u32[]{:S(2)}, u32[]{:S(2)}) %collective-permute-start.5) | collective-permute-done | bytes 524320 | tf_op jit(solution)/shard_map/ppermute | solution.py:35
  257.6 2.7 reduce_sum.75
  260.3 1.6 copy-done.28
  261.9 1.6 copy-done.30
  263.5 7.0 %shard_map.512 = bf16[2048,1024]{1,0:T(8,128)(2,1)S(1)} custom-call(bf16[2048,512]{1,0:T(8,128)(2,1)S(1)} %bitcast.201, bf16[2048,512]{1,0:T(8,128)(2,1)S(1)} %bitcast.202, bf16[2048,8]{1,0:T(8,128)(2,1)S(1)} %bitcast.207, bf16[1024,512]{1,0:T(8,128)(2,1)S(1)} %copy-done.23, bf16[1024,512]{1,0:T(8,128)(2,1)S(1)} %copy-done.25, ...), custom_call_target="tpu_custom_call" | custom-call | bytes 22140000 | tf_op jit(solution)/shard_map/pallas_call | solution.py:630
  272.1 4.1 add_convert_fusion.1.part_ref
  276.8 3.5 bitcast_convert_fusion
  280.3 2.3 fusion.3
  283.4 5.9 %all-to-all-start.5 = ((bf16[8,128,512]{2,1,0:T(8,128)(2,1)}), bf16[8,128,512]{2,1,0:T(8,128)(2,1)}, u32[]{:S(2)}, u32[]{:S(2)}) async-start(bf16[8,128,512]{2,1,0:T(8,128)(2,1)} %bitcast.221), calls=%async_computation.5 | async-start | bytes 2097152 | tf_op jit(solution)/shard_map/all_to_all | solution.py:87
  291.8 7.3 %shard_map.514 = (bf16[4,512,256]{2,1,0:T(8,128)(2,1)S(1)}, f32[4,8,256]{2,1,0:T(8,128)S(1)}, f32[4,8,256]{2,1,0:T(8,128)S(1)}, f32[8,256]{1,0:T(8,128)S(1)}) custom-call(s32[6]{0:T(128)S(1)} %pad_add_fusion.scalars_ref, bf16[2,512,256]{2,1,0:T(8,128)(2,1)} %bitcast.48.part_ref, bf16[2,512,256]{2,1,0:T(8,128)(2,1)S(1)} %bitcast.208, ...), custom_call_target="tpu_custom_call" | custom-call | bytes 18450000 | tf_op jit(solution)/shard_map/pallas_call | solution.py:582
  300.1 1.5 collective-permute-start.10
  302.1 2.2 copy-done.7
  304.3 8.8 %shard_map.513 = bf16[2048,1024]{1,0:T(8,128)(2,1)} custom-call(s32[6]{0:T(128)S(1)} %pad_add_fusion.scalars_ref, bf16[1024,1024]{1,0:T(8,128)(2,1)} %add_convert_fusion.1.part_ref, bf16[1024,1024]{1,0:T(8,128)(2,1)} %collective-permute-done.8.got_ref, bf16[2048,1024]{1,0:T(8,128)(2,1)S(1)} %bitcast.192, f32[2048,1]{1,0:T(8,128)S(1)} %bitcast.200), custom_call_target="tpu_custom_call" | custom-call | bytes 29520000 | tf_op jit(solution)/shard_map/pallas_call | solution.py:692
  313.1 15.4 %all-gather.5.cloned.1.call-done = bf16[2048,512]{1,0:T(8,128)(2,1)} async-done(((bf16[256,512]{1,0:T(8,128)(2,1)}), bf16[2048,512]{1,0:T(8,128)(2,1)}) %all-gather.5.cloned.1.call-update) | async-done | bytes 2097168 | tf_op jit(solution)/shard_map/all_gather | solution.py:893
  328.5 7.0 %multiply_subtract_fusion = (f32[1024,512]{1,0:T(8,128)}, f32[1024,512]{1,0:T(8,128)}, f32[1024,512]{1,0:T(8,128)}) fusion(f32[1024,512]{1,0:T(8,128)} %param.57, bf16[2048,512]{1,0:T(8,128)(2,1)} %all-gather.5.cloned.1.call-done, f32[1024,512]{1,0:T(8,128)} %param.59, f32[1024,512]{1,0:T(8,128)} %param.58), kind=kLoop, calls=%fused_computation.39 | loop fusion | flops 8388608 | bytes 13631488 | tf_op jit(solution)/shard_map/sub | solution.py:753
  335.5 4.9 %fusion.16 = bf16[1024,256]{1,0:T(8,128)(2,1)} fusion(bf16[4,512,256]{2,1,0:T(8,128)(2,1)S(1)} %fusion.54, bf16[4,512,1024]{2,1,0:T(8,128)(2,1)} %param.30, f32[1024]{0:T(1024)S(1)} %copy-done.43, f32[4,512]{1,0:T(4,128)S(1)} %copy-done.86), kind=kOutput, calls=%fused_computation.54 | convolution fusion | flops 1082392576 | bytes 5779456 | tf_op jit(solution)/shard_map/btd,btc->dc/dot_general | solution.py:932
  340.5 2.6 add_convert_fusion.part_ref
  343.1 5.6 %all-to-all-start.6 = ((bf16[8,128,256]{2,1,0:T(8,128)(2,1)}), bf16[8,128,256]{2,1,0:T(8,128)(2,1)S(1)}, u32[]{:S(2)}, u32[]{:S(2)}) async-start(bf16[8,128,256]{2,1,0:T(8,128)(2,1)} %bitcast.223), calls=%async_computation.6 | async-start | bytes 1048576 | tf_op jit(solution)/shard_map/all_to_all | solution.py:87
  348.8 2.1 reduce_sum.77
  350.9 13.0 %all-to-all-done.6 = bf16[8,128,256]{2,1,0:T(8,128)(2,1)S(1)} async-done(((bf16[8,128,256]{2,1,0:T(8,128)(2,1)}), bf16[8,128,256]{2,1,0:T(8,128)(2,1)S(1)}, u32[]{:S(2)}, u32[]{:S(2)}) %all-to-all-start.6) | async-done | bytes 524320 | tf_op jit(solution)/shard_map/all_to_all | solution.py:87
  364.8 4.2 all-to-all-start.7
  369.0 3.4 convolution_bitcast_fusion.1
  372.6 2.2 copy-done.8
  374.8 2.2 copy-done.19
  378.2 11.2 %shard_map.515 = (f32[2048,1024]{1,0:T(8,128)}, f32[1,1024]{1,0:T(1,128)S(1)}) custom-call(s32[6]{0:T(128)S(1)} %pad_add_fusion.scalars_ref, bf16[1024,1024]{1,0:T(8,128)(2,1)S(1)} %add_convert_fusion.part_ref, bf16[1024,1024]{1,0:T(8,128)(2,1)} %collective-permute-done.11.got_ref, bf16[2048,256]{1,0:T(8,128)(2,1)S(1)} %bitcast.203, ...), custom_call_target="tpu_custom_call" | custom-call | bytes 29520000 | tf_op jit(solution)/shard_map/pallas_call | solution.py:692
  389.4 1.9 collective-permute-start.12
  393.7 1.9 collective-permute-start.13
  395.6 3.9 multiply_subtract_fusion.1
  401.0 2.4 collective-permute-start.14
  403.4 1.5 maximum_bitcast_fusion
  404.9 4.7 %copy.133 = bf16[1024,4,2,128]{3,2,1,0:T(2,128)(2,1)S(1)} copy(bf16[1024,4,2,128]{0,3,1,2:T(8,128)(2,1)} %maximum_bitcast_fusion) | data formatting | bytes 4194304 | tf_op jit(solution)/shard_map/transpose | solution.py:115
  409.7 2.2 copy-done.10
  411.9 2.2 copy-done.20
  414.2 9.8 %shard_map.516 = (f32[1024,8,128]{2,1,0:T(8,128)}, f32[1024,8,128]{2,1,0:T(8,128)}, f32[1024,8,128]{2,1,0:T(8,128)}) custom-call(bf16[1024,8,128]{2,1,0:T(8,128)(2,1)S(1)} %bitcast.197, f32[1024,8,128]{2,1,0:T(8,128)S(1)} %bitcast.194, f32[1024,8,128]{2,1,0:T(8,128)S(1)} %bitcast.199, f32[1024,8,128]{2,1,0:T(8,128)} %bitcast.214), custom_call_target="tpu_custom_call" | custom-call | bytes 33210000 | tf_op jit(solution)/shard_map/pallas_call | solution.py:731
  (312 shorter events, 65.2 us)
Async XLA Ops:
  10.7 16.1 %copy-start.84 = (f32[4,512]{1,0:T(4,128)}, f32[4,512]{1,0:T(4,128)S(1)}, u32[]{:S(2)}) copy-start(f32[4,512]{1,0:T(4,128)S(1)} %add_rsqrt_fusion) | copy-start | bytes 24580
  15.7 10.9 %copy-start.57 = (f32[1024,8]{0,1:T(8,128)S(1)}, f32[1024,8]{0,1:T(8,128)}, u32[]{:S(2)}) copy-start(f32[1024,8]{0,1:T(8,128)} %param.42) | copy-start | bytes 98308
  21.2 11.5 %collective-permute-start = (bf16[4,3,768]{2,1,0:T(4,128)(2,1)S(1)}, bf16[4,3,768]{2,1,0:T(4,128)(2,1)S(1)}, u32[]{:S(2)}, u32[]{:S(2)}) collective-permute-start(bf16[4,3,768]{2,1,0:T(4,128)(2,1)S(1)} %slice.274), channel_id=1, source_target_pairs={{0,4},{4,8},{8,12},{12,16},{16,20},{20,24},{24,28},{1,5},{5,9},{9,... | collective-permute-start | bytes 55304 | tf_op jit(solution)/shard_map/ppermute | solution.py:31
  32.7 12.5 %copy-start.11 = (f32[4,512,8]{2,1,0:T(8,128)}, f32[4,512,8]{2,1,0:T(8,128)S(1)}, u32[]{:S(2)}) copy-start(f32[4,512,8]{2,1,0:T(8,128)S(1)} %get-tuple-element.147.decay_ref) | copy-start | bytes 196612
  32.7 12.5 %copy-start.14 = (f32[4,512,8]{2,1,0:T(8,128)}, f32[4,512,8]{2,1,0:T(8,128)S(1)}, u32[]{:S(2)}) copy-start(f32[4,512,8]{2,1,0:T(8,128)S(1)} %get-tuple-element.148.step_ref) | copy-start | bytes 196612
  46.1 22.0 %all-to-all-start = ((bf16[8,80,512]{2,1,0:T(8,128)(2,1)}), bf16[8,80,512]{2,1,0:T(8,128)(2,1)}, u32[]{:S(2)}, u32[]{:S(2)}) async-start(bf16[8,80,512]{2,1,0:T(8,128)(2,1)} %bitcast.206), calls=%async_computation | async-start | bytes 1310720 | tf_op jit(solution)/shard_map/all_to_all | solution.py:87
  70.0 38.8 %copy-start.72 = (f32[1,1,512]{2,1,0:T(1,128)}, f32[1,1,512]{2,1,0:T(1,128)S(1)}, u32[]{:S(2)}) copy-start(f32[1,1,512]{2,1,0:T(1,128)S(1)} %get-tuple-element.163) | copy-start | bytes 6148
  70.0 38.8 %copy-start.74 = (f32[1,1,512]{2,1,0:T(1,128)}, f32[1,1,512]{2,1,0:T(1,128)S(1)}, u32[]{:S(2)}) copy-start(f32[1,1,512]{2,1,0:T(1,128)S(1)} %get-tuple-element.165) | copy-start | bytes 6148
  74.6 18.9 %all-to-all-start.1 = ((bf16[8,64,512]{2,1,0:T(8,128)(2,1)}), bf16[8,64,512]{2,1,0:T(8,128)(2,1)}, u32[]{:S(2)}, u32[]{:S(2)}) async-start(bf16[8,64,512]{2,1,0:T(8,128)(2,1)} %fusion.48), calls=%async_computation.1 | async-start | bytes 1048576 | tf_op jit(solution)/shard_map/all_to_all | solution.py:87
  80.0 28.9 %copy-start.65 = (f32[8,64]{1,0:T(8,128)}, f32[8,64]{1,0:T(8,128)S(1)}, u32[]{:S(2)}) copy-start(f32[8,64]{1,0:T(8,128)S(1)} %broadcast_in_dim.14) | copy-start | bytes 6148
  96.0 14.9 %copy-start.5 = (bf16[4,512,1024]{2,1,0:T(8,128)(2,1)S(1)}, bf16[4,512,1024]{2,1,0:T(8,128)(2,1)}, u32[]{:S(2)}) copy-start(bf16[4,512,1024]{2,1,0:T(8,128)(2,1)} %param.30) | copy-start | bytes 12582916
  96.0 14.9 %copy-start.51 = (bf16[1024,2,512]{2,0,1:T(8,128)(2,1)S(1)}, bf16[1024,2,512]{2,0,1:T(8,128)(2,1)}, u32[]{:S(2)}) copy-start(bf16[1024,2,512]{2,0,1:T(8,128)(2,1)} %copy-done.50) | copy-start | bytes 6291460
  96.0 14.9 %copy-start.85 = (f32[4,512]{1,0:T(4,128)S(1)}, f32[4,512]{1,0:T(4,128)}, u32[]{:S(2)}) copy-start(f32[4,512]{1,0:T(4,128)} %copy-done.84) | copy-start | bytes 24580
  96.0 14.9 %copy-start.99 = (f32[512]{0:T(512)S(1)}, f32[512]{0:T(512)}, u32[]{:S(2)}) copy-start(f32[512]{0:T(512)} %mul.699) | copy-start | bytes 6148
  132.9 10.5 %copy-start.83 = (f32[4,512]{1,0:T(4,128)}, f32[4,512]{1,0:T(4,128)S(1)}, u32[]{:S(2)}) copy-start(f32[4,512]{1,0:T(4,128)S(1)} %get-tuple-element.156) | copy-start | bytes 24580
  148.7 18.8 %all-to-all-start.2 = ((bf16[8,64,512]{2,1,0:T(8,128)(2,1)}), bf16[8,64,512]{2,1,0:T(8,128)(2,1)}, u32[]{:S(2)}, u32[]{:S(2)}) async-start(bf16[8,64,512]{2,1,0:T(8,128)(2,1)} %bitcast.220), calls=%async_computation.2 | async-start | bytes 1048576 | tf_op jit(solution)/shard_map/all_to_all | solution.py:87
  157.0 11.7 %copy-start.71 = (f32[1,1,512]{2,1,0:T(1,128)S(1)}, f32[1,1,512]{2,1,0:T(1,128)}, u32[]{:S(2)}) copy-start(f32[1,1,512]{2,1,0:T(1,128)} %copy-done.70) | copy-start | bytes 6148
  157.0 11.7 %copy-start.73 = (f32[1,1,512]{2,1,0:T(1,128)S(1)}, f32[1,1,512]{2,1,0:T(1,128)}, u32[]{:S(2)}) copy-start(f32[1,1,512]{2,1,0:T(1,128)} %copy-done.72) | copy-start | bytes 6148
  157.0 11.8 %copy-start.75 = (f32[1,1,512]{2,1,0:T(1,128)S(1)}, f32[1,1,512]{2,1,0:T(1,128)}, u32[]{:S(2)}) copy-start(f32[1,1,512]{2,1,0:T(1,128)} %copy-done.74) | copy-start | bytes 6148
  157.0 11.8 %copy-start.76 = (f32[1,1,512]{2,1,0:T(1,128)S(1)}, f32[1,1,512]{2,1,0:T(1,128)}, u32[]{:S(2)}) copy-start(f32[1,1,512]{2,1,0:T(1,128)} %get-tuple-element.160) | copy-start | bytes 6148
  157.0 28.8 %collective-permute-start.1 = (bf16[1024,1024]{1,0:T(8,128)(2,1)}, bf16[1024,1024]{1,0:T(8,128)(2,1)}, u32[]{:S(2)}, u32[]{:S(2)}) collective-permute-start(bf16[1024,1024]{1,0:T(8,128)(2,1)} %dynamic-slice_bitcast_fusion.1), channel_id=1, source_target_pairs={{0,1},{1,0},{2,3},{3,2},{4,5},{5,4},{6,7},{7,6},{8,9},{9,8},{10,11... | collective-permute-start | bytes 6291464 | tf_op jit(solution)/shard_map/ppermute | solution.py:35
  174.7 17.5 %all-to-all-start.3 = ((bf16[8,64,512]{2,1,0:T(8,128)(2,1)}), bf16[8,64,512]{2,1,0:T(8,128)(2,1)}, u32[]{:S(2)}, u32[]{:S(2)}) async-start(bf16[8,64,512]{2,1,0:T(8,128)(2,1)} %constant_dynamic-update-slice_fusion.1), calls=%async_computation.3 | async-start | bytes 1048576 | tf_op jit(solution)/shard_map/all_to_all | solution.py:87
  185.8 12.1 %copy-start.66 = (f32[8,64]{1,0:T(8,128)S(1)}, f32[8,64]{1,0:T(8,128)}, u32[]{:S(2)}) copy-start(f32[8,64]{1,0:T(8,128)} %copy-done.65) | copy-start | bytes 6148
  192.2 63.9 %all-to-all-start.4 = ((bf16[8,256,512]{2,1,0:T(8,128)(2,1)}), bf16[8,256,512]{2,1,0:T(8,128)(2,1)}, u32[]{:S(2)}, u32[]{:S(2)}) async-start(bf16[8,256,512]{2,1,0:T(8,128)(2,1)} %bitcast.213), calls=%async_computation.4 | async-start | bytes 4194304 | tf_op jit(solution)/shard_map/all_to_all | solution.py:87
  197.0 131.5 %all-gather.5.cloned.1.call-start = ((), (), s32[]{:S(2)}) async-start(), calls=%async_computation.8 | async-start | bytes 2359296 | tf_op jit(solution)/shard_map/all_gather | solution.py:893
  197.1 59.0 %collective-permute-start.2 = (bf16[1024,1024]{1,0:T(8,128)(2,1)}, bf16[1024,1024]{1,0:T(8,128)(2,1)}, u32[]{:S(2)}, u32[]{:S(2)}) collective-permute-start(bf16[1024,1024]{1,0:T(8,128)(2,1)} %fusion.4), channel_id=1, source_target_pairs={{0,2},{1,3},{2,0},{3,1},{4,6},{5,7},{6,4},{7,5},{8,10},{9,11},{10,... | collective-permute-start | bytes 6291464 | tf_op jit(solution)/shard_map/ppermute | solution.py:35
  239.0 21.3 %copy-start.23 = (bf16[1024,512]{1,0:T(8,128)(2,1)S(1)}, bf16[1024,512]{1,0:T(8,128)(2,1)}, u32[]{:S(2)}) copy-start(bf16[1024,512]{1,0:T(8,128)(2,1)} %get-tuple-element.144.z_weight_ref) | copy-start | bytes 3145732
  239.0 21.3 %copy-start.25 = (bf16[1024,512]{1,0:T(8,128)(2,1)S(1)}, bf16[1024,512]{1,0:T(8,128)(2,1)}, u32[]{:S(2)}) copy-start(bf16[1024,512]{1,0:T(8,128)(2,1)} %copy-done.24) | copy-start | bytes 3145732
  239.0 2.0 collective-permute-start.4
  241.2 14.0 %collective-permute-start.5 = (bf16[1024,256]{1,0:T(8,128)(2,1)S(1)}, bf16[1024,256]{1,0:T(8,128)(2,1)S(1)}, u32[]{:S(2)}, u32[]{:S(2)}) collective-permute-start(bf16[1024,256]{1,0:T(8,128)(2,1)S(1)} %fusion.25), channel_id=1, source_target_pairs={{0,2},{1,3},{2,0},{3,1},{4,6},{5,7},{6,4},{7,5},{8,10},{9,11},{10,... | collective-permute-start | bytes 1572872 | tf_op jit(solution)/shard_map/ppermute | solution.py:35
  242.5 17.8 %copy-start.38 = (bf16[4,512,8]{2,1,0:T(8,128)(2,1)S(1)}, bf16[4,512,8]{2,1,0:T(8,128)(2,1)}, u32[]{:S(2)}) copy-start(bf16[4,512,8]{2,1,0:T(8,128)(2,1)} %copy-done.37) | copy-start | bytes 98308
  244.1 12.1 %collective-permute-start.3 = (f32[4,3,512]{2,1,0:T(4,128)}, f32[4,3,512]{2,1,0:T(4,128)}, u32[]{:S(2)}, u32[]{:S(2)}) collective-permute-start(f32[4,3,512]{2,1,0:T(4,128)} %pad_maximum_fusion.1), channel_id=1, source_target_pairs={{4,0},{8,4},{12,8},{16,12},{20,16},{24,20},{28,24},{5,1},{9,5},{13... | collective-permute-start | bytes 73736 | tf_op jit(solution)/shard_map/ppermute | solution.py:31
  270.8 9.5 %collective-permute-start.6 = (bf16[1024,1024]{1,0:T(8,128)(2,1)S(1)}, bf16[1024,1024]{1,0:T(8,128)(2,1)S(1)}, u32[]{:S(2)}, u32[]{:S(2)}) collective-permute-start(bf16[1024,1024]{1,0:T(8,128)(2,1)S(1)} %dynamic-slice_bitcast_fusion), channel_id=1, source_target_pairs={{0,1},{1,0},{2,3},{3,2},{4,5},{5,4},{6,7},{7,6},{8,9},{9,8},{10,11... | collective-permute-start | bytes 6291464 | tf_op jit(solution)/shard_map/ppermute | solution.py:35
  276.3 25.8 %collective-permute-start.8 = (bf16[1024,1024]{1,0:T(8,128)(2,1)}, bf16[1024,1024]{1,0:T(8,128)(2,1)}, u32[]{:S(2)}, u32[]{:S(2)}) collective-permute-start(bf16[1024,1024]{1,0:T(8,128)(2,1)} %add_convert_fusion.1.part_ref), channel_id=1, source_target_pairs={{0,1},{1,0},{2,3},{3,2},{4,5},{5,4},{6,7},{7,6},{8,9},{9,8},{10,11... | collective-permute-start | bytes 6291464 | tf_op jit(solution)/shard_map/ppermute | solution.py:35
  276.3 6.3 %collective-permute-start.9 = (bf16[1024,256]{1,0:T(8,128)(2,1)}, bf16[1024,256]{1,0:T(8,128)(2,1)S(1)}, u32[]{:S(2)}, u32[]{:S(2)}) collective-permute-start(bf16[1024,256]{1,0:T(8,128)(2,1)} %add_convert_fusion.2), channel_id=1, source_target_pairs={{0,1},{1,0},{2,3},{3,2},{4,5},{5,4},{6,7},{7,6},{8,9},{9,8},{10,11... | collective-permute-start | bytes 1572872 | tf_op jit(solution)/shard_map/ppermute | solution.py:35
  283.4 52.2 %all-to-all-start.5 = ((bf16[8,128,512]{2,1,0:T(8,128)(2,1)}), bf16[8,128,512]{2,1,0:T(8,128)(2,1)}, u32[]{:S(2)}, u32[]{:S(2)}) async-start(bf16[8,128,512]{2,1,0:T(8,128)(2,1)} %bitcast.221), calls=%async_computation.5 | async-start | bytes 2097152 | tf_op jit(solution)/shard_map/all_to_all | solution.py:87
  289.3 12.4 %copy-start.69 = (f32[1,1,4,512]{3,2,1,0:T(4,128)S(1)}, f32[1,1,4,512]{3,2,1,0:T(4,128)}, u32[]{:S(2)}) copy-start(f32[1,1,4,512]{3,2,1,0:T(4,128)} %get-tuple-element.155) | copy-start | bytes 24580
  289.3 51.2 %collective-permute-start.7 = (bf16[1024,1024]{1,0:T(8,128)(2,1)}, bf16[1024,1024]{1,0:T(8,128)(2,1)}, u32[]{:S(2)}, u32[]{:S(2)}) collective-permute-start(bf16[1024,1024]{1,0:T(8,128)(2,1)} %fusion.3), channel_id=1, source_target_pairs={{0,2},{1,3},{2,0},{3,1},{4,6},{5,7},{6,4},{7,5},{8,10},{9,11},{10,... | collective-permute-start | bytes 6291464 | tf_op jit(solution)/shard_map/ppermute | solution.py:35
  300.1 12.9 %collective-permute-start.10 = (f32[4,3,256]{2,1,0:T(4,128)S(1)}, f32[4,3,256]{2,1,0:T(4,128)S(1)}, u32[]{:S(2)}, u32[]{:S(2)}) collective-permute-start(f32[4,3,256]{2,1,0:T(4,128)S(1)} %pad_maximum_fusion.3), channel_id=1, source_target_pairs={{4,0},{8,4},{12,8},{16,12},{20,16},{24,20},{28,24},{5,1},{9,5},{13... | collective-permute-start | bytes 36872 | tf_op jit(solution)/shard_map/ppermute | solution.py:31
  313.1 22.5 %copy-start.34 = (bf16[4,512,256]{2,1,0:T(8,128)(2,1)}, bf16[4,512,256]{2,1,0:T(8,128)(2,1)S(1)}, u32[]{:S(2)}) copy-start(bf16[4,512,256]{2,1,0:T(8,128)(2,1)S(1)} %fusion.54) | copy-start | bytes 3145732
  340.4 28.5 %copy-start.39 = (bf16[4,512,8]{2,1,0:T(8,128)(2,1)S(1)}, bf16[4,512,8]{2,1,0:T(8,128)(2,1)}, u32[]{:S(2)}) copy-start(bf16[4,512,8]{2,1,0:T(8,128)(2,1)} %copy-done.37) | copy-start | bytes 98308
  343.1 29.5 %collective-permute-start.11 = (bf16[1024,1024]{1,0:T(8,128)(2,1)S(1)}, bf16[1024,1024]{1,0:T(8,128)(2,1)}, u32[]{:S(2)}, u32[]{:S(2)}) collective-permute-start(bf16[1024,1024]{1,0:T(8,128)(2,1)S(1)} %add_convert_fusion.part_ref), channel_id=1, source_target_pairs={{0,1},{1,0},{2,3},{3,2},{4,5},{5,4},{6,7},{7,6},{8,9},{9,8},{10,11... | collective-permute-start | bytes 6291464 | tf_op jit(solution)/shard_map/ppermute | solution.py:35
  343.1 20.7 %all-to-all-start.6 = ((bf16[8,128,256]{2,1,0:T(8,128)(2,1)}), bf16[8,128,256]{2,1,0:T(8,128)(2,1)S(1)}, u32[]{:S(2)}, u32[]{:S(2)}) async-start(bf16[8,128,256]{2,1,0:T(8,128)(2,1)} %bitcast.223), calls=%async_computation.6 | async-start | bytes 1048576 | tf_op jit(solution)/shard_map/all_to_all | solution.py:87
  348.7 50.7 %all-gather.7.cloned.1.call-start = ((), (), s32[]{:S(2)}) async-start(), calls=%async_computation.9 | async-start | bytes 1179648 | tf_op jit(solution)/shard_map/all_gather | solution.py:930
  364.8 30.8 %all-to-all-start.7 = ((bf16[8,128,256]{2,1,0:T(8,128)(2,1)}), bf16[8,128,256]{2,1,0:T(8,128)(2,1)}, u32[]{:S(2)}, u32[]{:S(2)}) async-start(bf16[8,128,256]{2,1,0:T(8,128)(2,1)} %broadcast_in_dim.19), calls=%async_computation.7 | async-start | bytes 1048576 | tf_op jit(solution)/shard_map/all_to_all | solution.py:87
  378.2 11.2 %copy-start.92 = (f32[512]{0:T(512)S(1)}, f32[512]{0:T(512)}, u32[]{:S(2)}) copy-start(f32[512]{0:T(512)} %get-tuple-element.141) | copy-start | bytes 6148
  389.4 4.2 collective-permute-start.12
  393.7 7.3 %collective-permute-start.13 = (f32[112,128]{1,0:T(8,128)S(1)}, f32[112,128]{1,0:T(8,128)S(1)}, u32[]{:S(2)}, u32[]{:S(2)}) collective-permute-start(f32[112,128]{1,0:T(8,128)S(1)} %fusion.70), channel_id=1, source_target_pairs={{0,8},{4,12},{8,0},{12,4},{16,24},{20,28},{24,16},{28,20},{1,9},{5... | collective-permute-start | bytes 172040 | tf_op jit(solution)/shard_map/ppermute | solution.py:35
  401.0 23.0 %collective-permute-start.14 = (f32[112,128]{1,0:T(8,128)S(1)}, f32[112,128]{1,0:T(8,128)S(1)}, u32[]{:S(2)}, u32[]{:S(2)}) collective-permute-start(f32[112,128]{1,0:T(8,128)S(1)} %fusion.100), channel_id=1, source_target_pairs={{0,16},{4,20},{8,24},{12,28},{16,0},{20,4},{24,8},{28,12},{1,17},{... | collective-permute-start | bytes 172040 | tf_op jit(solution)/shard_map/ppermute | solution.py:35
  414.1 10.5 %copy-start.91 = (f32[1024]{0:T(1024)S(1)}, f32[1024]{0:T(1024)}, u32[]{:S(2)}) copy-start(f32[1024]{0:T(1024)} %param.34) | copy-start | bytes 12292
  414.1 11.2 %copy-start.89 = (f32[3,8]{1,0:T(4,128)S(1)}, f32[3,8]{1,0:T(4,128)}, u32[]{:S(2)}) copy-start(f32[3,8]{1,0:T(4,128)} %param.51) | copy-start | bytes 292
  414.1 11.2 %copy-start.93 = (f32[3,8]{1,0:T(4,128)S(1)}, f32[3,8]{1,0:T(4,128)}, u32[]{:S(2)}) copy-start(f32[3,8]{1,0:T(4,128)} %param.53) | copy-start | bytes 292
  414.1 11.1 %copy-start.94 = (f32[3,8]{1,0:T(4,128)S(1)}, f32[3,8]{1,0:T(4,128)}, u32[]{:S(2)}) copy-start(f32[3,8]{1,0:T(4,128)} %param.52) | copy-start | bytes 292
  414.1 11.7 %copy-start.58 = (f32[1024,8]{0,1:T(8,128)S(1)}, f32[1024,8]{0,1:T(8,128)}, u32[]{:S(2)}) copy-start(f32[1024,8]{0,1:T(8,128)} %param.42) | copy-start | bytes 98308
  414.1 11.7 %copy-start.67 = (f32[1024,8]{0,1:T(8,128)S(1)}, f32[1024,8]{0,1:T(8,128)}, u32[]{:S(2)}) copy-start(f32[1024,8]{0,1:T(8,128)} %param.44) | copy-start | bytes 98308
  414.1 11.7 %copy-start.68 = (f32[1024,8]{0,1:T(8,128)S(1)}, f32[1024,8]{0,1:T(8,128)}, u32[]{:S(2)}) copy-start(f32[1024,8]{0,1:T(8,128)} %param.43) | copy-start | bytes 98308
  414.1 12.4 %copy-start.60 = (f32[5,512]{1,0:T(8,128)S(1)}, f32[5,512]{1,0:T(8,128)}, u32[]{:S(2)}) copy-start(f32[5,512]{1,0:T(8,128)} %param.45) | copy-start | bytes 30724
  414.1 12.4 %copy-start.79 = (f32[5,512]{1,0:T(8,128)S(1)}, f32[5,512]{1,0:T(8,128)}, u32[]{:S(2)}) copy-start(f32[5,512]{1,0:T(8,128)} %param.47) | copy-start | bytes 30724
  414.1 12.4 %copy-start.80 = (f32[5,512]{1,0:T(8,128)S(1)}, f32[5,512]{1,0:T(8,128)}, u32[]{:S(2)}) copy-start(f32[5,512]{1,0:T(8,128)} %param.46) | copy-start | bytes 30724
  414.2 13.0 %copy-start.81 = (f32[5,256]{1,0:T(8,128)S(1)}, f32[5,256]{1,0:T(8,128)}, u32[]{:S(2)}) copy-start(f32[5,256]{1,0:T(8,128)} %param.50) | copy-start | bytes 15364
  414.2 13.0 %copy-start.82 = (f32[5,256]{1,0:T(8,128)S(1)}, f32[5,256]{1,0:T(8,128)}, u32[]{:S(2)}) copy-start(f32[5,256]{1,0:T(8,128)} %param.49) | copy-start | bytes 15364
  414.2 13.6 %copy-start.96 = (f32[512]{0:T(512)S(1)}, f32[512]{0:T(512)}, u32[]{:S(2)}) copy-start(f32[512]{0:T(512)} %param.54) | copy-start | bytes 6148
  414.2 13.6 %copy-start.97 = (f32[512]{0:T(512)S(1)}, f32[512]{0:T(512)}, u32[]{:S(2)}) copy-start(f32[512]{0:T(512)} %param.56) | copy-start | bytes 6148
  414.2 13.6 %copy-start.98 = (f32[512]{0:T(512)S(1)}, f32[512]{0:T(512)}, u32[]{:S(2)}) copy-start(f32[512]{0:T(512)} %param.55) | copy-start | bytes 6148
  (64 other events, 264.5 us)
Sparse Core Ops, SparseCore 0:
  260.4 68.0 all-gather.4
  352.3 43.6 all-gather.6

commit v7 on v6

--- a/solution.py
+++ b/solution.py
@@ -894,8 +894,6 @@
     bc_sum = halved(bc_grad.reshape(rows, 2 * state_width), "head")
     x_in_grad = joined_edges(x_raw, x_first, x_last, conv_weight[:, :local_inner])
     bc_far = swapped(bc_sum, "head", axis_masks("head")[-1])
-    x_in_grad, bc_added = lax.optimization_barrier((x_in_grad, added(bc_sum, bc_far)))
-    bc_half, bc_other = regathered(bc_added, "head")
     normed_partial = normed_products(
         gate_grad.reshape(rows, local_inner),
         x_in_grad.reshape(rows, local_inner),
@@ -904,7 +902,9 @@
         x_weight,
         step_weight,
     )
-    x_weight_grad = jnp.einsum("btd,btc->dc", normed, x_in_grad, preferred_element_type=F32)
+    x_in_late, bc_added = lax.optimization_barrier((x_in_grad, added(bc_sum, bc_far)))
+    bc_half, bc_other = regathered(bc_added, "head")
+    x_weight_grad = jnp.einsum("btd,btc->dc", normed, x_in_late, preferred_element_type=F32)
     normed_sum = halved(normed_partial, "head")
     x_blocks, bc_other, _ = lax.optimization_barrier(
         (to_blocks(x_weight_grad, seq_size), bc_other, normed_sum)
@@ -915,7 +915,6 @@
     scalars = jnp.concatenate(
         [lengths, jnp.stack([seq_index * local_len, near_bit("head", 1)]).astype(jnp.int32)]
     )
-    early_sums = early_all.reshape(2, model_width, local_inner)
     bc_raw_grad, bc_first, bc_last, bc_tap_sums = bc_backward(
         scalars,
         bc_half,
@@ -932,6 +931,8 @@
     bc_weight_grad = jnp.einsum("btd,btc->dc", normed, bc_in_grad, preferred_element_type=F32)
     bc_blocks = to_blocks(bc_weight_grad, seq_size)
     bc_parts = exchanged(bc_blocks, "seq")
+    early_all, _ = lax.optimization_barrier((early_all, bc_blocks))
+    early_sums = early_all.reshape(2, model_width, local_inner)
     flat_tokens = inputs.reshape(rows, model_width)
     block_out = merge_call(
         out_kernel,
@@ -955,7 +956,9 @@
         (normed_far, block_out, out_updated, bc_blocks)
     )
     block_out = block_out.reshape(inputs.shape)
-    normed_half, normed_other = regathered(added(normed_sum, normed_far), "head")
+    normed_added = added(normed_sum, normed_far)
+    bc_parts, _ = lax.optimization_barrier((bc_parts, normed_added))
+    normed_half, normed_other = regathered(normed_added, "head")
     input_grad, norm_gain_grad = merge_call(
         functools.partial(tail_kernel, local_len),
         scalars,

time: 444 us -> 453 us (1.020)
  waiting for transfers between devices: 66.1 us -> 72.9 us
    all_to_all x8, waiting for transfers between devices: 38.6 us -> 55.5 us  [exchanged(): return lax.all_to_all(blocks, axis, 0, 0, tiled=True)]
    all_gather x1, waiting for transfers between devices: 15.4 us -> 0.01 us  [shards(): early_all = lax.all_gather(early_own, 'seq')]
    unnamed x213 -> x219, local copies, waits for them, and re-layouts: 42.6 us -> 44 us
  transfers between devices with their start and end apart: 25 -> 25, of which waited for: 9 -> 11; matrix products, arithmetic and copies ran while one was open for 21% -> 22% of each run, Pallas kernels for 18% -> 17%
where the time goes in v7:
time: 453 us; the launch traced here: 444 us
  Pallas kernels  103 us (23%)
  waiting for transfers between devices  72.9 us (16%)
  local copies, waits for them, and re-layouts  66.6 us (15%)
  matrix products  63.5 us (14%)
  other arithmetic  56.6 us (12%)
  starting transfers between devices  55.8 us (12%)
  between operations  15.5 us (3%)
  blocking collectives  10.7 us (2%)
    all_to_all x8, waiting for transfers between devices, exchanged(): return lax.all_to_all(blocks, axis, 0, 0, tiled=True)  55.5 us
    unnamed x219, local copies, waits for them, and re-layouts  44 us
    all_to_all x8, starting transfers between devices, exchanged(): return lax.all_to_all(blocks, axis, 0, 0, tiled=True)  37.5 us
    pallas_call x1, Pallas kernels, scan_backward(): pl.pallas_call(back_kernel, grid=(seqs // GROUP, chunks), in_specs=act_bl...  33.5 us
    pallas_call x2, Pallas kernels, merge_call(): pl.pallas_call(kernel, grid_spec=pltpu.PrefetchScalarGridSpec(num_scalar_...  20 us
    convert_element_type x6, other arithmetic, added(): return (a.astype(F32) + b.astype(F32)).astype(BF16)  16.4 us
    ppermute x12, waiting for transfers between devices, swapped(): lax.ppermute(block, axis, [(i, i ^ mask) for i in range(lax.axis_size(axi...  14.3 us
    sub x8, other arithmetic, adam_update(): weight - step_rate * (corrected_mean / (jnp.sqrt(corrected_square) + ADAM...  13.6 us
  transfers between devices with their start and end apart: 25, of which 11 were waited for; matrix products, arithmetic and copies ran while one was open for 22% of the time, Pallas kernels for 17%

profile of v7, /device:TPU:0, one launch (start us, length us, event | category | flops | bytes accessed | tf_op | source)
XLA Modules:
  0.0 444.3 jit_solution(11596085275295424946)
XLA Ops:
  8.5 3.0 copy.152
  14.9 3.7 convolution_convert_fusion.mixed_ref.previous_ref
  18.7 1.7 copy-done
  20.4 4.9 %collective-permute-start = (bf16[4,3,768]{2,1,0:T(4,128)(2,1)S(1)}, bf16[4,3,768]{2,1,0:T(4,128)(2,1)S(1)}, u32[]{:S(2)}, u32[]{:S(2)}) collective-permute-start(bf16[4,3,768]{2,1,0:T(4,128)(2,1)S(1)} %slice.272), channel_id=1, source_target_pairs={{0,4},{4,8},{8,12},{12,16},{16,20},{20,24},{24,28},{1,5},{5,9},{9,... | collective-permute-start | bytes 55304 | tf_op jit(solution)/shard_map/ppermute | solution.py:31
  26.3 5.6 %add_divide_fusion.1 = (f32[4,512,8]{2,1,0:T(8,128)}, f32[4,512,8]{2,1,0:T(8,128)S(1)}, f32[4,512,8]{2,1,0:T(8,128)S(1)}, f32[4,512,8]{2,1,0:T(8,128)}) fusion(f32[8]{0:T(128)S(1)} %get-tuple-element.178, f32[8]{0:T(128)S(1)} %get-tuple-element.179, bf16[1024,8]{1,0:T(8,128)(2,1)S(1)} %copy.113.step_weight_ref, bf16[4,512,1024]{2,1,0:T(8,128)(2,1)} %param.30, ...), kind=kOutput, calls=%fused_computation.71 | convolution fusion | flops 42139648 | bytes 4485184 | tf_op jit(solution)/shard_map/btd,dh->bth/dot_general | solution.py:817
  32.0 12.4 %shard_map.509 = (bf16[4,512,768]{2,1,0:T(8,128)(2,1)S(1)}, bf16[4,2,80,512]{3,2,1,0:T(8,128)(2,1)S(1)}) custom-call(bf16[4,512,768]{2,1,0:T(8,128)(2,1)S(1)} %copy-done.1, bf16[4,512,768]{2,1,0:T(8,128)(2,1)S(1)} %copy-done.1, bf16[4,16,768]{2,1,0:T(8,128)(2,1)S(1)} %pad.20.edge_ref, f32[8,768]{1,0:T(8,128)S(1)} %select_maximum_fusion.taps_ref, ...), custom_call_target="tpu_custom_call" | custom-call | bytes 33210000 | tf_op jit(solution)/shard_map/pallas_call | solution.py:413
  45.3 4.9 %all-to-all-start = ((bf16[8,80,512]{2,1,0:T(8,128)(2,1)}), bf16[8,80,512]{2,1,0:T(8,128)(2,1)}, u32[]{:S(2)}, u32[]{:S(2)}) async-start(bf16[8,80,512]{2,1,0:T(8,128)(2,1)} %bitcast.212), calls=%async_computation | async-start | bytes 1310720 | tf_op jit(solution)/shard_map/all_to_all | solution.py:87
  50.8 16.5 %all-to-all-done = bf16[8,80,512]{2,1,0:T(8,128)(2,1)} async-done(((bf16[8,80,512]{2,1,0:T(8,128)(2,1)}), bf16[8,80,512]{2,1,0:T(8,128)(2,1)}, u32[]{:S(2)}, u32[]{:S(2)}) %all-to-all-start) | async-done | bytes 655392 | tf_op jit(solution)/shard_map/all_to_all | solution.py:87
  73.8 4.3 all-to-all-start.1
  83.0 5.6 %fusion.20 = f32[4,512,8]{1,2,0:T(8,128)} fusion(f32[8]{0:T(128)} %copy-done.104, f32[4,512,8]{2,1,0:T(8,128)} %get-tuple-element.181), kind=kOutput, calls=%fused_computation.56 | convolution fusion | flops 101318656 | bytes 131104 | tf_op jit(solution)/shard_map/ts,bsh->bth/dot_general | solution.py:836
  88.7 3.8 all-to-all-done.1
  94.9 12.8 %shard_map.510 = (f32[4,512,512]{2,1,0:T(8,128)S(1)}, f32[4,4,128,512]{3,2,1,0:T(8,128)S(1)}) custom-call(bf16[4,512,768]{2,1,0:T(8,128)(2,1)S(1)} %get-tuple-element.68.x_ref.b_ref.c_ref, bf16[4,512,768]{2,1,0:T(8,128)(2,1)S(1)} %get-tuple-element.68.x_ref.b_ref.c_ref, bf16[4,512,768]{2,1,0:T(8,128)(2,1)S(1)} %get-tuple-element.68.x_ref.b_ref.c_ref, ...), custom_call_target="tpu_custom_call" | custom-call | bytes 47970000 | tf_op jit(solution)/shard_map/pallas_call | solution.py:446
  107.8 2.0 copy-done.23
  109.9 5.1 %multiply_reduce_fusion.2 = (f32[4,512]{1,0:T(4,128)S(1)}, f32[4,512,512]{2,1,0:T(8,128)S(1)}, f32[4,512,512]{2,1,0:T(8,128)}) fusion(f32[4,512,512]{2,1,0:T(8,128)S(1)} %get-tuple-element.70.y_ref, bf16[4,512,768]{2,1,0:T(8,128)(2,1)S(1)} %get-tuple-element.68.x_ref.b_ref.c_ref, f32[512]{0:T(512)S(1)} %copy-done.102, ...), kind=kOutput, calls=%fused_computation.20 | convolution fusion | flops 2166355968 | bytes 19945472 | tf_op jit(solution)/shard_map/btd,dc->btc/dot_general | solution.py:818
  115.6 4.4 fusion.90
  120.6 10.7 %psum.7 = f32[2,4,512]{2,1,0:T(4,128)S(1)} all-reduce(f32[2,4,512]{2,1,0:T(4,128)} %pad_maximum_fusion.2), channel_id=1, replica_groups=mesh['seq'=8,'head'=4] {'head'}, use_global_device_ids=true, to_apply=%region_3.4 | all-reduce | flops 4096 | bytes 32768 | tf_op jit(solution)/shard_map/psum | solution.py:848
  131.9 10.5 %fusion.15 = (f32[4,512,512]{2,1,0:T(8,128)S(1)}, bf16[4,512,512]{2,1,0:T(8,128)(2,1)}, f32[512]{0:T(512)}) fusion(f32[4,512,512]{2,1,0:T(8,128)} %copy-done.105, f32[4,512]{1,0:T(4,128)S(1)} %fusion.55, f32[512]{0:T(512)} %param.54, f32[4,512,512]{2,1,0:T(8,128)} %get-tuple-element.182, f32[4,512,512]{2,1,0:T(8,128)} %copy-done.22, ...), kind=kOutput, calls=%fused_computation.52 | convolution fusion | flops 2177367552 | bytes 27293696 | tf_op jit(solution)/shard_map/btd,di->bti/dot_general | solution.py:853
  142.4 3.9 multiply_convert_fusion.1
  147.6 5.2 %all-to-all-start.2 = ((bf16[8,64,512]{2,1,0:T(8,128)(2,1)}), bf16[8,64,512]{2,1,0:T(8,128)(2,1)}, u32[]{:S(2)}, u32[]{:S(2)}) async-start(bf16[8,64,512]{2,1,0:T(8,128)(2,1)} %bitcast.226), calls=%async_computation.2 | async-start | bytes 1048576 | tf_op jit(solution)/shard_map/all_to_all | solution.py:87
  152.9 3.2 dynamic-slice_bitcast_fusion.1
  156.2 6.2 %bitcast_convert_fusion.2 = bf16[1024,512]{1,0:T(8,128)(2,1)} fusion(bf16[4,512,1024]{2,1,0:T(8,128)(2,1)S(1)} %copy-done.19, f32[4,512]{1,0:T(4,128)} %copy-done.86, f32[4,512]{1,0:T(4,128)} %compare_convert_fusion, f32[4,512,512]{2,1,0:T(8,128)} %copy-done.105, f32[512]{0:T(512)} %param.54), kind=kOutput, calls=%fused_computation.38 | convolution fusion | flops 2158493696 | bytes 9455616 | tf_op jit(solution)/shard_map/btd,bti->di/dot_general | solution.py:852
  162.5 4.3 all-to-all-done.2
  173.9 4.2 all-to-all-start.3
  178.0 5.4 %bitcast_convert_fusion.1 = bf16[1024,512]{1,0:T(8,128)(2,1)S(1)} fusion(bf16[4,512,512]{2,1,0:T(8,128)(2,1)} %get-tuple-element.144, bf16[4,512,1024]{2,1,0:T(8,128)(2,1)} %param.30, f32[1024]{0:T(1024)S(1)} %copy-done.47, f32[4,512]{1,0:T(4,128)} %copy-done.87), kind=kOutput, calls=%fused_computation.37 | convolution fusion | flops 2156396544 | bytes 7352320 | tf_op jit(solution)/shard_map/btd,btc->dc/dot_general | solution.py:868
  186.4 3.9 fusion.4
  191.4 4.8 %all-to-all-start.4 = ((bf16[8,256,512]{2,1,0:T(8,128)(2,1)}), bf16[8,256,512]{2,1,0:T(8,128)(2,1)}, u32[]{:S(2)}, u32[]{:S(2)}) async-start(bf16[8,256,512]{2,1,0:T(8,128)(2,1)} %bitcast.219), calls=%async_computation.4 | async-start | bytes 4194304 | tf_op jit(solution)/shard_map/all_to_all | solution.py:87
  198.0 1.9 copy-done.2
  204.2 33.5 %shard_map.511 = (bf16[4,512,512]{2,1,0:T(8,128)(2,1)S(1)}, bf16[4,512,256]{2,1,0:T(8,128)(2,1)S(1)}, bf16[4,512,8]{2,1,0:T(8,128)(2,1)S(1)}, f32[4,8,512]{2,1,0...) custom-call(bf16[4,512,768]{2,1,0:T(8,128)(2,1)S(1)} %get-tuple-element.68.x_ref.b_ref.c_ref, ...), custom_call_target="tpu_custom_call" | custom-call | bytes 110700000 | tf_op jit(solution)/shard_map/pallas_call | solution.py:508
  243.0 3.1 collective-permute-done.3
  250.0 1.6 copy-done.29
  251.6 1.6 copy-done.31
  254.2 7.0 %shard_map.512 = bf16[2048,1024]{1,0:T(8,128)(2,1)S(1)} custom-call(bf16[2048,512]{1,0:T(8,128)(2,1)S(1)} %bitcast.207, bf16[2048,512]{1,0:T(8,128)(2,1)S(1)} %bitcast.208, bf16[2048,8]{1,0:T(8,128)(2,1)S(1)} %bitcast.213, bf16[1024,512]{1,0:T(8,128)(2,1)S(1)} %copy-done.24, bf16[1024,512]{1,0:T(8,128)(2,1)S(1)} %copy-done.26, ...), custom_call_target="tpu_custom_call" | custom-call | bytes 22140000 | tf_op jit(solution)/shard_map/pallas_call | solution.py:630
  261.3 2.0 copy-done.10
  263.3 1.5 dynamic-slice_bitcast_fusion
  266.3 13.0 %collective-permute-done.8 = bf16[1024,256]{1,0:T(8,128)(2,1)S(1)} collective-permute-done((bf16[1024,256]{1,0:T(8,128)(2,1)S(1)}, bf16[1024,256]{1,0:T(8,128)(2,1)S(1)}, u32[]{:S(2)}, u32[]{:S(2)}) %collective-permute-start.8) | collective-permute-done | bytes 524320 | tf_op jit(solution)/shard_map/ppermute | solution.py:35
  280.3 2.8 reduce_sum.75
  283.1 4.7 %add_convert_fusion.1.part_ref = bf16[1024,1024]{1,0:T(8,128)(2,1)} fusion(bf16[1024,1024]{1,0:T(8,128)(2,1)} %collective-permute-done.2, bf16[1024,1024]{1,0:T(8,128)(2,1)} %fusion.4), kind=kLoop, calls=%fused_computation.15 | loop fusion | flops 4194304 | bytes 6291456 | tf_op jit(solution)/shard_map/convert_element_type | solution.py:53
  288.3 3.5 bitcast_convert_fusion
  291.8 4.1 fusion.3
  296.7 5.7 %all-to-all-start.5 = ((bf16[8,128,512]{2,1,0:T(8,128)(2,1)}), bf16[8,128,512]{2,1,0:T(8,128)(2,1)}, u32[]{:S(2)}, u32[]{:S(2)}) async-start(bf16[8,128,512]{2,1,0:T(8,128)(2,1)} %bitcast.227), calls=%async_computation.5 | async-start | bytes 2097152 | tf_op jit(solution)/shard_map/all_to_all | solution.py:87
  305.0 7.3 %shard_map.514 = (bf16[4,512,256]{2,1,0:T(8,128)(2,1)S(1)}, f32[4,8,256]{2,1,0:T(8,128)S(1)}, f32[4,8,256]{2,1,0:T(8,128)S(1)}, f32[8,256]{1,0:T(8,128)S(1)}) custom-call(s32[6]{0:T(128)S(1)} %pad_add_fusion.scalars_ref, bf16[2,512,256]{2,1,0:T(8,128)(2,1)} %bitcast.49.part_ref, bf16[2,512,256]{2,1,0:T(8,128)(2,1)S(1)} %bitcast.214, ...), custom_call_target="tpu_custom_call" | custom-call | bytes 18450000 | tf_op jit(solution)/shard_map/pallas_call | solution.py:582
  315.1 2.2 copy-done.7
  317.2 8.8 %shard_map.513 = bf16[2048,1024]{1,0:T(8,128)(2,1)} custom-call(s32[6]{0:T(128)S(1)} %pad_add_fusion.scalars_ref, bf16[1024,1024]{1,0:T(8,128)(2,1)} %add_convert_fusion.1.part_ref, bf16[1024,1024]{1,0:T(8,128)(2,1)} %collective-permute-done.6.got_ref, bf16[2048,1024]{1,0:T(8,128)(2,1)S(1)} %bitcast.198, f32[2048,1]{1,0:T(8,128)S(1)} %bitcast.206), custom_call_target="tpu_custom_call" | custom-call | bytes 29520000 | tf_op jit(solution)/shard_map/pallas_call | solution.py:692
  326.1 15.9 %all-to-all-done.5 = bf16[8,128,512]{2,1,0:T(8,128)(2,1)} async-done(((bf16[8,128,512]{2,1,0:T(8,128)(2,1)}), bf16[8,128,512]{2,1,0:T(8,128)(2,1)}, u32[]{:S(2)}, u32[]{:S(2)}) %all-to-all-start.5) | async-done | bytes 1048608 | tf_op jit(solution)/shard_map/all_to_all | solution.py:87
  341.9 4.8 %fusion.16 = bf16[1024,256]{1,0:T(8,128)(2,1)} fusion(bf16[4,512,256]{2,1,0:T(8,128)(2,1)S(1)} %fusion.54, bf16[4,512,1024]{2,1,0:T(8,128)(2,1)} %param.30, f32[1024]{0:T(1024)S(1)} %copy-done.47, f32[4,512]{1,0:T(4,128)S(1)} %copy-done.89), kind=kOutput, calls=%fused_computation.54 | convolution fusion | flops 1082392576 | bytes 5779456 | tf_op jit(solution)/shard_map/btd,btc->dc/dot_general | solution.py:931
  346.7 2.8 fusion.91
  349.7 5.6 %multiply_subtract_fusion = (f32[1024,512]{1,0:T(8,128)}, f32[1024,512]{1,0:T(8,128)}, f32[1024,512]{1,0:T(8,128)}) fusion(f32[1024,512]{1,0:T(8,128)S(1)} %copy-done.57, bf16[4,256,512]{2,1,0:T(8,128)(2,1)S(1)} %get-tuple-element.149, f32[1024,512]{1,0:T(8,128)S(1)} %copy-done.58, f32[1024,512]{1,0:T(8,128)} %param.58), kind=kLoop, calls=%fused_computation.39 | loop fusion | flops 8388608 | bytes 13631488 | tf_op jit(solution)/shard_map/sub | solution.py:753
  355.3 2.6 add_convert_fusion.part_ref
  358.0 4.0 all-to-all-start.6
  362.0 2.1 reduce_sum.77
  364.1 13.0 %all-to-all-done.6 = bf16[8,128,256]{2,1,0:T(8,128)(2,1)S(1)} async-done(((bf16[8,128,256]{2,1,0:T(8,128)(2,1)}), bf16[8,128,256]{2,1,0:T(8,128)(2,1)S(1)}, u32[]{:S(2)}, u32[]{:S(2)}) %all-to-all-start.6) | async-done | bytes 524320 | tf_op jit(solution)/shard_map/all_to_all | solution.py:87
  378.0 4.4 all-to-all-start.7
  382.4 3.4 convolution_bitcast_fusion.1
  386.0 2.2 copy-done.8
  388.2 2.2 copy-done.20
  391.6 11.2 %shard_map.515 = (f32[2048,1024]{1,0:T(8,128)}, f32[1,1024]{1,0:T(1,128)S(1)}) custom-call(s32[6]{0:T(128)S(1)} %pad_add_fusion.scalars_ref, bf16[1024,1024]{1,0:T(8,128)(2,1)S(1)} %add_convert_fusion.part_ref, bf16[1024,1024]{1,0:T(8,128)(2,1)} %collective-permute-done.11.got_ref, bf16[2048,256]{1,0:T(8,128)(2,1)S(1)} %bitcast.209, ...), custom_call_target="tpu_custom_call" | custom-call | bytes 29520000 | tf_op jit(solution)/shard_map/pallas_call | solution.py:692
  402.9 2.0 collective-permute-start.12
  407.1 2.0 collective-permute-start.13
  409.1 4.2 multiply_subtract_fusion.1
  413.3 1.5 copy.130
  415.6 2.4 collective-permute-start.14
  418.1 1.5 maximum_bitcast_fusion
  419.6 3.2 copy.132
  423.0 9.7 %shard_map.516 = (f32[1024,8,128]{2,1,0:T(8,128)}, f32[1024,8,128]{2,1,0:T(8,128)}, f32[1024,8,128]{2,1,0:T(8,128)}) custom-call(bf16[1024,8,128]{2,1,0:T(8,128)(2,1)S(1)} %bitcast.203, f32[1024,8,128]{2,1,0:T(8,128)S(1)} %bitcast.200, f32[1024,8,128]{2,1,0:T(8,128)S(1)} %bitcast.205, f32[1024,8,128]{2,1,0:T(8,128)} %bitcast.220), custom_call_target="tpu_custom_call" | custom-call | bytes 33210000 | tf_op jit(solution)/shard_map/pallas_call | solution.py:731
  (319 shorter events, 70.8 us)
Async XLA Ops:
  14.9 11.1 %copy-start.87 = (f32[4,512]{1,0:T(4,128)}, f32[4,512]{1,0:T(4,128)S(1)}, u32[]{:S(2)}) copy-start(f32[4,512]{1,0:T(4,128)S(1)} %add_rsqrt_fusion) | copy-start | bytes 24580
  14.9 10.9 %copy-start.60 = (f32[1024,8]{0,1:T(8,128)S(1)}, f32[1024,8]{0,1:T(8,128)}, u32[]{:S(2)}) copy-start(f32[1024,8]{0,1:T(8,128)} %param.42) | copy-start | bytes 98308
  20.4 11.5 %collective-permute-start = (bf16[4,3,768]{2,1,0:T(4,128)(2,1)S(1)}, bf16[4,3,768]{2,1,0:T(4,128)(2,1)S(1)}, u32[]{:S(2)}, u32[]{:S(2)}) collective-permute-start(bf16[4,3,768]{2,1,0:T(4,128)(2,1)S(1)} %slice.272), channel_id=1, source_target_pairs={{0,4},{4,8},{8,12},{12,16},{16,20},{20,24},{24,28},{1,5},{5,9},{9,... | collective-permute-start | bytes 55304 | tf_op jit(solution)/shard_map/ppermute | solution.py:31
  31.9 12.5 %copy-start.12 = (f32[4,512,8]{2,1,0:T(8,128)}, f32[4,512,8]{2,1,0:T(8,128)S(1)}, u32[]{:S(2)}) copy-start(f32[4,512,8]{2,1,0:T(8,128)S(1)} %get-tuple-element.153.decay_ref) | copy-start | bytes 196612
  31.9 12.5 %copy-start.15 = (f32[4,512,8]{2,1,0:T(8,128)}, f32[4,512,8]{2,1,0:T(8,128)S(1)}, u32[]{:S(2)}) copy-start(f32[4,512,8]{2,1,0:T(8,128)S(1)} %get-tuple-element.154.step_ref) | copy-start | bytes 196612
  45.3 22.0 %all-to-all-start = ((bf16[8,80,512]{2,1,0:T(8,128)(2,1)}), bf16[8,80,512]{2,1,0:T(8,128)(2,1)}, u32[]{:S(2)}, u32[]{:S(2)}) async-start(bf16[8,80,512]{2,1,0:T(8,128)(2,1)} %bitcast.212), calls=%async_computation | async-start | bytes 1310720 | tf_op jit(solution)/shard_map/all_to_all | solution.py:87
  69.2 38.5 %copy-start.75 = (f32[1,1,512]{2,1,0:T(1,128)}, f32[1,1,512]{2,1,0:T(1,128)S(1)}, u32[]{:S(2)}) copy-start(f32[1,1,512]{2,1,0:T(1,128)S(1)} %get-tuple-element.169) | copy-start | bytes 6148
  69.2 38.6 %copy-start.77 = (f32[1,1,512]{2,1,0:T(1,128)}, f32[1,1,512]{2,1,0:T(1,128)S(1)}, u32[]{:S(2)}) copy-start(f32[1,1,512]{2,1,0:T(1,128)S(1)} %get-tuple-element.171) | copy-start | bytes 6148
  73.8 18.6 %all-to-all-start.1 = ((bf16[8,64,512]{2,1,0:T(8,128)(2,1)}), bf16[8,64,512]{2,1,0:T(8,128)(2,1)}, u32[]{:S(2)}, u32[]{:S(2)}) async-start(bf16[8,64,512]{2,1,0:T(8,128)(2,1)} %fusion.48), calls=%async_computation.1 | async-start | bytes 1048576 | tf_op jit(solution)/shard_map/all_to_all | solution.py:87
  78.9 28.9 %copy-start.68 = (f32[8,64]{1,0:T(8,128)}, f32[8,64]{1,0:T(8,128)S(1)}, u32[]{:S(2)}) copy-start(f32[8,64]{1,0:T(8,128)S(1)} %broadcast_in_dim.14) | copy-start | bytes 6148
  94.9 14.9 %copy-start.5 = (bf16[4,512,1024]{2,1,0:T(8,128)(2,1)S(1)}, bf16[4,512,1024]{2,1,0:T(8,128)(2,1)}, u32[]{:S(2)}) copy-start(bf16[4,512,1024]{2,1,0:T(8,128)(2,1)} %param.30) | copy-start | bytes 12582916
  94.9 14.9 %copy-start.54 = (bf16[1024,2,512]{2,0,1:T(8,128)(2,1)S(1)}, bf16[1024,2,512]{2,0,1:T(8,128)(2,1)}, u32[]{:S(2)}) copy-start(bf16[1024,2,512]{2,0,1:T(8,128)(2,1)} %copy-done.53) | copy-start | bytes 6291460
  94.9 14.9 %copy-start.88 = (f32[4,512]{1,0:T(4,128)S(1)}, f32[4,512]{1,0:T(4,128)}, u32[]{:S(2)}) copy-start(f32[4,512]{1,0:T(4,128)} %copy-done.87) | copy-start | bytes 24580
  94.9 14.9 %copy-start.102 = (f32[512]{0:T(512)S(1)}, f32[512]{0:T(512)}, u32[]{:S(2)}) copy-start(f32[512]{0:T(512)} %mul.699) | copy-start | bytes 6148
  147.6 19.1 %all-to-all-start.2 = ((bf16[8,64,512]{2,1,0:T(8,128)(2,1)}), bf16[8,64,512]{2,1,0:T(8,128)(2,1)}, u32[]{:S(2)}, u32[]{:S(2)}) async-start(bf16[8,64,512]{2,1,0:T(8,128)(2,1)} %bitcast.226), calls=%async_computation.2 | async-start | bytes 1048576 | tf_op jit(solution)/shard_map/all_to_all | solution.py:87
  156.1 11.7 %copy-start.74 = (f32[1,1,512]{2,1,0:T(1,128)S(1)}, f32[1,1,512]{2,1,0:T(1,128)}, u32[]{:S(2)}) copy-start(f32[1,1,512]{2,1,0:T(1,128)} %copy-done.73) | copy-start | bytes 6148
  156.1 11.8 %copy-start.76 = (f32[1,1,512]{2,1,0:T(1,128)S(1)}, f32[1,1,512]{2,1,0:T(1,128)}, u32[]{:S(2)}) copy-start(f32[1,1,512]{2,1,0:T(1,128)} %copy-done.75) | copy-start | bytes 6148
  156.1 11.8 %copy-start.78 = (f32[1,1,512]{2,1,0:T(1,128)S(1)}, f32[1,1,512]{2,1,0:T(1,128)}, u32[]{:S(2)}) copy-start(f32[1,1,512]{2,1,0:T(1,128)} %copy-done.77) | copy-start | bytes 6148
  156.1 11.8 %copy-start.79 = (f32[1,1,512]{2,1,0:T(1,128)S(1)}, f32[1,1,512]{2,1,0:T(1,128)}, u32[]{:S(2)}) copy-start(f32[1,1,512]{2,1,0:T(1,128)} %get-tuple-element.166) | copy-start | bytes 6148
  156.1 28.8 %collective-permute-start.1 = (bf16[1024,1024]{1,0:T(8,128)(2,1)}, bf16[1024,1024]{1,0:T(8,128)(2,1)}, u32[]{:S(2)}, u32[]{:S(2)}) collective-permute-start(bf16[1024,1024]{1,0:T(8,128)(2,1)} %dynamic-slice_bitcast_fusion.1), channel_id=1, source_target_pairs={{0,1},{1,0},{2,3},{3,2},{4,5},{5,4},{6,7},{7,6},{8,9},{9,8},{10,11... | collective-permute-start | bytes 6291464 | tf_op jit(solution)/shard_map/ppermute | solution.py:35
  173.9 17.5 %all-to-all-start.3 = ((bf16[8,64,512]{2,1,0:T(8,128)(2,1)}), bf16[8,64,512]{2,1,0:T(8,128)(2,1)}, u32[]{:S(2)}, u32[]{:S(2)}) async-start(bf16[8,64,512]{2,1,0:T(8,128)(2,1)} %constant_dynamic-update-slice_fusion.1), calls=%async_computation.3 | async-start | bytes 1048576 | tf_op jit(solution)/shard_map/all_to_all | solution.py:87
  185.0 12.1 %copy-start.69 = (f32[8,64]{1,0:T(8,128)S(1)}, f32[8,64]{1,0:T(8,128)}, u32[]{:S(2)}) copy-start(f32[8,64]{1,0:T(8,128)} %copy-done.68) | copy-start | bytes 6148
  191.4 51.6 %all-to-all-start.4 = ((bf16[8,256,512]{2,1,0:T(8,128)(2,1)}), bf16[8,256,512]{2,1,0:T(8,128)(2,1)}, u32[]{:S(2)}, u32[]{:S(2)}) async-start(bf16[8,256,512]{2,1,0:T(8,128)(2,1)} %bitcast.219), calls=%async_computation.4 | async-start | bytes 4194304 | tf_op jit(solution)/shard_map/all_to_all | solution.py:87
  196.2 150.5 %all-gather.5.cloned.1.call-start = ((), (), s32[]{:S(2)}) async-start(), calls=%async_computation.8 | async-start | bytes 2359296 | tf_op jit(solution)/shard_map/all_gather | solution.py:893
  196.3 45.8 %collective-permute-start.2 = (bf16[1024,1024]{1,0:T(8,128)(2,1)}, bf16[1024,1024]{1,0:T(8,128)(2,1)}, u32[]{:S(2)}, u32[]{:S(2)}) collective-permute-start(bf16[1024,1024]{1,0:T(8,128)(2,1)} %fusion.4), channel_id=1, source_target_pairs={{0,2},{1,3},{2,0},{3,1},{4,6},{5,7},{6,4},{7,5},{8,10},{9,11},{10,... | collective-permute-start | bytes 6291464 | tf_op jit(solution)/shard_map/ppermute | solution.py:35
  240.1 24.7 %collective-permute-start.7 = (bf16[1024,256]{1,0:T(8,128)(2,1)S(1)}, bf16[1024,256]{1,0:T(8,128)(2,1)S(1)}, u32[]{:S(2)}, u32[]{:S(2)}) collective-permute-start(bf16[1024,256]{1,0:T(8,128)(2,1)S(1)} %dynamic-slice_bitcast_fusion.2), channel_id=1, source_target_pairs={{0,1},{1,0},{2,3},{3,2},{4,5},{5,4},{6,7},{7,6},{8,9},{9,8},{10,11... | collective-permute-start | bytes 1572872 | tf_op jit(solution)/shard_map/ppermute | solution.py:35
  240.2 5.9 %collective-permute-start.3 = (f32[4,3,512]{2,1,0:T(4,128)S(1)}, f32[4,3,512]{2,1,0:T(4,128)S(1)}, u32[]{:S(2)}, u32[]{:S(2)}) collective-permute-start(f32[4,3,512]{2,1,0:T(4,128)S(1)} %pad_maximum_fusion.1), channel_id=1, source_target_pairs={{4,0},{8,4},{12,8},{16,12},{20,16},{24,20},{28,24},{5,1},{9,5},{13... | collective-permute-start | bytes 73736 | tf_op jit(solution)/shard_map/ppermute | solution.py:31
  264.8 27.0 %collective-permute-start.4 = (bf16[1024,1024]{1,0:T(8,128)(2,1)}, bf16[1024,1024]{1,0:T(8,128)(2,1)}, u32[]{:S(2)}, u32[]{:S(2)}) collective-permute-start(bf16[1024,1024]{1,0:T(8,128)(2,1)} %dynamic-slice_bitcast_fusion), channel_id=1, source_target_pairs={{0,1},{1,0},{2,3},{3,2},{4,5},{5,4},{6,7},{7,6},{8,9},{9,8},{10,11... | collective-permute-start | bytes 6291464 | tf_op jit(solution)/shard_map/ppermute | solution.py:35
  265.0 14.4 %collective-permute-start.8 = (bf16[1024,256]{1,0:T(8,128)(2,1)S(1)}, bf16[1024,256]{1,0:T(8,128)(2,1)S(1)}, u32[]{:S(2)}, u32[]{:S(2)}) collective-permute-start(bf16[1024,256]{1,0:T(8,128)(2,1)S(1)} %fusion.25), channel_id=1, source_target_pairs={{0,2},{1,3},{2,0},{3,1},{4,6},{5,7},{6,4},{7,5},{8,10},{9,11},{10,... | collective-permute-start | bytes 1572872 | tf_op jit(solution)/shard_map/ppermute | solution.py:35
  287.8 27.2 %collective-permute-start.6 = (bf16[1024,1024]{1,0:T(8,128)(2,1)}, bf16[1024,1024]{1,0:T(8,128)(2,1)}, u32[]{:S(2)}, u32[]{:S(2)}) collective-permute-start(bf16[1024,1024]{1,0:T(8,128)(2,1)} %add_convert_fusion.1.part_ref), channel_id=1, source_target_pairs={{0,1},{1,0},{2,3},{3,2},{4,5},{5,4},{6,7},{7,6},{8,9},{9,8},{10,11... | collective-permute-start | bytes 6291464 | tf_op jit(solution)/shard_map/ppermute | solution.py:35
  287.8 8.1 %collective-permute-start.9 = (bf16[1024,256]{1,0:T(8,128)(2,1)}, bf16[1024,256]{1,0:T(8,128)(2,1)S(1)}, u32[]{:S(2)}, u32[]{:S(2)}) collective-permute-start(bf16[1024,256]{1,0:T(8,128)(2,1)} %add_convert_fusion.2), channel_id=1, source_target_pairs={{0,1},{1,0},{2,3},{3,2},{4,5},{5,4},{6,7},{7,6},{8,9},{9,8},{10,11... | collective-permute-start | bytes 1572872 | tf_op jit(solution)/shard_map/ppermute | solution.py:35
  291.8 10.7 %copy-start.103 = (s32[4]{0:T(128)S(1)}, s32[4]{0:T(128)}, u32[]{:S(2)}) copy-start(s32[4]{0:T(128)} %param.32) | copy-start | bytes 52
  291.8 10.8 %copy-start.67 = (f32[5,256]{1,0:T(8,128)S(1)}, f32[5,256]{1,0:T(8,128)}, u32[]{:S(2)}) copy-start(f32[5,256]{1,0:T(8,128)} %param.48) | copy-start | bytes 15364
  291.8 12.2 %copy-start.3 = (bf16[4,512,768]{2,1,0:T(8,128)(2,1)S(1)}, bf16[4,512,768]{2,1,0:T(8,128)(2,1)}, u32[]{:S(2)}) copy-start(bf16[4,512,768]{2,1,0:T(8,128)(2,1)} %copy-done) | copy-start | bytes 9437188
  296.7 45.2 %all-to-all-start.5 = ((bf16[8,128,512]{2,1,0:T(8,128)(2,1)}), bf16[8,128,512]{2,1,0:T(8,128)(2,1)}, u32[]{:S(2)}, u32[]{:S(2)}) async-start(bf16[8,128,512]{2,1,0:T(8,128)(2,1)} %bitcast.227), calls=%async_computation.5 | async-start | bytes 2097152 | tf_op jit(solution)/shard_map/all_to_all | solution.py:87
  302.5 12.2 %copy-start.72 = (f32[1,1,4,512]{3,2,1,0:T(4,128)S(1)}, f32[1,1,4,512]{3,2,1,0:T(4,128)}, u32[]{:S(2)}) copy-start(f32[1,1,4,512]{3,2,1,0:T(4,128)} %get-tuple-element.161) | copy-start | bytes 24580
  302.6 52.7 %collective-permute-start.5 = (bf16[1024,1024]{1,0:T(8,128)(2,1)}, bf16[1024,1024]{1,0:T(8,128)(2,1)}, u32[]{:S(2)}, u32[]{:S(2)}) collective-permute-start(bf16[1024,1024]{1,0:T(8,128)(2,1)} %fusion.3), channel_id=1, source_target_pairs={{0,2},{1,3},{2,0},{3,1},{4,6},{5,7},{6,4},{7,5},{8,10},{9,11},{10,... | collective-permute-start | bytes 6291464 | tf_op jit(solution)/shard_map/ppermute | solution.py:35
  313.3 12.7 %collective-permute-start.10 = (f32[4,3,256]{2,1,0:T(4,128)S(1)}, f32[4,3,256]{2,1,0:T(4,128)S(1)}, u32[]{:S(2)}, u32[]{:S(2)}) collective-permute-start(f32[4,3,256]{2,1,0:T(4,128)S(1)} %pad_maximum_fusion.3), channel_id=1, source_target_pairs={{4,0},{8,4},{12,8},{16,12},{20,16},{24,20},{28,24},{5,1},{9,5},{13... | collective-permute-start | bytes 36872 | tf_op jit(solution)/shard_map/ppermute | solution.py:31
  326.0 20.7 %copy-start.36 = (bf16[4,512,256]{2,1,0:T(8,128)(2,1)}, bf16[4,512,256]{2,1,0:T(8,128)(2,1)S(1)}, u32[]{:S(2)}) copy-start(bf16[4,512,256]{2,1,0:T(8,128)(2,1)S(1)} %fusion.54) | copy-start | bytes 3145732
  355.3 27.1 %copy-start.43 = (bf16[4,512,8]{2,1,0:T(8,128)(2,1)S(1)}, bf16[4,512,8]{2,1,0:T(8,128)(2,1)}, u32[]{:S(2)}) copy-start(bf16[4,512,8]{2,1,0:T(8,128)(2,1)} %copy-done.41) | copy-start | bytes 98308
  358.0 28.1 %collective-permute-start.11 = (bf16[1024,1024]{1,0:T(8,128)(2,1)S(1)}, bf16[1024,1024]{1,0:T(8,128)(2,1)}, u32[]{:S(2)}, u32[]{:S(2)}) collective-permute-start(bf16[1024,1024]{1,0:T(8,128)(2,1)S(1)} %add_convert_fusion.part_ref), channel_id=1, source_target_pairs={{0,1},{1,0},{2,3},{3,2},{4,5},{5,4},{6,7},{7,6},{8,9},{9,8},{10,11... | collective-permute-start | bytes 6291464 | tf_op jit(solution)/shard_map/ppermute | solution.py:35
  358.0 19.1 %all-to-all-start.6 = ((bf16[8,128,256]{2,1,0:T(8,128)(2,1)}), bf16[8,128,256]{2,1,0:T(8,128)(2,1)S(1)}, u32[]{:S(2)}, u32[]{:S(2)}) async-start(bf16[8,128,256]{2,1,0:T(8,128)(2,1)} %bitcast.229), calls=%async_computation.6 | async-start | bytes 1048576 | tf_op jit(solution)/shard_map/all_to_all | solution.py:87
  362.0 51.3 %all-gather.7.cloned.1.call-start = ((), (), s32[]{:S(2)}) async-start(), calls=%async_computation.9 | async-start | bytes 1179648 | tf_op jit(solution)/shard_map/all_gather | solution.py:929
  378.0 31.1 %all-to-all-start.7 = ((bf16[8,128,256]{2,1,0:T(8,128)(2,1)}), bf16[8,128,256]{2,1,0:T(8,128)(2,1)}, u32[]{:S(2)}, u32[]{:S(2)}) async-start(bf16[8,128,256]{2,1,0:T(8,128)(2,1)} %broadcast_in_dim.19), calls=%async_computation.7 | async-start | bytes 1048576 | tf_op jit(solution)/shard_map/all_to_all | solution.py:87
  391.6 11.2 %copy-start.95 = (f32[512]{0:T(512)S(1)}, f32[512]{0:T(512)}, u32[]{:S(2)}) copy-start(f32[512]{0:T(512)} %get-tuple-element.145) | copy-start | bytes 6148
  402.9 4.2 collective-permute-start.12
  407.1 8.5 %collective-permute-start.13 = (f32[112,128]{1,0:T(8,128)S(1)}, f32[112,128]{1,0:T(8,128)S(1)}, u32[]{:S(2)}, u32[]{:S(2)}) collective-permute-start(f32[112,128]{1,0:T(8,128)S(1)} %fusion.70), channel_id=1, source_target_pairs={{0,8},{4,12},{8,0},{12,4},{16,24},{20,28},{24,16},{28,20},{1,9},{5... | collective-permute-start | bytes 172040 | tf_op jit(solution)/shard_map/ppermute | solution.py:35
  415.6 17.1 %collective-permute-start.14 = (f32[112,128]{1,0:T(8,128)S(1)}, f32[112,128]{1,0:T(8,128)S(1)}, u32[]{:S(2)}, u32[]{:S(2)}) collective-permute-start(f32[112,128]{1,0:T(8,128)S(1)} %fusion.101), channel_id=1, source_target_pairs={{0,16},{4,20},{8,24},{12,28},{16,0},{20,4},{24,8},{28,12},{1,17},{... | collective-permute-start | bytes 172040 | tf_op jit(solution)/shard_map/ppermute | solution.py:35
  422.8 10.5 %copy-start.93 = (f32[1024]{0:T(1024)S(1)}, f32[1024]{0:T(1024)}, u32[]{:S(2)}) copy-start(f32[1024]{0:T(1024)} %param.35) | copy-start | bytes 12292
  422.8 10.5 %copy-start.94 = (f32[1024]{0:T(1024)S(1)}, f32[1024]{0:T(1024)}, u32[]{:S(2)}) copy-start(f32[1024]{0:T(1024)} %param.34) | copy-start | bytes 12292
  422.8 11.1 %copy-start.61 = (f32[1024,8]{0,1:T(8,128)S(1)}, f32[1024,8]{0,1:T(8,128)}, u32[]{:S(2)}) copy-start(f32[1024,8]{0,1:T(8,128)} %param.42) | copy-start | bytes 98308
  422.9 11.1 %copy-start.70 = (f32[1024,8]{0,1:T(8,128)S(1)}, f32[1024,8]{0,1:T(8,128)}, u32[]{:S(2)}) copy-start(f32[1024,8]{0,1:T(8,128)} %param.44) | copy-start | bytes 98308
  422.9 11.1 %copy-start.71 = (f32[1024,8]{0,1:T(8,128)S(1)}, f32[1024,8]{0,1:T(8,128)}, u32[]{:S(2)}) copy-start(f32[1024,8]{0,1:T(8,128)} %param.43) | copy-start | bytes 98308
  422.9 11.8 %copy-start.63 = (f32[5,512]{1,0:T(8,128)S(1)}, f32[5,512]{1,0:T(8,128)}, u32[]{:S(2)}) copy-start(f32[5,512]{1,0:T(8,128)} %param.45) | copy-start | bytes 30724
  422.9 11.8 %copy-start.82 = (f32[5,512]{1,0:T(8,128)S(1)}, f32[5,512]{1,0:T(8,128)}, u32[]{:S(2)}) copy-start(f32[5,512]{1,0:T(8,128)} %param.47) | copy-start | bytes 30724
  422.9 11.7 %copy-start.83 = (f32[5,512]{1,0:T(8,128)S(1)}, f32[5,512]{1,0:T(8,128)}, u32[]{:S(2)}) copy-start(f32[5,512]{1,0:T(8,128)} %param.46) | copy-start | bytes 30724
  422.9 12.4 %copy-start.84 = (f32[5,256]{1,0:T(8,128)S(1)}, f32[5,256]{1,0:T(8,128)}, u32[]{:S(2)}) copy-start(f32[5,256]{1,0:T(8,128)} %param.50) | copy-start | bytes 15364
  422.9 12.4 %copy-start.85 = (f32[5,256]{1,0:T(8,128)S(1)}, f32[5,256]{1,0:T(8,128)}, u32[]{:S(2)}) copy-start(f32[5,256]{1,0:T(8,128)} %param.49) | copy-start | bytes 15364
  422.9 13.0 %copy-start.92 = (f32[3,8]{1,0:T(4,128)S(1)}, f32[3,8]{1,0:T(4,128)}, u32[]{:S(2)}) copy-start(f32[3,8]{1,0:T(4,128)} %param.51) | copy-start | bytes 292
  422.9 13.0 %copy-start.96 = (f32[3,8]{1,0:T(4,128)S(1)}, f32[3,8]{1,0:T(4,128)}, u32[]{:S(2)}) copy-start(f32[3,8]{1,0:T(4,128)} %param.53) | copy-start | bytes 292
  423.0 13.0 %copy-start.97 = (f32[3,8]{1,0:T(4,128)S(1)}, f32[3,8]{1,0:T(4,128)}, u32[]{:S(2)}) copy-start(f32[3,8]{1,0:T(4,128)} %param.52) | copy-start | bytes 292
  423.0 13.6 %copy-start.99 = (f32[512]{0:T(512)S(1)}, f32[512]{0:T(512)}, u32[]{:S(2)}) copy-start(f32[512]{0:T(512)} %param.54) | copy-start | bytes 6148
  423.0 13.6 %copy-start.100 = (f32[512]{0:T(512)S(1)}, f32[512]{0:T(512)}, u32[]{:S(2)}) copy-start(f32[512]{0:T(512)} %param.56) | copy-start | bytes 6148
  423.0 13.5 %copy-start.101 = (f32[512]{0:T(512)S(1)}, f32[512]{0:T(512)}, u32[]{:S(2)}) copy-start(f32[512]{0:T(512)} %param.55) | copy-start | bytes 6148
  (67 other events, 252.3 us)
Sparse Core Ops, SparseCore 0:
  283.2 63.1 all-gather.4
  365.5 43.8 all-gather.6

commit v8 on v6

--- a/solution.py
+++ b/solution.py
@@ -890,11 +890,13 @@
     )
     projected_half, projected_other = regathered(added(projected, projected_far), "head")
     early_own = jnp.sum(early_parts.astype(F32), axis=0).astype(BF16)
-    early_all = lax.all_gather(early_own, "seq")
     bc_sum = halved(bc_grad.reshape(rows, 2 * state_width), "head")
     x_in_grad = joined_edges(x_raw, x_first, x_last, conv_weight[:, :local_inner])
     bc_far = swapped(bc_sum, "head", axis_masks("head")[-1])
-    x_in_grad, bc_added = lax.optimization_barrier((x_in_grad, added(bc_sum, bc_far)))
+    x_in_grad, bc_added, early_own = lax.optimization_barrier(
+        (x_in_grad, added(bc_sum, bc_far), early_own)
+    )
+    early_all = lax.all_gather(early_own, "seq")
     bc_half, bc_other = regathered(bc_added, "head")
     normed_partial = normed_products(
         gate_grad.reshape(rows, local_inner),
@@ -915,7 +917,6 @@
     scalars = jnp.concatenate(
         [lengths, jnp.stack([seq_index * local_len, near_bit("head", 1)]).astype(jnp.int32)]
     )
-    early_sums = early_all.reshape(2, model_width, local_inner)
     bc_raw_grad, bc_first, bc_last, bc_tap_sums = bc_backward(
         scalars,
         bc_half,
@@ -925,13 +926,12 @@
         taps,
     )
     bc_in_grad = joined_edges(bc_raw_grad, bc_first, bc_last, conv_weight[:, local_inner:])
-    bc_in_grad, x_parts = lax.optimization_barrier((bc_in_grad, x_parts))
     x_own = jnp.sum(x_parts.astype(F32), axis=0).astype(BF16)
-    x_all = lax.all_gather(x_own, "seq")
-    x_sum = x_all.reshape(model_width, local_inner)
     bc_weight_grad = jnp.einsum("btd,btc->dc", normed, bc_in_grad, preferred_element_type=F32)
     bc_blocks = to_blocks(bc_weight_grad, seq_size)
     bc_parts = exchanged(bc_blocks, "seq")
+    early_all, _ = lax.optimization_barrier((early_all, bc_blocks))
+    early_sums = early_all.reshape(2, model_width, local_inner)
     flat_tokens = inputs.reshape(rows, model_width)
     block_out = merge_call(
         out_kernel,
@@ -951,9 +951,11 @@
         LEARNING_RATES[-1],
         WEIGHT_DECAYS[-1],
     )
-    normed_far, block_out, out_updated, _ = lax.optimization_barrier(
-        (normed_far, block_out, out_updated, bc_blocks)
-    )
+    normed_far, block_out, out_updated, _, x_own = lax.optimization_barrier(
+        (normed_far, block_out, out_updated, bc_blocks, x_own)
+    )
+    x_all = lax.all_gather(x_own, "seq")
+    x_sum = x_all.reshape(model_width, local_inner)
     block_out = block_out.reshape(inputs.shape)
     normed_half, normed_other = regathered(added(normed_sum, normed_far), "head")
     input_grad, norm_gain_grad = merge_call(
@@ -981,6 +983,7 @@
             jax.ShapeDtypeStruct((1, model_width), F32),
         ],
     )
+    bc_parts, input_grad = lax.optimization_barrier((bc_parts, input_grad))
     input_grad = input_grad.reshape(inputs.shape)
     bc_own = jnp.sum(bc_parts.astype(F32), axis=0).astype(BF16)
     bc_all = exchanged(jnp.broadcast_to(bc_own[None], bc_parts.shape), "seq")

time: 444 us -> 447 us (level)
  waiting for transfers between devices: 66.1 us -> 70.8 us
    all_gather x1, waiting for transfers between devices: 0.01 us -> 11 us  [shards(): x_all = lax.all_gather(x_own, 'seq')]
    all_to_all x8, waiting for transfers between devices: 38.6 us -> 33.4 us  [exchanged(): return lax.all_to_all(blocks, axis, 0, 0, tiled=True)]
    unnamed x213 -> x217, local copies, waits for them, and re-layouts: 42.6 us -> 39.2 us
  transfers between devices with their start and end apart: 25 -> 25, of which waited for: 9 -> 10; matrix products, arithmetic and copies ran while one was open for 21% -> 21% of each run, Pallas kernels for 18% -> 18%
where the time goes in v8:
time: 447 us; the launch traced here: 438 us
  Pallas kernels  103 us (23%)
  waiting for transfers between devices  70.8 us (16%)
  local copies, waits for them, and re-layouts  61.4 us (14%)
  matrix products  61.2 us (14%)
  starting transfers between devices  58.7 us (13%)
  other arithmetic  57.3 us (13%)
  between operations  15.5 us (3%)
  blocking collectives  10.7 us (2%)
    all_to_all x8, starting transfers between devices, exchanged(): return lax.all_to_all(blocks, axis, 0, 0, tiled=True)  42.3 us
    unnamed x217, local copies, waits for them, and re-layouts  39.2 us
    pallas_call x1, Pallas kernels, scan_backward(): pl.pallas_call(back_kernel, grid=(seqs // GROUP, chunks), in_specs=act_bl...  33.5 us
    all_to_all x8, waiting for transfers between devices, exchanged(): return lax.all_to_all(blocks, axis, 0, 0, tiled=True)  33.4 us
    pallas_call x2, Pallas kernels, merge_call(): pl.pallas_call(kernel, grid_spec=pltpu.PrefetchScalarGridSpec(num_scalar_...  20 us
    convert_element_type x6, other arithmetic, added(): return (a.astype(F32) + b.astype(F32)).astype(BF16)  14.6 us
    ppermute x12, waiting for transfers between devices, swapped(): lax.ppermute(block, axis, [(i, i ^ mask) for i in range(lax.axis_size(axi...  14.4 us
    sub x8, other arithmetic, adam_update(): weight - step_rate * (corrected_mean / (jnp.sqrt(corrected_square) + ADAM...  13.4 us
  transfers between devices with their start and end apart: 25, of which 10 were waited for; matrix products, arithmetic and copies ran while one was open for 21% of the time, Pallas kernels for 18%

profile of v8, /device:TPU:0, one launch (start us, length us, event | category | flops | bytes accessed | tf_op | source)
XLA Modules:
  0.0 438.4 jit_solution(7081653413213379371)
XLA Ops:
  7.2 3.2 fusion
  13.8 2.0 copy-done.4
  15.7 3.7 convolution_convert_fusion.mixed_ref.previous_ref
  19.5 1.7 copy-done
  21.2 4.9 %collective-permute-start = (bf16[4,3,768]{2,1,0:T(4,128)(2,1)S(1)}, bf16[4,3,768]{2,1,0:T(4,128)(2,1)S(1)}, u32[]{:S(2)}, u32[]{:S(2)}) collective-permute-start(bf16[4,3,768]{2,1,0:T(4,128)(2,1)S(1)} %slice.272), channel_id=1, source_target_pairs={{0,4},{4,8},{8,12},{12,16},{16,20},{20,24},{24,28},{1,5},{5,9},{9,... | collective-permute-start | bytes 55304 | tf_op jit(solution)/shard_map/ppermute | solution.py:31
  27.1 5.6 %add_divide_fusion.1 = (f32[4,512,8]{2,1,0:T(8,128)}, f32[4,512,8]{2,1,0:T(8,128)S(1)}, f32[4,512,8]{2,1,0:T(8,128)S(1)}, f32[4,512,8]{2,1,0:T(8,128)}) fusion(f32[8]{0:T(128)S(1)} %get-tuple-element.180, f32[8]{0:T(128)S(1)} %get-tuple-element.181, bf16[1024,8]{1,0:T(8,128)(2,1)S(1)} %copy.113.step_weight_ref, bf16[4,512,1024]{2,1,0:T(8,128)(2,1)} %param.30, ...), kind=kOutput, calls=%fused_computation.71 | convolution fusion | flops 42139648 | bytes 4485184 | tf_op jit(solution)/shard_map/btd,dh->bth/dot_general | solution.py:817
  32.8 12.4 %shard_map.509 = (bf16[4,512,768]{2,1,0:T(8,128)(2,1)S(1)}, bf16[4,2,80,512]{3,2,1,0:T(8,128)(2,1)S(1)}) custom-call(bf16[4,512,768]{2,1,0:T(8,128)(2,1)S(1)} %copy-done.1, bf16[4,512,768]{2,1,0:T(8,128)(2,1)S(1)} %copy-done.1, bf16[4,16,768]{2,1,0:T(8,128)(2,1)S(1)} %pad.20.edge_ref, f32[8,768]{1,0:T(8,128)S(1)} %select_maximum_fusion.taps_ref, ...), custom_call_target="tpu_custom_call" | custom-call | bytes 33210000 | tf_op jit(solution)/shard_map/pallas_call | solution.py:413
  46.1 4.9 %all-to-all-start = ((bf16[8,80,512]{2,1,0:T(8,128)(2,1)}), bf16[8,80,512]{2,1,0:T(8,128)(2,1)}, u32[]{:S(2)}, u32[]{:S(2)}) async-start(bf16[8,80,512]{2,1,0:T(8,128)(2,1)} %bitcast.212), calls=%async_computation | async-start | bytes 1310720 | tf_op jit(solution)/shard_map/all_to_all | solution.py:87
  51.6 16.5 %all-to-all-done = bf16[8,80,512]{2,1,0:T(8,128)(2,1)} async-done(((bf16[8,80,512]{2,1,0:T(8,128)(2,1)}), bf16[8,80,512]{2,1,0:T(8,128)(2,1)}, u32[]{:S(2)}, u32[]{:S(2)}) %all-to-all-start) | async-done | bytes 655392 | tf_op jit(solution)/shard_map/all_to_all | solution.py:87
  74.6 4.3 all-to-all-start.1
  83.8 5.6 %fusion.20 = f32[4,512,8]{1,2,0:T(8,128)} fusion(f32[8]{0:T(128)} %copy-done.103, f32[4,512,8]{2,1,0:T(8,128)} %get-tuple-element.183), kind=kOutput, calls=%fused_computation.56 | convolution fusion | flops 101318656 | bytes 131104 | tf_op jit(solution)/shard_map/ts,bsh->bth/dot_general | solution.py:836
  89.4 3.8 all-to-all-done.1
  95.7 12.8 %shard_map.510 = (f32[4,512,512]{2,1,0:T(8,128)S(1)}, f32[4,4,128,512]{3,2,1,0:T(8,128)S(1)}) custom-call(bf16[4,512,768]{2,1,0:T(8,128)(2,1)S(1)} %get-tuple-element.69.x_ref.b_ref.c_ref, bf16[4,512,768]{2,1,0:T(8,128)(2,1)S(1)} %get-tuple-element.69.x_ref.b_ref.c_ref, bf16[4,512,768]{2,1,0:T(8,128)(2,1)S(1)} %get-tuple-element.69.x_ref.b_ref.c_ref, ...), custom_call_target="tpu_custom_call" | custom-call | bytes 47970000 | tf_op jit(solution)/shard_map/pallas_call | solution.py:446
  108.6 2.0 copy-done.22
  110.6 5.1 %multiply_reduce_fusion.2 = (f32[4,512]{1,0:T(4,128)S(1)}, f32[4,512,512]{2,1,0:T(8,128)S(1)}, f32[4,512,512]{2,1,0:T(8,128)}) fusion(f32[4,512,512]{2,1,0:T(8,128)S(1)} %get-tuple-element.71.y_ref, bf16[4,512,768]{2,1,0:T(8,128)(2,1)S(1)} %get-tuple-element.69.x_ref.b_ref.c_ref, f32[512]{0:T(512)S(1)} %copy-done.101, ...), kind=kOutput, calls=%fused_computation.20 | convolution fusion | flops 2166355968 | bytes 19945472 | tf_op jit(solution)/shard_map/btd,dc->btc/dot_general | solution.py:818
  116.4 4.4 %fusion.90 = (bf16[4,512,1024]{2,1,0:T(8,128)(2,1)}, f32[4,512]{1,0:T(4,128)S(1)}) fusion(f32[4,512]{1,0:T(4,128)S(1)} %copy-done.89, bf16[4,512,1024]{2,1,0:T(8,128)(2,1)S(1)} %copy-done.17, f32[1024,512]{1,0:T(8,128)S(1)} %copy-done.54, f32[4,512,512]{2,1,0:T(8,128)S(1)} %get-tuple-element.138, f32[512]{0:T(512)S(1)} %copy-done.97), kind=kOutput, calls=%fused_computation.189 | convolution fusion | flops 2160588800 | bytes 14698496 | tf_op jit(solution)/shard_map/bti,di->btd/dot_general | solution.py:845
  121.4 10.7 %psum.7 = f32[2,4,512]{2,1,0:T(4,128)S(1)} all-reduce(f32[2,4,512]{2,1,0:T(4,128)} %pad_maximum_fusion.2), channel_id=1, replica_groups=mesh['seq'=8,'head'=4] {'head'}, use_global_device_ids=true, to_apply=%region_3.4 | all-reduce | flops 4096 | bytes 32768 | tf_op jit(solution)/shard_map/psum | solution.py:848
  132.7 10.5 %fusion.15 = (f32[4,512,512]{2,1,0:T(8,128)S(1)}, bf16[4,512,512]{2,1,0:T(8,128)(2,1)}, f32[512]{0:T(512)}) fusion(f32[4,512,512]{2,1,0:T(8,128)} %copy-done.104, f32[4,512]{1,0:T(4,128)S(1)} %fusion.55, f32[512]{0:T(512)} %param.54, f32[4,512,512]{2,1,0:T(8,128)} %get-tuple-element.184, f32[4,512,512]{2,1,0:T(8,128)} %copy-done.21, ...), kind=kOutput, calls=%fused_computation.52 | convolution fusion | flops 2177367552 | bytes 27293696 | tf_op jit(solution)/shard_map/btd,di->bti/dot_general | solution.py:853
  143.2 3.9 multiply_convert_fusion.1
  148.4 5.2 %all-to-all-start.2 = ((bf16[8,64,512]{2,1,0:T(8,128)(2,1)}), bf16[8,64,512]{2,1,0:T(8,128)(2,1)}, u32[]{:S(2)}, u32[]{:S(2)}) async-start(bf16[8,64,512]{2,1,0:T(8,128)(2,1)} %bitcast.226), calls=%async_computation.2 | async-start | bytes 1048576 | tf_op jit(solution)/shard_map/all_to_all | solution.py:87
  153.7 3.2 dynamic-slice_bitcast_fusion.1
  157.0 6.2 %bitcast_convert_fusion.2 = bf16[1024,512]{1,0:T(8,128)(2,1)} fusion(bf16[4,512,1024]{2,1,0:T(8,128)(2,1)S(1)} %copy-done.18, f32[4,512]{1,0:T(4,128)} %copy-done.85, f32[4,512]{1,0:T(4,128)} %compare_convert_fusion, f32[4,512,512]{2,1,0:T(8,128)} %copy-done.104, f32[512]{0:T(512)} %param.54), kind=kOutput, calls=%fused_computation.38 | convolution fusion | flops 2158493696 | bytes 9455616 | tf_op jit(solution)/shard_map/btd,bti->di/dot_general | solution.py:852
  163.2 4.2 all-to-all-done.2
  174.5 4.1 all-to-all-start.3
  178.7 5.5 %bitcast_convert_fusion.1 = bf16[1024,512]{1,0:T(8,128)(2,1)S(1)} fusion(bf16[4,512,512]{2,1,0:T(8,128)(2,1)} %get-tuple-element.146, bf16[4,512,1024]{2,1,0:T(8,128)(2,1)} %param.30, f32[1024]{0:T(1024)S(1)} %copy-done.43, f32[4,512]{1,0:T(4,128)} %copy-done.86), kind=kOutput, calls=%fused_computation.37 | convolution fusion | flops 2156396544 | bytes 7352320 | tf_op jit(solution)/shard_map/btd,btc->dc/dot_general | solution.py:868
  187.1 3.9 fusion.4
  192.0 4.8 %all-to-all-start.4 = ((bf16[8,256,512]{2,1,0:T(8,128)(2,1)}), bf16[8,256,512]{2,1,0:T(8,128)(2,1)}, u32[]{:S(2)}, u32[]{:S(2)}) async-start(bf16[8,256,512]{2,1,0:T(8,128)(2,1)} %bitcast.219), calls=%async_computation.4 | async-start | bytes 4194304 | tf_op jit(solution)/shard_map/all_to_all | solution.py:87
  197.8 1.9 copy-done.2
  204.0 33.5 %shard_map.511 = (bf16[4,512,512]{2,1,0:T(8,128)(2,1)S(1)}, bf16[4,512,256]{2,1,0:T(8,128)(2,1)S(1)}, bf16[4,512,8]{2,1,0:T(8,128)(2,1)S(1)}, f32[4,8,512]{2,1,0...) custom-call(bf16[4,512,768]{2,1,0:T(8,128)(2,1)S(1)} %get-tuple-element.69.x_ref.b_ref.c_ref, ...), custom_call_target="tpu_custom_call" | custom-call | bytes 110700000 | tf_op jit(solution)/shard_map/pallas_call | solution.py:508
  239.0 1.9 collective-permute-done.4
  245.4 9.7 %collective-permute-done.5 = bf16[1024,256]{1,0:T(8,128)(2,1)S(1)} collective-permute-done((bf16[1024,256]{1,0:T(8,128)(2,1)S(1)}, bf16[1024,256]{1,0:T(8,128)(2,1)S(1)}, u32[]{:S(2)}, u32[]{:S(2)}) %collective-permute-start.5) | collective-permute-done | bytes 524320 | tf_op jit(solution)/shard_map/ppermute | solution.py:35
  256.0 2.7 reduce_sum.75
  260.2 1.6 copy-done.28
  261.8 1.6 copy-done.30
  263.4 7.0 %shard_map.512 = bf16[2048,1024]{1,0:T(8,128)(2,1)S(1)} custom-call(bf16[2048,512]{1,0:T(8,128)(2,1)S(1)} %bitcast.207, bf16[2048,512]{1,0:T(8,128)(2,1)S(1)} %bitcast.208, bf16[2048,8]{1,0:T(8,128)(2,1)S(1)} %bitcast.213, bf16[1024,512]{1,0:T(8,128)(2,1)S(1)} %copy-done.23, bf16[1024,512]{1,0:T(8,128)(2,1)S(1)} %copy-done.25, ...), custom_call_target="tpu_custom_call" | custom-call | bytes 22140000 | tf_op jit(solution)/shard_map/pallas_call | solution.py:630
  272.0 4.2 add_convert_fusion.1.part_ref
  276.8 3.5 bitcast_convert_fusion
  280.3 2.3 fusion.3
  284.7 6.0 %all-to-all-start.5 = ((bf16[8,128,512]{2,1,0:T(8,128)(2,1)}), bf16[8,128,512]{2,1,0:T(8,128)(2,1)}, u32[]{:S(2)}, u32[]{:S(2)}) async-start(bf16[8,128,512]{2,1,0:T(8,128)(2,1)} %bitcast.227), calls=%async_computation.5 | async-start | bytes 2097152 | tf_op jit(solution)/shard_map/all_to_all | solution.py:87
  291.8 7.3 %shard_map.514 = (bf16[4,512,256]{2,1,0:T(8,128)(2,1)S(1)}, f32[4,8,256]{2,1,0:T(8,128)S(1)}, f32[4,8,256]{2,1,0:T(8,128)S(1)}, f32[8,256]{1,0:T(8,128)S(1)}) custom-call(s32[6]{0:T(128)S(1)} %pad_add_fusion.scalars_ref, bf16[2,512,256]{2,1,0:T(8,128)(2,1)} %bitcast.49.part_ref, bf16[2,512,256]{2,1,0:T(8,128)(2,1)S(1)} %bitcast.214, ...), custom_call_target="tpu_custom_call" | custom-call | bytes 18450000 | tf_op jit(solution)/shard_map/pallas_call | solution.py:582
  301.9 2.2 copy-done.7
  304.0 8.8 %shard_map.513 = bf16[2048,1024]{1,0:T(8,128)(2,1)} custom-call(s32[6]{0:T(128)S(1)} %pad_add_fusion.scalars_ref, bf16[1024,1024]{1,0:T(8,128)(2,1)} %add_convert_fusion.1.part_ref, bf16[1024,1024]{1,0:T(8,128)(2,1)} %collective-permute-done.8.got_ref, bf16[2048,1024]{1,0:T(8,128)(2,1)S(1)} %bitcast.198, f32[2048,1]{1,0:T(8,128)S(1)} %bitcast.206), custom_call_target="tpu_custom_call" | custom-call | bytes 29520000 | tf_op jit(solution)/shard_map/pallas_call | solution.py:692
  312.9 2.6 fusion.16
  316.4 12.0 %all-gather.5.cloned.1.call-done = bf16[2048,512]{1,0:T(8,128)(2,1)} async-done(((bf16[256,512]{1,0:T(8,128)(2,1)}), bf16[2048,512]{1,0:T(8,128)(2,1)}) %all-gather.5.cloned.1.call-update) | async-done | bytes 2097168 | tf_op jit(solution)/shard_map/all_gather | solution.py:899
  328.5 2.8 fusion.91
  331.3 5.5 %multiply_subtract_fusion = (f32[1024,512]{1,0:T(8,128)}, f32[1024,512]{1,0:T(8,128)}, f32[1024,512]{1,0:T(8,128)}) fusion(f32[1024,512]{1,0:T(8,128)S(1)} %copy-done.55, bf16[4,256,512]{2,1,0:T(8,128)(2,1)S(1)} %get-tuple-element.151, f32[1024,512]{1,0:T(8,128)S(1)} %copy-done.56, f32[1024,512]{1,0:T(8,128)} %param.58), kind=kLoop, calls=%fused_computation.39 | loop fusion | flops 8388608 | bytes 13631488 | tf_op jit(solution)/shard_map/sub | solution.py:753
  336.7 2.1 reduce_sum.76
  338.9 3.2 add_convert_fusion.part_ref
  342.2 9.0 %all-to-all-start.6 = ((bf16[8,128,256]{2,1,0:T(8,128)(2,1)}), bf16[8,128,256]{2,1,0:T(8,128)(2,1)}, u32[]{:S(2)}, u32[]{:S(2)}) async-start(bf16[8,128,256]{2,1,0:T(8,128)(2,1)} %bitcast.57), calls=%async_computation.6 | async-start | bytes 1048576 | tf_op jit(solution)/shard_map/all_to_all | solution.py:87
  351.3 3.4 convolution_bitcast_fusion.1
  354.9 2.2 copy-done.8
  357.0 2.2 copy-done.19
  360.5 11.2 %shard_map.515 = (f32[2048,1024]{1,0:T(8,128)}, f32[1,1024]{1,0:T(1,128)S(1)}) custom-call(s32[6]{0:T(128)S(1)} %pad_add_fusion.scalars_ref, bf16[1024,1024]{1,0:T(8,128)(2,1)S(1)} %add_convert_fusion.part_ref, bf16[1024,1024]{1,0:T(8,128)(2,1)} %collective-permute-done.11.got_ref, bf16[2048,256]{1,0:T(8,128)(2,1)S(1)} %bitcast.209, ...), custom_call_target="tpu_custom_call" | custom-call | bytes 29520000 | tf_op jit(solution)/shard_map/pallas_call | solution.py:692
  371.7 2.1 collective-permute-start.12
  373.8 2.8 collective-permute-done.12
  376.6 1.5 collective-permute-start.13
  379.4 11.0 %all-gather.7.cloned.1.call-done = bf16[1024,512]{1,0:T(8,128)(2,1)} async-done(((bf16[128,512]{1,0:T(8,128)(2,1)}), bf16[1024,512]{1,0:T(8,128)(2,1)}) %all-gather.7.cloned.1.call-update) | async-done | bytes 1048592 | tf_op jit(solution)/shard_map/all_gather | solution.py:957
  390.4 1.5 copy.130
  393.4 1.5 maximum_bitcast_fusion
  394.9 3.2 copy.132
  398.4 9.7 %shard_map.516 = (f32[1024,8,128]{2,1,0:T(8,128)}, f32[1024,8,128]{2,1,0:T(8,128)}, f32[1024,8,128]{2,1,0:T(8,128)}) custom-call(bf16[1024,8,128]{2,1,0:T(8,128)(2,1)S(1)} %bitcast.203, f32[1024,8,128]{2,1,0:T(8,128)S(1)} %bitcast.200, f32[1024,8,128]{2,1,0:T(8,128)S(1)} %bitcast.205, f32[1024,8,128]{2,1,0:T(8,128)} %bitcast.220), custom_call_target="tpu_custom_call" | custom-call | bytes 33210000 | tf_op jit(solution)/shard_map/pallas_call | solution.py:731
  410.2 3.9 all-to-all-start.7
  420.1 7.8 %all-to-all-done.7 = bf16[8,128,256]{2,1,0:T(8,128)(2,1)S(1)} async-done(((bf16[8,128,256]{2,1,0:T(8,128)(2,1)}), bf16[8,128,256]{2,1,0:T(8,128)(2,1)S(1)}, u32[]{:S(2)}, u32[]{:S(2)}) %all-to-all-start.7) | async-done | bytes 524320 | tf_op jit(solution)/shard_map/all_to_all | solution.py:87
  427.9 3.4 multiply_subtract_fusion.1
  (317 shorter events, 69.2 us)
Async XLA Ops:
  10.7 16.1 %copy-start.86 = (f32[4,512]{1,0:T(4,128)}, f32[4,512]{1,0:T(4,128)S(1)}, u32[]{:S(2)}) copy-start(f32[4,512]{1,0:T(4,128)S(1)} %add_rsqrt_fusion) | copy-start | bytes 24580
  21.2 11.5 %collective-permute-start = (bf16[4,3,768]{2,1,0:T(4,128)(2,1)S(1)}, bf16[4,3,768]{2,1,0:T(4,128)(2,1)S(1)}, u32[]{:S(2)}, u32[]{:S(2)}) collective-permute-start(bf16[4,3,768]{2,1,0:T(4,128)(2,1)S(1)} %slice.272), channel_id=1, source_target_pairs={{0,4},{4,8},{8,12},{12,16},{16,20},{20,24},{24,28},{1,5},{5,9},{9,... | collective-permute-start | bytes 55304 | tf_op jit(solution)/shard_map/ppermute | solution.py:31
  32.7 12.5 %copy-start.11 = (f32[4,512,8]{2,1,0:T(8,128)}, f32[4,512,8]{2,1,0:T(8,128)S(1)}, u32[]{:S(2)}) copy-start(f32[4,512,8]{2,1,0:T(8,128)S(1)} %get-tuple-element.155.decay_ref) | copy-start | bytes 196612
  32.7 12.5 %copy-start.14 = (f32[4,512,8]{2,1,0:T(8,128)}, f32[4,512,8]{2,1,0:T(8,128)S(1)}, u32[]{:S(2)}) copy-start(f32[4,512,8]{2,1,0:T(8,128)S(1)} %get-tuple-element.156.step_ref) | copy-start | bytes 196612
  46.1 22.0 %all-to-all-start = ((bf16[8,80,512]{2,1,0:T(8,128)(2,1)}), bf16[8,80,512]{2,1,0:T(8,128)(2,1)}, u32[]{:S(2)}, u32[]{:S(2)}) async-start(bf16[8,80,512]{2,1,0:T(8,128)(2,1)} %bitcast.212), calls=%async_computation | async-start | bytes 1310720 | tf_op jit(solution)/shard_map/all_to_all | solution.py:87
  70.0 38.5 %copy-start.74 = (f32[1,1,512]{2,1,0:T(1,128)}, f32[1,1,512]{2,1,0:T(1,128)S(1)}, u32[]{:S(2)}) copy-start(f32[1,1,512]{2,1,0:T(1,128)S(1)} %get-tuple-element.171) | copy-start | bytes 6148
  70.0 38.5 %copy-start.76 = (f32[1,1,512]{2,1,0:T(1,128)}, f32[1,1,512]{2,1,0:T(1,128)S(1)}, u32[]{:S(2)}) copy-start(f32[1,1,512]{2,1,0:T(1,128)S(1)} %get-tuple-element.173) | copy-start | bytes 6148
  74.6 18.6 %all-to-all-start.1 = ((bf16[8,64,512]{2,1,0:T(8,128)(2,1)}), bf16[8,64,512]{2,1,0:T(8,128)(2,1)}, u32[]{:S(2)}, u32[]{:S(2)}) async-start(bf16[8,64,512]{2,1,0:T(8,128)(2,1)} %fusion.48), calls=%async_computation.1 | async-start | bytes 1048576 | tf_op jit(solution)/shard_map/all_to_all | solution.py:87
  79.7 28.9 %copy-start.67 = (f32[8,64]{1,0:T(8,128)}, f32[8,64]{1,0:T(8,128)S(1)}, u32[]{:S(2)}) copy-start(f32[8,64]{1,0:T(8,128)S(1)} %broadcast_in_dim.14) | copy-start | bytes 6148
  95.7 14.9 %copy-start.5 = (bf16[4,512,1024]{2,1,0:T(8,128)(2,1)S(1)}, bf16[4,512,1024]{2,1,0:T(8,128)(2,1)}, u32[]{:S(2)}) copy-start(bf16[4,512,1024]{2,1,0:T(8,128)(2,1)} %param.30) | copy-start | bytes 12582916
  95.7 14.9 %copy-start.50 = (bf16[1024,2,512]{2,0,1:T(8,128)(2,1)S(1)}, bf16[1024,2,512]{2,0,1:T(8,128)(2,1)}, u32[]{:S(2)}) copy-start(bf16[1024,2,512]{2,0,1:T(8,128)(2,1)} %copy-done.49) | copy-start | bytes 6291460
  95.7 14.9 %copy-start.87 = (f32[4,512]{1,0:T(4,128)S(1)}, f32[4,512]{1,0:T(4,128)}, u32[]{:S(2)}) copy-start(f32[4,512]{1,0:T(4,128)} %copy-done.86) | copy-start | bytes 24580
  95.7 14.9 %copy-start.101 = (f32[512]{0:T(512)S(1)}, f32[512]{0:T(512)}, u32[]{:S(2)}) copy-start(f32[512]{0:T(512)} %mul.699) | copy-start | bytes 6148
  148.4 19.1 %all-to-all-start.2 = ((bf16[8,64,512]{2,1,0:T(8,128)(2,1)}), bf16[8,64,512]{2,1,0:T(8,128)(2,1)}, u32[]{:S(2)}, u32[]{:S(2)}) async-start(bf16[8,64,512]{2,1,0:T(8,128)(2,1)} %bitcast.226), calls=%async_computation.2 | async-start | bytes 1048576 | tf_op jit(solution)/shard_map/all_to_all | solution.py:87
  156.9 11.7 %copy-start.73 = (f32[1,1,512]{2,1,0:T(1,128)S(1)}, f32[1,1,512]{2,1,0:T(1,128)}, u32[]{:S(2)}) copy-start(f32[1,1,512]{2,1,0:T(1,128)} %copy-done.72) | copy-start | bytes 6148
  156.9 11.7 %copy-start.75 = (f32[1,1,512]{2,1,0:T(1,128)S(1)}, f32[1,1,512]{2,1,0:T(1,128)}, u32[]{:S(2)}) copy-start(f32[1,1,512]{2,1,0:T(1,128)} %copy-done.74) | copy-start | bytes 6148
  156.9 11.7 %copy-start.77 = (f32[1,1,512]{2,1,0:T(1,128)S(1)}, f32[1,1,512]{2,1,0:T(1,128)}, u32[]{:S(2)}) copy-start(f32[1,1,512]{2,1,0:T(1,128)} %copy-done.76) | copy-start | bytes 6148
  156.9 11.7 %copy-start.78 = (f32[1,1,512]{2,1,0:T(1,128)S(1)}, f32[1,1,512]{2,1,0:T(1,128)}, u32[]{:S(2)}) copy-start(f32[1,1,512]{2,1,0:T(1,128)} %get-tuple-element.168) | copy-start | bytes 6148
  156.9 28.7 %collective-permute-start.1 = (bf16[1024,1024]{1,0:T(8,128)(2,1)}, bf16[1024,1024]{1,0:T(8,128)(2,1)}, u32[]{:S(2)}, u32[]{:S(2)}) collective-permute-start(bf16[1024,1024]{1,0:T(8,128)(2,1)} %dynamic-slice_bitcast_fusion.1), channel_id=1, source_target_pairs={{0,1},{1,0},{2,3},{3,2},{4,5},{5,4},{6,7},{7,6},{8,9},{9,8},{10,11... | collective-permute-start | bytes 6291464 | tf_op jit(solution)/shard_map/ppermute | solution.py:35
  174.5 17.5 %all-to-all-start.3 = ((bf16[8,64,512]{2,1,0:T(8,128)(2,1)}), bf16[8,64,512]{2,1,0:T(8,128)(2,1)}, u32[]{:S(2)}, u32[]{:S(2)}) async-start(bf16[8,64,512]{2,1,0:T(8,128)(2,1)} %constant_dynamic-update-slice_fusion.1), calls=%async_computation.3 | async-start | bytes 1048576 | tf_op jit(solution)/shard_map/all_to_all | solution.py:87
  185.6 12.1 %copy-start.68 = (f32[8,64]{1,0:T(8,128)S(1)}, f32[8,64]{1,0:T(8,128)}, u32[]{:S(2)}) copy-start(f32[8,64]{1,0:T(8,128)} %copy-done.67) | copy-start | bytes 6148
  192.0 63.9 %all-to-all-start.4 = ((bf16[8,256,512]{2,1,0:T(8,128)(2,1)}), bf16[8,256,512]{2,1,0:T(8,128)(2,1)}, u32[]{:S(2)}, u32[]{:S(2)}) async-start(bf16[8,256,512]{2,1,0:T(8,128)(2,1)} %bitcast.219), calls=%async_computation.4 | async-start | bytes 4194304 | tf_op jit(solution)/shard_map/all_to_all | solution.py:87
  196.9 131.6 %all-gather.5.cloned.1.call-start = ((), (), s32[]{:S(2)}) async-start(), calls=%async_computation.8 | async-start | bytes 2359296 | tf_op jit(solution)/shard_map/all_gather | solution.py:899
  196.9 59.1 %collective-permute-start.2 = (bf16[1024,1024]{1,0:T(8,128)(2,1)}, bf16[1024,1024]{1,0:T(8,128)(2,1)}, u32[]{:S(2)}, u32[]{:S(2)}) collective-permute-start(bf16[1024,1024]{1,0:T(8,128)(2,1)} %fusion.4), channel_id=1, source_target_pairs={{0,2},{1,3},{2,0},{3,1},{4,6},{5,7},{6,4},{7,5},{8,10},{9,11},{10,... | collective-permute-start | bytes 6291464 | tf_op jit(solution)/shard_map/ppermute | solution.py:35
  238.8 21.3 %copy-start.23 = (bf16[1024,512]{1,0:T(8,128)(2,1)S(1)}, bf16[1024,512]{1,0:T(8,128)(2,1)}, u32[]{:S(2)}) copy-start(bf16[1024,512]{1,0:T(8,128)(2,1)} %get-tuple-element.152.z_weight_ref) | copy-start | bytes 3145732
  238.8 21.3 %copy-start.25 = (bf16[1024,512]{1,0:T(8,128)(2,1)S(1)}, bf16[1024,512]{1,0:T(8,128)(2,1)}, u32[]{:S(2)}) copy-start(bf16[1024,512]{1,0:T(8,128)(2,1)} %copy-done.24) | copy-start | bytes 3145732
  238.9 2.0 collective-permute-start.4
  241.0 14.0 %collective-permute-start.5 = (bf16[1024,256]{1,0:T(8,128)(2,1)S(1)}, bf16[1024,256]{1,0:T(8,128)(2,1)S(1)}, u32[]{:S(2)}, u32[]{:S(2)}) collective-permute-start(bf16[1024,256]{1,0:T(8,128)(2,1)S(1)} %fusion.25), channel_id=1, source_target_pairs={{0,2},{1,3},{2,0},{3,1},{4,6},{5,7},{6,4},{7,5},{8,10},{9,11},{10,... | collective-permute-start | bytes 1572872 | tf_op jit(solution)/shard_map/ppermute | solution.py:35
  242.4 17.8 %copy-start.38 = (bf16[4,512,8]{2,1,0:T(8,128)(2,1)S(1)}, bf16[4,512,8]{2,1,0:T(8,128)(2,1)}, u32[]{:S(2)}) copy-start(bf16[4,512,8]{2,1,0:T(8,128)(2,1)} %copy-done.37) | copy-start | bytes 98308
  243.9 14.7 %collective-permute-start.3 = (f32[4,3,512]{2,1,0:T(4,128)}, f32[4,3,512]{2,1,0:T(4,128)}, u32[]{:S(2)}, u32[]{:S(2)}) collective-permute-start(f32[4,3,512]{2,1,0:T(4,128)} %pad_maximum_fusion.1), channel_id=1, source_target_pairs={{4,0},{8,4},{12,8},{16,12},{20,16},{24,20},{28,24},{5,1},{9,5},{13... | collective-permute-start | bytes 73736 | tf_op jit(solution)/shard_map/ppermute | solution.py:31
  270.6 9.6 %collective-permute-start.6 = (bf16[1024,1024]{1,0:T(8,128)(2,1)S(1)}, bf16[1024,1024]{1,0:T(8,128)(2,1)S(1)}, u32[]{:S(2)}, u32[]{:S(2)}) collective-permute-start(bf16[1024,1024]{1,0:T(8,128)(2,1)S(1)} %dynamic-slice_bitcast_fusion), channel_id=1, source_target_pairs={{0,1},{1,0},{2,3},{3,2},{4,5},{5,4},{6,7},{7,6},{8,9},{9,8},{10,11... | collective-permute-start | bytes 6291464 | tf_op jit(solution)/shard_map/ppermute | solution.py:35
  276.2 25.7 %collective-permute-start.8 = (bf16[1024,1024]{1,0:T(8,128)(2,1)}, bf16[1024,1024]{1,0:T(8,128)(2,1)}, u32[]{:S(2)}, u32[]{:S(2)}) collective-permute-start(bf16[1024,1024]{1,0:T(8,128)(2,1)} %add_convert_fusion.1.part_ref), channel_id=1, source_target_pairs={{0,1},{1,0},{2,3},{3,2},{4,5},{5,4},{6,7},{7,6},{8,9},{9,8},{10,11... | collective-permute-start | bytes 6291464 | tf_op jit(solution)/shard_map/ppermute | solution.py:35
  276.2 7.6 %collective-permute-start.9 = (bf16[1024,256]{1,0:T(8,128)(2,1)}, bf16[1024,256]{1,0:T(8,128)(2,1)S(1)}, u32[]{:S(2)}, u32[]{:S(2)}) collective-permute-start(bf16[1024,256]{1,0:T(8,128)(2,1)} %add_convert_fusion.2), channel_id=1, source_target_pairs={{0,1},{1,0},{2,3},{3,2},{4,5},{5,4},{6,7},{7,6},{8,9},{9,8},{10,11... | collective-permute-start | bytes 1572872 | tf_op jit(solution)/shard_map/ppermute | solution.py:35
  282.6 56.3 %collective-permute-start.7 = (bf16[1024,1024]{1,0:T(8,128)(2,1)}, bf16[1024,1024]{1,0:T(8,128)(2,1)}, u32[]{:S(2)}, u32[]{:S(2)}) collective-permute-start(bf16[1024,1024]{1,0:T(8,128)(2,1)} %fusion.3), channel_id=1, source_target_pairs={{0,2},{1,3},{2,0},{3,1},{4,6},{5,7},{6,4},{7,5},{8,10},{9,11},{10,... | collective-permute-start | bytes 6291464 | tf_op jit(solution)/shard_map/ppermute | solution.py:35
  284.7 16.8 %copy-start.71 = (f32[1,1,4,512]{3,2,1,0:T(4,128)S(1)}, f32[1,1,4,512]{3,2,1,0:T(4,128)}, u32[]{:S(2)}) copy-start(f32[1,1,4,512]{3,2,1,0:T(4,128)} %get-tuple-element.163) | copy-start | bytes 24580
  284.7 52.1 %all-to-all-start.5 = ((bf16[8,128,512]{2,1,0:T(8,128)(2,1)}), bf16[8,128,512]{2,1,0:T(8,128)(2,1)}, u32[]{:S(2)}, u32[]{:S(2)}) async-start(bf16[8,128,512]{2,1,0:T(8,128)(2,1)} %bitcast.227), calls=%async_computation.5 | async-start | bytes 2097152 | tf_op jit(solution)/shard_map/all_to_all | solution.py:87
  290.7 99.7 %all-gather.7.cloned.1.call-start = ((), (), s32[]{:S(2)}) async-start(), calls=%async_computation.9 | async-start | bytes 1179648 | tf_op jit(solution)/shard_map/all_gather | solution.py:957
  300.1 12.7 %collective-permute-start.10 = (f32[4,3,256]{2,1,0:T(4,128)S(1)}, f32[4,3,256]{2,1,0:T(4,128)S(1)}, u32[]{:S(2)}, u32[]{:S(2)}) collective-permute-start(f32[4,3,256]{2,1,0:T(4,128)S(1)} %pad_maximum_fusion.3), channel_id=1, source_target_pairs={{4,0},{8,4},{12,8},{16,12},{20,16},{24,20},{28,24},{5,1},{9,5},{13... | collective-permute-start | bytes 36872 | tf_op jit(solution)/shard_map/ppermute | solution.py:31
  316.4 14.8 %copy-start.55 = (f32[1024,512]{1,0:T(8,128)S(1)}, f32[1024,512]{1,0:T(8,128)}, u32[]{:S(2)}) copy-start(f32[1024,512]{1,0:T(8,128)} %param.57) | copy-start | bytes 6291460
  336.7 14.5 %copy-start.39 = (bf16[4,512,8]{2,1,0:T(8,128)(2,1)S(1)}, bf16[4,512,8]{2,1,0:T(8,128)(2,1)}, u32[]{:S(2)}) copy-start(bf16[4,512,8]{2,1,0:T(8,128)(2,1)} %copy-done.37) | copy-start | bytes 98308
  342.1 12.8 %collective-permute-start.11 = (bf16[1024,1024]{1,0:T(8,128)(2,1)S(1)}, bf16[1024,1024]{1,0:T(8,128)(2,1)}, u32[]{:S(2)}, u32[]{:S(2)}) collective-permute-start(bf16[1024,1024]{1,0:T(8,128)(2,1)S(1)} %add_convert_fusion.part_ref), channel_id=1, source_target_pairs={{0,1},{1,0},{2,3},{3,2},{4,5},{5,4},{6,7},{7,6},{8,9},{9,8},{10,11... | collective-permute-start | bytes 6291464 | tf_op jit(solution)/shard_map/ppermute | solution.py:35
  342.2 65.9 %all-to-all-start.6 = ((bf16[8,128,256]{2,1,0:T(8,128)(2,1)}), bf16[8,128,256]{2,1,0:T(8,128)(2,1)}, u32[]{:S(2)}, u32[]{:S(2)}) async-start(bf16[8,128,256]{2,1,0:T(8,128)(2,1)} %bitcast.57), calls=%async_computation.6 | async-start | bytes 1048576 | tf_op jit(solution)/shard_map/all_to_all | solution.py:87
  371.7 4.8 %collective-permute-start.12 = (f32[112,128]{1,0:T(8,128)S(1)}, f32[112,128]{1,0:T(8,128)S(1)}, u32[]{:S(2)}, u32[]{:S(2)}) collective-permute-start(f32[112,128]{1,0:T(8,128)S(1)} %pad_bitcast_fusion), channel_id=1, source_target_pairs={{0,4},{4,0},{8,12},{12,8},{16,20},{20,16},{24,28},{28,24},{1,5},{5... | collective-permute-start | bytes 172040 | tf_op jit(solution)/shard_map/ppermute | solution.py:35
  376.6 16.1 %collective-permute-start.13 = (f32[112,128]{1,0:T(8,128)S(1)}, f32[112,128]{1,0:T(8,128)S(1)}, u32[]{:S(2)}, u32[]{:S(2)}) collective-permute-start(f32[112,128]{1,0:T(8,128)S(1)} %fusion.70), channel_id=1, source_target_pairs={{0,8},{4,12},{8,0},{12,4},{16,24},{20,28},{24,16},{28,20},{1,9},{5... | collective-permute-start | bytes 172040 | tf_op jit(solution)/shard_map/ppermute | solution.py:35
  392.7 21.4 %collective-permute-start.14 = (f32[112,128]{1,0:T(8,128)S(1)}, f32[112,128]{1,0:T(8,128)S(1)}, u32[]{:S(2)}, u32[]{:S(2)}) collective-permute-start(f32[112,128]{1,0:T(8,128)S(1)} %fusion.101), channel_id=1, source_target_pairs={{0,16},{4,20},{8,24},{12,28},{16,0},{20,4},{24,8},{28,12},{1,17},{... | collective-permute-start | bytes 172040 | tf_op jit(solution)/shard_map/ppermute | solution.py:35
  398.2 17.3 %copy-start.91 = (f32[3,8]{1,0:T(4,128)S(1)}, f32[3,8]{1,0:T(4,128)}, u32[]{:S(2)}) copy-start(f32[3,8]{1,0:T(4,128)} %param.51) | copy-start | bytes 292
  398.2 17.3 %copy-start.95 = (f32[3,8]{1,0:T(4,128)S(1)}, f32[3,8]{1,0:T(4,128)}, u32[]{:S(2)}) copy-start(f32[3,8]{1,0:T(4,128)} %param.53) | copy-start | bytes 292
  398.2 17.3 %copy-start.96 = (f32[3,8]{1,0:T(4,128)S(1)}, f32[3,8]{1,0:T(4,128)}, u32[]{:S(2)}) copy-start(f32[3,8]{1,0:T(4,128)} %param.52) | copy-start | bytes 292
  398.2 18.6 %copy-start.98 = (f32[512]{0:T(512)S(1)}, f32[512]{0:T(512)}, u32[]{:S(2)}) copy-start(f32[512]{0:T(512)} %param.54) | copy-start | bytes 6148
  398.2 18.6 %copy-start.99 = (f32[512]{0:T(512)S(1)}, f32[512]{0:T(512)}, u32[]{:S(2)}) copy-start(f32[512]{0:T(512)} %param.56) | copy-start | bytes 6148
  398.2 18.6 %copy-start.100 = (f32[512]{0:T(512)S(1)}, f32[512]{0:T(512)}, u32[]{:S(2)}) copy-start(f32[512]{0:T(512)} %param.55) | copy-start | bytes 6148
  398.2 19.3 %copy-start.92 = (f32[1024]{0:T(1024)S(1)}, f32[1024]{0:T(1024)}, u32[]{:S(2)}) copy-start(f32[1024]{0:T(1024)} %param.35) | copy-start | bytes 12292
  398.3 19.3 %copy-start.93 = (f32[1024]{0:T(1024)S(1)}, f32[1024]{0:T(1024)}, u32[]{:S(2)}) copy-start(f32[1024]{0:T(1024)} %param.34) | copy-start | bytes 12292
  398.3 19.9 %copy-start.83 = (f32[5,256]{1,0:T(8,128)S(1)}, f32[5,256]{1,0:T(8,128)}, u32[]{:S(2)}) copy-start(f32[5,256]{1,0:T(8,128)} %param.50) | copy-start | bytes 15364
  398.3 19.9 %copy-start.84 = (f32[5,256]{1,0:T(8,128)S(1)}, f32[5,256]{1,0:T(8,128)}, u32[]{:S(2)}) copy-start(f32[5,256]{1,0:T(8,128)} %param.49) | copy-start | bytes 15364
  398.3 20.5 %copy-start.62 = (f32[5,512]{1,0:T(8,128)S(1)}, f32[5,512]{1,0:T(8,128)}, u32[]{:S(2)}) copy-start(f32[5,512]{1,0:T(8,128)} %param.45) | copy-start | bytes 30724
  398.3 20.5 %copy-start.81 = (f32[5,512]{1,0:T(8,128)S(1)}, f32[5,512]{1,0:T(8,128)}, u32[]{:S(2)}) copy-start(f32[5,512]{1,0:T(8,128)} %param.47) | copy-start | bytes 30724
  398.3 20.5 %copy-start.82 = (f32[5,512]{1,0:T(8,128)S(1)}, f32[5,512]{1,0:T(8,128)}, u32[]{:S(2)}) copy-start(f32[5,512]{1,0:T(8,128)} %param.46) | copy-start | bytes 30724
  398.3 21.1 %copy-start.60 = (f32[1024,8]{0,1:T(8,128)S(1)}, f32[1024,8]{0,1:T(8,128)}, u32[]{:S(2)}) copy-start(f32[1024,8]{0,1:T(8,128)} %param.42) | copy-start | bytes 98308
  398.3 21.1 %copy-start.69 = (f32[1024,8]{0,1:T(8,128)S(1)}, f32[1024,8]{0,1:T(8,128)}, u32[]{:S(2)}) copy-start(f32[1024,8]{0,1:T(8,128)} %param.44) | copy-start | bytes 98308
  398.4 21.1 %copy-start.70 = (f32[1024,8]{0,1:T(8,128)S(1)}, f32[1024,8]{0,1:T(8,128)}, u32[]{:S(2)}) copy-start(f32[1024,8]{0,1:T(8,128)} %param.43) | copy-start | bytes 98308
  408.1 19.8 %copy-start.53 = (f32[1024,256]{1,0:T(8,128)S(1)}, f32[1024,256]{1,0:T(8,128)}, u32[]{:S(2)}) copy-start(f32[1024,256]{1,0:T(8,128)} %param.39) | copy-start | bytes 3145732
  408.1 19.8 %copy-start.57 = (f32[1024,256]{1,0:T(8,128)S(1)}, f32[1024,256]{1,0:T(8,128)}, u32[]{:S(2)}) copy-start(f32[1024,256]{1,0:T(8,128)} %param.41) | copy-start | bytes 3145732
  410.2 17.7 %all-to-all-start.7 = ((bf16[8,128,256]{2,1,0:T(8,128)(2,1)}), bf16[8,128,256]{2,1,0:T(8,128)(2,1)S(1)}, u32[]{:S(2)}, u32[]{:S(2)}) async-start(bf16[8,128,256]{2,1,0:T(8,128)(2,1)} %broadcast_in_dim.19), calls=%async_computation.7 | async-start | bytes 1048576 | tf_op jit(solution)/shard_map/all_to_all | solution.py:87
  (66 other events, 276.0 us)
Sparse Core Ops, SparseCore 0:
  260.3 68.1 all-gather.4
  342.3 48.0 all-gather.6

commit v9 on v8

--- a/solution.py
+++ b/solution.py
@@ -986,6 +986,7 @@
     bc_parts, input_grad = lax.optimization_barrier((bc_parts, input_grad))
     input_grad = input_grad.reshape(inputs.shape)
     bc_own = jnp.sum(bc_parts.astype(F32), axis=0).astype(BF16)
+    x_sum, bc_own = lax.optimization_barrier((x_sum, bc_own))
     bc_all = exchanged(jnp.broadcast_to(bc_own[None], bc_parts.shape), "seq")
     step_weight_grad = jnp.einsum("btd,bth->hd", normed, step_in_grad, preferred_element_type=F32)
     conv_inner_grad = x_tap_sums[: CONV + 1]

time: 447 us -> 443 us (level)
  waiting for transfers between devices: 70.8 us -> 62 us
    all_to_all x8, waiting for transfers between devices: 33.4 us -> 25.7 us  [exchanged(): return lax.all_to_all(blocks, axis, 0, 0, tiled=True)]
    unnamed x217 -> x209, local copies, waits for them, and re-layouts: 39.2 us -> 43.5 us
  transfers between devices with their start and end apart: 25 -> 25, of which waited for: 10 -> 9; matrix products, arithmetic and copies ran while one was open for 21% -> 22% of each run, Pallas kernels for 18% -> 18%
where the time goes in v9:
time: 443 us; the launch traced here: 435 us
  Pallas kernels  103 us (23%)
  local copies, waits for them, and re-layouts  64.8 us (15%)
  waiting for transfers between devices  62 us (14%)
  matrix products  61.2 us (14%)
  other arithmetic  59 us (13%)
  starting transfers between devices  58.9 us (13%)
  between operations  15.4 us (3%)
  blocking collectives  10.7 us (2%)
    unnamed x209, local copies, waits for them, and re-layouts  43.5 us
    all_to_all x8, starting transfers between devices, exchanged(): return lax.all_to_all(blocks, axis, 0, 0, tiled=True)  42.6 us
    pallas_call x1, Pallas kernels, scan_backward(): pl.pallas_call(back_kernel, grid=(seqs // GROUP, chunks), in_specs=act_bl...  33.5 us
    all_to_all x8, waiting for transfers between devices, exchanged(): return lax.all_to_all(blocks, axis, 0, 0, tiled=True)  25.7 us
    pallas_call x2, Pallas kernels, merge_call(): pl.pallas_call(kernel, grid_spec=pltpu.PrefetchScalarGridSpec(num_scalar_...  19.9 us
    sub x8, other arithmetic, adam_update(): weight - step_rate * (corrected_mean / (jnp.sqrt(corrected_square) + ADAM...  15.3 us
    convert_element_type x6, other arithmetic, added(): return (a.astype(F32) + b.astype(F32)).astype(BF16)  14.6 us
    ppermute x12, waiting for transfers between devices, swapped(): lax.ppermute(block, axis, [(i, i ^ mask) for i in range(lax.axis_size(axi...  14.4 us
  transfers between devices with their start and end apart: 25, of which 9 were waited for; matrix products, arithmetic and copies ran while one was open for 22% of the time, Pallas kernels for 18%

profile of v9, /device:TPU:0, one launch (start us, length us, event | category | flops | bytes accessed | tf_op | source)
XLA Modules:
  0.0 434.9 jit_solution(9630300033242065024)
XLA Ops:
  7.2 3.2 fusion
  13.8 2.0 copy-done.4
  15.7 3.7 convolution_convert_fusion.mixed_ref.previous_ref
  19.5 1.7 copy-done
  21.2 4.9 %collective-permute-start = (bf16[4,3,768]{2,1,0:T(4,128)(2,1)S(1)}, bf16[4,3,768]{2,1,0:T(4,128)(2,1)S(1)}, u32[]{:S(2)}, u32[]{:S(2)}) collective-permute-start(bf16[4,3,768]{2,1,0:T(4,128)(2,1)S(1)} %slice.272), channel_id=1, source_target_pairs={{0,4},{4,8},{8,12},{12,16},{16,20},{20,24},{24,28},{1,5},{5,9},{9,... | collective-permute-start | bytes 55304 | tf_op jit(solution)/shard_map/ppermute | solution.py:31
  27.1 5.6 %add_divide_fusion.1 = (f32[4,512,8]{2,1,0:T(8,128)}, f32[4,512,8]{2,1,0:T(8,128)S(1)}, f32[4,512,8]{2,1,0:T(8,128)S(1)}, f32[4,512,8]{2,1,0:T(8,128)}) fusion(f32[8]{0:T(128)S(1)} %get-tuple-element.184, f32[8]{0:T(128)S(1)} %get-tuple-element.185, bf16[1024,8]{1,0:T(8,128)(2,1)S(1)} %copy.113.step_weight_ref, bf16[4,512,1024]{2,1,0:T(8,128)(2,1)} %param.30, ...), kind=kOutput, calls=%fused_computation.71 | convolution fusion | flops 42139648 | bytes 4485184 | tf_op jit(solution)/shard_map/btd,dh->bth/dot_general | solution.py:817
  32.8 12.4 %shard_map.509 = (bf16[4,512,768]{2,1,0:T(8,128)(2,1)S(1)}, bf16[4,2,80,512]{3,2,1,0:T(8,128)(2,1)S(1)}) custom-call(bf16[4,512,768]{2,1,0:T(8,128)(2,1)S(1)} %copy-done.1, bf16[4,512,768]{2,1,0:T(8,128)(2,1)S(1)} %copy-done.1, bf16[4,16,768]{2,1,0:T(8,128)(2,1)S(1)} %pad.20.edge_ref, f32[8,768]{1,0:T(8,128)S(1)} %select_maximum_fusion.taps_ref, ...), custom_call_target="tpu_custom_call" | custom-call | bytes 33210000 | tf_op jit(solution)/shard_map/pallas_call | solution.py:413
  46.1 4.9 %all-to-all-start = ((bf16[8,80,512]{2,1,0:T(8,128)(2,1)}), bf16[8,80,512]{2,1,0:T(8,128)(2,1)}, u32[]{:S(2)}, u32[]{:S(2)}) async-start(bf16[8,80,512]{2,1,0:T(8,128)(2,1)} %bitcast.212), calls=%async_computation | async-start | bytes 1310720 | tf_op jit(solution)/shard_map/all_to_all | solution.py:87
  51.6 16.5 %all-to-all-done = bf16[8,80,512]{2,1,0:T(8,128)(2,1)} async-done(((bf16[8,80,512]{2,1,0:T(8,128)(2,1)}), bf16[8,80,512]{2,1,0:T(8,128)(2,1)}, u32[]{:S(2)}, u32[]{:S(2)}) %all-to-all-start) | async-done | bytes 655392 | tf_op jit(solution)/shard_map/all_to_all | solution.py:87
  74.6 4.3 all-to-all-start.1
  83.8 5.6 %fusion.20 = f32[4,512,8]{1,2,0:T(8,128)} fusion(f32[8]{0:T(128)} %copy-done.99, f32[4,512,8]{2,1,0:T(8,128)} %get-tuple-element.187), kind=kOutput, calls=%fused_computation.56 | convolution fusion | flops 101318656 | bytes 131104 | tf_op jit(solution)/shard_map/ts,bsh->bth/dot_general | solution.py:836
  89.4 3.8 all-to-all-done.1
  95.7 12.8 %shard_map.510 = (f32[4,512,512]{2,1,0:T(8,128)S(1)}, f32[4,4,128,512]{3,2,1,0:T(8,128)S(1)}) custom-call(bf16[4,512,768]{2,1,0:T(8,128)(2,1)S(1)} %get-tuple-element.71.x_ref.b_ref.c_ref, bf16[4,512,768]{2,1,0:T(8,128)(2,1)S(1)} %get-tuple-element.71.x_ref.b_ref.c_ref, bf16[4,512,768]{2,1,0:T(8,128)(2,1)S(1)} %get-tuple-element.71.x_ref.b_ref.c_ref, ...), custom_call_target="tpu_custom_call" | custom-call | bytes 47970000 | tf_op jit(solution)/shard_map/pallas_call | solution.py:446
  108.6 2.0 copy-done.22
  110.6 5.1 %multiply_reduce_fusion.2 = (f32[4,512]{1,0:T(4,128)S(1)}, f32[4,512,512]{2,1,0:T(8,128)S(1)}, f32[4,512,512]{2,1,0:T(8,128)}) fusion(f32[4,512,512]{2,1,0:T(8,128)S(1)} %get-tuple-element.73.y_ref, bf16[4,512,768]{2,1,0:T(8,128)(2,1)S(1)} %get-tuple-element.71.x_ref.b_ref.c_ref, f32[512]{0:T(512)S(1)} %copy-done.97, ...), kind=kOutput, calls=%fused_computation.20 | convolution fusion | flops 2166355968 | bytes 19945472 | tf_op jit(solution)/shard_map/btd,dc->btc/dot_general | solution.py:818
  116.3 4.4 %fusion.90 = (bf16[4,512,1024]{2,1,0:T(8,128)(2,1)}, f32[4,512]{1,0:T(4,128)S(1)}) fusion(f32[4,512]{1,0:T(4,128)S(1)} %copy-done.86, bf16[4,512,1024]{2,1,0:T(8,128)(2,1)S(1)} %copy-done.17, f32[1024,512]{1,0:T(8,128)S(1)} %copy-done.54, f32[4,512,512]{2,1,0:T(8,128)S(1)} %get-tuple-element.142, f32[512]{0:T(512)S(1)} %copy-done.93), kind=kOutput, calls=%fused_computation.189 | convolution fusion | flops 2160588800 | bytes 14698496 | tf_op jit(solution)/shard_map/bti,di->btd/dot_general | solution.py:845
  121.4 10.7 %psum.7 = f32[2,4,512]{2,1,0:T(4,128)S(1)} all-reduce(f32[2,4,512]{2,1,0:T(4,128)} %pad_maximum_fusion.2), channel_id=1, replica_groups=mesh['seq'=8,'head'=4] {'head'}, use_global_device_ids=true, to_apply=%region_3.4 | all-reduce | flops 4096 | bytes 32768 | tf_op jit(solution)/shard_map/psum | solution.py:848
  132.7 10.5 %fusion.15 = (f32[4,512,512]{2,1,0:T(8,128)S(1)}, bf16[4,512,512]{2,1,0:T(8,128)(2,1)}, f32[512]{0:T(512)}) fusion(f32[4,512,512]{2,1,0:T(8,128)} %copy-done.100, f32[4,512]{1,0:T(4,128)S(1)} %fusion.55, f32[512]{0:T(512)} %param.54, f32[4,512,512]{2,1,0:T(8,128)} %get-tuple-element.188, f32[4,512,512]{2,1,0:T(8,128)} %copy-done.21, ...), kind=kOutput, calls=%fused_computation.52 | convolution fusion | flops 2177367552 | bytes 27293696 | tf_op jit(solution)/shard_map/btd,di->bti/dot_general | solution.py:853
  143.2 3.9 multiply_convert_fusion.1
  148.4 5.2 %all-to-all-start.2 = ((bf16[8,64,512]{2,1,0:T(8,128)(2,1)}), bf16[8,64,512]{2,1,0:T(8,128)(2,1)}, u32[]{:S(2)}, u32[]{:S(2)}) async-start(bf16[8,64,512]{2,1,0:T(8,128)(2,1)} %bitcast.226), calls=%async_computation.2 | async-start | bytes 1048576 | tf_op jit(solution)/shard_map/all_to_all | solution.py:87
  153.6 3.2 dynamic-slice_bitcast_fusion.1
  157.0 6.2 %bitcast_convert_fusion.2 = bf16[1024,512]{1,0:T(8,128)(2,1)} fusion(bf16[4,512,1024]{2,1,0:T(8,128)(2,1)S(1)} %copy-done.18, f32[4,512]{1,0:T(4,128)} %copy-done.82, f32[4,512]{1,0:T(4,128)} %compare_convert_fusion, f32[4,512,512]{2,1,0:T(8,128)} %copy-done.100, f32[512]{0:T(512)} %param.54), kind=kOutput, calls=%fused_computation.38 | convolution fusion | flops 2158493696 | bytes 9455616 | tf_op jit(solution)/shard_map/btd,bti->di/dot_general | solution.py:852
  163.2 4.3 all-to-all-done.2
  174.5 4.1 all-to-all-start.3
  178.6 5.4 %bitcast_convert_fusion.1 = bf16[1024,512]{1,0:T(8,128)(2,1)S(1)} fusion(bf16[4,512,512]{2,1,0:T(8,128)(2,1)} %get-tuple-element.150, bf16[4,512,1024]{2,1,0:T(8,128)(2,1)} %param.30, f32[1024]{0:T(1024)S(1)} %copy-done.43, f32[4,512]{1,0:T(4,128)} %copy-done.83), kind=kOutput, calls=%fused_computation.37 | convolution fusion | flops 2156396544 | bytes 7352320 | tf_op jit(solution)/shard_map/btd,btc->dc/dot_general | solution.py:868
  187.1 3.9 fusion.4
  192.0 4.8 %all-to-all-start.4 = ((bf16[8,256,512]{2,1,0:T(8,128)(2,1)}), bf16[8,256,512]{2,1,0:T(8,128)(2,1)}, u32[]{:S(2)}, u32[]{:S(2)}) async-start(bf16[8,256,512]{2,1,0:T(8,128)(2,1)} %bitcast.219), calls=%async_computation.4 | async-start | bytes 4194304 | tf_op jit(solution)/shard_map/all_to_all | solution.py:87
  197.8 1.9 copy-done.2
  204.0 33.5 %shard_map.511 = (bf16[4,512,512]{2,1,0:T(8,128)(2,1)S(1)}, bf16[4,512,256]{2,1,0:T(8,128)(2,1)S(1)}, bf16[4,512,8]{2,1,0:T(8,128)(2,1)S(1)}, f32[4,8,512]{2,1,0...) custom-call(bf16[4,512,768]{2,1,0:T(8,128)(2,1)S(1)} %get-tuple-element.71.x_ref.b_ref.c_ref, ...), custom_call_target="tpu_custom_call" | custom-call | bytes 110700000 | tf_op jit(solution)/shard_map/pallas_call | solution.py:508
  238.9 1.9 collective-permute-done.4
  245.3 9.7 %collective-permute-done.5 = bf16[1024,256]{1,0:T(8,128)(2,1)S(1)} collective-permute-done((bf16[1024,256]{1,0:T(8,128)(2,1)S(1)}, bf16[1024,256]{1,0:T(8,128)(2,1)S(1)}, u32[]{:S(2)}, u32[]{:S(2)}) %collective-permute-start.5) | collective-permute-done | bytes 524320 | tf_op jit(solution)/shard_map/ppermute | solution.py:35
  255.9 2.7 reduce_sum.75
  260.1 1.6 copy-done.28
  261.7 1.6 copy-done.30
  263.3 7.0 %shard_map.512 = bf16[2048,1024]{1,0:T(8,128)(2,1)S(1)} custom-call(bf16[2048,512]{1,0:T(8,128)(2,1)S(1)} %bitcast.207, bf16[2048,512]{1,0:T(8,128)(2,1)S(1)} %bitcast.208, bf16[2048,8]{1,0:T(8,128)(2,1)S(1)} %bitcast.213, bf16[1024,512]{1,0:T(8,128)(2,1)S(1)} %copy-done.23, bf16[1024,512]{1,0:T(8,128)(2,1)S(1)} %copy-done.25, ...), custom_call_target="tpu_custom_call" | custom-call | bytes 22140000 | tf_op jit(solution)/shard_map/pallas_call | solution.py:630
  272.0 4.2 add_convert_fusion.1.part_ref
  276.8 3.5 bitcast_convert_fusion
  280.3 2.3 fusion.3
  284.6 6.0 %all-to-all-start.5 = ((bf16[8,128,512]{2,1,0:T(8,128)(2,1)}), bf16[8,128,512]{2,1,0:T(8,128)(2,1)}, u32[]{:S(2)}, u32[]{:S(2)}) async-start(bf16[8,128,512]{2,1,0:T(8,128)(2,1)} %bitcast.227), calls=%async_computation.5 | async-start | bytes 2097152 | tf_op jit(solution)/shard_map/all_to_all | solution.py:87
  291.8 7.3 %shard_map.514 = (bf16[4,512,256]{2,1,0:T(8,128)(2,1)S(1)}, f32[4,8,256]{2,1,0:T(8,128)S(1)}, f32[4,8,256]{2,1,0:T(8,128)S(1)}, f32[8,256]{1,0:T(8,128)S(1)}) custom-call(s32[6]{0:T(128)S(1)} %pad_add_fusion.scalars_ref, bf16[2,512,256]{2,1,0:T(8,128)(2,1)} %bitcast.49.part_ref, bf16[2,512,256]{2,1,0:T(8,128)(2,1)S(1)} %bitcast.214, ...), custom_call_target="tpu_custom_call" | custom-call | bytes 18450000 | tf_op jit(solution)/shard_map/pallas_call | solution.py:582
  301.8 2.2 copy-done.7
  304.0 8.8 %shard_map.513 = bf16[2048,1024]{1,0:T(8,128)(2,1)} custom-call(s32[6]{0:T(128)S(1)} %pad_add_fusion.scalars_ref, bf16[1024,1024]{1,0:T(8,128)(2,1)} %add_convert_fusion.1.part_ref, bf16[1024,1024]{1,0:T(8,128)(2,1)} %collective-permute-done.8.got_ref, bf16[2048,1024]{1,0:T(8,128)(2,1)S(1)} %bitcast.198, f32[2048,1]{1,0:T(8,128)S(1)} %bitcast.206), custom_call_target="tpu_custom_call" | custom-call | bytes 29520000 | tf_op jit(solution)/shard_map/pallas_call | solution.py:692
  312.8 2.6 fusion.16
  316.4 12.0 %all-gather.5.cloned.1.call-done = bf16[2048,512]{1,0:T(8,128)(2,1)} async-done(((bf16[256,512]{1,0:T(8,128)(2,1)}), bf16[2048,512]{1,0:T(8,128)(2,1)}) %all-gather.5.cloned.1.call-update) | async-done | bytes 2097168 | tf_op jit(solution)/shard_map/all_gather | solution.py:899
  328.4 2.8 fusion.91
  331.2 5.5 %multiply_subtract_fusion = (f32[1024,512]{1,0:T(8,128)}, f32[1024,512]{1,0:T(8,128)}, f32[1024,512]{1,0:T(8,128)}) fusion(f32[1024,512]{1,0:T(8,128)S(1)} %copy-done.55, bf16[4,256,512]{2,1,0:T(8,128)(2,1)S(1)} %get-tuple-element.155, f32[1024,512]{1,0:T(8,128)S(1)} %copy-done.56, f32[1024,512]{1,0:T(8,128)} %param.58), kind=kLoop, calls=%fused_computation.39 | loop fusion | flops 8388608 | bytes 13631488 | tf_op jit(solution)/shard_map/sub | solution.py:753
  336.7 2.1 reduce_sum.76
  338.8 3.2 add_convert_fusion.part_ref
  342.2 9.0 %all-to-all-start.6 = ((bf16[8,128,256]{2,1,0:T(8,128)(2,1)}), bf16[8,128,256]{2,1,0:T(8,128)(2,1)}, u32[]{:S(2)}, u32[]{:S(2)}) async-start(bf16[8,128,256]{2,1,0:T(8,128)(2,1)} %bitcast.57), calls=%async_computation.6 | async-start | bytes 1048576 | tf_op jit(solution)/shard_map/all_to_all | solution.py:87
  351.2 3.4 convolution_bitcast_fusion.1
  354.8 2.2 copy-done.8
  357.0 2.2 copy-done.19
  360.4 11.2 %shard_map.515 = (f32[2048,1024]{1,0:T(8,128)}, f32[1,1024]{1,0:T(1,128)S(1)}) custom-call(s32[6]{0:T(128)S(1)} %pad_add_fusion.scalars_ref, bf16[1024,1024]{1,0:T(8,128)(2,1)S(1)} %add_convert_fusion.part_ref, bf16[1024,1024]{1,0:T(8,128)(2,1)} %collective-permute-done.11.got_ref, bf16[2048,256]{1,0:T(8,128)(2,1)S(1)} %bitcast.209, ...), custom_call_target="tpu_custom_call" | custom-call | bytes 29520000 | tf_op jit(solution)/shard_map/pallas_call | solution.py:692
  371.7 2.1 collective-permute-start.12
  373.7 2.8 collective-permute-done.12
  376.5 1.5 collective-permute-start.13
  380.5 9.9 %all-gather.7.cloned.1.call-done = bf16[1024,512]{1,0:T(8,128)(2,1)} async-done(((bf16[128,512]{1,0:T(8,128)(2,1)}), bf16[1024,512]{1,0:T(8,128)(2,1)}) %all-gather.7.cloned.1.call-update) | async-done | bytes 1048592 | tf_op jit(solution)/shard_map/all_gather | solution.py:957
  390.3 1.5 copy.130
  394.9 3.2 copy.132
  398.9 4.2 all-to-all-start.7
  403.1 2.2 copy-done.10
  405.3 2.2 copy-done.20
  407.6 9.8 %shard_map.516 = (f32[1024,8,128]{2,1,0:T(8,128)}, f32[1024,8,128]{2,1,0:T(8,128)}, f32[1024,8,128]{2,1,0:T(8,128)}) custom-call(bf16[1024,8,128]{2,1,0:T(8,128)(2,1)S(1)} %bitcast.203, f32[1024,8,128]{2,1,0:T(8,128)S(1)} %bitcast.200, f32[1024,8,128]{2,1,0:T(8,128)S(1)} %bitcast.205, f32[1024,8,128]{2,1,0:T(8,128)} %bitcast.220), custom_call_target="tpu_custom_call" | custom-call | bytes 33210000 | tf_op jit(solution)/shard_map/pallas_call | solution.py:731
  423.9 3.9 multiply_subtract_fusion.1
  (309 shorter events, 71.0 us)
Async XLA Ops:
  10.7 16.1 %copy-start.83 = (f32[4,512]{1,0:T(4,128)}, f32[4,512]{1,0:T(4,128)S(1)}, u32[]{:S(2)}) copy-start(f32[4,512]{1,0:T(4,128)S(1)} %add_rsqrt_fusion) | copy-start | bytes 24580
  15.7 10.9 %copy-start.58 = (f32[1024,8]{0,1:T(8,128)S(1)}, f32[1024,8]{0,1:T(8,128)}, u32[]{:S(2)}) copy-start(f32[1024,8]{0,1:T(8,128)} %param.42) | copy-start | bytes 98308
  21.2 11.6 %collective-permute-start = (bf16[4,3,768]{2,1,0:T(4,128)(2,1)S(1)}, bf16[4,3,768]{2,1,0:T(4,128)(2,1)S(1)}, u32[]{:S(2)}, u32[]{:S(2)}) collective-permute-start(bf16[4,3,768]{2,1,0:T(4,128)(2,1)S(1)} %slice.272), channel_id=1, source_target_pairs={{0,4},{4,8},{8,12},{12,16},{16,20},{20,24},{24,28},{1,5},{5,9},{9,... | collective-permute-start | bytes 55304 | tf_op jit(solution)/shard_map/ppermute | solution.py:31
  32.7 12.5 %copy-start.11 = (f32[4,512,8]{2,1,0:T(8,128)}, f32[4,512,8]{2,1,0:T(8,128)S(1)}, u32[]{:S(2)}) copy-start(f32[4,512,8]{2,1,0:T(8,128)S(1)} %get-tuple-element.159.decay_ref) | copy-start | bytes 196612
  32.7 12.5 %copy-start.14 = (f32[4,512,8]{2,1,0:T(8,128)}, f32[4,512,8]{2,1,0:T(8,128)S(1)}, u32[]{:S(2)}) copy-start(f32[4,512,8]{2,1,0:T(8,128)S(1)} %get-tuple-element.160.step_ref) | copy-start | bytes 196612
  46.1 22.0 %all-to-all-start = ((bf16[8,80,512]{2,1,0:T(8,128)(2,1)}), bf16[8,80,512]{2,1,0:T(8,128)(2,1)}, u32[]{:S(2)}, u32[]{:S(2)}) async-start(bf16[8,80,512]{2,1,0:T(8,128)(2,1)} %bitcast.212), calls=%async_computation | async-start | bytes 1310720 | tf_op jit(solution)/shard_map/all_to_all | solution.py:87
  70.0 38.5 %copy-start.73 = (f32[1,1,512]{2,1,0:T(1,128)}, f32[1,1,512]{2,1,0:T(1,128)S(1)}, u32[]{:S(2)}) copy-start(f32[1,1,512]{2,1,0:T(1,128)S(1)} %get-tuple-element.175) | copy-start | bytes 6148
  70.0 38.5 %copy-start.75 = (f32[1,1,512]{2,1,0:T(1,128)}, f32[1,1,512]{2,1,0:T(1,128)S(1)}, u32[]{:S(2)}) copy-start(f32[1,1,512]{2,1,0:T(1,128)S(1)} %get-tuple-element.177) | copy-start | bytes 6148
  74.6 18.6 %all-to-all-start.1 = ((bf16[8,64,512]{2,1,0:T(8,128)(2,1)}), bf16[8,64,512]{2,1,0:T(8,128)(2,1)}, u32[]{:S(2)}, u32[]{:S(2)}) async-start(bf16[8,64,512]{2,1,0:T(8,128)(2,1)} %fusion.48), calls=%async_computation.1 | async-start | bytes 1048576 | tf_op jit(solution)/shard_map/all_to_all | solution.py:87
  79.7 28.9 %copy-start.66 = (f32[8,64]{1,0:T(8,128)}, f32[8,64]{1,0:T(8,128)S(1)}, u32[]{:S(2)}) copy-start(f32[8,64]{1,0:T(8,128)S(1)} %broadcast_in_dim.14) | copy-start | bytes 6148
  95.7 14.9 %copy-start.5 = (bf16[4,512,1024]{2,1,0:T(8,128)(2,1)S(1)}, bf16[4,512,1024]{2,1,0:T(8,128)(2,1)}, u32[]{:S(2)}) copy-start(bf16[4,512,1024]{2,1,0:T(8,128)(2,1)} %param.30) | copy-start | bytes 12582916
  95.7 14.9 %copy-start.50 = (bf16[1024,2,512]{2,0,1:T(8,128)(2,1)S(1)}, bf16[1024,2,512]{2,0,1:T(8,128)(2,1)}, u32[]{:S(2)}) copy-start(bf16[1024,2,512]{2,0,1:T(8,128)(2,1)} %copy-done.49) | copy-start | bytes 6291460
  95.7 14.9 %copy-start.84 = (f32[4,512]{1,0:T(4,128)S(1)}, f32[4,512]{1,0:T(4,128)}, u32[]{:S(2)}) copy-start(f32[4,512]{1,0:T(4,128)} %copy-done.83) | copy-start | bytes 24580
  95.7 14.9 %copy-start.97 = (f32[512]{0:T(512)S(1)}, f32[512]{0:T(512)}, u32[]{:S(2)}) copy-start(f32[512]{0:T(512)} %mul.699) | copy-start | bytes 6148
  132.6 10.5 %copy-start.82 = (f32[4,512]{1,0:T(4,128)}, f32[4,512]{1,0:T(4,128)S(1)}, u32[]{:S(2)}) copy-start(f32[4,512]{1,0:T(4,128)S(1)} %get-tuple-element.168) | copy-start | bytes 24580
  132.6 10.5 %copy-start.62 = (f32[4,512,8]{1,2,0:T(8,128)S(1)}, f32[4,512,8]{1,2,0:T(8,128)}, u32[]{:S(2)}) copy-start(f32[4,512,8]{1,2,0:T(8,128)} %fusion.20) | copy-start | bytes 196612
  132.7 10.5 %copy-start.63 = (f32[8,512,1]{1,0,2:T(8,128)S(1)}, f32[8,512,1]{1,0,2:T(8,128)}, u32[]{:S(2)}) copy-start(f32[8,512,1]{1,0,2:T(8,128)} %reshape.778) | copy-start | bytes 49156
  148.4 19.1 %all-to-all-start.2 = ((bf16[8,64,512]{2,1,0:T(8,128)(2,1)}), bf16[8,64,512]{2,1,0:T(8,128)(2,1)}, u32[]{:S(2)}, u32[]{:S(2)}) async-start(bf16[8,64,512]{2,1,0:T(8,128)(2,1)} %bitcast.226), calls=%async_computation.2 | async-start | bytes 1048576 | tf_op jit(solution)/shard_map/all_to_all | solution.py:87
  156.9 11.7 %copy-start.72 = (f32[1,1,512]{2,1,0:T(1,128)S(1)}, f32[1,1,512]{2,1,0:T(1,128)}, u32[]{:S(2)}) copy-start(f32[1,1,512]{2,1,0:T(1,128)} %copy-done.71) | copy-start | bytes 6148
  156.9 11.7 %copy-start.74 = (f32[1,1,512]{2,1,0:T(1,128)S(1)}, f32[1,1,512]{2,1,0:T(1,128)}, u32[]{:S(2)}) copy-start(f32[1,1,512]{2,1,0:T(1,128)} %copy-done.73) | copy-start | bytes 6148
  156.9 11.7 %copy-start.76 = (f32[1,1,512]{2,1,0:T(1,128)S(1)}, f32[1,1,512]{2,1,0:T(1,128)}, u32[]{:S(2)}) copy-start(f32[1,1,512]{2,1,0:T(1,128)} %copy-done.75) | copy-start | bytes 6148
  156.9 11.7 %copy-start.77 = (f32[1,1,512]{2,1,0:T(1,128)S(1)}, f32[1,1,512]{2,1,0:T(1,128)}, u32[]{:S(2)}) copy-start(f32[1,1,512]{2,1,0:T(1,128)} %get-tuple-element.172) | copy-start | bytes 6148
  156.9 28.7 %collective-permute-start.1 = (bf16[1024,1024]{1,0:T(8,128)(2,1)}, bf16[1024,1024]{1,0:T(8,128)(2,1)}, u32[]{:S(2)}, u32[]{:S(2)}) collective-permute-start(bf16[1024,1024]{1,0:T(8,128)(2,1)} %dynamic-slice_bitcast_fusion.1), channel_id=1, source_target_pairs={{0,1},{1,0},{2,3},{3,2},{4,5},{5,4},{6,7},{7,6},{8,9},{9,8},{10,11... | collective-permute-start | bytes 6291464 | tf_op jit(solution)/shard_map/ppermute | solution.py:35
  174.5 17.5 %all-to-all-start.3 = ((bf16[8,64,512]{2,1,0:T(8,128)(2,1)}), bf16[8,64,512]{2,1,0:T(8,128)(2,1)}, u32[]{:S(2)}, u32[]{:S(2)}) async-start(bf16[8,64,512]{2,1,0:T(8,128)(2,1)} %constant_dynamic-update-slice_fusion.1), calls=%async_computation.3 | async-start | bytes 1048576 | tf_op jit(solution)/shard_map/all_to_all | solution.py:87
  185.6 12.1 %copy-start.67 = (f32[8,64]{1,0:T(8,128)S(1)}, f32[8,64]{1,0:T(8,128)}, u32[]{:S(2)}) copy-start(f32[8,64]{1,0:T(8,128)} %copy-done.66) | copy-start | bytes 6148
  192.0 63.9 %all-to-all-start.4 = ((bf16[8,256,512]{2,1,0:T(8,128)(2,1)}), bf16[8,256,512]{2,1,0:T(8,128)(2,1)}, u32[]{:S(2)}, u32[]{:S(2)}) async-start(bf16[8,256,512]{2,1,0:T(8,128)(2,1)} %bitcast.219), calls=%async_computation.4 | async-start | bytes 4194304 | tf_op jit(solution)/shard_map/all_to_all | solution.py:87
  196.8 131.6 %all-gather.5.cloned.1.call-start = ((), (), s32[]{:S(2)}) async-start(), calls=%async_computation.8 | async-start | bytes 2359296 | tf_op jit(solution)/shard_map/all_gather | solution.py:899
  196.9 59.1 %collective-permute-start.2 = (bf16[1024,1024]{1,0:T(8,128)(2,1)}, bf16[1024,1024]{1,0:T(8,128)(2,1)}, u32[]{:S(2)}, u32[]{:S(2)}) collective-permute-start(bf16[1024,1024]{1,0:T(8,128)(2,1)} %fusion.4), channel_id=1, source_target_pairs={{0,2},{1,3},{2,0},{3,1},{4,6},{5,7},{6,4},{7,5},{8,10},{9,11},{10,... | collective-permute-start | bytes 6291464 | tf_op jit(solution)/shard_map/ppermute | solution.py:35
  238.8 21.3 %copy-start.23 = (bf16[1024,512]{1,0:T(8,128)(2,1)S(1)}, bf16[1024,512]{1,0:T(8,128)(2,1)}, u32[]{:S(2)}) copy-start(bf16[1024,512]{1,0:T(8,128)(2,1)} %get-tuple-element.156.z_weight_ref) | copy-start | bytes 3145732
  238.8 21.3 %copy-start.25 = (bf16[1024,512]{1,0:T(8,128)(2,1)S(1)}, bf16[1024,512]{1,0:T(8,128)(2,1)}, u32[]{:S(2)}) copy-start(bf16[1024,512]{1,0:T(8,128)(2,1)} %copy-done.24) | copy-start | bytes 3145732
  238.9 2.0 collective-permute-start.4
  241.0 14.0 %collective-permute-start.5 = (bf16[1024,256]{1,0:T(8,128)(2,1)S(1)}, bf16[1024,256]{1,0:T(8,128)(2,1)S(1)}, u32[]{:S(2)}, u32[]{:S(2)}) collective-permute-start(bf16[1024,256]{1,0:T(8,128)(2,1)S(1)} %fusion.25), channel_id=1, source_target_pairs={{0,2},{1,3},{2,0},{3,1},{4,6},{5,7},{6,4},{7,5},{8,10},{9,11},{10,... | collective-permute-start | bytes 1572872 | tf_op jit(solution)/shard_map/ppermute | solution.py:35
  242.3 17.8 %copy-start.38 = (bf16[4,512,8]{2,1,0:T(8,128)(2,1)S(1)}, bf16[4,512,8]{2,1,0:T(8,128)(2,1)}, u32[]{:S(2)}) copy-start(bf16[4,512,8]{2,1,0:T(8,128)(2,1)} %copy-done.37) | copy-start | bytes 98308
  243.9 14.7 %collective-permute-start.3 = (f32[4,3,512]{2,1,0:T(4,128)}, f32[4,3,512]{2,1,0:T(4,128)}, u32[]{:S(2)}, u32[]{:S(2)}) collective-permute-start(f32[4,3,512]{2,1,0:T(4,128)} %pad_maximum_fusion.1), channel_id=1, source_target_pairs={{4,0},{8,4},{12,8},{16,12},{20,16},{24,20},{28,24},{5,1},{9,5},{13... | collective-permute-start | bytes 73736 | tf_op jit(solution)/shard_map/ppermute | solution.py:31
  270.6 9.6 %collective-permute-start.6 = (bf16[1024,1024]{1,0:T(8,128)(2,1)S(1)}, bf16[1024,1024]{1,0:T(8,128)(2,1)S(1)}, u32[]{:S(2)}, u32[]{:S(2)}) collective-permute-start(bf16[1024,1024]{1,0:T(8,128)(2,1)S(1)} %dynamic-slice_bitcast_fusion), channel_id=1, source_target_pairs={{0,1},{1,0},{2,3},{3,2},{4,5},{5,4},{6,7},{7,6},{8,9},{9,8},{10,11... | collective-permute-start | bytes 6291464 | tf_op jit(solution)/shard_map/ppermute | solution.py:35
  276.1 25.7 %collective-permute-start.8 = (bf16[1024,1024]{1,0:T(8,128)(2,1)}, bf16[1024,1024]{1,0:T(8,128)(2,1)}, u32[]{:S(2)}, u32[]{:S(2)}) collective-permute-start(bf16[1024,1024]{1,0:T(8,128)(2,1)} %add_convert_fusion.1.part_ref), channel_id=1, source_target_pairs={{0,1},{1,0},{2,3},{3,2},{4,5},{5,4},{6,7},{7,6},{8,9},{9,8},{10,11... | collective-permute-start | bytes 6291464 | tf_op jit(solution)/shard_map/ppermute | solution.py:35
  276.2 7.6 %collective-permute-start.9 = (bf16[1024,256]{1,0:T(8,128)(2,1)}, bf16[1024,256]{1,0:T(8,128)(2,1)S(1)}, u32[]{:S(2)}, u32[]{:S(2)}) collective-permute-start(bf16[1024,256]{1,0:T(8,128)(2,1)} %add_convert_fusion.2), channel_id=1, source_target_pairs={{0,1},{1,0},{2,3},{3,2},{4,5},{5,4},{6,7},{7,6},{8,9},{9,8},{10,11... | collective-permute-start | bytes 1572872 | tf_op jit(solution)/shard_map/ppermute | solution.py:35
  280.3 10.5 %copy-start.3 = (bf16[4,512,768]{2,1,0:T(8,128)(2,1)S(1)}, bf16[4,512,768]{2,1,0:T(8,128)(2,1)}, u32[]{:S(2)}) copy-start(bf16[4,512,768]{2,1,0:T(8,128)(2,1)} %copy-done) | copy-start | bytes 9437188
  282.6 56.3 %collective-permute-start.7 = (bf16[1024,1024]{1,0:T(8,128)(2,1)}, bf16[1024,1024]{1,0:T(8,128)(2,1)}, u32[]{:S(2)}, u32[]{:S(2)}) collective-permute-start(bf16[1024,1024]{1,0:T(8,128)(2,1)} %fusion.3), channel_id=1, source_target_pairs={{0,2},{1,3},{2,0},{3,1},{4,6},{5,7},{6,4},{7,5},{8,10},{9,11},{10,... | collective-permute-start | bytes 6291464 | tf_op jit(solution)/shard_map/ppermute | solution.py:35
  284.6 16.8 %copy-start.70 = (f32[1,1,4,512]{3,2,1,0:T(4,128)S(1)}, f32[1,1,4,512]{3,2,1,0:T(4,128)}, u32[]{:S(2)}) copy-start(f32[1,1,4,512]{3,2,1,0:T(4,128)} %get-tuple-element.167) | copy-start | bytes 24580
  284.6 52.1 %all-to-all-start.5 = ((bf16[8,128,512]{2,1,0:T(8,128)(2,1)}), bf16[8,128,512]{2,1,0:T(8,128)(2,1)}, u32[]{:S(2)}, u32[]{:S(2)}) async-start(bf16[8,128,512]{2,1,0:T(8,128)(2,1)} %bitcast.227), calls=%async_computation.5 | async-start | bytes 2097152 | tf_op jit(solution)/shard_map/all_to_all | solution.py:87
  290.7 99.7 %all-gather.7.cloned.1.call-start = ((), (), s32[]{:S(2)}) async-start(), calls=%async_computation.9 | async-start | bytes 1179648 | tf_op jit(solution)/shard_map/all_gather | solution.py:957
  300.1 12.7 %collective-permute-start.10 = (f32[4,3,256]{2,1,0:T(4,128)S(1)}, f32[4,3,256]{2,1,0:T(4,128)S(1)}, u32[]{:S(2)}, u32[]{:S(2)}) collective-permute-start(f32[4,3,256]{2,1,0:T(4,128)S(1)} %pad_maximum_fusion.3), channel_id=1, source_target_pairs={{4,0},{8,4},{12,8},{16,12},{20,16},{24,20},{28,24},{5,1},{9,5},{13... | collective-permute-start | bytes 36872 | tf_op jit(solution)/shard_map/ppermute | solution.py:31
  316.4 14.8 %copy-start.55 = (f32[1024,512]{1,0:T(8,128)S(1)}, f32[1024,512]{1,0:T(8,128)}, u32[]{:S(2)}) copy-start(f32[1024,512]{1,0:T(8,128)} %param.57) | copy-start | bytes 6291460
  336.7 14.5 %copy-start.39 = (bf16[4,512,8]{2,1,0:T(8,128)(2,1)S(1)}, bf16[4,512,8]{2,1,0:T(8,128)(2,1)}, u32[]{:S(2)}) copy-start(bf16[4,512,8]{2,1,0:T(8,128)(2,1)} %copy-done.37) | copy-start | bytes 98308
  342.0 12.8 %collective-permute-start.11 = (bf16[1024,1024]{1,0:T(8,128)(2,1)S(1)}, bf16[1024,1024]{1,0:T(8,128)(2,1)}, u32[]{:S(2)}, u32[]{:S(2)}) collective-permute-start(bf16[1024,1024]{1,0:T(8,128)(2,1)S(1)} %add_convert_fusion.part_ref), channel_id=1, source_target_pairs={{0,1},{1,0},{2,3},{3,2},{4,5},{5,4},{6,7},{7,6},{8,9},{9,8},{10,11... | collective-permute-start | bytes 6291464 | tf_op jit(solution)/shard_map/ppermute | solution.py:35
  342.2 37.2 %all-to-all-start.6 = ((bf16[8,128,256]{2,1,0:T(8,128)(2,1)}), bf16[8,128,256]{2,1,0:T(8,128)(2,1)}, u32[]{:S(2)}, u32[]{:S(2)}) async-start(bf16[8,128,256]{2,1,0:T(8,128)(2,1)} %bitcast.57), calls=%async_computation.6 | async-start | bytes 1048576 | tf_op jit(solution)/shard_map/all_to_all | solution.py:87
  360.4 11.2 %copy-start.90 = (f32[512]{0:T(512)S(1)}, f32[512]{0:T(512)}, u32[]{:S(2)}) copy-start(f32[512]{0:T(512)} %get-tuple-element.151) | copy-start | bytes 6148
  371.7 4.8 %collective-permute-start.12 = (f32[112,128]{1,0:T(8,128)S(1)}, f32[112,128]{1,0:T(8,128)S(1)}, u32[]{:S(2)}, u32[]{:S(2)}) collective-permute-start(f32[112,128]{1,0:T(8,128)S(1)} %pad_bitcast_fusion), channel_id=1, source_target_pairs={{0,4},{4,0},{8,12},{12,8},{16,20},{20,16},{24,28},{28,24},{1,5},{5... | collective-permute-start | bytes 172040 | tf_op jit(solution)/shard_map/ppermute | solution.py:35
  376.5 16.1 %collective-permute-start.13 = (f32[112,128]{1,0:T(8,128)S(1)}, f32[112,128]{1,0:T(8,128)S(1)}, u32[]{:S(2)}, u32[]{:S(2)}) collective-permute-start(f32[112,128]{1,0:T(8,128)S(1)} %fusion.70), channel_id=1, source_target_pairs={{0,8},{4,12},{8,0},{12,4},{16,24},{20,28},{24,16},{28,20},{1,9},{5... | collective-permute-start | bytes 172040 | tf_op jit(solution)/shard_map/ppermute | solution.py:35
  392.6 24.8 %collective-permute-start.14 = (f32[112,128]{1,0:T(8,128)S(1)}, f32[112,128]{1,0:T(8,128)S(1)}, u32[]{:S(2)}, u32[]{:S(2)}) collective-permute-start(f32[112,128]{1,0:T(8,128)S(1)} %fusion.101), channel_id=1, source_target_pairs={{0,16},{4,20},{8,24},{12,28},{16,0},{20,4},{24,8},{28,12},{1,17},{... | collective-permute-start | bytes 172040 | tf_op jit(solution)/shard_map/ppermute | solution.py:35
  398.9 25.0 %all-to-all-start.7 = ((bf16[8,128,256]{2,1,0:T(8,128)(2,1)}), bf16[8,128,256]{2,1,0:T(8,128)(2,1)}, u32[]{:S(2)}, u32[]{:S(2)}) async-start(bf16[8,128,256]{2,1,0:T(8,128)(2,1)} %broadcast_in_dim.19), calls=%async_computation.7 | async-start | bytes 1048576 | tf_op jit(solution)/shard_map/all_to_all | solution.py:87
  407.5 10.4 %copy-start.92 = (f32[3,8]{1,0:T(4,128)S(1)}, f32[3,8]{1,0:T(4,128)}, u32[]{:S(2)}) copy-start(f32[3,8]{1,0:T(4,128)} %param.52) | copy-start | bytes 292
  407.5 11.1 %copy-start.94 = (f32[512]{0:T(512)S(1)}, f32[512]{0:T(512)}, u32[]{:S(2)}) copy-start(f32[512]{0:T(512)} %param.54) | copy-start | bytes 6148
  407.5 11.1 %copy-start.95 = (f32[512]{0:T(512)S(1)}, f32[512]{0:T(512)}, u32[]{:S(2)}) copy-start(f32[512]{0:T(512)} %param.56) | copy-start | bytes 6148
  407.5 11.0 %copy-start.96 = (f32[512]{0:T(512)S(1)}, f32[512]{0:T(512)}, u32[]{:S(2)}) copy-start(f32[512]{0:T(512)} %param.55) | copy-start | bytes 6148
  407.5 11.8 %copy-start.89 = (f32[1024]{0:T(1024)S(1)}, f32[1024]{0:T(1024)}, u32[]{:S(2)}) copy-start(f32[1024]{0:T(1024)} %param.35) | copy-start | bytes 12292
  407.5 13.1 %copy-start.81 = (f32[5,256]{1,0:T(8,128)S(1)}, f32[5,256]{1,0:T(8,128)}, u32[]{:S(2)}) copy-start(f32[5,256]{1,0:T(8,128)} %param.50) | copy-start | bytes 15364
  407.5 14.4 %copy-start.61 = (f32[5,512]{1,0:T(8,128)S(1)}, f32[5,512]{1,0:T(8,128)}, u32[]{:S(2)}) copy-start(f32[5,512]{1,0:T(8,128)} %param.45) | copy-start | bytes 30724
  407.5 14.4 %copy-start.80 = (f32[5,512]{1,0:T(8,128)S(1)}, f32[5,512]{1,0:T(8,128)}, u32[]{:S(2)}) copy-start(f32[5,512]{1,0:T(8,128)} %param.47) | copy-start | bytes 30724
  407.5 15.7 %copy-start.59 = (f32[1024,8]{0,1:T(8,128)S(1)}, f32[1024,8]{0,1:T(8,128)}, u32[]{:S(2)}) copy-start(f32[1024,8]{0,1:T(8,128)} %param.42) | copy-start | bytes 98308
  407.6 15.7 %copy-start.68 = (f32[1024,8]{0,1:T(8,128)S(1)}, f32[1024,8]{0,1:T(8,128)}, u32[]{:S(2)}) copy-start(f32[1024,8]{0,1:T(8,128)} %param.44) | copy-start | bytes 98308
  407.6 15.7 %copy-start.69 = (f32[1024,8]{0,1:T(8,128)S(1)}, f32[1024,8]{0,1:T(8,128)}, u32[]{:S(2)}) copy-start(f32[1024,8]{0,1:T(8,128)} %param.43) | copy-start | bytes 98308
  407.6 16.3 %copy-start.53 = (f32[1024,256]{1,0:T(8,128)S(1)}, f32[1024,256]{1,0:T(8,128)}, u32[]{:S(2)}) copy-start(f32[1024,256]{1,0:T(8,128)} %param.39) | copy-start | bytes 3145732
  (62 other events, 226.1 us)
Sparse Core Ops, SparseCore 0:
  260.2 68.1 all-gather.4
  342.3 48.0 all-gather.6
